TPU v7x, 128 devices: a whole 4x4x4 slice. The times are simulated.
128 devices in a mesh: section: 2 (over core), dp: 64 (over y, z, x).
Axes of the slice: x: 4, y: 4, z: 4, core: 2. Of those that a mesh axis runs over, the one named last changes fastest.
Arguments:
- tokens: bfloat16 [128, 112, 768], P('dp'), may hold values from -6 to 6
- frames: int32 [128], P('dp'), may hold values from 8 to 16, as said below
- visible: int32 [128, 14], P('dp'), may hold values from 0 to 143, as said below
- out_grad: bfloat16 [128, 1152, 384], P('dp'), may hold values from -6 to 6
- enc_vectors: bfloat16 [8, 768], replicated, may hold values from -3 to 3
- enc_qkv: bfloat16 [768, 2304], replicated, may hold values from -0.21875 to 0.21875
- enc_out: bfloat16 [768, 768], replicated, may hold values from -2.5 to 2.5
- enc_up: bfloat16 [768, 3072], replicated, may hold values from -0.21875 to 0.21875
- enc_up_bias: bfloat16 [3072], replicated, may hold values from -3 to 3
- enc_down: bfloat16 [3072, 768], replicated, may hold values from -0.109375 to 0.109375
- proj_weight: bfloat16 [768, 384], replicated, may hold values from -0.21875 to 0.21875
- dec_vectors: bfloat16 [9, 384], replicated, may hold values from -3 to 3
- dec_qkv: bfloat16 [384, 1152], replicated, may hold values from -0.3125 to 0.3125
- dec_out: bfloat16 [384, 384], replicated, may hold values from -6 to 6
- dec_up: bfloat16 [384, 1536], replicated, may hold values from -0.3125 to 0.3125
- dec_up_bias: bfloat16 [1536], replicated, may hold values from -3 to 3
- dec_down: bfloat16 [1536, 384], replicated, may hold values from -0.15625 to 0.15625
- time_pos: bfloat16 [8, 384], replicated, may hold values from -3 to 3
- space_pos: bfloat16 [144, 384], replicated, may hold values from -3 to 3
Outputs:
- decoded: bfloat16 [128, 1152, 384], P('dp', None, 'section')
- token_grad: bfloat16 [128, 112, 768], P('dp', None, 'section')
- grad_enc_vectors: float32 [8, 768], P(None, 'section')
- grad_enc_qkv: float32 [768, 2304], P(None, 'section')
- grad_enc_out: float32 [768, 768], P(None, 'section')
- grad_enc_up: float32 [768, 3072], P(None, 'section')
- grad_enc_up_bias: float32 [3072], P('section')
- grad_enc_down: float32 [3072, 768], P(None, 'section')
- grad_proj_weight: float32 [768, 384], P(None, 'section')
- grad_dec_vectors: float32 [9, 384], P(None, 'section')
- grad_dec_qkv: float32 [384, 1152], P(None, 'section')
- grad_dec_out: float32 [384, 384], P(None, 'section')
- grad_dec_up: float32 [384, 1536], P(None, 'section')
- grad_dec_up_bias: float32 [1536], P('section')
- grad_dec_down: float32 [1536, 384], P(None, 'section')
- grad_time_pos: float32 [8, 384], P(None, 'section')
- grad_space_pos: float32 [144, 384], P(None, 'section')
- grad_norms: float32 [2], P('section')
Inputs may be any that keep to these rules, and one draw needn't show every extreme that they name: `frames`: each entry is 8 or 16; at least one clip has 16. `visible`: the 14 entries of a row are distinct.
All inputs are finite; a program needn't handle non-finite values.
Results may differ from a plain program's by a relative error of at most 0.017.
Values may be sent and summed in bfloat16 or wider, within the bound.
No kernel may reach another device: no remote copies, remote signals or barrier semaphores. Data moves between devices by JAX's collectives and lax.ppermute only.
A program may use at most 384 MiB of HBM per device.

v0:
```python
import jax
import jax.numpy as jnp
from jax import lax
from jax.sharding import PartitionSpec as P

HEAD_SIZE = 64


EPSILON = 1e-06
NEGATIVE = -1000000000.0


def from_partner(value, axis, apart):
    mask = 2**apart
    pairs = [(source, source ^ mask) for source in range(lax.axis_size(axis))]
    return lax.ppermute(value, axis, pairs)


def layer_norm(value, gain, shift):
    center = value - jnp.mean(value, axis=-1, keepdims=True)
    spread = jnp.mean(center * center, axis=-1, keepdims=True)
    return center * lax.rsqrt(spread + EPSILON) * gain + shift


def exact_gelu(value):
    return jax.nn.gelu(value, approximate=False)


def multiply(left, right):
    return jnp.dot(left, right, preferred_element_type=jnp.float32)


def left_transposed(left, right):
    return lax.dot_general(
        left, right, (((0,), (0,)), ((), ())), preferred_element_type=jnp.float32
    )


def right_transposed(left, right):
    return lax.dot_general(
        left, right, (((1,), (1,)), ((), ())), preferred_element_type=jnp.float32
    )


def attention_scores(queries, keys, key_valid, scale):
    scores = jnp.einsum("qhd,khd->hqk", queries, keys, preferred_element_type=jnp.float32) * scale
    return jnp.where(key_valid[None, None, :], scores, NEGATIVE)


def block_forward(inputs, weights, heads, key_valid):
    vectors, qkv_weight, out_weight, up_weight, up_bias, down_weight = weights
    rows = vectors.astype(jnp.float32)
    count, width = inputs.shape
    size = width // heads
    scale = size ** (-0.5)
    normed = layer_norm(inputs, rows[0], rows[1]).astype(jnp.bfloat16)
    joined = multiply(normed, qkv_weight)
    queries = (joined[:, :width] + rows[2]).astype(jnp.bfloat16).reshape(count, heads, size)
    keys = joined[:, width : 2 * width].astype(jnp.bfloat16).reshape(count, heads, size)
    values = (joined[:, 2 * width :] + rows[3]).astype(jnp.bfloat16).reshape(count, heads, size)
    scores = attention_scores(queries, keys, key_valid, scale)
    peak = jnp.max(scores, axis=-1, keepdims=True)
    expo = jnp.exp(scores - peak)
    total = jnp.sum(expo, axis=-1, keepdims=True)
    probs = expo / total
    log_total = peak + jnp.log(total)
    mixed = jnp.einsum(
        "hqk,khd->qhd", probs.astype(jnp.bfloat16), values, preferred_element_type=jnp.float32
    )
    mixed = mixed.reshape(count, width).astype(jnp.bfloat16)
    middle = inputs + (multiply(mixed, out_weight) + rows[4])
    normed_two = layer_norm(middle, rows[5], rows[6]).astype(jnp.bfloat16)
    hidden_pre = multiply(normed_two, up_weight) + up_bias.astype(jnp.float32)
    activated = exact_gelu(hidden_pre).astype(jnp.bfloat16)
    output = middle + (multiply(activated, down_weight) + rows[7])
    saved = (
        inputs,
        normed,
        queries,
        keys,
        values,
        log_total,
        mixed,
        middle,
        normed_two,
        hidden_pre,
        activated,
    )
    return (output, saved)


def block_backward(grad_out, weights, heads, key_valid, saved):
    vectors, qkv_weight, out_weight, up_weight, up_bias, down_weight = weights
    rows = vectors.astype(jnp.float32)
    (
        inputs,
        normed,
        queries,
        keys,
        values,
        log_total,
        mixed,
        middle,
        normed_two,
        hidden_pre,
        activated,
    ) = saved
    count, width = inputs.shape
    size = width // heads
    scale = size ** (-0.5)
    grad_low = grad_out.astype(jnp.bfloat16)
    grad_down = left_transposed(activated, grad_low)
    grad_act = right_transposed(grad_low, down_weight)
    grad_hidden = jax.vjp(exact_gelu, hidden_pre)[1](grad_act)[0].astype(jnp.bfloat16)
    grad_up_bias = jnp.sum(grad_hidden.astype(jnp.float32), axis=0)
    grad_up = left_transposed(normed_two, grad_hidden)
    grad_normed_two = right_transposed(grad_hidden, up_weight)
    norm_pull = jax.vjp(layer_norm, middle, rows[5], rows[6])[1]
    grad_mid_norm, grad_gain_two, grad_shift_two = norm_pull(grad_normed_two)
    grad_middle = grad_out + grad_mid_norm
    grad_branch = grad_middle.astype(jnp.bfloat16)
    grad_out_weight = left_transposed(mixed, grad_branch)
    grad_mixed = (
        right_transposed(grad_branch, out_weight).astype(jnp.bfloat16).reshape(count, heads, size)
    )
    scores = attention_scores(queries, keys, key_valid, scale)
    probs = jnp.exp(scores - log_total)
    grad_values = jnp.einsum(
        "hqk,qhd->khd", probs.astype(jnp.bfloat16), grad_mixed, preferred_element_type=jnp.float32
    ).astype(jnp.bfloat16)
    grad_probs = jnp.einsum("qhd,khd->hqk", grad_mixed, values, preferred_element_type=jnp.float32)
    grad_scores = (
        probs * (grad_probs - jnp.sum(grad_probs * probs, axis=-1, keepdims=True))
    ).astype(jnp.bfloat16)
    grad_queries = (
        jnp.einsum("hqk,khd->qhd", grad_scores, keys, preferred_element_type=jnp.float32) * scale
    ).astype(jnp.bfloat16)
    grad_keys = (
        jnp.einsum("hqk,qhd->khd", grad_scores, queries, preferred_element_type=jnp.float32) * scale
    ).astype(jnp.bfloat16)
    grad_queries = grad_queries.reshape(count, width)
    grad_keys = grad_keys.reshape(count, width)
    grad_values = grad_values.reshape(count, width)
    grad_joined = jnp.concatenate([grad_queries, grad_keys, grad_values], axis=1)
    grad_qkv = left_transposed(normed, grad_joined)
    grad_normed = right_transposed(grad_joined, qkv_weight)
    grad_in_norm, grad_gain, grad_shift = jax.vjp(layer_norm, inputs, rows[0], rows[1])[1](
        grad_normed
    )
    grad_rows = jnp.stack(
        [
            grad_gain,
            grad_shift,
            jnp.sum(grad_queries.astype(jnp.float32), axis=0),
            jnp.sum(grad_values.astype(jnp.float32), axis=0),
            jnp.sum(grad_branch.astype(jnp.float32), axis=0),
            grad_gain_two,
            grad_shift_two,
            jnp.sum(grad_low.astype(jnp.float32), axis=0),
        ]
    )
    return (
        grad_middle + grad_in_norm,
        (grad_rows, grad_qkv, grad_out_weight, grad_up, grad_up_bias, grad_down),
    )


def gather_plan(visible_row, slot_count, patch_count):
    seen_count = visible_row.shape[0]
    patch = jnp.arange(patch_count, dtype=jnp.int32)
    match = visible_row[None, :] == patch[:, None]
    seen = jnp.any(match, axis=1)
    rank = jnp.sum(jnp.where(match, jnp.arange(seen_count, dtype=jnp.int32)[None, :], 0), axis=1)
    slot = jnp.arange(slot_count, dtype=jnp.int32)
    source = (slot[:, None] * seen_count + rank[None, :]).reshape(-1)
    seen_row = jnp.broadcast_to(seen[None, :], (slot_count, patch_count)).reshape(-1)
    return (source, seen_row)


def slot_table(slots_used, slot_count):
    slot = jnp.arange(slot_count, dtype=jnp.int32)
    divisor = slots_used - 1
    numerator = slot * (slot_count - 1)
    lower = numerator // divisor
    fraction = (numerator - lower * divisor).astype(jnp.float32) / divisor.astype(jnp.float32)
    upper = jnp.minimum(lower + 1, slot_count - 1)
    column = slot[None, :]
    first = (column == lower[:, None]).astype(jnp.float32)
    second = (column == upper[:, None]).astype(jnp.float32)
    return (1.0 - fraction)[:, None] * first + fraction[:, None] * second


def square_sum(arrays):
    return sum((jnp.sum(item * item) for item in arrays))


def shards(
    tokens,
    frames,
    visible,
    out_grad,
    enc_vectors,
    enc_qkv,
    enc_out,
    enc_up,
    enc_up_bias,
    enc_down,
    proj_weight,
    dec_vectors,
    dec_qkv,
    dec_out,
    dec_up,
    dec_up_bias,
    dec_down,
    time_pos,
    space_pos,
):
    enc_weights = (enc_vectors, enc_qkv, enc_out, enc_up, enc_up_bias, enc_down)
    dec_block = (dec_vectors[:8], dec_qkv, dec_out, dec_up, dec_up_bias, dec_down)
    dec_params = (
        proj_weight,
        dec_vectors,
        dec_qkv,
        dec_out,
        dec_up,
        dec_up_bias,
        dec_down,
        time_pos,
        space_pos,
    )
    batch, vis_cap, enc_width = tokens.shape
    long_cap, dec_width = (out_grad.shape[1], out_grad.shape[2])
    slot_count = time_pos.shape[0]
    patch_count = space_pos.shape[0]
    seen_count = visible.shape[1]
    enc_heads = enc_width // HEAD_SIZE
    dec_heads = dec_width // HEAD_SIZE
    section = lax.axis_index("section")

    def encoder_run(index):
        clip_rows = lax.dynamic_index_in_dim(tokens, index, 0, keepdims=False).astype(jnp.float32)
        used = lax.dynamic_index_in_dim(frames, index, 0, keepdims=False) // 2
        key_valid = jnp.arange(vis_cap) < used * seen_count
        output, saved = block_forward(clip_rows, enc_weights, enc_heads, key_valid)
        return (output, saved, key_valid)

    def tick(step, state):
        received, enc_acc, dec_acc, tok_grads, decoded_acc = state

        def first_section(inner):
            received, enc_acc, dec_acc, tok_grads, decoded_acc = inner

            def backward_step(parts):
                acc_in, grads_in = parts
                index = jnp.maximum(step - 2, 0)
                output, saved, key_valid = encoder_run(index)
                grad_in, grads = block_backward(
                    received.astype(jnp.float32), enc_weights, enc_heads, key_valid, saved
                )
                acc_out = tuple((total + term for total, term in zip(acc_in, grads)))
                grads_out = lax.dynamic_update_index_in_dim(grads_in, grad_in, index, 0)
                return (acc_out, grads_out)

            enc_acc, tok_grads = lax.cond(
                step >= 2, backward_step, lambda parts: parts, (enc_acc, tok_grads)
            )

            def forward_step(unused):
                output, saved, key_valid = encoder_run(jnp.minimum(step, batch - 1))
                return output.astype(jnp.bfloat16)

            def blank_payload(unused):
                return jnp.zeros((vis_cap, enc_width), jnp.bfloat16)

            payload = lax.cond(step < batch, forward_step, blank_payload, 0)
            return (payload, enc_acc, dec_acc, tok_grads, decoded_acc)

        def second_section(inner):
            received, enc_acc, dec_acc, tok_grads, decoded_acc = inner

            def decoder_step(parts):
                acc_in, decoded_in = parts
                index = jnp.clip(step - 1, 0, batch - 1)
                used = lax.dynamic_index_in_dim(frames, index, 0, keepdims=False) // 2
                seen_row = lax.dynamic_index_in_dim(visible, index, 0, keepdims=False)
                cotangent = lax.dynamic_index_in_dim(out_grad, index, 0, keepdims=False).astype(
                    jnp.float32
                )
                source, seen_mask = gather_plan(seen_row, slot_count, patch_count)
                target = (
                    jnp.arange(slot_count, dtype=jnp.int32)[:, None] * patch_count
                    + seen_row[None, :]
                ).reshape(-1)
                projected = multiply(received, proj_weight)
                base = jnp.where(
                    seen_mask[:, None],
                    jnp.take(projected, source, axis=0),
                    dec_vectors[8].astype(jnp.float32),
                )
                table = slot_table(used, slot_count)
                slot_pos = jnp.dot(
                    table, time_pos.astype(jnp.float32), precision=lax.Precision.HIGHEST
                )
                start = (
                    base.reshape(slot_count, patch_count, dec_width)
                    + slot_pos[:, None, :]
                    + space_pos.astype(jnp.float32)[None]
                )
                start = start.reshape(long_cap, dec_width)
                row_valid = jnp.arange(long_cap) < used * patch_count
                output, saved = block_forward(start, dec_block, dec_heads, row_valid)
                decoded_row = jnp.where(row_valid[:, None], output, 0.0)
                grad_start, block_grads = block_backward(
                    jnp.where(row_valid[:, None], cotangent, 0.0),
                    dec_block,
                    dec_heads,
                    row_valid,
                    saved,
                )
                grad_grid = grad_start.reshape(slot_count, patch_count, dec_width)
                grad_space = jnp.sum(grad_grid, axis=0)
                grad_time = jnp.dot(
                    table.T, jnp.sum(grad_grid, axis=1), precision=lax.Precision.HIGHEST
                )
                grad_mask = jnp.sum(jnp.where(seen_mask[:, None], 0.0, grad_start), axis=0)
                grad_projected = jnp.take(grad_start, target, axis=0).astype(jnp.bfloat16)
                grad_proj = left_transposed(received, grad_projected)
                grad_sent = right_transposed(grad_projected, proj_weight).astype(jnp.bfloat16)
                grad_rows = jnp.concatenate([block_grads[0], grad_mask[None, :]], axis=0)
                new_terms = (
                    grad_proj,
                    grad_rows,
                    block_grads[1],
                    block_grads[2],
                    block_grads[3],
                    block_grads[4],
                    block_grads[5],
                    grad_time,
                    grad_space,
                )
                acc_out = tuple((total + term for total, term in zip(acc_in, new_terms)))
                decoded_out = lax.dynamic_update_index_in_dim(decoded_in, decoded_row, index, 0)
                return (grad_sent, acc_out, decoded_out)

            def nothing_step(parts):
                return (jnp.zeros((vis_cap, enc_width), jnp.bfloat16), parts[0], parts[1])

            active = (step >= 1) & (step <= batch)
            payload, dec_acc, decoded_acc = lax.cond(
                active, decoder_step, nothing_step, (dec_acc, decoded_acc)
            )
            return (payload, enc_acc, dec_acc, tok_grads, decoded_acc)

        payload, enc_acc, dec_acc, tok_grads, decoded_acc = lax.cond(
            section == 0, first_section, second_section, state
        )
        received = from_partner(payload, "section", 0)
        return (received, enc_acc, dec_acc, tok_grads, decoded_acc)

    initial = (
        jnp.zeros((vis_cap, enc_width), jnp.bfloat16),
        tuple((jnp.zeros(item.shape, jnp.float32) for item in enc_weights)),
        tuple((jnp.zeros(item.shape, jnp.float32) for item in dec_params)),
        jnp.zeros((batch, vis_cap, enc_width), jnp.float32),
        jnp.zeros((batch, long_cap, dec_width), jnp.float32),
    )
    received, enc_acc, dec_acc, tok_grads, decoded_acc = lax.fori_loop(0, batch + 2, tick, initial)
    grad_enc_vectors, grad_enc_qkv, grad_enc_out, grad_enc_up, grad_enc_up_bias, grad_enc_down = (
        enc_acc
    )
    (
        grad_proj_weight,
        grad_dec_vectors,
        grad_dec_qkv,
        grad_dec_out,
        grad_dec_up,
        grad_dec_up_bias,
        grad_dec_down,
        grad_time_pos,
        grad_space_pos,
    ) = dec_acc
    summed = lax.psum(
        (
            grad_enc_vectors,
            grad_enc_qkv,
            grad_enc_out,
            grad_enc_up,
            grad_enc_up_bias,
            grad_enc_down,
            grad_proj_weight,
            grad_dec_vectors,
            grad_dec_qkv,
            grad_dec_out,
            grad_dec_up,
            grad_dec_up_bias,
            grad_dec_down,
            grad_time_pos,
            grad_space_pos,
        ),
        "dp",
    )
    enc_square = square_sum(summed[:6])
    dec_square = square_sum(summed[6:])
    norms = jnp.where(section == 0, enc_square, dec_square).reshape(1)
    halves = (
        lax.psum_scatter(
            summed[0].astype(jnp.bfloat16), "section", scatter_dimension=1, tiled=True
        ).astype(jnp.float32),
        lax.psum_scatter(
            summed[1].astype(jnp.bfloat16), "section", scatter_dimension=1, tiled=True
        ).astype(jnp.float32),
        lax.psum_scatter(
            summed[2].astype(jnp.bfloat16), "section", scatter_dimension=1, tiled=True
        ).astype(jnp.float32),
        lax.psum_scatter(
            summed[3].astype(jnp.bfloat16), "section", scatter_dimension=1, tiled=True
        ).astype(jnp.float32),
        lax.psum_scatter(
            summed[4].astype(jnp.bfloat16), "section", scatter_dimension=0, tiled=True
        ).astype(jnp.float32),
        lax.psum_scatter(
            summed[5].astype(jnp.bfloat16), "section", scatter_dimension=1, tiled=True
        ).astype(jnp.float32),
        lax.psum_scatter(
            summed[6].astype(jnp.bfloat16), "section", scatter_dimension=1, tiled=True
        ).astype(jnp.float32),
        lax.psum_scatter(
            summed[7].astype(jnp.bfloat16), "section", scatter_dimension=1, tiled=True
        ).astype(jnp.float32),
        lax.psum_scatter(
            summed[8].astype(jnp.bfloat16), "section", scatter_dimension=1, tiled=True
        ).astype(jnp.float32),
        lax.psum_scatter(
            summed[9].astype(jnp.bfloat16), "section", scatter_dimension=1, tiled=True
        ).astype(jnp.float32),
        lax.psum_scatter(
            summed[10].astype(jnp.bfloat16), "section", scatter_dimension=1, tiled=True
        ).astype(jnp.float32),
        lax.psum_scatter(
            summed[11].astype(jnp.bfloat16), "section", scatter_dimension=0, tiled=True
        ).astype(jnp.float32),
        lax.psum_scatter(
            summed[12].astype(jnp.bfloat16), "section", scatter_dimension=1, tiled=True
        ).astype(jnp.float32),
        lax.psum_scatter(
            summed[13].astype(jnp.bfloat16), "section", scatter_dimension=1, tiled=True
        ).astype(jnp.float32),
        lax.psum_scatter(
            summed[14].astype(jnp.bfloat16), "section", scatter_dimension=1, tiled=True
        ).astype(jnp.float32),
        lax.psum_scatter(
            tok_grads.astype(jnp.bfloat16), "section", scatter_dimension=2, tiled=True
        ).astype(jnp.float32),
        lax.psum_scatter(
            decoded_acc.astype(jnp.bfloat16), "section", scatter_dimension=2, tiled=True
        ).astype(jnp.float32),
    )
    weight_halves = halves[:15]
    token_half = halves[15]
    decoded_half = halves[16]
    return (
        decoded_half.astype(jnp.bfloat16),
        token_half.astype(jnp.bfloat16),
        weight_halves[0],
        weight_halves[1],
        weight_halves[2],
        weight_halves[3],
        weight_halves[4],
        weight_halves[5],
        weight_halves[6],
        weight_halves[7],
        weight_halves[8],
        weight_halves[9],
        weight_halves[10],
        weight_halves[11],
        weight_halves[12],
        weight_halves[13],
        weight_halves[14],
        norms,
    )


def solution(mesh):
    placed = (
        P("dp", None, None),
        P("dp"),
        P("dp", None),
        P("dp", None, None),
        P(),
        P(),
        P(),
        P(),
        P(),
        P(),
        P(),
        P(),
        P(),
        P(),
        P(),
        P(),
        P(),
        P(),
        P(),
    )
    return jax.shard_map(
        shards,
        mesh=mesh,
        in_specs=placed,
        out_specs=(
            P("dp", None, "section"),
            P("dp", None, "section"),
            P(None, "section"),
            P(None, "section"),
            P(None, "section"),
            P(None, "section"),
            P("section"),
            P(None, "section"),
            P(None, "section"),
            P(None, "section"),
            P(None, "section"),
            P(None, "section"),
            P(None, "section"),
            P("section"),
            P(None, "section"),
            P(None, "section"),
            P(None, "section"),
            P("section"),
        ),
        check_vma=False,
    )
```

profile of v0, /device:TPU:1, one launch (start us, length us, event | category | flops | bytes accessed | tf_op | source)
XLA Modules:
  0.0 1389.0 jit_solution(14087356872374952745)
XLA Ops:
  34.9 609.5 %while.49 = (s32[]{:T(128)}, bf16[112,768]{1,0:T(8,128)(2,1)S(1)}, f32[8,768]{1,0:T(8,128)}, f32[768,2304]{1,0:T(8,128)}, f32[768,768]{1,0:T(8,128)}, /*index=5*...) while((s32[]{:T(128)}, bf16[112,768]{1,0:T(8,128)(2,1)S(1)}, ...), condition=%wide.region_60.61_spmd, body=%wide.region_0.60_spmd.sunk | while | flops 18894690304 | bytes 540424512 | solution.py:367
  35.2 28.5 %conditional.5 = (bf16[112,768]{1,0:T(8,128)(2,1)}, f32[8,768]{1,0:T(8,128)}, f32[768,2304]{1,0:T(8,128)}, f32[768,768]{1,0:T(8,128)}, f32[768,3072]{1,0:T(8,128...) conditional(s32[]{:T(128)} %convert_element_type.586, ...), branch_computations={%region_1.28_spmd, %region_29.59_spmd} | conditional | flops 18894690304 | bytes 539735488 | solution.py:354
  63.6 16.1 %collective-permute-start = (bf16[112,768]{1,0:T(8,128)(2,1)}, bf16[112,768]{1,0:T(8,128)(2,1)S(1)}, u32[]{:S(2)}, u32[]{:S(2)}) collective-permute-start(bf16[112,768]{1,0:T(8,128)(2,1)} %get-tuple-element.1877), channel_id=1, source_target_pairs={{0,64},{64,0},{1,65},{65,1},{2,66},{66,2},{3,67},{67,3},{4,68},{68... | collective-permute-start | bytes 516104 | tf_op jit(solution)/shard_map/while/body/eval_jaxpr/ppermute | solution.py:16
  81.5 239.3 %conditional.5 = (bf16[112,768]{1,0:T(8,128)(2,1)}, f32[8,768]{1,0:T(8,128)}, f32[768,2304]{1,0:T(8,128)}, f32[768,768]{1,0:T(8,128)}, f32[768,3072]{1,0:T(8,128...) conditional(s32[]{:T(128)} %convert_element_type.586, ...), branch_computations={%region_1.28_spmd, %region_29.59_spmd} | conditional | flops 18894690304 | bytes 539735488 | solution.py:354
  81.5 222.8 %conditional = (bf16[112,768]{1,0:T(8,128)(2,1)}, f32[768,384]{0,1:T(8,128)}, f32[9,384]{1,0:T(8,128)}, f32[384,1152]{1,0:T(8,128)}, f32[384,384]{1,0:T(8,128)},...) conditional(s32[]{:T(128)} %convert_element_type.300, ...), branch_computations={%region_2.0_spmd, %region_3.27_spmd} | conditional | flops 18894690304 | bytes 539735040 | solution.py:349
  145.9 18.7 %multiply_convert_fusion.4 = (bf16[1152,1536]{1,0:T(8,128)(2,1)S(1)}, f32[1152,1536]{1,0:T(8,128)S(1)}, f32[1152,1536]{1,0:T(8,128)}) fusion(f32[1536]{0:T(1024)S(1)} %copy-done.74, bf16[384,1536]{1,0:T(8,128)(2,1)S(1)} %copy-done.92, f32[1152,384]{1,0:T(8,128)S(1)} %get-tuple-element.1576, f32[384]{0:T(512)S(1)} %copy-done.59, ...), kind=kOutput, calls=%fused_computation.254 | convolution fusion | flops 1477951488 | bytes 20662272 | tf_op jit(solution)/shard_map/while/body/eval_jaxpr/cond/branch_0_fun/cond/branch_1_fun/dot_general | solution.py:30
  194.5 13.6 convert_reduce_fusion.10
  208.8 27.1 %multiply_reduce_fusion.5 = (f32[6,1152]{1,0:T(8,128)S(1)}, f32[6,1152,1152]{1,2,0:T(8,128)}) fusion(f32[6,1152,1152]{1,2,0:T(8,128)} %get-tuple-element.1574, f32[6,1152]{1,0:T(8,128)} %copy-done.18, bf16[1152,6,64]{0,2,1:T(8,128)(2,1)} %bitcast.238, bf16[1152,6,64]{0,2,1:T(8,128)(2,1)} %bitcast.240), kind=kOutput, calls=%fused_computation.242 | convolution fusion | flops 1043096832 | bytes 65525760 | tf_op jit(solution)/shard_map/while/body/eval_jaxpr/cond/branch_0_fun/cond/branch_1_fun/qhd,khd->hqk/dot_general | solution.py:131
  235.9 26.4 %multiply_convert_fusion.3 = bf16[6,1152,1152]{1,2,0:T(8,128)(2,1)} fusion(f32[6,1152,1152]{1,2,0:T(8,128)} %get-tuple-element.1580, f32[6,1152,1152]{1,2,0:T(8,128)} %get-tuple-element.1574, f32[6,1152]{1,0:T(8,128)S(1)} %get-tuple-element.1579, f32[6,1152]{1,0:T(8,128)S(1)} %copy-done.19), kind=kLoop, calls=%fused_computation.241 | loop fusion | flops 31850496 | bytes 79681536 | tf_op jit(solution)/shard_map/while/body/eval_jaxpr/cond/branch_0_fun/cond/branch_1_fun/convert_element_type | solution.py:134
  329.1 239.4 %conditional.5 = (bf16[112,768]{1,0:T(8,128)(2,1)}, f32[8,768]{1,0:T(8,128)}, f32[768,2304]{1,0:T(8,128)}, f32[768,768]{1,0:T(8,128)}, f32[768,3072]{1,0:T(8,128...) conditional(s32[]{:T(128)} %convert_element_type.586, ...), branch_computations={%region_1.28_spmd, %region_29.59_spmd} | conditional | flops 18894690304 | bytes 539735488 | solution.py:354
  329.1 222.9 %conditional = (bf16[112,768]{1,0:T(8,128)(2,1)}, f32[768,384]{0,1:T(8,128)}, f32[9,384]{1,0:T(8,128)}, f32[384,1152]{1,0:T(8,128)}, f32[384,384]{1,0:T(8,128)},...) conditional(s32[]{:T(128)} %convert_element_type.300, ...), branch_computations={%region_2.0_spmd, %region_3.27_spmd} | conditional | flops 18894690304 | bytes 539735040 | solution.py:349
  393.5 18.7 %multiply_convert_fusion.4 = (bf16[1152,1536]{1,0:T(8,128)(2,1)S(1)}, f32[1152,1536]{1,0:T(8,128)S(1)}, f32[1152,1536]{1,0:T(8,128)}) fusion(f32[1536]{0:T(1024)S(1)} %copy-done.74, bf16[384,1536]{1,0:T(8,128)(2,1)S(1)} %copy-done.92, f32[1152,384]{1,0:T(8,128)S(1)} %get-tuple-element.1576, f32[384]{0:T(512)S(1)} %copy-done.59, ...), kind=kOutput, calls=%fused_computation.254 | convolution fusion | flops 1477951488 | bytes 20662272 | tf_op jit(solution)/shard_map/while/body/eval_jaxpr/cond/branch_0_fun/cond/branch_1_fun/dot_general | solution.py:30
  442.2 13.6 convert_reduce_fusion.10
  456.5 27.1 %multiply_reduce_fusion.5 = (f32[6,1152]{1,0:T(8,128)S(1)}, f32[6,1152,1152]{1,2,0:T(8,128)}) fusion(f32[6,1152,1152]{1,2,0:T(8,128)} %get-tuple-element.1574, f32[6,1152]{1,0:T(8,128)} %copy-done.18, bf16[1152,6,64]{0,2,1:T(8,128)(2,1)} %bitcast.238, bf16[1152,6,64]{0,2,1:T(8,128)(2,1)} %bitcast.240), kind=kOutput, calls=%fused_computation.242 | convolution fusion | flops 1043096832 | bytes 65525760 | tf_op jit(solution)/shard_map/while/body/eval_jaxpr/cond/branch_0_fun/cond/branch_1_fun/qhd,khd->hqk/dot_general | solution.py:131
  483.6 26.4 %multiply_convert_fusion.3 = bf16[6,1152,1152]{1,2,0:T(8,128)(2,1)} fusion(f32[6,1152,1152]{1,2,0:T(8,128)} %get-tuple-element.1580, f32[6,1152,1152]{1,2,0:T(8,128)} %get-tuple-element.1574, f32[6,1152]{1,0:T(8,128)S(1)} %get-tuple-element.1579, f32[6,1152]{1,0:T(8,128)S(1)} %copy-done.19), kind=kLoop, calls=%fused_computation.241 | loop fusion | flops 31850496 | bytes 79681536 | tf_op jit(solution)/shard_map/while/body/eval_jaxpr/cond/branch_0_fun/cond/branch_1_fun/convert_element_type | solution.py:134
  576.8 28.3 %conditional.5 = (bf16[112,768]{1,0:T(8,128)(2,1)}, f32[8,768]{1,0:T(8,128)}, f32[768,2304]{1,0:T(8,128)}, f32[768,768]{1,0:T(8,128)}, f32[768,3072]{1,0:T(8,128...) conditional(s32[]{:T(128)} %convert_element_type.586, ...), branch_computations={%region_1.28_spmd, %region_29.59_spmd} | conditional | flops 18894690304 | bytes 539735488 | solution.py:354
  605.1 29.4 %collective-permute-start = (bf16[112,768]{1,0:T(8,128)(2,1)}, bf16[112,768]{1,0:T(8,128)(2,1)S(1)}, u32[]{:S(2)}, u32[]{:S(2)}) collective-permute-start(bf16[112,768]{1,0:T(8,128)(2,1)} %get-tuple-element.1877), channel_id=1, source_target_pairs={{0,64},{64,0},{1,65},{65,1},{2,66},{66,2},{3,67},{67,3},{4,68},{68... | collective-permute-start | bytes 516104 | tf_op jit(solution)/shard_map/while/body/eval_jaxpr/ppermute | solution.py:16
  652.5 116.7 %all-reduce.8.cloned.1.call-done = (f32[8,768]{1,0:T(8,128)}, f32[3072]{0:T(1024)}, f32[9,384]{1,0:T(8,128)}, f32[1536]{0:T(1024)}, f32[8,384]{1,0:T(8,128)}) async-done(((f32[8,768]{1,0:T(8,128)}, f32[3072]{0:T(1024)}, f32[9,384]{1,0:T(8,128)}, f32[1536]{0:T(1024)}, f32[8,384]{1,0:T(8,128)}), (f32[8,768]{1,0:T(8,128)}, f32[3072]{0:T(1024)}, f32[9,384]{1,0:T(8,128)}, f32[1536]{0:T(1024)}, ...) | async-done | bytes 69136 | tf_op jit(solution)/shard_map/psum | solution.py:382
  777.6 367.9 %all-reduce.10.cloned.1.call-done = (f32[768,2304]{1,0:T(8,128)}, f32[768,768]{1,0:T(8,128)}, f32[768,3072]{1,0:T(8,128)}, f32[3072,768]{1,0:T(8,128)}, f32[768,...) async-done(((f32[768,2304]{1,0:T(8,128)}, f32[768,768]{1,0:T(8,128)}, ...) | async-done | bytes 36790288 | tf_op jit(solution)/shard_map/psum | solution.py:382
  1248.4 13.4 reduce-scatter.38.cloned.1.call-done
  1263.7 13.7 reduce-scatter.52.cloned.1.call-done
  1310.4 16.0 %reduce-scatter.50.cloned.1.call-done = bf16[1152,768]{1,0:T(8,128)(2,1)} async-done(((bf16[2304,768]{1,0:T(8,128)(2,1)}), bf16[1152,768]{1,0:T(8,128)(2,1)}) %reduce-scatter.50.cloned.1.call-update) | async-done | bytes 1769488
  1331.2 14.2 %reduce-scatter.54.cloned.1.call-done = bf16[384,3072]{1,0:T(8,128)(2,1)} async-done(((bf16[768,3072]{1,0:T(8,128)(2,1)}), bf16[384,3072]{1,0:T(8,128)(2,1)}) %reduce-scatter.54.cloned.1.call-update) | async-done | bytes 2359312
  1350.9 14.2 %reduce-scatter.34.cloned.1.call-done = bf16[768,1536]{1,0:T(8,128)(2,1)} async-done(((bf16[768,3072]{1,0:T(8,128)(2,1)}), bf16[768,1536]{1,0:T(8,128)(2,1)}) %reduce-scatter.34.cloned.1.call-update) | async-done | bytes 2359312 | tf_op jit(solution)/shard_map/reduce_scatter | solution.py:415
  (539 shorter events, 494.3 us)
Async XLA Ops:
  7.2 762.0 %all-reduce.8.cloned.1.call-start = ((), (), s32[]{:S(2)}) async-start(), calls=%async_computation.30 | async-start | bytes 163840 | tf_op jit(solution)/shard_map/psum | solution.py:382
  63.6 17.4 %collective-permute-start = (bf16[112,768]{1,0:T(8,128)(2,1)}, bf16[112,768]{1,0:T(8,128)(2,1)S(1)}, u32[]{:S(2)}, u32[]{:S(2)}) collective-permute-start(bf16[112,768]{1,0:T(8,128)(2,1)} %get-tuple-element.1877), channel_id=1, source_target_pairs={{0,64},{64,0},{1,65},{65,1},{2,66},{66,2},{3,67},{67,3},{4,68},{68... | collective-permute-start | bytes 516104 | tf_op jit(solution)/shard_map/while/body/eval_jaxpr/ppermute | solution.py:16
  86.6 103.7 %copy-start.49 = (pred[1152]{0:T(1024)(128)(4,1)}, pred[1152]{0:T(1024)(128)(4,1)S(1)}, u32[]{:S(2)}) copy-start(pred[1152]{0:T(1024)(128)(4,1)S(1)} %iota_compare_fusion.3) | copy-start | bytes 3460 | tf_op jit(solution)/shard_map/while/body/eval_jaxpr/cond/branch_0_fun/cond
  320.9 1.7 collective-permute-start
  334.1 103.8 %copy-start.49 = (pred[1152]{0:T(1024)(128)(4,1)}, pred[1152]{0:T(1024)(128)(4,1)S(1)}, u32[]{:S(2)}) copy-start(pred[1152]{0:T(1024)(128)(4,1)S(1)} %iota_compare_fusion.3) | copy-start | bytes 3460 | tf_op jit(solution)/shard_map/while/body/eval_jaxpr/cond/branch_0_fun/cond
  568.5 1.7 collective-permute-start
  605.1 30.6 %collective-permute-start = (bf16[112,768]{1,0:T(8,128)(2,1)}, bf16[112,768]{1,0:T(8,128)(2,1)S(1)}, u32[]{:S(2)}, u32[]{:S(2)}) collective-permute-start(bf16[112,768]{1,0:T(8,128)(2,1)} %get-tuple-element.1877), channel_id=1, source_target_pairs={{0,64},{64,0},{1,65},{65,1},{2,66},{66,2},{3,67},{67,3},{4,68},{68... | collective-permute-start | bytes 516104 | tf_op jit(solution)/shard_map/while/body/eval_jaxpr/ppermute | solution.py:16
  644.4 501.1 %all-reduce.10.cloned.1.call-start = ((), (), s32[]{:S(2)}) async-start(), calls=%async_computation.31 | async-start | bytes 73580544 | tf_op jit(solution)/shard_map/psum | solution.py:382
  652.4 123.7 %copy-start.48 = (bf16[2,112,768]{2,1,0:T(8,128)(2,1)S(1)}, bf16[2,112,768]{2,1,0:T(8,128)(2,1)}, u32[]{:S(2)}) copy-start(bf16[2,112,768]{2,1,0:T(8,128)(2,1)} %get-tuple-element.1379) | copy-start | bytes 1032196
  652.4 571.2 %reduce-scatter.58.cloned.1.call-start = ((), (), s32[]{:S(2)}) async-start(), calls=%async_computation.28 | async-start | bytes 147456
  771.4 453.7 %reduce-scatter.56.cloned.1.call-start = ((), (), s32[]{:S(2)}) async-start(), calls=%async_computation.27 | async-start | bytes 147456
  773.8 452.9 %reduce-scatter.48.cloned.1.call-start = ((), (), s32[]{:S(2)}) async-start(), calls=%async_computation.23 | async-start | bytes 294912
  776.1 452.2 %reduce-scatter.46.cloned.1.call-start = ((), (), s32[]{:S(2)}) async-start(), calls=%async_computation.22 | async-start | bytes 589824
  777.5 462.1 %reduce-scatter.60.cloned.1.call-start = ((), (), s32[]{:S(2)}) async-start(), calls=%async_computation.29 | async-start | bytes 294912
  1148.1 93.1 %reduce-scatter.40.cloned.1.call-start = ((), (), s32[]{:S(2)}) async-start(), calls=%async_computation.19 | async-start | bytes 442368 | tf_op jit(solution)/shard_map/reduce_scatter | solution.py:433
  1150.9 95.7 %reduce-scatter.36.cloned.1.call-start = ((), (), s32[]{:S(2)}) async-start(), calls=%async_computation.17 | async-start | bytes 884736 | tf_op jit(solution)/shard_map/reduce_scatter | solution.py:424
  1152.6 109.1 %reduce-scatter.38.cloned.1.call-start = ((), (), s32[]{:S(2)}) async-start(), calls=%async_computation.18 | async-start | bytes 1327104 | tf_op jit(solution)/shard_map/reduce_scatter | solution.py:430
  1156.8 120.6 %reduce-scatter.52.cloned.1.call-start = ((), (), s32[]{:S(2)}) async-start(), calls=%async_computation.25 | async-start | bytes 1769472
  1159.5 133.5 %reduce-scatter.42.cloned.1.call-start = ((), (), s32[]{:S(2)}) async-start(), calls=%async_computation.20 | async-start | bytes 1769472 | tf_op jit(solution)/shard_map/reduce_scatter | solution.py:436
  1164.3 143.8 %reduce-scatter.44.cloned.1.call-start = ((), (), s32[]{:S(2)}) async-start(), calls=%async_computation.21 | async-start | bytes 1769472 | tf_op jit(solution)/shard_map/reduce_scatter | solution.py:442
  1166.5 159.8 %reduce-scatter.50.cloned.1.call-start = ((), (), s32[]{:S(2)}) async-start(), calls=%async_computation.24 | async-start | bytes 5308416
  1177.8 167.6 %reduce-scatter.54.cloned.1.call-start = ((), (), s32[]{:S(2)}) async-start(), calls=%async_computation.26 | async-start | bytes 7077888
  1196.3 168.8 %reduce-scatter.34.cloned.1.call-start = ((), (), s32[]{:S(2)}) async-start(), calls=%async_computation.16 | async-start | bytes 7077888 | tf_op jit(solution)/shard_map/reduce_scatter | solution.py:415
  1208.1 173.1 %reduce-scatter.32.cloned.1.call-start = ((), (), s32[]{:S(2)}) async-start(), calls=%async_computation.15 | async-start | bytes 2654208 | tf_op jit(solution)/shard_map/reduce_scatter | solution.py:454
  (118 other events, 844.4 us)
Sparse Core Ops, SparseCore 0:
  644.5 124.5 all-reduce.7
  777.9 367.5 all-reduce.9
  1148.4 11.3 reduce-scatter.57
  1162.5 11.4 reduce-scatter.55
  1176.3 11.5 reduce-scatter.47
  1190.7 11.7 reduce-scatter.45
  1205.0 11.5 reduce-scatter.59
  1219.6 11.7 reduce-scatter.39
  1234.4 12.0 reduce-scatter.35
  1249.4 12.3 reduce-scatter.37
  1264.7 12.6 reduce-scatter.51
  1280.3 12.7 reduce-scatter.41
  1295.4 12.6 reduce-scatter.43
  1311.1 15.2 reduce-scatter.49
  1328.7 16.6 reduce-scatter.53
  1348.3 16.6 reduce-scatter.33
  1367.8 13.3 reduce-scatter.31
where the time goes:
time: 1400 us; the launch traced here: 1390 us
  waiting for transfers between devices  603 us (43%)
  matrix products  295 us (21%)
  other arithmetic  187 us (13%)
  loops' own time  119 us (8%)
  local copies, waits for them, and re-layouts  106 us (8%)
  starting transfers between devices  46.4 us (3%)
  between operations  26.2 us (2%)
    psum x2, waiting for transfers between devices, shards(): lax.psum((grad_enc_vectors, grad_enc_qkv, grad_enc_out, grad_enc_up, grad...  485 us
    another operation x4, loops' own time, tick(): lax.cond(section == 0, first_section, second_section, state)  66.4 us
    reduce_sum x15, other arithmetic, square_sum(): return sum((jnp.sum(item * item) for item in arrays))  55.1 us
    dot_general x2, matrix products, block_backward(): jnp.einsum('qhd,khd->hqk', grad_mixed, values, preferred_element_type=jnp...  54.2 us
    convert_element_type x2, other arithmetic, block_backward(): grad_scores = (probs * (grad_probs - jnp.sum(grad_probs * probs, axis=-1,...  52.8 us
    dot_general x10, matrix products, multiply(): return jnp.dot(left, right, preferred_element_type=jnp.float32)  51.7 us
    ppermute x4, starting transfers between devices, from_partner(): return lax.ppermute(value, axis, pairs)  45.7 us
    unnamed x25, waiting for transfers between devices  44.2 us
  transfers between devices with their start and end apart: 21, of which 15 were waited for; matrix products, arithmetic and copies ran while one was open for 9% of the time, Pallas kernels for 0%

commit v1 on v0

v1 whole, which is shorter than its diff:
```python
import jax
import jax.numpy as jnp
from jax import lax
from jax.sharding import PartitionSpec as P

HEAD_SIZE = 64


EPSILON = 1e-06
NEGATIVE = -1000000000.0


def from_partner(value, axis, apart):
    mask = 2**apart
    pairs = [(source, source ^ mask) for source in range(lax.axis_size(axis))]
    return lax.ppermute(value, axis, pairs)


def layer_norm(value, gain, shift):
    center = value - jnp.mean(value, axis=-1, keepdims=True)
    spread = jnp.mean(center * center, axis=-1, keepdims=True)
    return center * lax.rsqrt(spread + EPSILON) * gain + shift


def exact_gelu(value):
    return jax.nn.gelu(value, approximate=False)


def multiply(left, right):
    return jnp.dot(left, right, preferred_element_type=jnp.float32)


def left_transposed(left, right):
    return lax.dot_general(
        left, right, (((0,), (0,)), ((), ())), preferred_element_type=jnp.float32
    )


def right_transposed(left, right):
    return lax.dot_general(
        left, right, (((1,), (1,)), ((), ())), preferred_element_type=jnp.float32
    )


def attention_scores(queries, keys, key_valid, scale):
    scores = jnp.einsum("qhd,khd->hqk", queries, keys, preferred_element_type=jnp.float32) * scale
    return jnp.where(key_valid[None, None, :], scores, NEGATIVE)


def block_forward(inputs, weights, heads, key_valid):
    vectors, qkv_weight, out_weight, up_weight, up_bias, down_weight = weights
    rows = vectors.astype(jnp.float32)
    count, width = inputs.shape
    size = width // heads
    scale = size ** (-0.5)
    normed = layer_norm(inputs, rows[0], rows[1]).astype(jnp.bfloat16)
    joined = multiply(normed, qkv_weight)
    queries = (joined[:, :width] + rows[2]).astype(jnp.bfloat16).reshape(count, heads, size)
    keys = joined[:, width : 2 * width].astype(jnp.bfloat16).reshape(count, heads, size)
    values = (joined[:, 2 * width :] + rows[3]).astype(jnp.bfloat16).reshape(count, heads, size)
    scores = attention_scores(queries, keys, key_valid, scale)
    peak = jnp.max(scores, axis=-1, keepdims=True)
    expo = jnp.exp(scores - peak)
    total = jnp.sum(expo, axis=-1, keepdims=True)
    probs = expo / total
    log_total = peak + jnp.log(total)
    mixed = jnp.einsum(
        "hqk,khd->qhd", probs.astype(jnp.bfloat16), values, preferred_element_type=jnp.float32
    )
    mixed = mixed.reshape(count, width).astype(jnp.bfloat16)
    middle = inputs + (multiply(mixed, out_weight) + rows[4])
    normed_two = layer_norm(middle, rows[5], rows[6]).astype(jnp.bfloat16)
    hidden_pre = multiply(normed_two, up_weight) + up_bias.astype(jnp.float32)
    activated = exact_gelu(hidden_pre).astype(jnp.bfloat16)
    output = middle + (multiply(activated, down_weight) + rows[7])
    saved = (
        inputs,
        normed,
        queries,
        keys,
        values,
        log_total,
        mixed,
        middle,
        normed_two,
        hidden_pre,
        activated,
    )
    return (output, saved)


def block_backward(grad_out, weights, heads, key_valid, saved):
    vectors, qkv_weight, out_weight, up_weight, up_bias, down_weight = weights
    rows = vectors.astype(jnp.float32)
    (
        inputs,
        normed,
        queries,
        keys,
        values,
        log_total,
        mixed,
        middle,
        normed_two,
        hidden_pre,
        activated,
    ) = saved
    count, width = inputs.shape
    size = width // heads
    scale = size ** (-0.5)
    grad_low = grad_out.astype(jnp.bfloat16)
    grad_down = left_transposed(activated, grad_low)
    grad_act = right_transposed(grad_low, down_weight)
    grad_hidden = jax.vjp(exact_gelu, hidden_pre)[1](grad_act)[0].astype(jnp.bfloat16)
    grad_up_bias = jnp.sum(grad_hidden.astype(jnp.float32), axis=0)
    grad_up = left_transposed(normed_two, grad_hidden)
    grad_normed_two = right_transposed(grad_hidden, up_weight)
    norm_pull = jax.vjp(layer_norm, middle, rows[5], rows[6])[1]
    grad_mid_norm, grad_gain_two, grad_shift_two = norm_pull(grad_normed_two)
    grad_middle = grad_out + grad_mid_norm
    grad_branch = grad_middle.astype(jnp.bfloat16)
    grad_out_weight = left_transposed(mixed, grad_branch)
    grad_mixed = (
        right_transposed(grad_branch, out_weight).astype(jnp.bfloat16).reshape(count, heads, size)
    )
    scores = attention_scores(queries, keys, key_valid, scale)
    probs = jnp.exp(scores - log_total)
    grad_values = jnp.einsum(
        "hqk,qhd->khd", probs.astype(jnp.bfloat16), grad_mixed, preferred_element_type=jnp.float32
    ).astype(jnp.bfloat16)
    grad_probs = jnp.einsum("qhd,khd->hqk", grad_mixed, values, preferred_element_type=jnp.float32)
    grad_scores = (
        probs * (grad_probs - jnp.sum(grad_probs * probs, axis=-1, keepdims=True))
    ).astype(jnp.bfloat16)
    grad_queries = (
        jnp.einsum("hqk,khd->qhd", grad_scores, keys, preferred_element_type=jnp.float32) * scale
    ).astype(jnp.bfloat16)
    grad_keys = (
        jnp.einsum("hqk,qhd->khd", grad_scores, queries, preferred_element_type=jnp.float32) * scale
    ).astype(jnp.bfloat16)
    grad_queries = grad_queries.reshape(count, width)
    grad_keys = grad_keys.reshape(count, width)
    grad_values = grad_values.reshape(count, width)
    grad_joined = jnp.concatenate([grad_queries, grad_keys, grad_values], axis=1)
    grad_qkv = left_transposed(normed, grad_joined)
    grad_normed = right_transposed(grad_joined, qkv_weight)
    grad_in_norm, grad_gain, grad_shift = jax.vjp(layer_norm, inputs, rows[0], rows[1])[1](
        grad_normed
    )
    grad_rows = jnp.stack(
        [
            grad_gain,
            grad_shift,
            jnp.sum(grad_queries.astype(jnp.float32), axis=0),
            jnp.sum(grad_values.astype(jnp.float32), axis=0),
            jnp.sum(grad_branch.astype(jnp.float32), axis=0),
            grad_gain_two,
            grad_shift_two,
            jnp.sum(grad_low.astype(jnp.float32), axis=0),
        ]
    )
    return (
        grad_middle + grad_in_norm,
        (grad_rows, grad_qkv, grad_out_weight, grad_up, grad_up_bias, grad_down),
    )


def gather_plan(visible_row, slot_count, patch_count):
    seen_count = visible_row.shape[0]
    patch = jnp.arange(patch_count, dtype=jnp.int32)
    match = visible_row[None, :] == patch[:, None]
    seen = jnp.any(match, axis=1)
    rank = jnp.sum(jnp.where(match, jnp.arange(seen_count, dtype=jnp.int32)[None, :], 0), axis=1)
    slot = jnp.arange(slot_count, dtype=jnp.int32)
    source = (slot[:, None] * seen_count + rank[None, :]).reshape(-1)
    seen_row = jnp.broadcast_to(seen[None, :], (slot_count, patch_count)).reshape(-1)
    return (source, seen_row)


def slot_table(slots_used, slot_count):
    slot = jnp.arange(slot_count, dtype=jnp.int32)
    divisor = slots_used - 1
    numerator = slot * (slot_count - 1)
    lower = numerator // divisor
    fraction = (numerator - lower * divisor).astype(jnp.float32) / divisor.astype(jnp.float32)
    upper = jnp.minimum(lower + 1, slot_count - 1)
    column = slot[None, :]
    first = (column == lower[:, None]).astype(jnp.float32)
    second = (column == upper[:, None]).astype(jnp.float32)
    return (1.0 - fraction)[:, None] * first + fraction[:, None] * second


def square_sum(arrays):
    return sum((jnp.sum(item * item) for item in arrays))


def shards(
    tokens,
    frames,
    visible,
    out_grad,
    enc_vectors,
    enc_qkv,
    enc_out,
    enc_up,
    enc_up_bias,
    enc_down,
    proj_weight,
    dec_vectors,
    dec_qkv,
    dec_out,
    dec_up,
    dec_up_bias,
    dec_down,
    time_pos,
    space_pos,
):
    enc_weights = (enc_vectors, enc_qkv, enc_out, enc_up, enc_up_bias, enc_down)
    dec_block = (dec_vectors[:8], dec_qkv, dec_out, dec_up, dec_up_bias, dec_down)
    dec_params = (
        proj_weight,
        dec_vectors,
        dec_qkv,
        dec_out,
        dec_up,
        dec_up_bias,
        dec_down,
        time_pos,
        space_pos,
    )
    batch, vis_cap, enc_width = tokens.shape
    long_cap, dec_width = (out_grad.shape[1], out_grad.shape[2])
    slot_count = time_pos.shape[0]
    patch_count = space_pos.shape[0]
    seen_count = visible.shape[1]
    enc_heads = enc_width // HEAD_SIZE
    dec_heads = dec_width // HEAD_SIZE
    section = lax.axis_index("section")

    def mine(array):
        return lax.dynamic_index_in_dim(array, section, 0, keepdims=False)

    used = mine(frames) // 2
    seen_row = mine(visible)
    cotangent = mine(out_grad).astype(jnp.float32)
    enc_valid = jnp.arange(vis_cap) < used * seen_count
    enc_output, enc_saved = block_forward(
        mine(tokens).astype(jnp.float32), enc_weights, enc_heads, enc_valid
    )
    sent = enc_output.astype(jnp.bfloat16)
    source, seen_mask = gather_plan(seen_row, slot_count, patch_count)
    target = (
        jnp.arange(slot_count, dtype=jnp.int32)[:, None] * patch_count + seen_row[None, :]
    ).reshape(-1)
    projected = multiply(sent, proj_weight)
    base = jnp.where(
        seen_mask[:, None],
        jnp.take(projected, source, axis=0),
        dec_vectors[8].astype(jnp.float32),
    )
    table = slot_table(used, slot_count)
    slot_pos = jnp.dot(table, time_pos.astype(jnp.float32), precision=lax.Precision.HIGHEST)
    start = (
        base.reshape(slot_count, patch_count, dec_width)
        + slot_pos[:, None, :]
        + space_pos.astype(jnp.float32)[None]
    )
    start = start.reshape(long_cap, dec_width)
    row_valid = jnp.arange(long_cap) < used * patch_count
    output, saved = block_forward(start, dec_block, dec_heads, row_valid)
    decoded_row = jnp.where(row_valid[:, None], output, 0.0).astype(jnp.bfloat16)
    grad_start, block_grads = block_backward(
        jnp.where(row_valid[:, None], cotangent, 0.0), dec_block, dec_heads, row_valid, saved
    )
    grad_grid = grad_start.reshape(slot_count, patch_count, dec_width)
    grad_space = jnp.sum(grad_grid, axis=0)
    grad_time = jnp.dot(table.T, jnp.sum(grad_grid, axis=1), precision=lax.Precision.HIGHEST)
    grad_mask = jnp.sum(jnp.where(seen_mask[:, None], 0.0, grad_start), axis=0)
    grad_projected = jnp.take(grad_start, target, axis=0).astype(jnp.bfloat16)
    grad_proj = left_transposed(sent, grad_projected)
    grad_sent = right_transposed(grad_projected, proj_weight).astype(jnp.bfloat16)
    grad_rows = jnp.concatenate([block_grads[0], grad_mask[None, :]], axis=0)
    grad_in, enc_grads = block_backward(
        grad_sent.astype(jnp.float32), enc_weights, enc_heads, enc_valid, enc_saved
    )
    grads = (
        *enc_grads,
        grad_proj,
        grad_rows,
        *block_grads[1:],
        grad_time,
        grad_space,
    )

    def halves(array):
        axis = array.ndim - 1
        half = array.shape[axis] // 2
        keep = lax.dynamic_slice_in_dim(array, section * half, half, axis)
        give = lax.dynamic_slice_in_dim(array, (1 - section) * half, half, axis)
        return (keep, from_partner(give.astype(jnp.bfloat16), "section", 0))

    def both_clips(array):
        keep, came = halves(array)
        pair = jnp.stack([keep, came])
        return jnp.where(section == 0, pair, pair[::-1])

    decoded_half = both_clips(decoded_row)
    token_half = both_clips(grad_in.astype(jnp.bfloat16))
    local = []
    for item in grads:
        keep, came = halves(item)
        local.append((keep + came.astype(jnp.float32)).astype(jnp.bfloat16))
    summed = [item.astype(jnp.float32) for item in lax.psum(tuple(local), "dp")]
    squares = lax.psum(jnp.stack([square_sum(summed[:6]), square_sum(summed[6:])]), "section")
    norms = lax.dynamic_slice_in_dim(squares, section, 1, 0)
    return (decoded_half, token_half, *summed, norms)


def solution(mesh):
    placed = (
        P("dp", None, None),
        P("dp"),
        P("dp", None),
        P("dp", None, None),
        P(),
        P(),
        P(),
        P(),
        P(),
        P(),
        P(),
        P(),
        P(),
        P(),
        P(),
        P(),
        P(),
        P(),
        P(),
    )
    return jax.shard_map(
        shards,
        mesh=mesh,
        in_specs=placed,
        out_specs=(
            P("dp", None, "section"),
            P("dp", None, "section"),
            P(None, "section"),
            P(None, "section"),
            P(None, "section"),
            P(None, "section"),
            P("section"),
            P(None, "section"),
            P(None, "section"),
            P(None, "section"),
            P(None, "section"),
            P(None, "section"),
            P(None, "section"),
            P("section"),
            P(None, "section"),
            P(None, "section"),
            P(None, "section"),
            P("section"),
        ),
        check_vma=False,
    )
```

time: 1400 us -> 772 us (0.55)
  waiting for transfers between devices: 603 us -> 264 us
  loops' own time: 119 us -> 0 us
  matrix products: 295 us -> 194 us
  starting transfers between devices: 46.4 us -> 6.05 us
  other arithmetic: 187 us -> 149 us
    psum x2, waiting for transfers between devices: 485 us -> 264 us  [shards(): summed = [item.astype(jnp.float32) for item in lax.psum(tuple(local), 'dp')]]
    another operation x9 -> x0, loops' own time: 119 us -> none  [the longest x4 66.4 us: tick(): lax.cond(section == 0, first_section, second_section, state)]
    reduce_scatter x7 -> x0, waiting for transfers between devices: 69 us -> none  [the longest x1 14.2 us: shards(): lax.psum_scatter(summed[3].astype(jnp.bfloat16), 'section', scatter_dimen...]
    unnamed x25 -> x2, waiting for transfers between devices: 44.2 us -> 0.03 us
    ppermute x4 -> x17, starting transfers between devices: 45.7 us -> 5.97 us  [from_partner(): return lax.ppermute(value, axis, pairs)]
    convert_element_type x0 -> x16, local copies, waits for them, and re-layouts: none -> 30.2 us  [the longest x13 25.1 us: halves(): return (keep, from_partner(give.astype(jnp.bfloat16), 'section', 0))]
    dot_general x2, matrix products: 54.2 us -> 25.6 us  [block_backward(): jnp.einsum('qhd,khd->hqk', grad_mixed, values, preferred_element_type=jnp...]
    convert_element_type x2, other arithmetic: 52.8 us -> 26.5 us  [block_backward(): grad_scores = (probs * (grad_probs - jnp.sum(grad_probs * probs, axis=-1,...]
  transfers between devices with their start and end apart: 21 -> 19, of which waited for: 15 -> 2; matrix products, arithmetic and copies ran while one was open for 9% -> 37% of each run, Pallas kernels for 0% -> 0%
where the time goes in v1:
time: 772 us; the launch traced here: 760 us
  waiting for transfers between devices  264 us (34%)
  matrix products  194 us (25%)
  other arithmetic  149 us (19%)
  local copies, waits for them, and re-layouts  114 us (15%)
  between operations  28.1 us (4%)
    psum x2, waiting for transfers between devices, shards(): summed = [item.astype(jnp.float32) for item in lax.psum(tuple(local), 'dp')]  264 us
    dot_general x9, matrix products, multiply(): return jnp.dot(left, right, preferred_element_type=jnp.float32)  42.2 us
    reduce_sum x15, other arithmetic, square_sum(): return sum((jnp.sum(item * item) for item in arrays))  35.3 us
    convert_element_type x15, other arithmetic, shards(): local.append((keep + came.astype(jnp.float32)).astype(jnp.bfloat16))  30.9 us
    dot_general x9, matrix products, right_transposed(): lax.dot_general(left, right, (((1,), (1,)), ((), ())), preferred_element_...  30.7 us
    dot_general x9, matrix products, left_transposed(): lax.dot_general(left, right, (((0,), (0,)), ((), ())), preferred_element_...  30.1 us
    convert_element_type x2, other arithmetic, block_backward(): grad_scores = (probs * (grad_probs - jnp.sum(grad_probs * probs, axis=-1,...  26.5 us
    dot_general x2, matrix products, block_backward(): jnp.einsum('qhd,khd->hqk', grad_mixed, values, preferred_element_type=jnp...  25.6 us
  transfers between devices with their start and end apart: 19, of which 2 were waited for; matrix products, arithmetic and copies ran while one was open for 37% of the time, Pallas kernels for 0%

profile of v1, /device:TPU:1, one launch (start us, length us, event | category | flops | bytes accessed | tf_op | source)
XLA Modules:
  0.0 759.7 jit_solution(7828411090295234722)
XLA Ops:
  59.8 7.7 %multiply_convert_fusion.2 = (bf16[112,3072]{1,0:T(8,128)(2,1)S(1)}, f32[112,3072]{1,0:T(8,128)}, f32[112,3072]{1,0:T(8,128)}) fusion(f32[3072]{0:T(1024)} %convert_element_type.418, bf16[768,3072]{1,0:T(8,128)(2,1)} %param.26, f32[112,768]{1,0:T(8,128)} %copy-done.12, f32[768]{0:T(1024)S(1)} %get-tuple-element.86, f32[768]{0:T(1024)S(1)} %get-tuple-element.87, ...), kind=kOutput, calls=%fused_computation.87 | convolution fusion | flops 551620608 | bytes 8522624 | tf_op jit(solution)/shard_map/dot_general | solution.py:30
  72.7 5.4 gather_fusion
  89.2 12.7 %fusion.117 = (f32[6,1152]{1,0:T(8,128)S(1)}, f32[6,1152,1152]{1,2,0:T(8,128)}) fusion(bf16[1152,6,64]{0,2,1:T(8,128)(2,1)S(1)} %bitcast.166, bf16[1152,6,64]{0,2,1:T(8,128)(2,1)S(1)} %bitcast.164, pred[1152]{0:T(1024)(128)(4,1)S(1)} %copy-done.88), kind=kOutput, calls=%fused_computation.318 | convolution fusion | flops 1043096832 | bytes 33648768 | tf_op jit(solution)/shard_map/qhd,khd->hqk/dot_general | solution.py:46
  101.9 12.7 %fusion.1 = f32[6,1152]{1,0:T(8,128)S(1)} fusion(f32[6,1152,1152]{1,2,0:T(8,128)} %get-tuple-element.183, f32[6,1152]{1,0:T(8,128)S(1)} %get-tuple-element.182), kind=kLoop, calls=%fused_computation.9 | loop fusion | flops 15918336 | bytes 31905792 | tf_op jit(solution)/shard_map/reduce_sum | solution.py:64
  114.6 12.6 %fusion.16 = bf16[6,64,1152]{2,1,0:T(8,128)(2,1)S(1)} fusion(bf16[1152,6,64]{0,2,1:T(8,128)(2,1)S(1)} %bitcast.172, f32[6,1152,1152]{1,2,0:T(8,128)} %get-tuple-element.183, f32[6,1152]{1,0:T(8,128)S(1)} %fusion.1, f32[6,1152]{1,0:T(8,128)S(1)} %get-tuple-element.182), kind=kOutput, calls=%fused_computation.50 | convolution fusion | flops 1043546112 | bytes 33675264 | tf_op jit(solution)/shard_map/hqk,khd->qhd/dot_general | solution.py:67
  130.2 20.9 %multiply_convert_fusion.1 = (bf16[1152,1536]{1,0:T(8,128)(2,1)}, f32[1152,1536]{1,0:T(8,128)S(1)}, f32[1152,1536]{1,0:T(8,128)S(1)}) fusion(f32[1536]{0:T(1024)} %convert_element_type.435, bf16[384,1536]{1,0:T(8,128)(2,1)} %param.33, f32[1152,384]{0,1:T(8,128)} %copy-done.3, f32[384]{0:T(512)} %get-tuple-element.94, f32[384]{0:T(512)} %get-tuple-element.95, ...), kind=kOutput, calls=%fused_computation.19 | convolution fusion | flops 1477951488 | bytes 20662272 | tf_op jit(solution)/shard_map/dot_general | solution.py:30
  151.1 4.3 convert_reduce_fusion
  181.1 13.3 %convert_reduce_fusion.3 = (f32[6,64]{1,0:T(8,128)S(1)}, bf16[6,64,1152]{2,1,0:T(8,128)(2,1)}) fusion(bf16[1152,6,64]{0,2,1:T(8,128)(2,1)S(1)} %bitcast.168, f32[6,1152,1152]{1,2,0:T(8,128)} %get-tuple-element.183, f32[6,1152]{1,0:T(8,128)S(1)} %log_add_fusion), kind=kOutput, calls=%fused_computation.72 | convolution fusion | flops 1036467840 | bytes 33649152 | tf_op jit(solution)/shard_map/hqk,qhd->khd/dot_general | solution.py:128
  194.4 24.0 %multiply_reduce_fusion = (f32[6,1152]{1,0:T(8,128)S(1)}, f32[6,1152,1152]{1,2,0:T(8,128)}) fusion(f32[6,1152,1152]{1,2,0:T(8,128)} %get-tuple-element.183, f32[6,1152]{1,0:T(8,128)S(1)} %log_add_fusion, bf16[1152,6,64]{0,2,1:T(8,128)(2,1)S(1)} %bitcast.169, bf16[1152,6,64]{0,2,1:T(8,128)(2,1)} %bitcast.173), kind=kOutput, calls=%fused_computation.5 | convolution fusion | flops 1043096832 | bytes 65525760 | tf_op jit(solution)/shard_map/qhd,khd->hqk/dot_general | solution.py:131
  218.4 26.4 %multiply_convert_fusion = bf16[6,1152,1152]{1,2,0:T(8,128)(2,1)} fusion(f32[6,1152,1152]{1,2,0:T(8,128)} %get-tuple-element.188, f32[6,1152,1152]{1,2,0:T(8,128)} %get-tuple-element.183, f32[6,1152]{1,0:T(8,128)S(1)} %get-tuple-element.187, f32[6,1152]{1,0:T(8,128)S(1)} %log_add_fusion), kind=kLoop, calls=%fused_computation.4 | loop fusion | flops 31850496 | bytes 79681536 | tf_op jit(solution)/shard_map/convert_element_type | solution.py:134
  244.8 11.6 %fusion.22 = bf16[6,64,1152]{2,1,0:T(8,128)(2,1)} fusion(bf16[1152,6,64]{0,2,1:T(8,128)(2,1)} %bitcast.167, bf16[6,1152,1152]{1,2,0:T(8,128)(2,1)} %multiply_convert_fusion), kind=kOutput, calls=%fused_computation.54 | convolution fusion | flops 1020100608 | bytes 17694720 | tf_op jit(solution)/shard_map/hqk,qhd->khd/dot_general | solution.py:139
  256.5 9.4 %convert_reduce_fusion.4 = (f32[6,64]{1,0:T(8,128)S(1)}, bf16[6,64,1152]{2,1,0:T(8,128)(2,1)}) fusion(bf16[1152,6,64]{0,2,1:T(8,128)(2,1)} %bitcast.165, bf16[6,1152,1152]{1,2,0:T(8,128)(2,1)} %multiply_convert_fusion), kind=kOutput, calls=%fused_computation.73 | convolution fusion | flops 1020984960 | bytes 17696256 | tf_op jit(solution)/shard_map/hqk,khd->qhd/dot_general | solution.py:136
  269.4 4.9 fusion.119
  302.9 5.8 convert_reduce_fusion.5
  311.8 5.0 fusion.39
  316.9 4.7 multiply_reduce_fusion.16
  342.0 5.1 fusion.102
  347.2 5.1 fusion.123
  375.0 4.2 dynamic-slice_convert_fusion.1
  412.6 4.7 add_convert_fusion.3
  417.3 5.1 add_convert_fusion.1
  426.2 4.6 fusion.17
  434.2 92.0 %all-reduce.5.cloned.1.call-done = (bf16[8,384]{1,0:T(8,128)(2,1)}, bf16[1536]{0:T(1024)(128)(2,1)}, bf16[9,192]{1,0:T(8,128)(2,1)}, bf16[768]{0:T(1024)(128)(2,...) async-done(((bf16[8,384]{1,0:T(8,128)(2,1)}, bf16[1536]{0:T(1024)(128)(2,1)}, bf16[9,192]{1,0:T(8,128)(2,1)}, bf16[768]{0:T(1024)(128)(2,1)}, ...) | async-done | bytes 72592 | tf_op jit(solution)/shard_map/psum | solution.py:313
  540.3 172.3 %all-reduce.7.cloned.1.call-done = (bf16[384,576]{1,0:T(8,128)(2,1)}, bf16[768,1152]{1,0:T(8,128)(2,1)}, bf16[768,384]{1,0:T(8,128)(2,1)}, bf16[768,1536]{1,0:T(...) async-done(((bf16[384,576]{1,0:T(8,128)(2,1)}, ...) | async-done | bytes 9142288 | tf_op jit(solution)/shard_map/psum | solution.py:313
  (526 shorter events, 257.2 us)
Async XLA Ops:
  7.2 30.0 %copy-start = (bf16[768,2304]{1,0:T(8,128)(2,1)S(1)}, bf16[768,2304]{1,0:T(8,128)(2,1)}, u32[]{:S(2)}) copy-start(bf16[768,2304]{1,0:T(8,128)(2,1)} %param.24) | copy-start | bytes 10616836
  7.2 519.0 %all-reduce.5.cloned.1.call-start = ((), (), s32[]{:S(2)}) async-start(), calls=%async_computation | async-start | bytes 196608 | tf_op jit(solution)/shard_map/psum | solution.py:313
  32.8 27.0 %copy-start.70 = (f32[768]{0:T(1024)}, f32[768]{0:T(1024)S(1)}, u32[]{:S(2)}) copy-start(f32[768]{0:T(1024)S(1)} %get-tuple-element.87) | copy-start | bytes 9220
  32.8 27.0 %copy-start.77 = (f32[768]{0:T(1024)}, f32[768]{0:T(1024)S(1)}, u32[]{:S(2)}) copy-start(f32[768]{0:T(1024)S(1)} %get-tuple-element.86) | copy-start | bytes 9220
  84.1 43.2 %copy-start.1 = (f32[1152,384]{0,1:T(8,128)}, f32[1152,384]{0,1:T(8,128)S(1)}, u32[]{:S(2)}) copy-start(f32[1152,384]{0,1:T(8,128)S(1)} %get-tuple-element.165) | copy-start | bytes 5308420
  88.8 25.8 %copy-start.30 = (bf16[1152,384]{0,1:T(8,128)(2,1)}, bf16[1152,384]{0,1:T(8,128)(2,1)S(1)}, u32[]{:S(2)}) copy-start(bf16[1152,384]{0,1:T(8,128)(2,1)S(1)} %get-tuple-element.167) | copy-start | bytes 2654212
  156.1 233.6 %collective-permute-start.13 = (bf16[768]{0:T(1024)(128)(2,1)}, bf16[768]{0:T(1024)(128)(2,1)}, u32[]{:S(2)}, u32[]{:S(2)}) collective-permute-start(bf16[768]{0:T(1024)(128)(2,1)} %dynamic_slice.218), channel_id=1, source_target_pairs={{0,64},{64,0},{1,65},{65,1},{2,66},{66,2},{3,67},{67,3},{4,68},{68... | collective-permute-start | bytes 4616 | tf_op jit(solution)/shard_map/ppermute | solution.py:16
  161.8 245.1 %collective-permute-start.12 = (bf16[384,768]{1,0:T(8,128)(2,1)}, bf16[384,768]{1,0:T(8,128)(2,1)}, u32[]{:S(2)}, u32[]{:S(2)}) collective-permute-start(bf16[384,768]{1,0:T(8,128)(2,1)} %dynamic-slice_convert_fusion.4), channel_id=1, source_target_pairs={{0,64},{64,0},{1,65},{65,1},{2,66},{66,2},{3,67},{67,3},{4,68},{68... | collective-permute-start | bytes 1769480 | tf_op jit(solution)/shard_map/ppermute | solution.py:16
  177.9 222.0 %collective-permute-start.11 = (bf16[384,192]{0,1:T(8,128)(2,1)}, bf16[384,192]{0,1:T(8,128)(2,1)}, u32[]{:S(2)}, u32[]{:S(2)}) collective-permute-start(bf16[384,192]{0,1:T(8,128)(2,1)} %dynamic-slice_convert_fusion.8), channel_id=1, source_target_pairs={{0,64},{64,0},{1,65},{65,1},{2,66},{66,2},{3,67},{67,3},{4,68},{68... | collective-permute-start | bytes 442376 | tf_op jit(solution)/shard_map/ppermute | solution.py:16
  289.4 105.0 %collective-permute-start.9 = (bf16[9,192]{1,0:T(8,128)(2,1)}, bf16[9,192]{1,0:T(8,128)(2,1)}, u32[]{:S(2)}, u32[]{:S(2)}) collective-permute-start(bf16[9,192]{1,0:T(8,128)(2,1)} %dynamic-slice_convert_fusion.10), channel_id=1, source_target_pairs={{0,64},{64,0},{1,65},{65,1},{2,66},{66,2},{3,67},{67,3},{4,68},{68... | collective-permute-start | bytes 10376 | tf_op jit(solution)/shard_map/ppermute | solution.py:16
  310.0 81.2 %collective-permute-start.6 = (bf16[1536]{0:T(1024)(128)(2,1)}, bf16[1536]{0:T(1024)(128)(2,1)}, u32[]{:S(2)}, u32[]{:S(2)}) collective-permute-start(bf16[1536]{0:T(1024)(128)(2,1)} %dynamic_slice.217), channel_id=1, source_target_pairs={{0,64},{64,0},{1,65},{65,1},{2,66},{66,2},{3,67},{67,3},{4,68},{68... | collective-permute-start | bytes 9224 | tf_op jit(solution)/shard_map/ppermute | solution.py:16
  389.8 3.3 collective-permute-start.15
  391.2 6.5 collective-permute-start.16
  393.0 3.3 collective-permute-start.2
  394.4 7.5 collective-permute-start.8
  396.3 16.3 %collective-permute-start.3 = (bf16[768,1152]{1,0:T(8,128)(2,1)}, bf16[768,1152]{1,0:T(8,128)(2,1)}, u32[]{:S(2)}, u32[]{:S(2)}) collective-permute-start(bf16[768,1152]{1,0:T(8,128)(2,1)} %dynamic-slice_convert_fusion.2), channel_id=1, source_target_pairs={{0,64},{64,0},{1,65},{65,1},{2,66},{66,2},{3,67},{67,3},{4,68},{68... | collective-permute-start | bytes 5308424 | tf_op jit(solution)/shard_map/ppermute | solution.py:16
  397.7 19.6 %collective-permute-start.7 = (bf16[3072,384]{1,0:T(8,128)(2,1)}, bf16[3072,384]{1,0:T(8,128)(2,1)}, u32[]{:S(2)}, u32[]{:S(2)}) collective-permute-start(bf16[3072,384]{1,0:T(8,128)(2,1)} %dynamic-slice_convert_fusion), channel_id=1, source_target_pairs={{0,64},{64,0},{1,65},{65,1},{2,66},{66,2},{3,67},{67,3},{4,68},{68... | collective-permute-start | bytes 7077896 | tf_op jit(solution)/shard_map/ppermute | solution.py:16
  399.8 312.7 %all-reduce.7.cloned.1.call-start = ((), (), s32[]{:S(2)}) async-start(), calls=%async_computation.1 | async-start | bytes 18382848 | tf_op jit(solution)/shard_map/psum | solution.py:313
  399.9 4.4 collective-permute-start.10
  401.9 7.9 %collective-permute-start.4 = (bf16[768,384]{1,0:T(8,128)(2,1)}, bf16[768,384]{1,0:T(8,128)(2,1)S(1)}, u32[]{:S(2)}, u32[]{:S(2)}) collective-permute-start(bf16[768,384]{1,0:T(8,128)(2,1)} %dynamic-slice_convert_fusion.5), channel_id=1, source_target_pairs={{0,64},{64,0},{1,65},{65,1},{2,66},{66,2},{3,67},{67,3},{4,68},{68... | collective-permute-start | bytes 1769480 | tf_op jit(solution)/shard_map/ppermute | solution.py:16
  404.3 6.5 collective-permute-start.14
  406.9 15.5 %collective-permute-start.5 = (bf16[768,1536]{1,0:T(8,128)(2,1)S(1)}, bf16[768,1536]{1,0:T(8,128)(2,1)S(1)}, u32[]{:S(2)}, u32[]{:S(2)}) collective-permute-start(bf16[768,1536]{1,0:T(8,128)(2,1)S(1)} %copy-done.42), channel_id=1, source_target_pairs={{0,64},{64,0},{1,65},{65,1},{2,66},{66,2},{3,67},{67,3},{4,68},{68... | collective-permute-start | bytes 7077896 | tf_op jit(solution)/shard_map/ppermute | solution.py:16
  426.2 6.4 collective-permute-start.1
  431.9 106.1 %collective-permute-start = (bf16[1152,192]{0,1:T(8,128)(2,1)}, bf16[1152,192]{0,1:T(8,128)(2,1)}, u32[]{:S(2)}, u32[]{:S(2)}) collective-permute-start(bf16[1152,192]{0,1:T(8,128)(2,1)} %get-tuple-element.172), channel_id=1, source_target_pairs={{0,64},{64,0},{1,65},{65,1},{2,66},{66,2},{3,67},{67,3},{4,68},{68... | collective-permute-start | bytes 1327112 | tf_op jit(solution)/shard_map/ppermute | solution.py:16
  (146 other events, 585.8 us)
Sparse Core Ops, SparseCore 0:
  399.9 126.2 all-reduce.4
  534.9 177.5 all-reduce.6

commit v2 on v1

--- a/solution.py
+++ b/solution.py
@@ -1,7 +1,255 @@
-import jax
-import jax.numpy as jnp
+import functools
+import jax, jax.numpy as jnp, numpy as np
 from jax import lax
-from jax.sharding import PartitionSpec as P
+from jax.experimental import pallas as pl
+from jax.experimental.pallas import tpu as pltpu
+
+EPS = 1e-6
+NEG = -1e9
+LOG2E = 1.4426950408889634
+LN2 = 0.6931471805599453
+F32, BF = jnp.float32, jnp.bfloat16
+
+
+def dot(a, b, ca=1, cb=0):
+    return lax.dot_general(a, b, (((ca,), (cb,)), ((), ())), preferred_element_type=F32)
+
+
+def tiles_of(total, size):
+    return [(s, min(size, total - s)) for s in range(0, total, size)]
+
+
+def over(total, size, body, carry):
+    full = total // size
+    if full:
+        carry = lax.fori_loop(0, full, lambda i, k: body(pl.ds(pl.multiple_of(i * size, 128), size), size, k), carry)
+    if total % size:
+        carry = body(pl.ds(full * size, total % size), total % size, carry)
+    return carry
+
+
+def norm_c(x):
+    mean = jnp.mean(x, axis=0, keepdims=True)
+    c = x - mean
+    r = lax.rsqrt(jnp.mean(c * c, axis=0, keepdims=True) + EPS)
+    return c * r, r
+
+
+def gelu_pair(u):
+    a = jnp.abs(u)
+    t = 1.0 / (1.0 + (0.3275911 * 0.7071067811865476) * a)
+    e = jnp.exp2((-0.5 * LOG2E) * (u * u))
+    poly = t * (0.5 * 0.254829592 + t * (0.5 * -0.284496736 + t * (0.5 * 1.421413741 + t * (0.5 * -1.453152027 + t * (0.5 * 1.061405429)))))
+    tail = poly * e
+    phi = jnp.where(u >= 0, 1.0 - tail, tail)
+    return u * phi, phi + u * (e * 0.3989422804014327)
+
+
+def dec_kernel(used_ref, tgt_ref, proj_ref, posm_ref, space_ref, vec_ref, wqkv_ref, wo_ref, w1_ref, b1_ref, w2_ref, dy_ref,
+               decoded_ref, dz_ref, gpos_ref, gvec_ref, gqkv_ref, go_ref, g1_ref, gb1_ref, g2_ref,
+               x_s, a1_s, qkv_s, e_s, l_s, o_s, m_s, a2_s, g_s, gp_s, dy_s, db_s, sel_s, doa_s, do_s, o32_s, *, W, L, H, FF, patches, TQ, TA):
+    dqkv_s, ds_s = g_s, gp_s
+    valid = used_ref[0] * patches
+    col = lambda i: vec_ref[:, i:i + 1]
+    HS = 64
+    lane = lax.broadcasted_iota(jnp.int32, (1, L), 1)
+    V = tgt_ref.shape[0]
+    onehot = (tgt_ref[...] == lax.broadcasted_iota(jnp.int32, (V, L), 1)).astype(F32)
+    slot = lane // patches
+    patch_oh = (lax.broadcasted_iota(jnp.int32, (patches, L), 0) == lane - slot * patches).astype(BF)
+    seen = jnp.sum(onehot, axis=0, keepdims=True)
+    srow = lax.broadcasted_iota(jnp.int32, (32, L), 0)
+    slot_oh = jnp.where(srow < 16, ((srow & 7) == slot).astype(F32), jnp.where(srow == 16, 1.0 - seen, 0.0)).astype(BF)
+    sel_s[:V, :] = onehot.astype(BF)
+    sel_s[V:V + patches, :] = patch_oh
+    sel_s[V + patches:, :] = slot_oh
+    proj = proj_ref[...]
+    hi = proj.astype(BF)
+    lo = (proj - hi.astype(F32)).astype(BF)
+    src = jnp.concatenate([hi, space_ref[...], posm_ref[...]], axis=0)
+
+    def first(c, n, k):
+        x = dot(src, sel_s[:, c], 0, 0) + dot(lo, sel_s[:V, c], 0, 0)
+        x_s[:, c] = x
+        xh, _ = norm_c(x)
+        a1 = (xh * col(0) + col(1)).astype(BF)
+        a1_s[:, c] = a1
+        j = dot(wqkv_ref[...], a1, 0, 0)
+        qkv_s[:W, c] = ((j[:W] + col(2)) * (0.125 * LOG2E)).astype(BF)
+        qkv_s[W:2 * W, c] = j[W:2 * W].astype(BF)
+        qkv_s[2 * W:, c] = (j[2 * W:] + col(3)).astype(BF)
+        return k
+
+    over(L, TQ, first, 0)
+    arow = lax.broadcasted_iota(jnp.int32, (16, L), 0)
+    kbias = jnp.where((arow == 0) & (lane >= valid), NEG, 0.0).astype(BF)
+    one0 = (arow == 0).astype(BF)
+    one01 = (arow < 2).astype(BF)
+
+    def fwd_head(h, carry):
+        hs = pl.ds(pl.multiple_of(h * HS, HS), HS)
+        ks = pl.ds(pl.multiple_of(W + h * HS, HS), HS)
+        vs = pl.ds(pl.multiple_of(2 * W + h * HS, HS), HS)
+        kr = jnp.concatenate([qkv_s[ks, :], kbias], axis=0).T
+        vc = jnp.concatenate([qkv_s[vs, :], one0], axis=0)
+
+        def tile(c, n, exact):
+            qc = jnp.concatenate([qkv_s[hs, c], one0[:, :n]], axis=0)
+            st = dot(kr, qc)
+            if exact:
+                st = st - jnp.max(st, axis=0, keepdims=True)
+            e = jnp.exp2(st).astype(BF)
+            e_s[h, :, c] = e
+            oa = dot(vc, e)
+            rl = 1.0 / oa[HS:HS + 1]
+            l_s[h, :, c] = jnp.broadcast_to(rl, (8, n))
+            o = oa[:HS] * rl
+            o32_s[hs, c] = o
+            o_s[hs, c] = o.astype(BF)
+
+        square = lambda v: jnp.max(jnp.sum(v * v, axis=0))
+        bound = square(qkv_s[hs, :].astype(F32)) * square(qkv_s[ks, :].astype(F32))
+
+        @pl.when(bound <= 60.0 * 60.0)
+        def _():
+            over(L, TA, lambda c, n, k: (tile(c, n, False), k)[1], 0)
+
+        @pl.when(jnp.logical_not(bound <= 60.0 * 60.0))
+        def _():
+            over(L, TA, lambda c, n, k: (tile(c, n, True), k)[1], 0)
+
+        return carry
+
+    lax.fori_loop(0, H, fwd_head, 0)
+
+    def middle(c, n, sums):
+        sum_b1, sum_dy, sum_g2, sum_s2, sum_db = sums
+        live = (lax.broadcasted_iota(jnp.int32, (1, n), 1) + c.start < valid).astype(F32)
+        mid = x_s[:, c] + (dot(wo_ref[...], o_s[:, c], 0, 0) + col(4))
+        xh, r = norm_c(mid)
+        a2 = (xh * col(5) + col(6)).astype(BF)
+        a2_s[:, c] = a2
+        u = dot(w1_ref[...], a2, 0, 0) + b1_ref[...]
+        g, gp = gelu_pair(u)
+        g = g.astype(BF)
+        g_s[:, c] = g
+        y = mid + (dot(w2_ref[...], g, 0, 0) + col(7))
+        decoded_ref[c, :] = (y * live).astype(BF).T
+        dyf = dy_ref[c, :].astype(F32).T * live
+        dy = dyf.astype(BF)
+        dy_s[:, c] = dy
+        duf = gp * dot(w2_ref[...], dy)
+        du = duf.astype(BF)
+        gp_s[:, c] = du
+        da2 = dot(w1_ref[...], du)
+        dg = da2 * col(5)
+        dm = dyf + r * (dg - jnp.mean(dg, axis=0, keepdims=True) - xh * jnp.mean(dg * xh, axis=0, keepdims=True))
+        db = dm.astype(BF)
+        db_s[:, c] = db
+        do_s[:, c] = dot(wo_ref[...], db).astype(BF)
+        m_s[:, c] = dm
+        rs = lambda v: jnp.sum(v, axis=1, keepdims=True)
+        return (sum_b1 + rs(duf), sum_dy + rs(dyf), sum_g2 + rs(da2 * xh), sum_s2 + rs(da2), sum_db + rs(dm))
+
+    zero = jnp.zeros((W, 1), F32)
+    sum_b1, sum_dy, sum_g2, sum_s2, sum_db = over(L, TQ, middle, (jnp.zeros((FF, 1), F32), zero, zero, zero, zero))
+    gvec_ref[:, 4:5] = sum_db
+    gvec_ref[:, 5:6] = sum_g2
+    gvec_ref[:, 6:7] = sum_s2
+    gvec_ref[:, 7:8] = sum_dy
+    gb1_ref[...] = sum_b1
+    g2_ref[...] = dot(g_s[...], dy_s[...], 1, 1).astype(BF)
+    g1_ref[...] = dot(a2_s[...], gp_s[...], 1, 1).astype(BF)
+    go_ref[...] = dot(o_s[...], db_s[...], 1, 1).astype(BF)
+
+    def bwd_head(h, carry):
+        hs = pl.ds(pl.multiple_of(h * HS, HS), HS)
+        ks = pl.ds(pl.multiple_of(W + h * HS, HS), HS)
+        vs = pl.ds(pl.multiple_of(2 * W + h * HS, HS), HS)
+        vr = jnp.concatenate([qkv_s[vs, :], one01], axis=0).T
+        kc = qkv_s[ks, :]
+        dob = (do_s[hs, :].astype(F32) * l_s[h, 0:1, :]).astype(BF)
+        dl = -jnp.sum(dob.astype(F32) * o32_s[hs, :], axis=0, keepdims=True)
+        dlh = dl.astype(BF).astype(F32)
+        doa_s[:HS, :] = dob
+        doa_s[HS:, :] = jnp.where(arow == 0, dlh, jnp.where(arow == 1, dl - dlh, 0.0)).astype(BF)
+        def tile(c, n, k):
+            dp = dot(vr, doa_s[:, c])
+            ds = (e_s[h, :, c].astype(F32) * dp).astype(BF)
+            ds_s[:L, c] = ds
+            dqkv_s[hs, c] = (dot(kc, ds) * 0.125).astype(BF)
+            return k
+
+        over(L, TA, tile, 0)
+        dor = doa_s[:HS, :].T
+        qr = qkv_s[hs, :].T
+
+        def tile2(c, n, k):
+            dqkv_s[vs, c] = dot(e_s[h, c, :], dor).T.astype(BF)
+            dqkv_s[ks, c] = (dot(ds_s[c, :], qr) * LN2).T.astype(BF)
+            return k
+
+        return over(L, TA, tile2, carry)
+
+    lax.fori_loop(0, H, bwd_head, 0)
+    gqkv_ref[...] = dot(a1_s[...], dqkv_s[:3 * W, :], 1, 1).astype(BF)
+
+    def last(c, n, sums):
+        sum_g1, sum_s1, sum_q, sum_v, gsel = sums
+        rs = lambda v: jnp.sum(v, axis=1, keepdims=True)
+        da = dot(wqkv_ref[...], dqkv_s[:3 * W, c])
+        xh, r = norm_c(x_s[:, c])
+        dg = da * col(0)
+        dx = m_s[:, c] + r * (dg - jnp.mean(dg, axis=0, keepdims=True) - xh * jnp.mean(dg * xh, axis=0, keepdims=True))
+        return (sum_g1 + rs(da * xh), sum_s1 + rs(da), sum_q + rs(dqkv_s[:W, c].astype(F32)), sum_v + rs(dqkv_s[2 * W:3 * W, c].astype(F32)),
+                gsel + dot(dx.astype(BF), sel_s[:, c], 1, 1))
+
+    sum_g1, sum_s1, sum_q, sum_v, gsel = over(L, TQ, last, (zero, zero, zero, zero, jnp.zeros((W, sel_s.shape[0]), F32)))
+    gvec_ref[:, 0:1] = sum_g1
+    gvec_ref[:, 1:2] = sum_s1
+    gvec_ref[:, 2:3] = sum_q
+    gvec_ref[:, 3:4] = sum_v
+    gvec_ref[:, 8:] = jnp.zeros((W, gvec_ref.shape[1] - 8), F32)
+    gs = gsel.T
+    dz_ref[...] = gs[:V].astype(BF)
+    gpos_ref[...] = gs[V:]
+
+
+def dec_block_call(used, tgt, proj, posm, space, vec, wqkv, wo, w1, b1, w2, dy, TQ=256, TA=256):
+    W, L, FF = wqkv.shape[0], dy.shape[0], w1.shape[1]
+    H = W // 64
+    patches = space.shape[0]
+    V = tgt.shape[0]
+    vm = pl.BlockSpec(memory_space=pltpu.VMEM)
+    S = jax.ShapeDtypeStruct
+    return pl.pallas_call(
+        functools.partial(dec_kernel, W=W, L=L, H=H, FF=FF, patches=patches, TQ=TQ, TA=TA),
+        in_specs=[pl.BlockSpec(memory_space=pltpu.SMEM)] + [vm] * 11,
+        out_specs=[vm] * 9,
+        out_shape=[S((L, W), BF), S((V, W), BF), S((patches + 32, W), F32), S((W, 128), F32), S((W, 3 * W), BF), S((W, W), BF), S((W, FF), BF), S((FF, 1), F32), S((FF, W), BF)],
+        scratch_shapes=[
+            pltpu.VMEM((W, L), F32),
+            pltpu.VMEM((W, L), BF),
+            pltpu.VMEM((3 * W, L), BF),
+            pltpu.VMEM((H, L, L), BF),
+            pltpu.VMEM((H, 8, L), F32),
+            pltpu.VMEM((W, L), BF),
+            pltpu.VMEM((W, L), F32),
+            pltpu.VMEM((W, L), BF),
+            pltpu.VMEM((FF, L), BF),
+            pltpu.VMEM((FF, L), BF),
+            pltpu.VMEM((W, L), BF),
+            pltpu.VMEM((W, L), BF),
+            pltpu.VMEM((V + patches + 32, L), BF),
+            pltpu.VMEM((80, L), BF),
+            pltpu.VMEM((W, L), BF),
+            pltpu.VMEM((W, L), F32),
+        ],
+        compiler_params=pltpu.CompilerParams(vmem_limit_bytes=63 * 1024 * 1024),
+        cost_estimate=pl.CostEstimate(flops=28_000_000_000, bytes_accessed=12_000_000, transcendentals=10_000_000),
+        name="decoder",
+    )(used, tgt, proj, posm, space, vec, wqkv, wo, w1, b1, w2, dy)
+
 
 HEAD_SIZE = 64
 
@@ -165,18 +413,6 @@
     )
 
 
-def gather_plan(visible_row, slot_count, patch_count):
-    seen_count = visible_row.shape[0]
-    patch = jnp.arange(patch_count, dtype=jnp.int32)
-    match = visible_row[None, :] == patch[:, None]
-    seen = jnp.any(match, axis=1)
-    rank = jnp.sum(jnp.where(match, jnp.arange(seen_count, dtype=jnp.int32)[None, :], 0), axis=1)
-    slot = jnp.arange(slot_count, dtype=jnp.int32)
-    source = (slot[:, None] * seen_count + rank[None, :]).reshape(-1)
-    seen_row = jnp.broadcast_to(seen[None, :], (slot_count, patch_count)).reshape(-1)
-    return (source, seen_row)
-
-
 def slot_table(slots_used, slot_count):
     slot = jnp.arange(slot_count, dtype=jnp.int32)
     divisor = slots_used - 1
@@ -216,7 +452,6 @@
     space_pos,
 ):
     enc_weights = (enc_vectors, enc_qkv, enc_out, enc_up, enc_up_bias, enc_down)
-    dec_block = (dec_vectors[:8], dec_qkv, dec_out, dec_up, dec_up_bias, dec_down)
     dec_params = (
         proj_weight,
         dec_vectors,
@@ -229,12 +464,11 @@
         space_pos,
     )
     batch, vis_cap, enc_width = tokens.shape
-    long_cap, dec_width = (out_grad.shape[1], out_grad.shape[2])
+    dec_width = out_grad.shape[2]
     slot_count = time_pos.shape[0]
     patch_count = space_pos.shape[0]
     seen_count = visible.shape[1]
     enc_heads = enc_width // HEAD_SIZE
-    dec_heads = dec_width // HEAD_SIZE
     section = lax.axis_index("section")
 
     def mine(array):
@@ -242,44 +476,56 @@
 
     used = mine(frames) // 2
     seen_row = mine(visible)
-    cotangent = mine(out_grad).astype(jnp.float32)
     enc_valid = jnp.arange(vis_cap) < used * seen_count
     enc_output, enc_saved = block_forward(
         mine(tokens).astype(jnp.float32), enc_weights, enc_heads, enc_valid
     )
     sent = enc_output.astype(jnp.bfloat16)
-    source, seen_mask = gather_plan(seen_row, slot_count, patch_count)
     target = (
         jnp.arange(slot_count, dtype=jnp.int32)[:, None] * patch_count + seen_row[None, :]
-    ).reshape(-1)
+    ).reshape(-1, 1)
     projected = multiply(sent, proj_weight)
-    base = jnp.where(
-        seen_mask[:, None],
-        jnp.take(projected, source, axis=0),
-        dec_vectors[8].astype(jnp.float32),
-    )
     table = slot_table(used, slot_count)
     slot_pos = jnp.dot(table, time_pos.astype(jnp.float32), precision=lax.Precision.HIGHEST)
-    start = (
-        base.reshape(slot_count, patch_count, dec_width)
-        + slot_pos[:, None, :]
-        + space_pos.astype(jnp.float32)[None]
-    )
-    start = start.reshape(long_cap, dec_width)
-    row_valid = jnp.arange(long_cap) < used * patch_count
-    output, saved = block_forward(start, dec_block, dec_heads, row_valid)
-    decoded_row = jnp.where(row_valid[:, None], output, 0.0).astype(jnp.bfloat16)
-    grad_start, block_grads = block_backward(
-        jnp.where(row_valid[:, None], cotangent, 0.0), dec_block, dec_heads, row_valid, saved
-    )
-    grad_grid = grad_start.reshape(slot_count, patch_count, dec_width)
-    grad_space = jnp.sum(grad_grid, axis=0)
-    grad_time = jnp.dot(table.T, jnp.sum(grad_grid, axis=1), precision=lax.Precision.HIGHEST)
-    grad_mask = jnp.sum(jnp.where(seen_mask[:, None], 0.0, grad_start), axis=0)
-    grad_projected = jnp.take(grad_start, target, axis=0).astype(jnp.bfloat16)
+    slot_high = slot_pos.astype(jnp.bfloat16)
+    slot_low = (slot_pos - slot_high.astype(jnp.float32)).astype(jnp.bfloat16)
+    positions = jnp.concatenate(
+        [slot_high, slot_low, dec_vectors[8:9], jnp.zeros((15, dec_width), jnp.bfloat16)]
+    )
+    columns = jnp.pad(dec_vectors[:8].astype(jnp.float32).T, ((0, 0), (0, 120)))
+    (
+        decoded_row,
+        grad_projected,
+        grad_positions,
+        grad_columns,
+        grad_dec_qkv,
+        grad_dec_out,
+        grad_dec_up,
+        grad_dec_up_bias,
+        grad_dec_down,
+    ) = dec_block_call(
+        used.reshape(1),
+        target,
+        projected,
+        positions,
+        space_pos,
+        columns,
+        dec_qkv,
+        dec_out,
+        dec_up,
+        dec_up_bias.astype(jnp.float32)[:, None],
+        dec_down,
+        mine(out_grad),
+        TQ=384,
+        TA=640,
+    )
+    grad_space = grad_positions[:patch_count]
+    by_slot = grad_positions[patch_count : patch_count + slot_count]
+    grad_time = jnp.dot(table.T, by_slot, precision=lax.Precision.HIGHEST)
+    grad_mask = grad_positions[patch_count + 2 * slot_count]
     grad_proj = left_transposed(sent, grad_projected)
     grad_sent = right_transposed(grad_projected, proj_weight).astype(jnp.bfloat16)
-    grad_rows = jnp.concatenate([block_grads[0], grad_mask[None, :]], axis=0)
+    grad_rows = jnp.concatenate([grad_columns[:, :8].T, grad_mask[None, :]], axis=0)
     grad_in, enc_grads = block_backward(
         grad_sent.astype(jnp.float32), enc_weights, enc_heads, enc_valid, enc_saved
     )
@@ -287,7 +533,11 @@
         *enc_grads,
         grad_proj,
         grad_rows,
-        *block_grads[1:],
+        grad_dec_qkv,
+        grad_dec_out,
+        grad_dec_up,
+        grad_dec_up_bias[:, 0],
+        grad_dec_down,
         grad_time,
         grad_space,
     )
@@ -309,11 +559,14 @@
     local = []
     for item in grads:
         keep, came = halves(item)
-        local.append((keep + came.astype(jnp.float32)).astype(jnp.bfloat16))
+        local.append((keep.astype(jnp.float32) + came.astype(jnp.float32)).astype(jnp.bfloat16))
     summed = [item.astype(jnp.float32) for item in lax.psum(tuple(local), "dp")]
     squares = lax.psum(jnp.stack([square_sum(summed[:6]), square_sum(summed[6:])]), "section")
     norms = lax.dynamic_slice_in_dim(squares, section, 1, 0)
     return (decoded_half, token_half, *summed, norms)
+
+
+from jax.sharding import PartitionSpec as P
 
 
 def solution(mesh):

time: 772 us -> 549 us (0.71)
  matrix products: 194 us -> 44.8 us
  other arithmetic: 149 us -> 75.5 us
  local copies, waits for them, and re-layouts: 114 us -> 51.5 us
  Pallas kernels: 0 us -> 61.5 us
    pallas_call x0 -> x1, Pallas kernels: none -> 61.5 us  [dec_block_call(): pl.pallas_call(functools.partial(dec_kernel, W=W, L=L, H=H, FF=FF, patche...]
    dot_general x9 -> x5, matrix products: 42.2 us -> 12.5 us  [multiply(): return jnp.dot(left, right, preferred_element_type=jnp.float32)]
    convert_element_type x2 -> x1, other arithmetic: 26.5 us -> 0.15 us  [block_backward(): grad_scores = (probs * (grad_probs - jnp.sum(grad_probs * probs, axis=-1,...]
    dot_general x2 -> x1, matrix products: 25.6 us -> 0.32 us  [block_backward(): jnp.einsum('qhd,khd->hqk', grad_mixed, values, preferred_element_type=jnp...]
    dot_general x9 -> x5, matrix products: 30.7 us -> 12.9 us  [right_transposed(): lax.dot_general(left, right, (((1,), (1,)), ((), ())), preferred_element_...]
    dot_general x2 -> x1, matrix products: 15 us -> 0.43 us  [block_backward(): jnp.einsum('hqk,qhd->khd', probs.astype(jnp.bfloat16), grad_mixed, prefer...]
    dot_general x9 -> x5, matrix products: 30.1 us -> 16.2 us  [left_transposed(): lax.dot_general(left, right, (((0,), (0,)), ((), ())), preferred_element_...]
    dot_general x2 -> x1, matrix products: 14.1 us -> 0.33 us  [attention_scores(): jnp.einsum('qhd,khd->hqk', queries, keys, preferred_element_type=jnp.floa...]
  transfers between devices with their start and end apart: 19 -> 19, of which waited for: 2 -> 3; matrix products, arithmetic and copies ran while one was open for 37% -> 20% of each run, Pallas kernels for 0% -> 0%
where the time goes in v2:
time: 549 us; the launch traced here: 541 us
  waiting for transfers between devices  270 us (49%)
  other arithmetic  75.5 us (14%)
  Pallas kernels  61.5 us (11%)
  local copies, waits for them, and re-layouts  51.5 us (9%)
  matrix products  44.8 us (8%)
  between operations  27.5 us (5%)
  starting transfers between devices  6.28 us (1%)
    psum x2, waiting for transfers between devices, shards(): summed = [item.astype(jnp.float32) for item in lax.psum(tuple(local), 'dp')]  269 us
    pallas_call x1, Pallas kernels, dec_block_call(): pl.pallas_call(functools.partial(dec_kernel, W=W, L=L, H=H, FF=FF, patche...  61.5 us
    reduce_sum x15, other arithmetic, square_sum(): return sum((jnp.sum(item * item) for item in arrays))  33 us
    convert_element_type x15, other arithmetic, shards(): (keep.astype(jnp.float32) + came.astype(jnp.float32)).astype(jnp.bfloat16)  31.1 us
    convert_element_type x9, local copies, waits for them, and re-layouts, halves(): return (keep, from_partner(give.astype(jnp.bfloat16), 'section', 0))  16.6 us
    dot_general x5, matrix products, left_transposed(): lax.dot_general(left, right, (((0,), (0,)), ((), ())), preferred_element_...  16.2 us
    dot_general x5, matrix products, right_transposed(): lax.dot_general(left, right, (((1,), (1,)), ((), ())), preferred_element_...  12.9 us
    dot_general x5, matrix products, multiply(): return jnp.dot(left, right, preferred_element_type=jnp.float32)  12.5 us
  transfers between devices with their start and end apart: 19, of which 3 were waited for; matrix products, arithmetic and copies ran while one was open for 20% of the time, Pallas kernels for 0%

profile of v2, /device:TPU:1, one launch (start us, length us, event | category | flops | bytes accessed | tf_op | source)
XLA Modules:
  0.0 541.0 jit_solution(3837143603649470216)
XLA Ops:
  22.8 2.7 fusion.63
  28.7 7.7 %multiply_convert_fusion = (bf16[112,3072]{1,0:T(8,128)(2,1)S(1)}, f32[112,3072]{1,0:T(8,128)}, f32[112,3072]{1,0:T(8,128)}) fusion(f32[3072]{0:T(1024)S(1)} %convert_element_type.325, bf16[768,3072]{1,0:T(8,128)(2,1)} %param.26, f32[112,768]{1,0:T(8,128)S(1)} %get-tuple-element.186, f32[768]{0:T(1024)S(1)} %get-tuple-element.116, ...), kind=kOutput, calls=%fused_computation.16 | convolution fusion | flops 551620608 | bytes 8522624 | tf_op jit(solution)/shard_map/dot_general | solution.py:278
  39.1 61.5 %decoder.1 = (bf16[1152,384]{1,0:T(8,128)(2,1)}, bf16[112,384]{1,0:T(8,128)(2,1)}, f32[176,384]{1,0:T(8,128)}, f32[384,128]{1,0:T(8,128)}, bf16[384,1152]{1,0:T(...) custom-call(s32[1]{0:T(128)} %bitcast.1.used_ref, ...), custom_call_target="tpu_custom_call" | custom-call | flops 28000000000 | bytes 12000000 | tf_op jit(solution)/shard_map/decoder/pallas_call | solution.py:225
  109.7 4.9 convert_reduce_fusion
  117.6 4.1 multiply_reduce_fusion.10
  130.8 4.2 fusion.30
  135.0 5.1 fusion.66
  140.1 5.1 fusion.75
  154.0 4.0 dynamic-slice_convert_fusion.1
  158.0 4.0 dynamic-slice_convert_fusion
  164.1 3.5 dynamic-slice_convert_fusion.2
  167.8 2.2 copy.106
  183.8 2.2 add_convert_fusion.7
  186.7 2.2 copy.107
  194.2 4.3 add_convert_fusion.2
  198.5 5.1 add_convert_fusion
  203.5 3.8 add_convert_fusion.1
  210.8 95.0 %all-reduce.6.cloned.1.call-done = (bf16[8,384]{1,0:T(8,128)(2,1)}, bf16[1536]{0:T(1024)(128)(2,1)}, bf16[9,192]{1,0:T(8,128)(2,1)}, bf16[768]{0:T(1024)(128)(2,...) async-done(((bf16[8,384]{1,0:T(8,128)(2,1)}, bf16[1536]{0:T(1024)(128)(2,1)}, bf16[9,192]{1,0:T(8,128)(2,1)}, bf16[768]{0:T(1024)(128)(2,1)}, ...) | async-done | bytes 72592 | tf_op jit(solution)/shard_map/psum | solution.py:563
  315.4 2.2 multiply_reduce_fusion.13
  318.7 174.2 %all-reduce.8.cloned.1.call-done = (bf16[384,576]{1,0:T(8,128)(2,1)}, bf16[384,192]{1,0:T(8,128)(2,1)}, bf16[1536,192]{1,0:T(8,128)(2,1)}, bf16[768,1152]{1,0:T(...) async-done(((bf16[384,576]{1,0:T(8,128)(2,1)}, ...) | async-done | bytes 9142288 | tf_op jit(solution)/shard_map/psum | solution.py:563
  506.9 3.2 multiply_reduce_fusion.2
  510.1 4.0 multiply_reduce_fusion.1
  514.1 4.0 multiply_reduce_fusion
  529.0 4.2 psum.127
  (287 shorter events, 100.0 us)
Async XLA Ops:
  7.2 30.1 %copy-start = (bf16[768,384]{1,0:T(8,128)(2,1)S(1)}, bf16[768,384]{1,0:T(8,128)(2,1)}, u32[]{:S(2)}) copy-start(bf16[768,384]{1,0:T(8,128)(2,1)} %param.29) | copy-start | bytes 1769476
  7.2 298.6 %all-reduce.6.cloned.1.call-start = ((), (), s32[]{:S(2)}) async-start(), calls=%async_computation | async-start | bytes 196608 | tf_op jit(solution)/shard_map/psum | solution.py:563
  12.7 25.5 %copy-start.53 = (f32[8]{0:T(128)}, f32[8]{0:T(128)S(1)}, u32[]{:S(2)}) copy-start(f32[8]{0:T(128)S(1)} %get-tuple-element.170) | copy-start | bytes 100
  12.7 25.5 %copy-start.54 = (f32[8]{0:T(128)}, f32[8]{0:T(128)S(1)}, u32[]{:S(2)}) copy-start(f32[8]{0:T(128)S(1)} %get-tuple-element.171) | copy-start | bytes 100
  12.7 25.5 %copy-start.55 = (s32[8]{0:T(128)}, s32[8]{0:T(128)S(1)}, u32[]{:S(2)}) copy-start(s32[8]{0:T(128)S(1)} %get-tuple-element.172) | copy-start | bytes 100
  12.7 25.5 %copy-start.57 = (s32[8]{0:T(128)}, s32[8]{0:T(128)S(1)}, u32[]{:S(2)}) copy-start(s32[8]{0:T(128)S(1)} %add_minimum_fusion) | copy-start | bytes 100
  102.4 67.6 %collective-permute-start.13 = (bf16[768]{0:T(1024)(128)(2,1)}, bf16[768]{0:T(1024)(128)(2,1)}, u32[]{:S(2)}, u32[]{:S(2)}) collective-permute-start(bf16[768]{0:T(1024)(128)(2,1)} %fusion.33), channel_id=1, source_target_pairs={{0,64},{64,0},{1,65},{65,1},{2,66},{66,2},{3,67},{67,3},{4,68},{68... | collective-permute-start | bytes 4616 | tf_op jit(solution)/shard_map/ppermute | solution.py:264
  105.6 65.7 %collective-permute-start.15 = (bf16[8,192]{1,0:T(8,128)(2,1)}, bf16[8,192]{1,0:T(8,128)(2,1)}, u32[]{:S(2)}, u32[]{:S(2)}) collective-permute-start(bf16[8,192]{1,0:T(8,128)(2,1)} %fusion.43), channel_id=1, source_target_pairs={{0,64},{64,0},{1,65},{65,1},{2,66},{66,2},{3,67},{67,3},{4,68},{68... | collective-permute-start | bytes 9224 | tf_op jit(solution)/shard_map/ppermute | solution.py:264
  107.9 69.3 %collective-permute-start.16 = (bf16[144,192]{1,0:T(8,128)(2,1)}, bf16[144,192]{1,0:T(8,128)(2,1)}, u32[]{:S(2)}, u32[]{:S(2)}) collective-permute-start(bf16[144,192]{1,0:T(8,128)(2,1)} %dynamic-slice_convert_fusion.6), channel_id=1, source_target_pairs={{0,64},{64,0},{1,65},{65,1},{2,66},{66,2},{3,67},{67,3},{4,68},{68... | collective-permute-start | bytes 165896 | tf_op jit(solution)/shard_map/ppermute | solution.py:264
  115.4 57.7 %collective-permute-start.6 = (bf16[1536]{0:T(1024)(128)(2,1)}, bf16[1536]{0:T(1024)(128)(2,1)}, u32[]{:S(2)}, u32[]{:S(2)}) collective-permute-start(bf16[1536]{0:T(1024)(128)(2,1)} %dynamic_slice.242), channel_id=1, source_target_pairs={{0,64},{64,0},{1,65},{65,1},{2,66},{66,2},{3,67},{67,3},{4,68},{68... | collective-permute-start | bytes 9224 | tf_op jit(solution)/shard_map/ppermute | solution.py:264
  116.9 57.6 %collective-permute-start.9 = (bf16[9,192]{1,0:T(8,128)(2,1)}, bf16[9,192]{1,0:T(8,128)(2,1)}, u32[]{:S(2)}, u32[]{:S(2)}) collective-permute-start(bf16[9,192]{1,0:T(8,128)(2,1)} %fusion.35), channel_id=1, source_target_pairs={{0,64},{64,0},{1,65},{65,1},{2,66},{66,2},{3,67},{67,3},{4,68},{68... | collective-permute-start | bytes 10376 | tf_op jit(solution)/shard_map/ppermute | solution.py:264
  170.0 9.4 %collective-permute-start.11 = (bf16[384,192]{1,0:T(8,128)(2,1)}, bf16[384,192]{1,0:T(8,128)(2,1)}, u32[]{:S(2)}, u32[]{:S(2)}) collective-permute-start(bf16[384,192]{1,0:T(8,128)(2,1)} %constant_dynamic-slice_fusion.4), channel_id=1, source_target_pairs={{0,64},{64,0},{1,65},{65,1},{2,66},{66,2},{3,67},{67,3},{4,68},{68... | collective-permute-start | bytes 442376 | tf_op jit(solution)/shard_map/ppermute | solution.py:264
  171.3 5.3 collective-permute-start.2
  173.1 8.6 %collective-permute-start.10 = (bf16[384,576]{1,0:T(8,128)(2,1)}, bf16[384,576]{1,0:T(8,128)(2,1)}, u32[]{:S(2)}, u32[]{:S(2)}) collective-permute-start(bf16[384,576]{1,0:T(8,128)(2,1)} %constant_dynamic-slice_fusion.5), channel_id=1, source_target_pairs={{0,64},{64,0},{1,65},{65,1},{2,66},{66,2},{3,67},{67,3},{4,68},{68... | collective-permute-start | bytes 1327112 | tf_op jit(solution)/shard_map/ppermute | solution.py:264
  174.5 5.0 collective-permute-start.8
  176.6 17.6 %collective-permute-start.3 = (bf16[768,1152]{1,0:T(8,128)(2,1)}, bf16[768,1152]{1,0:T(8,128)(2,1)}, u32[]{:S(2)}, u32[]{:S(2)}) collective-permute-start(bf16[768,1152]{1,0:T(8,128)(2,1)} %dynamic-slice_convert_fusion.2), channel_id=1, source_target_pairs={{0,64},{64,0},{1,65},{65,1},{2,66},{66,2},{3,67},{67,3},{4,68},{68... | collective-permute-start | bytes 5308424 | tf_op jit(solution)/shard_map/ppermute | solution.py:264
  177.2 21.2 %collective-permute-start.7 = (bf16[3072,384]{1,0:T(8,128)(2,1)}, bf16[3072,384]{1,0:T(8,128)(2,1)}, u32[]{:S(2)}, u32[]{:S(2)}) collective-permute-start(bf16[3072,384]{1,0:T(8,128)(2,1)} %dynamic-slice_convert_fusion), channel_id=1, source_target_pairs={{0,64},{64,0},{1,65},{65,1},{2,66},{66,2},{3,67},{67,3},{4,68},{68... | collective-permute-start | bytes 7077896 | tf_op jit(solution)/shard_map/ppermute | solution.py:264
  179.4 313.6 %all-reduce.8.cloned.1.call-start = ((), (), s32[]{:S(2)}) async-start(), calls=%async_computation.1 | async-start | bytes 18874368 | tf_op jit(solution)/shard_map/psum | solution.py:563
  179.4 9.5 %collective-permute-start.12 = (bf16[384,768]{1,0:T(8,128)(2,1)}, bf16[384,768]{1,0:T(8,128)(2,1)}, u32[]{:S(2)}, u32[]{:S(2)}) collective-permute-start(bf16[384,768]{1,0:T(8,128)(2,1)} %constant_dynamic-slice_fusion.3), channel_id=1, source_target_pairs={{0,64},{64,0},{1,65},{65,1},{2,66},{66,2},{3,67},{67,3},{4,68},{68... | collective-permute-start | bytes 1769480 | tf_op jit(solution)/shard_map/ppermute | solution.py:264
  179.5 7.0 %collective-permute-start.14 = (bf16[1536,192]{0,1:T(8,128)(2,1)}, bf16[1536,192]{0,1:T(8,128)(2,1)}, u32[]{:S(2)}, u32[]{:S(2)}) collective-permute-start(bf16[1536,192]{0,1:T(8,128)(2,1)} %copy.106), channel_id=1, source_target_pairs={{0,64},{64,0},{1,65},{65,1},{2,66},{66,2},{3,67},{67,3},{4,68},{68... | collective-permute-start | bytes 1769480 | tf_op jit(solution)/shard_map/ppermute | solution.py:264
  181.7 9.4 %collective-permute-start.4 = (bf16[768,384]{1,0:T(8,128)(2,1)}, bf16[768,384]{1,0:T(8,128)(2,1)S(1)}, u32[]{:S(2)}, u32[]{:S(2)}) collective-permute-start(bf16[768,384]{1,0:T(8,128)(2,1)} %dynamic-slice_convert_fusion.3), channel_id=1, source_target_pairs={{0,64},{64,0},{1,65},{65,1},{2,66},{66,2},{3,67},{67,3},{4,68},{68... | collective-permute-start | bytes 1769480 | tf_op jit(solution)/shard_map/ppermute | solution.py:264
  186.5 17.0 %collective-permute-start.5 = (bf16[768,1536]{1,0:T(8,128)(2,1)}, bf16[768,1536]{1,0:T(8,128)(2,1)}, u32[]{:S(2)}, u32[]{:S(2)}) collective-permute-start(bf16[768,1536]{1,0:T(8,128)(2,1)} %dynamic-slice_convert_fusion.1), channel_id=1, source_target_pairs={{0,64},{64,0},{1,65},{65,1},{2,66},{66,2},{3,67},{67,3},{4,68},{68... | collective-permute-start | bytes 7077896 | tf_op jit(solution)/shard_map/ppermute | solution.py:264
  207.5 2.6 collective-permute-start.1
  209.3 108.2 %collective-permute-start = (bf16[1152,192]{0,1:T(8,128)(2,1)S(1)}, bf16[1152,192]{0,1:T(8,128)(2,1)S(1)}, u32[]{:S(2)}, u32[]{:S(2)}) collective-permute-start(bf16[1152,192]{0,1:T(8,128)(2,1)S(1)} %copy.100), channel_id=1, source_target_pairs={{0,64},{64,0},{1,65},{65,1},{2,66},{66,2},{3,67},{67,3},{4,68},{68... | collective-permute-start | bytes 1327112 | tf_op jit(solution)/shard_map/ppermute | solution.py:264
  (58 other events, 266.4 us)
Sparse Core Ops, SparseCore 0:
  179.5 126.2 all-reduce.5
  314.5 178.3 all-reduce.7

commit v3 on v2

v3 whole, which is shorter than its diff:
```python
import functools
import jax, jax.numpy as jnp, numpy as np
from jax import lax
from jax.experimental import pallas as pl
from jax.experimental.pallas import tpu as pltpu

EPS = 1e-6
NEG = -1e9
LOG2E = 1.4426950408889634
LN2 = 0.6931471805599453
F32, BF = jnp.float32, jnp.bfloat16


def dot(a, b, ca=1, cb=0):
    return lax.dot_general(a, b, (((ca,), (cb,)), ((), ())), preferred_element_type=F32)


def tiles_of(total, size):
    return [(s, min(size, total - s)) for s in range(0, total, size)]


def over(total, size, body, carry):
    full = total // size
    if full:
        carry = lax.fori_loop(0, full, lambda i, k: body(pl.ds(pl.multiple_of(i * size, 128), size), size, k), carry)
    if total % size:
        carry = body(pl.ds(full * size, total % size), total % size, carry)
    return carry


def norm_c(x):
    mean = jnp.mean(x, axis=0, keepdims=True)
    c = x - mean
    r = lax.rsqrt(jnp.mean(c * c, axis=0, keepdims=True) + EPS)
    return c * r, r


def gelu_pair(u):
    a = jnp.abs(u)
    t = 1.0 / (1.0 + (0.3275911 * 0.7071067811865476) * a)
    e = jnp.exp2((-0.5 * LOG2E) * (u * u))
    poly = t * (0.5 * 0.254829592 + t * (0.5 * -0.284496736 + t * (0.5 * 1.421413741 + t * (0.5 * -1.453152027 + t * (0.5 * 1.061405429)))))
    tail = poly * e
    phi = jnp.where(u >= 0, 1.0 - tail, tail)
    return u * phi, phi + u * (e * 0.3989422804014327)


def dec_kernel(sec_ref, frames_ref, vis_ref, proj_ref, time_ref, space_ref, vecs_ref, wqkv_ref, wo_ref, w1_ref, bias_ref, w2_ref, dy_any,
               out_refs, dz_ref, pack_refs,
               x_s, a1_s, qkv_s, e_s, l_s, o_s, m_s, a2_s, g_s, gp_s, dy_s, db_s, sel_s, doa_s, do_s, o32_s, dy_ref, vec_ref, b1_ref, dec_s, dy_sem, *, W, L, H, FF, V, slots, patches, TQ, TA):
    dqkv_s, ds_s = g_s, gp_s
    sec = sec_ref[0]
    used = frames_ref[sec] // 2
    valid = used * patches
    dy_copy = pltpu.make_async_copy(dy_any.at[sec], dy_ref, dy_sem)
    dy_copy.start()
    seen_count = V // slots
    vecs = vecs_ref[...].astype(F32)
    vec_ref[...] = jnp.concatenate([vecs, jnp.zeros((16 - vecs.shape[0], W), F32)], axis=0).T
    b1_ref[...] = jnp.broadcast_to(bias_ref[...].reshape(1, FF).astype(F32), (8, FF)).T[:, 0:1]
    col = lambda i: vec_ref[:, i:i + 1]
    HS = 64
    lane = lax.broadcasted_iota(jnp.int32, (1, L), 1)
    vrow = lax.broadcasted_iota(jnp.int32, (V, 1), 0)
    vslot = jnp.zeros((V, 1), jnp.int32)
    for t in range(1, slots):
        vslot += (vrow >= t * seen_count).astype(jnp.int32)
    vrank = vrow - vslot * seen_count
    target = vslot * patches
    for j in range(seen_count):
        target += jnp.where(vrank == j, vis_ref[sec, j], 0)
    onehot = (target == lax.broadcasted_iota(jnp.int32, (V, L), 1)).astype(F32)
    slot = jnp.zeros((1, L), jnp.int32)
    for t in range(1, slots):
        slot += (lane >= t * patches).astype(jnp.int32)
    patch_oh = (lax.broadcasted_iota(jnp.int32, (patches, L), 0) == lane - slot * patches).astype(BF)
    seen = jnp.sum(onehot, axis=0, keepdims=True)
    srow = lax.broadcasted_iota(jnp.int32, (32, L), 0)
    slot_oh = jnp.where(srow < 16, ((srow & 7) == slot).astype(F32), jnp.where(srow == 16, 1.0 - seen, 0.0)).astype(BF)
    sel_s[:V, :] = onehot.astype(BF)
    sel_s[V:V + patches, :] = patch_oh
    sel_s[V + patches:, :] = slot_oh
    ti = lax.broadcasted_iota(jnp.int32, (slots, slots), 0)
    ii = lax.broadcasted_iota(jnp.int32, (slots, slots), 1)
    num = ti * (slots - 1)
    lower = jnp.zeros((slots, slots), jnp.int32)
    for q in range(1, (slots - 1) * (slots - 1) + 1):
        lower += (num >= q * (used - 1)).astype(jnp.int32)
    frac = (num - lower * (used - 1)).astype(F32) / jnp.full((slots, slots), used - 1, jnp.int32).astype(F32)
    upper = jnp.minimum(lower + 1, slots - 1)
    table = (1.0 - frac) * (ii == lower).astype(F32) + frac * (ii == upper).astype(F32)
    exact = lambda a, b, ca, cb: lax.dot_general(a, b, (((ca,), (cb,)), ((), ())), precision=lax.Precision.HIGHEST, preferred_element_type=F32)
    spos = exact(table, time_ref[...].astype(F32), 1, 0)
    shi = spos.astype(BF)
    slo = (spos - shi.astype(F32)).astype(BF)
    proj = proj_ref[...]
    hi = proj.astype(BF)
    lo = (proj - hi.astype(F32)).astype(BF)
    mask = vecs[8:9, :].astype(BF)
    src = jnp.concatenate([hi.astype(F32), space_ref[...].astype(F32), shi.astype(F32), slo.astype(F32), mask.astype(F32), jnp.zeros((15, W), F32)], axis=0).astype(BF)

    def first(c, n, k):
        x = dot(src, sel_s[:, c], 0, 0) + dot(lo, sel_s[:V, c], 0, 0)
        x_s[:, c] = x
        xh, _ = norm_c(x)
        a1 = (xh * col(0) + col(1)).astype(BF)
        a1_s[:, c] = a1
        j = dot(wqkv_ref[...], a1, 0, 0)
        qkv_s[:W, c] = ((j[:W] + col(2)) * (0.125 * LOG2E)).astype(BF)
        qkv_s[W:2 * W, c] = j[W:2 * W].astype(BF)
        qkv_s[2 * W:, c] = (j[2 * W:] + col(3)).astype(BF)
        return k

    over(L, TQ, first, 0)
    arow = lax.broadcasted_iota(jnp.int32, (16, L), 0)
    kbias = jnp.where((arow == 0) & (lane >= valid), NEG, 0.0).astype(BF)
    one0 = (arow == 0).astype(BF)
    one01 = (arow < 2).astype(BF)

    def fwd_head(h, carry):
        hs = pl.ds(pl.multiple_of(h * HS, HS), HS)
        ks = pl.ds(pl.multiple_of(W + h * HS, HS), HS)
        vs = pl.ds(pl.multiple_of(2 * W + h * HS, HS), HS)
        kr = jnp.concatenate([qkv_s[ks, :], kbias], axis=0).T
        vc = jnp.concatenate([qkv_s[vs, :], one0], axis=0)

        def tile(c, n, exact):
            qc = jnp.concatenate([qkv_s[hs, c], one0[:, :n]], axis=0)
            st = dot(kr, qc)
            if exact:
                st = st - jnp.max(st, axis=0, keepdims=True)
            e = jnp.exp2(st).astype(BF)
            e_s[h, :, c] = e
            oa = dot(vc, e)
            rl = 1.0 / oa[HS:HS + 1]
            l_s[h, :, c] = jnp.broadcast_to(rl, (8, n))
            o = oa[:HS] * rl
            o32_s[hs, c] = o
            o_s[hs, c] = o.astype(BF)

        square = lambda v: jnp.max(jnp.sum(v * v, axis=0))
        bound = square(qkv_s[hs, :].astype(F32)) * square(qkv_s[ks, :].astype(F32))

        @pl.when(bound <= 60.0 * 60.0)
        def _():
            over(L, TA, lambda c, n, k: (tile(c, n, False), k)[1], 0)

        @pl.when(jnp.logical_not(bound <= 60.0 * 60.0))
        def _():
            over(L, TA, lambda c, n, k: (tile(c, n, True), k)[1], 0)

        return carry

    lax.fori_loop(0, H, fwd_head, 0)

    def middle(c, n, sums):
        sum_b1, sum_dy, sum_g2, sum_s2, sum_db = sums
        live = (lax.broadcasted_iota(jnp.int32, (1, n), 1) + c.start < valid).astype(F32)
        mid = x_s[:, c] + (dot(wo_ref[...], o_s[:, c], 0, 0) + col(4))
        xh, r = norm_c(mid)
        a2 = (xh * col(5) + col(6)).astype(BF)
        a2_s[:, c] = a2
        u = dot(w1_ref[...], a2, 0, 0) + b1_ref[...]
        g, gp = gelu_pair(u)
        g = g.astype(BF)
        g_s[:, c] = g
        y = mid + (dot(w2_ref[...], g, 0, 0) + col(7))
        dec_s[:, c] = (y * live).astype(BF)
        dyf = dy_ref[c, :].astype(F32).T * live
        dy = dyf.astype(BF)
        dy_s[:, c] = dy
        duf = gp * dot(w2_ref[...], dy)
        du = duf.astype(BF)
        gp_s[:, c] = du
        da2 = dot(w1_ref[...], du)
        dg = da2 * col(5)
        dm = dyf + r * (dg - jnp.mean(dg, axis=0, keepdims=True) - xh * jnp.mean(dg * xh, axis=0, keepdims=True))
        db = dm.astype(BF)
        db_s[:, c] = db
        do_s[:, c] = dot(wo_ref[...], db).astype(BF)
        m_s[:, c] = dm
        rs = lambda v: jnp.sum(v, axis=1, keepdims=True)
        return (sum_b1 + rs(duf), sum_dy + rs(dyf), sum_g2 + rs(da2 * xh), sum_s2 + rs(da2), sum_db + rs(dm))

    dy_copy.wait()
    zero = jnp.zeros((W, 1), F32)
    sum_b1, sum_dy, sum_g2, sum_s2, sum_db = over(L, TQ, middle, (jnp.zeros((FF, 1), F32), zero, zero, zero, zero))
    blocks = dec_blocks(W, FF)
    for who, s in enumerate((sec, 1 - sec)):
        rows = lambda size, at=0: pl.ds(pl.multiple_of(s * (size // 2) + at, 16), W // 2)
        out_refs[who][...] = dec_s[rows(W), :]
        pack = pack_refs[who]
        for b in range(FF // W):
            r = blocks["down"] + b * (W // 2)
            pack[r:r + W // 2, :] = dot(dy_s[rows(W), :], g_s[b * W:b * W + W, :], 1, 1).astype(BF)
        for b in range(FF // 2 // W):
            r = blocks["up"] + b * W
            pack[r:r + W, :] = dot(a2_s[...], gp_s[pl.ds(pl.multiple_of(s * (FF // 2) + b * W, 16), W), :], 1, 1).astype(BF)
        r = blocks["out"]
        pack[r:r + W // 2, :] = dot(db_s[rows(W), :], o_s[...], 1, 1).astype(BF)

    def bwd_head(h, carry):
        hs = pl.ds(pl.multiple_of(h * HS, HS), HS)
        ks = pl.ds(pl.multiple_of(W + h * HS, HS), HS)
        vs = pl.ds(pl.multiple_of(2 * W + h * HS, HS), HS)
        vr = jnp.concatenate([qkv_s[vs, :], one01], axis=0).T
        kc = qkv_s[ks, :]
        dob = (do_s[hs, :].astype(F32) * l_s[h, 0:1, :]).astype(BF)
        dl = -jnp.sum(dob.astype(F32) * o32_s[hs, :], axis=0, keepdims=True)
        dlh = dl.astype(BF).astype(F32)
        doa_s[:HS, :] = dob
        doa_s[HS:, :] = jnp.where(arow == 0, dlh, jnp.where(arow == 1, dl - dlh, 0.0)).astype(BF)
        def tile(c, n, k):
            dp = dot(vr, doa_s[:, c])
            ds = (e_s[h, :, c].astype(F32) * dp).astype(BF)
            ds_s[:L, c] = ds
            dqkv_s[hs, c] = (dot(kc, ds) * 0.125).astype(BF)
            return k

        over(L, TA, tile, 0)
        dor = doa_s[:HS, :].T
        qr = qkv_s[hs, :].T

        def tile2(c, n, k):
            dqkv_s[vs, c] = dot(e_s[h, c, :], dor).T.astype(BF)
            dqkv_s[ks, c] = (dot(ds_s[c, :], qr) * LN2).T.astype(BF)
            return k

        return over(L, TA, tile2, carry)

    lax.fori_loop(0, H, bwd_head, 0)
    def last(c, n, sums):
        sum_g1, sum_s1, sum_q, sum_v, gsel = sums
        rs = lambda v: jnp.sum(v, axis=1, keepdims=True)
        da = dot(wqkv_ref[...], dqkv_s[:3 * W, c])
        xh, r = norm_c(x_s[:, c])
        dg = da * col(0)
        dx = m_s[:, c] + r * (dg - jnp.mean(dg, axis=0, keepdims=True) - xh * jnp.mean(dg * xh, axis=0, keepdims=True))
        return (sum_g1 + rs(da * xh), sum_s1 + rs(da), sum_q + rs(dqkv_s[:W, c].astype(F32)), sum_v + rs(dqkv_s[2 * W:3 * W, c].astype(F32)),
                gsel + dot(dx.astype(BF), sel_s[:, c], 1, 1))

    sum_g1, sum_s1, sum_q, sum_v, gsel = over(L, TQ, last, (zero, zero, zero, zero, jnp.zeros((W, sel_s.shape[0]), F32)))
    dz_ref[...] = gsel[:, :V].T.astype(BF)
    small = o32_s
    small[:, :8] = jnp.concatenate([sum_g1, sum_s1, sum_q, sum_v, sum_db, sum_g2, sum_s2, sum_dy], axis=1)
    small[:, 8:16] = gsel[:, V + patches + 16:V + patches + 24]
    small[:, 16:24] = exact(gsel[:, V + patches:V + patches + slots], table, 1, 0)
    small[:, 24:24 + patches] = gsel[:, V:V + patches]
    rows = 32 + patches
    small[:, 24 + patches:256] = jnp.zeros((W, 256 - 24 - patches), F32)
    wide = jnp.broadcast_to(sum_b1, (FF, 128))
    for who, s in enumerate((sec, 1 - sec)):
        pack = pack_refs[who]
        for b in range(3):
            r = blocks["qkv"] + b * (W // 2)
            pack[r:r + W // 2, :] = dot(dqkv_s[pl.ds(pl.multiple_of(s * (3 * W // 2) + b * (W // 2), 16), W // 2), :], a1_s[...], 1, 1).astype(BF)
        r = blocks["small"]
        pack[r:r + rows, :W // 2] = small[pl.ds(pl.multiple_of(s * (W // 2), 8), W // 2), :256].T[:rows].astype(BF)
        pack[r:r + rows, W // 2:] = jnp.zeros((rows, W - W // 2), BF)
        b1_ref[...] = sum_b1
        bias = jnp.broadcast_to(b1_ref[pl.ds(pl.multiple_of(s * (FF // 2), 8), FF // 2), :], (FF // 2, 128)).T[:16]
        r = blocks["bias"]
        for b in range(FF // 2 // W):
            pack[r + 16 * b:r + 16 * b + 16, :] = bias[:, b * W:b * W + W].astype(BF)


def dec_blocks(W, FF):
    at, rows = 0, {}
    for name, count in (("qkv", 3 * W // 2), ("out", W // 2), ("up", FF // 2), ("down", FF // 2), ("small", 176), ("bias", 16 * (FF // 2 // W))):
        rows[name] = at
        at += count
    rows["end"] = at
    return rows


def finish_kernel(pack_ref, qkv_ref, out_ref, up_ref, down_ref, vec_ref, bias_ref, time_ref, space_ref, sq_ref, *, W, FF, slots, patches):
    blocks = dec_blocks(W, FF)
    total = jnp.zeros((8, 128), F32)
    fold = lambda v: jnp.sum(jnp.sum((v * v).reshape(-1, 8, W), axis=0).reshape(8, W // 128, 128), axis=1)
    read = lambda name, at, n: pack_ref[blocks[name] + at:blocks[name] + at + n, :].astype(F32)
    g = read("qkv", 0, 3 * W // 2)
    qkv_ref[...] = g
    total += fold(g)
    g = read("out", 0, W // 2)
    out_ref[...] = g
    total += fold(g)
    for b in range(FF // 2 // W):
        g = read("up", b * W, W)
        up_ref[:, b * W:b * W + W] = g
        total += fold(g)
    for b in range(FF // W):
        g = read("down", b * (W // 2), W // 2)
        down_ref[:, b * W:b * W + W] = g
        total += fold(g)
    small = read("small", 0, 176)
    total += fold(small)
    vec_ref[...] = small[:9, :W // 2]
    time_ref[...] = small[16:16 + slots, :W // 2]
    space_ref[...] = small[16 + slots:16 + slots + patches, :W // 2]
    for b in range(FF // 2 // W):
        g = read("bias", 16 * b, 16)[:8]
        bias_ref[:, b * W:b * W + W] = g
        total += 0.125 * fold(g)
    sq_ref[...] = total


def finish_call(pack, W, FF, slots, patches):
    vm = pl.BlockSpec(memory_space=pltpu.VMEM)
    S = lambda *shape: jax.ShapeDtypeStruct(shape, F32)
    half = W // 2
    return pl.pallas_call(
        functools.partial(finish_kernel, W=W, FF=FF, slots=slots, patches=patches),
        in_specs=[vm],
        out_specs=[vm] * 9,
        out_shape=[S(3 * half, W), S(half, W), S(W, FF // 2), S(half, FF), S(9, half), S(8, FF // 2), S(slots, half), S(patches, half), S(8, 128)],
        compiler_params=pltpu.CompilerParams(vmem_limit_bytes=63 * 1024 * 1024),
        cost_estimate=pl.CostEstimate(flops=2_000_000, bytes_accessed=6_000_000, transcendentals=0),
        name="decoder_gradients",
    )(pack)


def dec_block_call(sec, frames, visible, proj, time_pos, space, vecs, wqkv, wo, w1, bias, w2, dy, TQ, TA):
    W, L, FF = wqkv.shape[0], dy.shape[1], w1.shape[1]
    H = W // 64
    patches, slots = space.shape[0], time_pos.shape[0]
    V = proj.shape[0]
    sm, vm = pl.BlockSpec(memory_space=pltpu.SMEM), pl.BlockSpec(memory_space=pltpu.VMEM)
    S = jax.ShapeDtypeStruct
    return pl.pallas_call(
        functools.partial(dec_kernel, W=W, L=L, H=H, FF=FF, V=V, slots=slots, patches=patches, TQ=TQ, TA=TA),
        in_specs=[sm, sm, sm] + [vm] * 9 + [pl.BlockSpec(memory_space=pl.ANY)],
        out_specs=[[vm] * 2, vm, [vm] * 2],
        out_shape=[[S((W // 2, L), BF)] * 2, S((V, W), BF), [S((dec_blocks(W, FF)["end"], W), BF)] * 2],
        scratch_shapes=[
            pltpu.VMEM((W, L), F32),
            pltpu.VMEM((W, L), BF),
            pltpu.VMEM((3 * W, L), BF),
            pltpu.VMEM((H, L, L), BF),
            pltpu.VMEM((H, 8, L), F32),
            pltpu.VMEM((W, L), BF),
            pltpu.VMEM((W, L), F32),
            pltpu.VMEM((W, L), BF),
            pltpu.VMEM((FF, L), BF),
            pltpu.VMEM((FF, L), BF),
            pltpu.VMEM((W, L), BF),
            pltpu.VMEM((W, L), BF),
            pltpu.VMEM((V + patches + 32, L), BF),
            pltpu.VMEM((80, L), BF),
            pltpu.VMEM((W, L), BF),
            pltpu.VMEM((W, L), F32),
            pltpu.VMEM((L, W), BF),
            pltpu.VMEM((W, 16), F32),
            pltpu.VMEM((FF, 1), F32),
            pltpu.VMEM((W, L), BF),
            pltpu.SemaphoreType.DMA,
        ],
        compiler_params=pltpu.CompilerParams(vmem_limit_bytes=63 * 1024 * 1024),
        cost_estimate=pl.CostEstimate(flops=28_000_000_000, bytes_accessed=12_000_000, transcendentals=10_000_000),
        name="decoder",
    )(sec, frames, visible, proj, time_pos, space, vecs, wqkv, wo, w1, bias, w2, dy)


VMEM = 63 * 1024 * 1024


def aligned(start, size):
    return pl.ds(pl.multiple_of(start, size), size)


def norm_r(x):
    mean = jnp.mean(x, axis=1, keepdims=True)
    c = x - mean
    r = lax.rsqrt(jnp.mean(c * c, axis=1, keepdims=True) + EPS)
    return c * r, r


def enc_probs(qm, k, valid):
    s = dot(qm, k, 1, 1)
    live = lax.broadcasted_iota(jnp.int32, s.shape, 1) < valid
    s = jnp.where(live, s, NEG)
    e = jnp.exp2(s - jnp.max(s, axis=1, keepdims=True))
    return e / jnp.sum(e, axis=1, keepdims=True)


def two_heads(v):
    low = lax.broadcasted_iota(jnp.int32, v.shape, 1) < 64
    zero = jnp.zeros_like(v)
    return jnp.concatenate([jnp.where(low, v, zero), jnp.where(low, zero, v)], axis=0)


def enc_fwd_kernel(sec_ref, frames_ref, tok_ref, vec_ref, b1_ref, wqkv_any, wo_any, w1_any, w2_any, wp_any,
                   acts_ref, qkv_ref, mid_ref, gp_ref, proj_ref,
                   wqkv_ref, wo_ref, w1_ref, w2_ref, wp_ref, sem, *, W, FF, seen):
    pairs = ((wqkv_any, wqkv_ref), (wo_any, wo_ref), (w1_any, w1_ref), (w2_any, w2_ref), (wp_any, wp_ref))
    copies = [pltpu.make_async_copy(a, b, sem.at[i]) for i, (a, b) in enumerate(pairs)]
    for c in copies:
        c.start()
    sec = sec_ref[0]
    valid = frames_ref[sec] // 2 * seen
    vec = vec_ref[...].astype(F32)
    row = lambda i: vec[i:i + 1, :]
    x = tok_ref[sec].astype(F32)
    n = x.shape[0]
    xh, _ = norm_r(x)
    a1 = (xh * row(0) + row(1)).astype(BF)
    acts_ref[:, :W] = a1
    copies[0].wait()
    j = dot(a1, wqkv_ref[...])
    qkv_ref[:, :W] = (j[:, :W] + row(2)).astype(BF)
    qkv_ref[:, W:2 * W] = j[:, W:2 * W].astype(BF)
    qkv_ref[:, 2 * W:] = (j[:, 2 * W:] + row(3)).astype(BF)
    for h in range(W // 128):
        s = slice(h * 128, h * 128 + 128)
        q = (qkv_ref[:, s].astype(F32) * (0.125 * LOG2E)).astype(BF)
        p = enc_probs(two_heads(q), qkv_ref[:, W + h * 128:W + h * 128 + 128], valid).astype(BF)
        v = two_heads(qkv_ref[:, 2 * W + h * 128:2 * W + h * 128 + 128])
        acts_ref[:, W + h * 128:W + h * 128 + 128] = (dot(p[:n], v[:n]) + dot(p[n:], v[n:])).astype(BF)
    copies[1].wait()
    mid = x + (dot(acts_ref[:, W:2 * W], wo_ref[...]) + row(4))
    mid_ref[...] = mid
    xh, _ = norm_r(mid)
    a2 = (xh * row(5) + row(6)).astype(BF)
    acts_ref[:, 2 * W:3 * W] = a2
    copies[2].wait()
    for f in range(0, FF, W):
        g, gp = gelu_pair(dot(a2, w1_ref[:, f:f + W]) + b1_ref[f:f + W].astype(F32).reshape(1, W))
        acts_ref[:, 3 * W + f:3 * W + f + W] = g.astype(BF)
        gp_ref[:, f:f + W] = gp.astype(BF)
    copies[3].wait()
    y = mid + (dot(acts_ref[:, 3 * W:3 * W + FF], w2_ref[...]) + row(7))
    enc = y.astype(BF)
    acts_ref[:, 3 * W + FF:] = enc
    copies[4].wait()
    proj_ref[...] = dot(enc, wp_ref[...])


def enc_fwd_call(sec, frames, seen, tokens, vec, b1, wqkv, wo, w1, w2, wp):
    n, W = tokens.shape[1], tokens.shape[2]
    FF = w1.shape[1]
    vm, hbm = pl.BlockSpec(memory_space=pltpu.VMEM), pl.BlockSpec(memory_space=pl.ANY)
    S = jax.ShapeDtypeStruct
    return pl.pallas_call(
        functools.partial(enc_fwd_kernel, W=W, FF=FF, seen=seen),
        in_specs=[pl.BlockSpec(memory_space=pltpu.SMEM)] * 2 + [vm] * 3 + [hbm] * 5,
        out_specs=[vm] * 5,
        out_shape=[S((n, 4 * W + FF), BF), S((n, 3 * W), BF), S((n, W), F32), S((n, FF), BF), S((n, wp.shape[1]), F32)],
        scratch_shapes=[pltpu.VMEM(w.shape, BF) for w in (wqkv, wo, w1, w2, wp)] + [pltpu.SemaphoreType.DMA((5,))],
        compiler_params=pltpu.CompilerParams(vmem_limit_bytes=VMEM),
        cost_estimate=pl.CostEstimate(flops=1_700_000_000, bytes_accessed=18_000_000, transcendentals=1_000_000),
        name="encoder_forward",
    )(sec, frames, tokens, vec, b1, wqkv, wo, w1, w2, wp)


def half_of(ref, start, size, s):
    return ref[:, pl.ds(pl.multiple_of(start + s * (size // 2), 128), size // 2)]


def enc_bwd_hidden_kernel(sec_ref, dz_ref, gp_ref, wp_any, w2_any, mine_ref, other_ref, full_ref, small_ref, wp_ref, w2_ref, sem, *, W, FF):
    copies = [pltpu.make_async_copy(a, b, sem.at[i]) for i, (a, b) in enumerate(((wp_any, wp_ref), (w2_any, w2_ref)))]
    for c in copies:
        c.start()
    sec = sec_ref[0]
    small_ref[...] = jnp.zeros_like(small_ref)
    copies[0].wait()
    de = dot(dz_ref[...], wp_ref[...], 1, 1).astype(BF)
    full_ref[:, :W] = de
    small_ref[7:8, :] = jnp.sum(de.astype(F32), axis=0, keepdims=True)
    copies[1].wait()
    for f in range(0, FF, W):
        duf = gp_ref[:, f:f + W].astype(F32) * dot(de, w2_ref[f:f + W, :], 1, 1)
        full_ref[:, W + f:2 * W + f] = duf.astype(BF)
        small_ref[8 + f // W:9 + f // W, :] = jnp.sum(duf, axis=0, keepdims=True)
    for ref, s in ((mine_ref, sec), (other_ref, 1 - sec)):
        ref[:, :W // 2] = half_of(full_ref, 0, W, s)
        ref[:, W // 2:] = half_of(full_ref, W, FF, s)


def enc_bwd_hidden_call(idx, dz, gp, wp, w2):
    n, FF = gp.shape
    W = w2.shape[1]
    vm, hbm = pl.BlockSpec(memory_space=pltpu.VMEM), pl.BlockSpec(memory_space=pl.ANY)
    S = jax.ShapeDtypeStruct
    return pl.pallas_call(
        functools.partial(enc_bwd_hidden_kernel, W=W, FF=FF),
        in_specs=[pl.BlockSpec(memory_space=pltpu.SMEM), vm, vm, hbm, hbm],
        out_specs=[vm] * 4,
        out_shape=[S((n, (W + FF) // 2), BF), S((n, (W + FF) // 2), BF), S((n, W + FF), BF), S((16, W), F32)],
        scratch_shapes=[pltpu.VMEM(w.shape, BF) for w in (wp, w2)] + [pltpu.SemaphoreType.DMA((2,))],
        compiler_params=pltpu.CompilerParams(vmem_limit_bytes=VMEM),
        cost_estimate=pl.CostEstimate(flops=600_000_000, bytes_accessed=8_000_000, transcendentals=0),
        name="encoder_backward_hidden",
    )(idx, dz, gp, wp, w2)


def enc_bwd_kernel(sec_ref, frames_ref, dz_ref, tok_ref, vec_ref, qkv_ref, mid_ref, du_ref, small_ref, w1_any, wo_any, wqkv_any,
                   mine_ref, other_ref, tok_mine_ref, tok_other_ref, w1_ref, wo_ref, wqkv_ref, full, tokg, small, sem, *, W, FF, seen):
    copies = [pltpu.make_async_copy(a, b, sem.at[i]) for i, (a, b) in enumerate(((w1_any, w1_ref), (wo_any, wo_ref), (wqkv_any, wqkv_ref)))]
    for c in copies:
        c.start()
    sec = sec_ref[0]
    valid = frames_ref[sec] // 2 * seen
    vec = vec_ref[...].astype(F32)
    row = lambda i: vec[i:i + 1, :]
    rsum = lambda v: jnp.sum(v, axis=0, keepdims=True)
    n = dz_ref.shape[0]
    small[...] = small_ref[...]
    def_ = du_ref[:, :W].astype(F32)
    copies[0].wait()
    da2 = dot(du_ref[:, W:], w1_ref[...], 1, 1)
    xh, r = norm_r(mid_ref[...])
    small[5:6, :] = rsum(da2 * xh)
    small[6:7, :] = rsum(da2)
    dg = da2 * row(5)
    dm = def_ + r * (dg - jnp.mean(dg, axis=1, keepdims=True) - xh * jnp.mean(dg * xh, axis=1, keepdims=True))
    small[4:5, :] = rsum(dm)
    db = dm.astype(BF)
    full[:, :W] = db
    copies[1].wait()
    do = dot(db, wo_ref[...], 1, 1).astype(BF)
    Q = W
    for h in range(W // 128):
        c = h * 128
        q = two_heads((qkv_ref[:, c:c + 128].astype(F32) * (0.125 * LOG2E)).astype(BF))
        k = qkv_ref[:, W + c:W + c + 128]
        v = qkv_ref[:, 2 * W + c:2 * W + c + 128]
        k2 = two_heads(k)
        do2 = two_heads(do[:, c:c + 128])
        p = enc_probs(q, k, valid)
        dp = dot(do2, v, 1, 1)
        ds = (p * (dp - jnp.sum(dp * p, axis=1, keepdims=True))).astype(BF)
        p16 = p.astype(BF)
        full[:, Q + c:Q + c + 128] = ((dot(ds[:n], k2[:n]) + dot(ds[n:], k2[n:])) * 0.125).astype(BF)
        full[:, Q + W + c:Q + W + c + 128] = (dot(ds, q, 0, 0) * LN2).astype(BF)
        full[:, Q + 2 * W + c:Q + 2 * W + c + 128] = dot(p16, do2, 0, 0).astype(BF)
    small[2:3, :] = rsum(full[:, Q:Q + W].astype(F32))
    small[3:4, :] = rsum(full[:, Q + 2 * W:Q + 3 * W].astype(F32))
    copies[2].wait()
    da = dot(full[:, Q:Q + 3 * W], wqkv_ref[...], 1, 1)
    xh, r = norm_r(tok_ref[sec].astype(F32))
    small[0:1, :] = rsum(da * xh)
    small[1:2, :] = rsum(da)
    dg = da * row(0)
    dx = dm + r * (dg - jnp.mean(dg, axis=1, keepdims=True) - xh * jnp.mean(dg * xh, axis=1, keepdims=True))
    tokg[...] = dx.astype(BF)
    half = W // 2
    for ref, tref, s in ((mine_ref, tok_mine_ref, sec), (other_ref, tok_other_ref, 1 - sec)):
        tref[...] = half_of(tokg, 0, W, s)
        ref[:n, :half] = half_of(full, 0, W, s)
        ref[:n, half:4 * half] = half_of(full, Q, 3 * W, s)
        ref[:n, 4 * half:] = dz_ref[...]
        ref[n:, :half] = half_of(small, 0, W, s).astype(BF)
        ref[n:, half:] = jnp.zeros((16, ref.shape[1] - half), BF)
        for t in range(FF // 2 // W):
            b = jnp.where(s == 0, small[8 + t:9 + t, :], small[8 + FF // 2 // W + t:9 + FF // 2 // W + t, :])
            ref[n + 8 + t:n + 9 + t, :W] = b.astype(BF)


def enc_bwd_call(sec, frames, seen, dz, tokens, vec, qkv, mid, du, small, w1, wo, wqkv):
    n, W = tokens.shape[1], tokens.shape[2]
    FF = w1.shape[1]
    vm, hbm = pl.BlockSpec(memory_space=pltpu.VMEM), pl.BlockSpec(memory_space=pl.ANY)
    S = jax.ShapeDtypeStruct
    width = 2 * W + dz.shape[1]
    return pl.pallas_call(
        functools.partial(enc_bwd_kernel, W=W, FF=FF, seen=seen),
        in_specs=[pl.BlockSpec(memory_space=pltpu.SMEM)] * 2 + [vm] * 7 + [hbm] * 3,
        out_specs=[vm] * 4,
        out_shape=[S((n + 16, width), BF), S((n + 16, width), BF), S((n, W // 2), BF), S((n, W // 2), BF)],
        scratch_shapes=[pltpu.VMEM(w.shape, BF) for w in (w1, wo, wqkv)]
        + [pltpu.VMEM((n, 4 * W), BF), pltpu.VMEM((n, W), BF), pltpu.VMEM((16, W), F32), pltpu.SemaphoreType.DMA((3,))],
        compiler_params=pltpu.CompilerParams(vmem_limit_bytes=VMEM),
        cost_estimate=pl.CostEstimate(flops=1_600_000_000, bytes_accessed=12_000_000, transcendentals=1_000_000),
        name="encoder_backward",
    )(sec, frames, dz, tokens, vec, qkv, mid, du, small, w1, wo, wqkv)


PIECES = 8


def flat_blocks(W, FF, WD):
    half = W // 2
    return ((("down", FF, half // 128),), (("up", W, FF // 2 // 128),), (("qkv", W, 3 * half // 128), ("out", W, half // 128), ("proj", WD // 2, W // 128)))


def flat_rows(part, W, FF, WD):
    rows = sum(r * b for _, r, b in flat_blocks(W, FF, WD)[part])
    if part == 2:
        rows += 8 * (W // 2 // 128) + FF // 2 // 128
    unit = PIECES * 16
    return -(-rows // unit) * unit


def weight_grad_kernel(idx_ref, acts_ref, came_ref, mine_ref, dcame_ref, give, keep, flat, acts, dy, dzt, small, sem, *, part, W, FF, WD):
    n = acts_ref.shape[0]
    half = W // 2
    lhs = {"qkv": (0, W), "out": (W, W), "up": (2 * W, W), "down": (3 * W, FF), "proj": (3 * W + FF, W)}
    cols = {"down": (0, half), "up": (half, FF // 2), "out": (0, half), "qkv": (half, 3 * half)}
    dy[:n, :] = mine_ref[:n, :]
    dy[n:, :] = dcame_ref[:n, :]
    at = 0
    step = 384
    for name, rows, blocks in flat_blocks(W, FF, WD)[part]:
        a0, an = lhs[name]
        acts[:n, :an] = acts_ref[:, a0:a0 + an]
        acts[n:, :an] = came_ref[:, a0:a0 + an]
        if name == "proj":
            dzt[...] = dy[:, 4 * half:4 * half + WD].T
            g = dot(dzt[pl.ds(pl.multiple_of(idx_ref[0] * (WD // 2), 16), WD // 2), :], acts[:, :an]).astype(BF)
            for b in range(blocks):
                flat[at:at + rows, :] = g[:, b * 128:b * 128 + 128]
                at += rows
            continue
        c0, cn = cols[name]
        for r in range(0, rows, W):
            lt = acts[:, r:r + W].T
            for c in range(0, cn, step):
                g = dot(lt, dy[:, c0 + c:c0 + c + step]).astype(BF)
                for b in range(step // 128):
                    o = at + (c // 128 + b) * rows + r
                    flat[o:o + W, :] = g[:, b * 128:b * 128 + 128]
        at += rows * blocks
    if part == 2:
        small[...] = mine_ref[n:, :W].astype(F32) + dcame_ref[n:, :W].astype(F32)
        for b in range(half // 128):
            flat[at:at + 8, :] = small[0:8, b * 128:b * 128 + 128].astype(BF)
            at += 8
        tail = flat.shape[0] - at
        bias = [small[8 + t:9 + t, b * 128:b * 128 + 128] for t in range(FF // 2 // W) for b in range(W // 128)]
        bias = jnp.concatenate(bias + [jnp.zeros((tail - len(bias), 128), F32)], axis=0)
        flat[at:, :] = bias.astype(BF)
    size = flat.shape[0] // PIECES
    me = idx_ref[1 + part]

    def send(p, k):
        src = lambda q: flat.at[pl.ds(pl.multiple_of((q ^ me) * size, 16), size), :]
        to = pl.ds(pl.multiple_of(p * size, 16), size)
        pltpu.make_async_copy(src(p), keep.at[to, :], sem).start()
        pltpu.make_async_copy(src(p + PIECES // 2), give.at[to, :], sem).start()
        return k

    lax.fori_loop(0, PIECES // 2, send, 0)
    pltpu.make_async_copy(flat, flat, sem).wait()


def weight_grad_call(part, idx, acts, came, mine, dcame, W, FF, WD):
    n = acts.shape[0]
    rows = flat_rows(part, W, FF, WD)
    vm, hbm = pl.BlockSpec(memory_space=pltpu.VMEM), pl.BlockSpec(memory_space=pl.ANY)
    S = jax.ShapeDtypeStruct
    return pl.pallas_call(
        functools.partial(weight_grad_kernel, part=part, W=W, FF=FF, WD=WD),
        in_specs=[pl.BlockSpec(memory_space=pltpu.SMEM)] + [vm] * 4,
        out_specs=[hbm] * 2,
        out_shape=[S((rows // 2, 128), BF)] * 2,
        scratch_shapes=[pltpu.VMEM((rows, 128), BF), pltpu.VMEM((2 * n, FF if part == 0 else W), BF), pltpu.VMEM((2 * n, mine.shape[1]), BF),
                        pltpu.VMEM((WD, 2 * n), BF), pltpu.VMEM((16, W), F32), pltpu.SemaphoreType.DMA],
        compiler_params=pltpu.CompilerParams(vmem_limit_bytes=VMEM),
        cost_estimate=pl.CostEstimate(flops=600_000_000, bytes_accessed=8_000_000, transcendentals=0),
        name=("gradient_down", "gradient_up", "gradient_qkv_out_proj")[part],
    )(idx, acts, came, mine, dcame)


def unpack_kernel(idx_ref, own0, own1, own2, came0, came1, came2, dec_mine, dec_came, tok_mine, tok_came, vec_ref, qkv_ref, out_ref, up_ref, bias_ref, down_ref, proj_ref, sq_ref, dec_ref, tok_ref,
                  flat0, flat1, flat2, sem, *, W, FF, WD):
    sec = idx_ref[0]
    flats = (flat0, flat1, flat2)
    for i, (own, came) in enumerate(((own0, came0), (own1, came1), (own2, came2))):
        me = idx_ref[1 + i]
        size = flats[i].shape[0] // PIECES

        def fetch(p, k, own=own, came=came, me=me, flat=flats[i], size=size, i=i):
            to = lambda q: flat.at[pl.ds(pl.multiple_of((q ^ me) * size, 16), size), :]
            src = pl.ds(pl.multiple_of(p * size, 16), size)
            pltpu.make_async_copy(own.at[src, :], to(p), sem.at[i]).start()
            pltpu.make_async_copy(came.at[src, :], to(p + PIECES // 2), sem.at[i]).start()
            return k

        lax.fori_loop(0, PIECES // 2, fetch, 0)
    for ref, mine, came in ((dec_ref, dec_mine, dec_came), (tok_ref, tok_mine, tok_came)):
        ref[sec] = mine[...]
        ref[1 - sec] = came[...]
    refs = {"qkv": qkv_ref, "out": out_ref, "up": up_ref, "down": down_ref}
    enc = jnp.zeros((8, 128), F32)
    dec = jnp.zeros((8, 128), F32)
    fold = lambda v: jnp.sum((v * v).reshape(-1, 8, 128), axis=0)
    for part, flat in enumerate(flats):
        pltpu.make_async_copy(flat, flat, sem.at[part]).wait()
        at = 0
        for name, rows, blocks in flat_blocks(W, FF, WD)[part]:
            for b in range(blocks):
                g = flat[at:at + rows, :].astype(F32)
                if name == "proj":
                    dec += fold(g)
                    proj_ref[:, b * 128:b * 128 + 128] = g
                else:
                    enc += fold(g)
                    refs[name][:, b * 128:b * 128 + 128] = g
                at += rows
    for b in range(W // 2 // 128):
        g = flat2[at:at + 8, :].astype(F32)
        enc += g * g
        vec_ref[:, b * 128:b * 128 + 128] = g
        at += 8
    g = flat2[at:at + 16, :].astype(F32)[:FF // 2 // 128]
    bias_ref[...] = g
    enc += jnp.concatenate([jnp.sum(g * g, axis=0, keepdims=True), jnp.zeros((7, 128), F32)], axis=0)
    sq_ref[:8, :] = enc
    sq_ref[8:, :] = dec


def unpack_call(idx, own, came, dec_mine, dec_came, tok_mine, tok_came, W, FF, WD):
    vm, hbm = pl.BlockSpec(memory_space=pltpu.VMEM), pl.BlockSpec(memory_space=pl.ANY)
    S = jax.ShapeDtypeStruct
    half = W // 2
    return pl.pallas_call(
        functools.partial(unpack_kernel, W=W, FF=FF, WD=WD),
        in_specs=[pl.BlockSpec(memory_space=pltpu.SMEM)] + [hbm] * 6 + [vm] * 4,
        out_specs=[vm] * 10,
        out_shape=[S((8, half), F32), S((W, 3 * half), F32), S((W, half), F32), S((W, FF // 2), F32), S((FF // 2 // 128, 128), F32),
                   S((FF, half), F32), S((WD // 2, W), F32), S((16, 128), F32), S((2, *dec_mine.shape), BF), S((2, *tok_mine.shape), BF)],
        scratch_shapes=[pltpu.VMEM((flat_rows(i, W, FF, WD), 128), BF) for i in range(3)] + [pltpu.SemaphoreType.DMA((3,))],
        compiler_params=pltpu.CompilerParams(vmem_limit_bytes=VMEM),
        cost_estimate=pl.CostEstimate(flops=10_000_000, bytes_accessed=23_000_000, transcendentals=0),
        name="unpack",
    )(idx, *own, *came, dec_mine, dec_came, tok_mine, tok_came)


SIDE = 4


def coordinates(index):
    return (index // (SIDE * SIDE), index // SIDE % SIDE, index % SIDE)


def flip(place, axis, kind):
    place = list(place)
    place[axis] = place[axis] ^ 1 if kind == 0 else SIDE - 1 - place[axis]
    return tuple(place)


def swap(value, axes, far):
    pairs = []
    for core in range(2):
        for index in range(SIDE**3):
            place = coordinates(index)
            for axis in axes:
                place = flip(place, axis, core ^ far)
            target = (place[0] * SIDE + place[1]) * SIDE + place[2]
            pairs.append((core * SIDE**3 + index, core * SIDE**3 + target))
    return lax.ppermute(value, ("section", "dp"), pairs)


def add(left, right):
    return (left.astype(jnp.float32) + right.astype(jnp.float32)).astype(jnp.bfloat16)


def piece_numbers():
    place = coordinates(lax.axis_index("dp"))
    near = [((p == 1) | (p == 2)).astype(jnp.int32) for p in place]
    far = [(p >= 2).astype(jnp.int32) for p in place]
    core = lax.axis_index("section")
    bits = [jnp.where(core == 0, a, b) for a, b in zip(near, far)]
    return [bits[i] * 4 + bits[(i + 1) % 3] * 2 + bits[(i + 2) % 3] for i in range(3)]


def reduce_part(i, give, keep):
    v = add(keep, swap(give, (i,), 0))
    for step in (1, 2):
        half = v.shape[0] // 2
        v = add(v[:half], swap(v[half:], ((i + step) % 3,), 0))
    for step in range(3):
        v = add(v, swap(v, ((i + step) % 3,), 1))
    return v


def gather_part(i, v):
    for step in (2, 1):
        v = jnp.concatenate([v, swap(v, ((i + step) % 3,), 0)])
    return (v, swap(v, (i,), 0))


def from_partner(value):
    return lax.ppermute(value, "section", [(0, 1), (1, 0)])


def shards(
    tokens,
    frames,
    visible,
    out_grad,
    enc_vectors,
    enc_qkv,
    enc_out,
    enc_up,
    enc_up_bias,
    enc_down,
    proj_weight,
    dec_vectors,
    dec_qkv,
    dec_out,
    dec_up,
    dec_up_bias,
    dec_down,
    time_pos,
    space_pos,
):
    enc_width, enc_hidden = enc_up.shape
    dec_width, dec_hidden = dec_up.shape
    slot_count = time_pos.shape[0]
    patch_count = space_pos.shape[0]
    seen_count = visible.shape[1]
    section = lax.axis_index("section").astype(jnp.int32)
    core = section.reshape(1)
    sizes = (enc_width, enc_hidden, dec_width)
    acts, qkv, mid, slopes, projected = enc_fwd_call(
        core, frames, seen_count, tokens, enc_vectors, enc_up_bias, enc_qkv, enc_out, enc_up, enc_down, proj_weight
    )
    acts_came = from_partner(acts)
    (decoded_mine, decoded_other), grad_projected, (dec_mine, dec_other) = dec_block_call(
        core,
        frames,
        visible,
        projected,
        time_pos,
        space_pos,
        dec_vectors,
        dec_qkv,
        dec_out,
        dec_up,
        dec_up_bias,
        dec_down,
        out_grad,
        TQ=384,
        TA=640,
    )
    dec_came = from_partner(dec_other)
    hidden_mine, hidden_other, hidden, small_sums = enc_bwd_hidden_call(core, grad_projected, slopes, proj_weight, enc_down)
    hidden_came = from_partner(hidden_other)
    dec_local = add(dec_mine, dec_came)
    dec_sum = lax.psum(dec_local, "dp")
    decoded_came = from_partner(decoded_other)
    places = jnp.stack([section, *piece_numbers()]).astype(jnp.int32)
    places, dec_local = lax.optimization_barrier((places, dec_local))
    parts = [weight_grad_call(i, places, acts, acts_came, hidden_mine, hidden_came, *sizes) for i in range(2)]
    dy_mine, dy_other, token_mine, token_other = enc_bwd_call(
        core, frames, seen_count, grad_projected, tokens, enc_vectors, qkv, mid, hidden, small_sums, enc_up, enc_out, enc_qkv
    )
    dy_came = from_partner(dy_other)
    token_came = from_partner(token_other)
    parts.append(weight_grad_call(2, places, acts, acts_came, dy_mine, dy_came, *sizes))
    parts = [reduce_part(i, give, keep) for i, (give, keep) in enumerate(parts)]
    own, came = zip(*(gather_part(i, v) for i, v in enumerate(parts)))
    g_vectors, g_enc_qkv, g_enc_out, g_enc_up, g_enc_bias, g_enc_down, g_proj, squares, decoded, token_grad = unpack_call(
        places, own, came, decoded_mine, decoded_came, token_mine, token_came, *sizes
    )
    g_dec_qkv, g_dec_out, g_dec_up, g_dec_down, g_dec_vectors, g_dec_bias, g_time, g_space, dec_squares = finish_call(
        dec_sum, dec_width, dec_hidden, slot_count, patch_count
    )
    norms = jnp.stack([jnp.sum(squares[:8]), jnp.sum(squares[8:]) + jnp.sum(dec_squares)])
    norms = norms + from_partner(norms)
    return (
        decoded.transpose(0, 2, 1),
        token_grad,
        g_vectors,
        g_enc_qkv,
        g_enc_out,
        g_enc_up,
        g_enc_bias.reshape(-1),
        g_enc_down,
        g_proj.T,
        g_dec_vectors,
        g_dec_qkv.T,
        g_dec_out.T,
        g_dec_up,
        g_dec_bias[0],
        g_dec_down.T,
        g_time,
        g_space,
        lax.dynamic_slice_in_dim(norms, section, 1, 0),
    )


from jax.sharding import PartitionSpec as P


def solution(mesh):
    placed = (
        P("dp", None, None),
        P("dp"),
        P("dp", None),
        P("dp", None, None),
        P(),
        P(),
        P(),
        P(),
        P(),
        P(),
        P(),
        P(),
        P(),
        P(),
        P(),
        P(),
        P(),
        P(),
        P(),
    )
    return jax.shard_map(
        shards,
        mesh=mesh,
        in_specs=placed,
        out_specs=(
            P("dp", None, "section"),
            P("dp", None, "section"),
            P(None, "section"),
            P(None, "section"),
            P(None, "section"),
            P(None, "section"),
            P("section"),
            P(None, "section"),
            P(None, "section"),
            P(None, "section"),
            P(None, "section"),
            P(None, "section"),
            P(None, "section"),
            P("section"),
            P(None, "section"),
            P(None, "section"),
            P(None, "section"),
            P("section"),
        ),
        check_vma=False,
    )
```

time: 549 us -> 285 us (0.52)
  waiting for transfers between devices: 270 us -> 78.4 us
  Pallas kernels: 61.5 us -> 120 us
  other arithmetic: 75.5 us -> 17.5 us
  local copies, waits for them, and re-layouts: 51.5 us -> 4.42 us
  matrix products: 44.8 us -> 0 us
  starting transfers between devices: 6.28 us -> 44.2 us
  between operations: 27.5 us -> 16.1 us
    psum x2 -> x1, waiting for transfers between devices: 269 us -> 15 us  [shards(): dec_sum = lax.psum(dec_local, 'dp')]
    ppermute x17 -> x34, waiting for transfers between devices: 0.57 us -> 63.3 us  [the longest x27 60.5 us: swap(): return lax.ppermute(value, ('section', 'dp'), pairs)]
    pallas_call x1 -> x9, Pallas kernels: 61.5 us -> 120 us  [the longest x1 63.5 us: dec_block_call(): pl.pallas_call(functools.partial(dec_kernel, W=W, L=L, H=H, FF=FF, V=V, s...]
    dot_general x23 -> x0, matrix products: 44.8 us -> none  [the longest x5 16.2 us: left_transposed(): lax.dot_general(left, right, (((0,), (0,)), ((), ())), preferred_element_...]
    ppermute x17 -> x34, starting transfers between devices: 6.2 us -> 44.2 us  [the longest x27 32.3 us: swap(): return lax.ppermute(value, ('section', 'dp'), pairs)]
    reduce_sum x23 -> x2, other arithmetic: 38.5 us -> 2.62 us  [the longest x1 1.31 us: shards(): jnp.sum(dec_squares)]
    convert_element_type x20 -> x19, other arithmetic: 33.4 us -> 9.31 us  [add(): (left.astype(jnp.float32) + right.astype(jnp.float32)).astype(jnp.bfloat16)]
    convert_element_type x12 -> x0, local copies, waits for them, and re-layouts: 17.1 us -> none  [the longest x9 16.6 us: halves(): return (keep, from_partner(give.astype(jnp.bfloat16), 'section', 0))]
  transfers between devices with their start and end apart: 19 -> 35, of which waited for: 3 -> 14; matrix products, arithmetic and copies ran while one was open for 20% -> 6% of each run, Pallas kernels for 0% -> 11%
where the time goes in v3:
time: 285 us; the launch traced here: 281 us
  Pallas kernels  120 us (42%)
  waiting for transfers between devices  78.4 us (28%)
  starting transfers between devices  44.2 us (16%)
  other arithmetic  17.5 us (6%)
  between operations  16.1 us (6%)
  local copies, waits for them, and re-layouts  4.42 us (2%)
    pallas_call x1, Pallas kernels, dec_block_call(): pl.pallas_call(functools.partial(dec_kernel, W=W, L=L, H=H, FF=FF, V=V, s...  63.5 us
    ppermute x27, waiting for transfers between devices, swap(): return lax.ppermute(value, ('section', 'dp'), pairs)  60.5 us
    ppermute x27, starting transfers between devices, swap(): return lax.ppermute(value, ('section', 'dp'), pairs)  32.3 us
    psum x1, waiting for transfers between devices, shards(): dec_sum = lax.psum(dec_local, 'dp')  15 us
    pallas_call x3, Pallas kernels, weight_grad_call(): pl.pallas_call(functools.partial(weight_grad_kernel, part=part, W=W, FF=F...  13.5 us
    pallas_call x1, Pallas kernels, enc_bwd_call(): pl.pallas_call(functools.partial(enc_bwd_kernel, W=W, FF=FF, seen=seen),...  12.4 us
    ppermute x7, starting transfers between devices, from_partner(): return lax.ppermute(value, 'section', [(0, 1), (1, 0)])  11.8 us
    pallas_call x1, Pallas kernels, unpack_call(): pl.pallas_call(functools.partial(unpack_kernel, W=W, FF=FF, WD=WD), in_sp...  10.3 us
  transfers between devices with their start and end apart: 35, of which 14 were waited for; matrix products, arithmetic and copies ran while one was open for 6% of the time, Pallas kernels for 11%

profile of v3, /device:TPU:1, one launch (start us, length us, event | category | flops | bytes accessed | tf_op | source)
XLA Modules:
  0.0 280.7 jit_solution(16987342590028800037)
XLA Ops:
  7.2 10.2 %encoder_forward.1 = (bf16[112,6144]{1,0:T(8,128)(2,1)}, bf16[112,2304]{1,0:T(8,128)(2,1)}, f32[112,768]{1,0:T(8,128)}, bf16[112,3072]{1,0:T(8,128)(2,1)}, f32[112,384]{1,0:T(8,128)}) custom-call(s32[1]{0:T(128)} %bitcast.sec_ref, s32[2]{0:T(128)} %frames_ref.5, bf16[2,112,768]{2,1,0:T(8,128)(2,1)} %tok_ref.3, bf16[8,768]{1,0:T(8,128)(2,1)} %vec_ref.3, ...), custom_call_target="tpu_custom_call" | custom-call | flops 1700000000 | bytes 18000000 | tf_op jit(solution)/shard_map/encoder_forward/pallas_call | solution.py:442
  17.5 63.5 %decoder.1 = (bf16[192,1152]{1,0:T(8,128)(2,1)}, bf16[192,1152]{1,0:T(8,128)(2,1)}, bf16[112,384]{1,0:T(8,128)(2,1)}, bf16[2512,384]{1,0:T(8,128)(2,1)}, bf16[2512,384]{1,0:T(8,128)(2,1)}) custom-call(s32[1]{0:T(128)} %bitcast.sec_ref, s32[2]{0:T(128)} %frames_ref.5, s32[2,14]{1,0:T(2,128)} %vis_ref.1, f32[112,384]{1,0:T(8,128)} %get-tuple-element.62.proj_ref, ...), custom_call_target="tpu_custom_call" | custom-call | flops 28000000000 | bytes 12000000 | tf_op jit(solution)/shard_map/decoder/pallas_call | solution.py:329
  82.6 6.6 %encoder_backward_hidden.1 = (bf16[112,1920]{1,0:T(8,128)(2,1)}, bf16[112,1920]{1,0:T(8,128)(2,1)}, bf16[112,3840]{1,0:T(8,128)(2,1)}, f32[16,768]{1,0:T(8,128)}) custom-call(s32[1]{0:T(128)} %bitcast.sec_ref, bf16[112,384]{1,0:T(8,128)(2,1)} %get-tuple-element.67.dz_ref, bf16[112,3072]{1,0:T(8,128)(2,1)} %get-tuple-element.68.gp_ref, ...), custom_call_target="tpu_custom_call" | custom-call | flops 600000000 | bytes 8000000 | tf_op jit(solution)/shard_map/encoder_backward_hidden/pallas_call | solution.py:483
  90.5 3.9 %add_convert_fusion = bf16[2512,384]{1,0:T(8,128)(2,1)} fusion(bf16[2512,384]{1,0:T(8,128)(2,1)} %collective-permute-done, bf16[2512,384]{1,0:T(8,128)(2,1)} %get-tuple-element.63), kind=kLoop, calls=%fused_computation | loop fusion | flops 3858432 | bytes 5787648 | tf_op jit(solution)/shard_map/convert_element_type | solution.py:754
  95.1 4.4 %gradient_up.1 = (bf16[4608,128]{1,0:T(8,128)(2,1)}, bf16[4608,128]{1,0:T(8,128)(2,1)}) custom-call(s32[4]{0:T(128)} %pad_add_fusion.idx_ref, bf16[112,6144]{1,0:T(8,128)(2,1)} %get-tuple-element.66.acts_ref, bf16[112,6144]{1,0:T(8,128)(2,1)} %collective-permute-done.1.came_ref, bf16[112,1920]{1,0:T(8,128)(2,1)} %get-tuple-element.69.mine_ref, ...), custom_call_target="tpu_custom_call" | custom-call | flops 600000000 | bytes 8000000 | tf_op jit(solution)/shard_map/gradient_up/pallas_call | solution.py:650
  99.6 3.9 %collective-permute-start.11 = (bf16[4608,128]{1,0:T(8,128)(2,1)}, bf16[4608,128]{1,0:T(8,128)(2,1)}, u32[]{:S(2)}, u32[]{:S(2)}) collective-permute-start(bf16[4608,128]{1,0:T(8,128)(2,1)} %get-tuple-element.74), channel_id=1, source_target_pairs={{0,4},{1,5},{2,6},{3,7},{4,0},{5,1},{6,2},{7,3},{8,12},{9,13},{10,... | collective-permute-start | bytes 3538952 | tf_op jit(solution)/shard_map/ppermute | solution.py:750
  103.5 12.4 %encoder_backward.1 = (bf16[128,1920]{1,0:T(8,128)(2,1)}, bf16[128,1920]{1,0:T(8,128)(2,1)}, bf16[112,384]{1,0:T(8,128)(2,1)}, bf16[112,384]{1,0:T(8,128)(2,1)}) custom-call(s32[1]{0:T(128)} %bitcast.sec_ref, s32[2]{0:T(128)} %frames_ref.5, bf16[112,384]{1,0:T(8,128)(2,1)} %get-tuple-element.67.dz_ref, bf16[2,112,768]{2,1,0:T(8,128)(2,1)} %tok_ref.3, ...), custom_call_target="tpu_custom_call" | custom-call | flops 1600000000 | bytes 12000000 | tf_op jit(solution)/shard_map/encoder_backward/pallas_call | solution.py:564
  118.8 4.7 %gradient_qkv_out_proj.1 = (bf16[5248,128]{1,0:T(8,128)(2,1)}, bf16[5248,128]{1,0:T(8,128)(2,1)}) custom-call(s32[4]{0:T(128)} %pad_add_fusion.idx_ref, bf16[112,6144]{1,0:T(8,128)(2,1)} %get-tuple-element.66.acts_ref, bf16[112,6144]{1,0:T(8,128)(2,1)} %collective-permute-done.1.came_ref, bf16[128,1920]{1,0:T(8,128)(2,1)} %get-tuple-element.79.mine_ref, ...), custom_call_target="tpu_custom_call" | custom-call | flops 600000000 | bytes 8000000 | tf_op jit(solution)/shard_map/gradient_qkv_out_proj/pallas_call | solution.py:650
  126.1 4.4 %gradient_down.1 = (bf16[4608,128]{1,0:T(8,128)(2,1)}, bf16[4608,128]{1,0:T(8,128)(2,1)}) custom-call(s32[4]{0:T(128)} %pad_add_fusion.idx_ref, bf16[112,6144]{1,0:T(8,128)(2,1)} %get-tuple-element.66.acts_ref, bf16[112,6144]{1,0:T(8,128)(2,1)} %collective-permute-done.1.came_ref, bf16[112,1920]{1,0:T(8,128)(2,1)} %get-tuple-element.69.mine_ref, ...), custom_call_target="tpu_custom_call" | custom-call | flops 600000000 | bytes 8000000 | tf_op jit(solution)/shard_map/gradient_down/pallas_call | solution.py:650
  130.5 2.8 %collective-permute-start.3 = (bf16[4608,128]{1,0:T(8,128)(2,1)}, bf16[4608,128]{1,0:T(8,128)(2,1)S(1)}, u32[]{:S(2)}, u32[]{:S(2)}) collective-permute-start(bf16[4608,128]{1,0:T(8,128)(2,1)} %get-tuple-element.72), channel_id=1, source_target_pairs={{0,16},{1,17},{2,18},{3,19},{4,20},{5,21},{6,22},{7,23},{8,24},{9,... | collective-permute-start | bytes 3538952 | tf_op jit(solution)/shard_map/ppermute | solution.py:750
  135.7 13.2 %collective-permute-done.3 = bf16[4608,128]{1,0:T(8,128)(2,1)S(1)} collective-permute-done((bf16[4608,128]{1,0:T(8,128)(2,1)}, bf16[4608,128]{1,0:T(8,128)(2,1)S(1)}, u32[]{:S(2)}, u32[]{:S(2)}) %collective-permute-start.3) | collective-permute-done | bytes 1179680 | tf_op jit(solution)/shard_map/ppermute | solution.py:750
  156.4 3.8 %collective-permute-done.4 = bf16[2304,128]{1,0:T(8,128)(2,1)S(1)} collective-permute-done((bf16[2304,128]{1,0:T(8,128)(2,1)S(1)}, bf16[2304,128]{1,0:T(8,128)(2,1)S(1)}, u32[]{:S(2)}, u32[]{:S(2)}) %collective-permute-start.4) | collective-permute-done | bytes 589856 | tf_op jit(solution)/shard_map/ppermute | solution.py:750
  168.1 5.9 %collective-permute-done.22 = bf16[1312,128]{1,0:T(8,128)(2,1)S(1)} collective-permute-done((bf16[1312,128]{1,0:T(8,128)(2,1)S(1)}, bf16[1312,128]{1,0:T(8,128)(2,1)S(1)}, u32[]{:S(2)}, u32[]{:S(2)}) %collective-permute-start.22) | collective-permute-done | bytes 335904 | tf_op jit(solution)/shard_map/ppermute | solution.py:750
  176.0 7.8 %collective-permute-done.15 = bf16[1152,128]{1,0:T(8,128)(2,1)S(1)} collective-permute-done((bf16[1152,128]{1,0:T(8,128)(2,1)S(1)}, bf16[1152,128]{1,0:T(8,128)(2,1)S(1)}, u32[]{:S(2)}, u32[]{:S(2)}) %collective-permute-start.15) | collective-permute-done | bytes 294944 | tf_op jit(solution)/shard_map/ppermute | solution.py:750
  185.8 4.0 %collective-permute-done.16 = bf16[1152,128]{1,0:T(8,128)(2,1)S(1)} collective-permute-done((bf16[1152,128]{1,0:T(8,128)(2,1)S(1)}, bf16[1152,128]{1,0:T(8,128)(2,1)S(1)}, u32[]{:S(2)}, u32[]{:S(2)}) %collective-permute-start.16) | collective-permute-done | bytes 294944 | tf_op jit(solution)/shard_map/ppermute | solution.py:750
  191.0 2.6 collective-permute-done.24
  194.1 6.2 %collective-permute-done.25 = bf16[1312,128]{1,0:T(8,128)(2,1)S(1)} collective-permute-done((bf16[1312,128]{1,0:T(8,128)(2,1)S(1)}, bf16[1312,128]{1,0:T(8,128)(2,1)S(1)}, u32[]{:S(2)}, u32[]{:S(2)}) %collective-permute-start.25) | collective-permute-done | bytes 335904 | tf_op jit(solution)/shard_map/ppermute | solution.py:750
  200.7 2.7 collective-permute-start.18
  203.4 7.0 %collective-permute-done.26 = bf16[1312,128]{1,0:T(8,128)(2,1)S(1)} collective-permute-done((bf16[1312,128]{1,0:T(8,128)(2,1)S(1)}, bf16[1312,128]{1,0:T(8,128)(2,1)S(1)}, u32[]{:S(2)}, u32[]{:S(2)}) %collective-permute-start.26) | collective-permute-done | bytes 335904 | tf_op jit(solution)/shard_map/ppermute | solution.py:750
  216.0 6.2 %collective-permute-done.27 = bf16[2624,128]{1,0:T(8,128)(2,1)S(1)} collective-permute-done((bf16[2624,128]{1,0:T(8,128)(2,1)S(1)}, bf16[2624,128]{1,0:T(8,128)(2,1)S(1)}, u32[]{:S(2)}, u32[]{:S(2)}) %collective-permute-start.27) | collective-permute-done | bytes 671776 | tf_op jit(solution)/shard_map/ppermute | solution.py:750
  226.2 7.5 %collective-permute-start.31 = (bf16[192,1152]{1,0:T(8,128)(2,1)S(1)}, bf16[192,1152]{1,0:T(8,128)(2,1)S(1)}, u32[]{:S(2)}, u32[]{:S(2)}) collective-permute-start(bf16[192,1152]{1,0:T(8,128)(2,1)S(1)} %copy-done.6), channel_id=1, source_target_pairs={{0,64},{64,0},{1,65},{65,1},{2,66},{66,2},{3,67},{67,3},{4,68},{68... | collective-permute-start | bytes 1327112 | tf_op jit(solution)/shard_map/ppermute | solution.py:783
  233.7 15.0 %all-reduce.2.cloned.1.call-done.pack_ref = bf16[2512,384]{1,0:T(8,128)(2,1)} async-done(((bf16[2512,384]{1,0:T(8,128)(2,1)}), bf16[2512,384]{1,0:T(8,128)(2,1)}) %all-reduce.2.cloned.1.call-update) | async-done | bytes 1929232 | tf_op jit(solution)/shard_map/psum | solution.py:840
  248.8 3.5 %decoder_gradients.1 = (f32[576,384]{1,0:T(8,128)}, f32[192,384]{1,0:T(8,128)}, f32[384,768]{1,0:T(8,128)}, f32[192,1536]{1,0:T(8,128)}, f32[9,192]{1,0:T(8,128)...) custom-call(bf16[2512,384]{1,0:T(8,128)(2,1)} %all-reduce.2.cloned.1.call-done.pack_ref), custom_call_target="tpu_custom_call" | custom-call | flops 2000000 | bytes 6000000 | tf_op jit(solution)/shard_map/decoder_gradients/pallas_call | solution.py:311
  255.8 10.3 %unpack.1 = (f32[8,384]{1,0:T(8,128)}, f32[768,1152]{1,0:T(8,128)}, f32[768,384]{1,0:T(8,128)}, f32[768,1536]{1,0:T(8,128)}, f32[12,128]{1,0:T(8,128)}, /*index=...) custom-call(s32[4]{0:T(128)} %pad_add_fusion.idx_ref, ...), custom_call_target="tpu_custom_call" | custom-call | flops 10000000 | bytes 23000000 | tf_op jit(solution)/shard_map/unpack/pallas_call | solution.py:715
  (108 shorter events, 51.8 us)
Async XLA Ops:
  7.2 241.6 %all-reduce.2.cloned.1.call-start = ((), (), s32[]{:S(2)}) async-start(), calls=%async_computation | async-start | bytes 3858432 | tf_op jit(solution)/shard_map/psum | solution.py:840
  81.0 9.5 %collective-permute-start = (bf16[2512,384]{1,0:T(8,128)(2,1)}, bf16[2512,384]{1,0:T(8,128)(2,1)}, u32[]{:S(2)}, u32[]{:S(2)}) collective-permute-start(bf16[2512,384]{1,0:T(8,128)(2,1)} %get-tuple-element.64), channel_id=1, source_target_pairs={{0,64},{64,0},{1,65},{65,1},{2,66},{66,2},{3,67},{67,3},{4,68},{68... | collective-permute-start | bytes 5787656 | tf_op jit(solution)/shard_map/ppermute | solution.py:783
  82.5 11.9 %collective-permute-start.1 = (bf16[112,6144]{1,0:T(8,128)(2,1)}, bf16[112,6144]{1,0:T(8,128)(2,1)}, u32[]{:S(2)}, u32[]{:S(2)}) collective-permute-start(bf16[112,6144]{1,0:T(8,128)(2,1)} %get-tuple-element.66.acts_ref), channel_id=1, source_target_pairs={{0,64},{64,0},{1,65},{65,1},{2,66},{66,2},{3,67},{67,3},{4,68},{68... | collective-permute-start | bytes 4128776 | tf_op jit(solution)/shard_map/ppermute | solution.py:783
  99.6 33.7 %collective-permute-start.11 = (bf16[4608,128]{1,0:T(8,128)(2,1)}, bf16[4608,128]{1,0:T(8,128)(2,1)}, u32[]{:S(2)}, u32[]{:S(2)}) collective-permute-start(bf16[4608,128]{1,0:T(8,128)(2,1)} %get-tuple-element.74), channel_id=1, source_target_pairs={{0,4},{1,5},{2,6},{3,7},{4,0},{5,1},{6,2},{7,3},{8,12},{9,13},{10,... | collective-permute-start | bytes 3538952 | tf_op jit(solution)/shard_map/ppermute | solution.py:750
  123.5 27.8 %collective-permute-start.20 = (bf16[5248,128]{1,0:T(8,128)(2,1)}, bf16[5248,128]{1,0:T(8,128)(2,1)}, u32[]{:S(2)}, u32[]{:S(2)}) collective-permute-start(bf16[5248,128]{1,0:T(8,128)(2,1)} %get-tuple-element.82), channel_id=1, source_target_pairs={{0,1},{1,0},{2,3},{3,2},{4,5},{5,4},{6,7},{7,6},{8,9},{9,8},{10,11... | collective-permute-start | bytes 4030472 | tf_op jit(solution)/shard_map/ppermute | solution.py:750
  130.5 18.4 %collective-permute-start.3 = (bf16[4608,128]{1,0:T(8,128)(2,1)}, bf16[4608,128]{1,0:T(8,128)(2,1)S(1)}, u32[]{:S(2)}, u32[]{:S(2)}) collective-permute-start(bf16[4608,128]{1,0:T(8,128)(2,1)} %get-tuple-element.72), channel_id=1, source_target_pairs={{0,16},{1,17},{2,18},{3,19},{4,20},{5,21},{6,22},{7,23},{8,24},{9,... | collective-permute-start | bytes 3538952 | tf_op jit(solution)/shard_map/ppermute | solution.py:750
  135.3 19.6 %collective-permute-start.12 = (bf16[2304,128]{1,0:T(8,128)(2,1)S(1)}, bf16[2304,128]{1,0:T(8,128)(2,1)S(1)}, u32[]{:S(2)}, u32[]{:S(2)}) collective-permute-start(bf16[2304,128]{1,0:T(8,128)(2,1)S(1)} %slice.65), channel_id=1, source_target_pairs={{0,1},{1,0},{2,3},{3,2},{4,5},{5,4},{6,7},{7,6},{8,9},{9,8},{10,11... | collective-permute-start | bytes 1769480 | tf_op jit(solution)/shard_map/ppermute | solution.py:750
  149.2 11.0 %collective-permute-start.4 = (bf16[2304,128]{1,0:T(8,128)(2,1)S(1)}, bf16[2304,128]{1,0:T(8,128)(2,1)S(1)}, u32[]{:S(2)}, u32[]{:S(2)}) collective-permute-start(bf16[2304,128]{1,0:T(8,128)(2,1)S(1)} %slice.61), channel_id=1, source_target_pairs={{0,4},{1,5},{2,6},{3,7},{4,0},{5,1},{6,2},{7,3},{8,12},{9,13},{10,... | collective-permute-start | bytes 1769480 | tf_op jit(solution)/shard_map/ppermute | solution.py:750
  153.0 11.3 %collective-permute-start.21 = (bf16[2624,128]{1,0:T(8,128)(2,1)S(1)}, bf16[2624,128]{1,0:T(8,128)(2,1)S(1)}, u32[]{:S(2)}, u32[]{:S(2)}) collective-permute-start(bf16[2624,128]{1,0:T(8,128)(2,1)S(1)} %slice.69), channel_id=1, source_target_pairs={{0,16},{1,17},{2,18},{3,19},{4,20},{5,21},{6,22},{7,23},{8,24},{9,... | collective-permute-start | bytes 2015240 | tf_op jit(solution)/shard_map/ppermute | solution.py:750
  155.1 12.5 %collective-permute-start.13 = (bf16[1152,128]{1,0:T(8,128)(2,1)S(1)}, bf16[1152,128]{1,0:T(8,128)(2,1)S(1)}, u32[]{:S(2)}, u32[]{:S(2)}) collective-permute-start(bf16[1152,128]{1,0:T(8,128)(2,1)S(1)} %slice.67), channel_id=1, source_target_pairs={{0,16},{1,17},{2,18},{3,19},{4,20},{5,21},{6,22},{7,23},{8,24},{9,... | collective-permute-start | bytes 884744 | tf_op jit(solution)/shard_map/ppermute | solution.py:750
  174.1 10.1 %collective-permute-start.23 = (bf16[1312,128]{1,0:T(8,128)(2,1)S(1)}, bf16[1312,128]{1,0:T(8,128)(2,1)S(1)}, u32[]{:S(2)}, u32[]{:S(2)}) collective-permute-start(bf16[1312,128]{1,0:T(8,128)(2,1)S(1)} %add_convert_fusion.10), channel_id=1, source_target_pairs={{0,3},{1,2},{2,1},{3,0},{4,7},{5,6},{6,5},{7,4},{8,11},{9,10},{10,... | collective-permute-start | bytes 1007624 | tf_op jit(solution)/shard_map/ppermute | solution.py:750
  174.3 9.5 %collective-permute-start.15 = (bf16[1152,128]{1,0:T(8,128)(2,1)S(1)}, bf16[1152,128]{1,0:T(8,128)(2,1)S(1)}, u32[]{:S(2)}, u32[]{:S(2)}) collective-permute-start(bf16[1152,128]{1,0:T(8,128)(2,1)S(1)} %add_convert_fusion.13), channel_id=1, source_target_pairs={{0,3},{1,2},{2,1},{3,0},{4,7},{5,6},{6,5},{7,4},{8,11},{9,10},{10,... | collective-permute-start | bytes 884744 | tf_op jit(solution)/shard_map/ppermute | solution.py:750
  184.1 9.7 %collective-permute-start.8 = (bf16[1152,128]{1,0:T(8,128)(2,1)S(1)}, bf16[1152,128]{1,0:T(8,128)(2,1)S(1)}, u32[]{:S(2)}, u32[]{:S(2)}) collective-permute-start(bf16[1152,128]{1,0:T(8,128)(2,1)S(1)} %add_convert_fusion.16), channel_id=1, source_target_pairs={{0,3},{1,2},{2,1},{3,0},{4,7},{5,6},{6,5},{7,4},{8,11},{9,10},{10,... | collective-permute-start | bytes 884744 | tf_op jit(solution)/shard_map/ppermute | solution.py:750
  189.9 10.7 %collective-permute-start.17 = (bf16[1152,128]{1,0:T(8,128)(2,1)S(1)}, bf16[1152,128]{1,0:T(8,128)(2,1)S(1)}, u32[]{:S(2)}, u32[]{:S(2)}) collective-permute-start(bf16[1152,128]{1,0:T(8,128)(2,1)S(1)} %add_convert_fusion.11), channel_id=1, source_target_pairs={{0,16},{1,17},{2,18},{3,19},{4,20},{5,21},{6,22},{7,23},{8,24},{9,... | collective-permute-start | bytes 884744 | tf_op jit(solution)/shard_map/ppermute | solution.py:750
  193.9 18.1 %collective-permute-start.9 = (bf16[1152,128]{1,0:T(8,128)(2,1)S(1)}, bf16[1152,128]{1,0:T(8,128)(2,1)S(1)}, u32[]{:S(2)}, u32[]{:S(2)}) collective-permute-start(bf16[1152,128]{1,0:T(8,128)(2,1)S(1)} %add_convert_fusion.15), channel_id=1, source_target_pairs={{0,1},{1,0},{2,3},{3,2},{4,5},{5,4},{6,7},{7,6},{8,9},{9,8},{10,11... | collective-permute-start | bytes 884744 | tf_op jit(solution)/shard_map/ppermute | solution.py:750
  200.3 10.0 %collective-permute-start.26 = (bf16[1312,128]{1,0:T(8,128)(2,1)S(1)}, bf16[1312,128]{1,0:T(8,128)(2,1)S(1)}, u32[]{:S(2)}, u32[]{:S(2)}) collective-permute-start(bf16[1312,128]{1,0:T(8,128)(2,1)S(1)} %add_convert_fusion.7), channel_id=1, source_target_pairs={{0,4},{1,5},{2,6},{3,7},{4,0},{5,1},{6,2},{7,3},{8,12},{9,13},{10,... | collective-permute-start | bytes 1007624 | tf_op jit(solution)/shard_map/ppermute | solution.py:750
  200.7 13.6 %collective-permute-start.18 = (bf16[2304,128]{1,0:T(8,128)(2,1)S(1)}, bf16[2304,128]{1,0:T(8,128)(2,1)S(1)}, u32[]{:S(2)}, u32[]{:S(2)}) collective-permute-start(bf16[2304,128]{1,0:T(8,128)(2,1)S(1)} %pad_maximum_fusion.5), channel_id=1, source_target_pairs={{0,1},{1,0},{2,3},{3,2},{4,5},{5,4},{6,7},{7,6},{8,9},{9,8},{10,11... | collective-permute-start | bytes 1769480 | tf_op jit(solution)/shard_map/ppermute | solution.py:750
  210.4 11.8 %collective-permute-start.27 = (bf16[2624,128]{1,0:T(8,128)(2,1)S(1)}, bf16[2624,128]{1,0:T(8,128)(2,1)S(1)}, u32[]{:S(2)}, u32[]{:S(2)}) collective-permute-start(bf16[2624,128]{1,0:T(8,128)(2,1)S(1)} %pad_maximum_fusion.3), channel_id=1, source_target_pairs={{0,16},{1,17},{2,18},{3,19},{4,20},{5,21},{6,22},{7,23},{8,24},{9,... | collective-permute-start | bytes 2015240 | tf_op jit(solution)/shard_map/ppermute | solution.py:750
  212.1 11.8 %collective-permute-start.10 = (bf16[2304,128]{1,0:T(8,128)(2,1)S(1)}, bf16[2304,128]{1,0:T(8,128)(2,1)S(1)}, u32[]{:S(2)}, u32[]{:S(2)}) collective-permute-start(bf16[2304,128]{1,0:T(8,128)(2,1)S(1)} %pad_maximum_fusion.4), channel_id=1, source_target_pairs={{0,4},{1,5},{2,6},{3,7},{4,0},{5,1},{6,2},{7,3},{8,12},{9,13},{10,... | collective-permute-start | bytes 1769480 | tf_op jit(solution)/shard_map/ppermute | solution.py:750
  215.4 39.6 %collective-permute-start.29 = (bf16[4608,128]{1,0:T(8,128)(2,1)}, bf16[4608,128]{1,0:T(8,128)(2,1)}, u32[]{:S(2)}, u32[]{:S(2)}) collective-permute-start(bf16[4608,128]{1,0:T(8,128)(2,1)} %pad_maximum_fusion.2.own1), channel_id=1, source_target_pairs={{0,4},{1,5},{2,6},{3,7},{4,0},{5,1},{6,2},{7,3},{8,12},{9,13},{10,... | collective-permute-start | bytes 3538952 | tf_op jit(solution)/shard_map/ppermute | solution.py:750
  223.4 31.6 %collective-permute-start.30 = (bf16[5248,128]{1,0:T(8,128)(2,1)}, bf16[5248,128]{1,0:T(8,128)(2,1)}, u32[]{:S(2)}, u32[]{:S(2)}) collective-permute-start(bf16[5248,128]{1,0:T(8,128)(2,1)} %pad_maximum_fusion.own2), channel_id=1, source_target_pairs={{0,1},{1,0},{2,3},{3,2},{4,5},{5,4},{6,7},{7,6},{8,9},{9,8},{10,11... | collective-permute-start | bytes 4030472 | tf_op jit(solution)/shard_map/ppermute | solution.py:750
  225.0 29.9 %collective-permute-start.28 = (bf16[4608,128]{1,0:T(8,128)(2,1)}, bf16[4608,128]{1,0:T(8,128)(2,1)}, u32[]{:S(2)}, u32[]{:S(2)}) collective-permute-start(bf16[4608,128]{1,0:T(8,128)(2,1)} %pad_maximum_fusion.1.own0), channel_id=1, source_target_pairs={{0,16},{1,17},{2,18},{3,19},{4,20},{5,21},{6,22},{7,23},{8,24},{9,... | collective-permute-start | bytes 3538952 | tf_op jit(solution)/shard_map/ppermute | solution.py:750
  226.2 28.8 %collective-permute-start.31 = (bf16[192,1152]{1,0:T(8,128)(2,1)S(1)}, bf16[192,1152]{1,0:T(8,128)(2,1)S(1)}, u32[]{:S(2)}, u32[]{:S(2)}) collective-permute-start(bf16[192,1152]{1,0:T(8,128)(2,1)S(1)} %copy-done.6), channel_id=1, source_target_pairs={{0,64},{64,0},{1,65},{65,1},{2,66},{66,2},{3,67},{67,3},{4,68},{68... | collective-permute-start | bytes 1327112 | tf_op jit(solution)/shard_map/ppermute | solution.py:783
  233.7 21.2 %collective-permute-start.32 = (bf16[112,384]{1,0:T(8,128)(2,1)}, bf16[112,384]{1,0:T(8,128)(2,1)S(1)}, u32[]{:S(2)}, u32[]{:S(2)}) collective-permute-start(bf16[112,384]{1,0:T(8,128)(2,1)} %get-tuple-element.86), channel_id=1, source_target_pairs={{0,64},{64,0},{1,65},{65,1},{2,66},{66,2},{3,67},{67,3},{4,68},{68... | collective-permute-start | bytes 258056 | tf_op jit(solution)/shard_map/ppermute | solution.py:783
  (18 other events, 93.0 us)
Sparse Core Ops, SparseCore 0:
  116.1 132.5 all-reduce.1

commit v4 on v3

--- a/solution.py
+++ b/solution.py
@@ -191,13 +191,10 @@
         out_refs[who][...] = dec_s[rows(W), :]
         pack = pack_refs[who]
         for b in range(FF // W):
-            r = blocks["down"] + b * (W // 2)
-            pack[r:r + W // 2, :] = dot(dy_s[rows(W), :], g_s[b * W:b * W + W, :], 1, 1).astype(BF)
+            put(pack, blocks["down"] + b * 3 * (W // 2), dot(dy_s[rows(W), :], g_s[b * W:b * W + W, :], 1, 1))
         for b in range(FF // 2 // W):
-            r = blocks["up"] + b * W
-            pack[r:r + W, :] = dot(a2_s[...], gp_s[pl.ds(pl.multiple_of(s * (FF // 2) + b * W, 16), W), :], 1, 1).astype(BF)
-        r = blocks["out"]
-        pack[r:r + W // 2, :] = dot(db_s[rows(W), :], o_s[...], 1, 1).astype(BF)
+            put(pack, blocks["up"] + b * 3 * W, dot(a2_s[...], gp_s[pl.ds(pl.multiple_of(s * (FF // 2) + b * W, 16), W), :], 1, 1))
+        put(pack, blocks["out"], dot(db_s[rows(W), :], o_s[...], 1, 1))
 
     def bwd_head(h, carry):
         hs = pl.ds(pl.multiple_of(h * HS, HS), HS)
@@ -246,77 +243,54 @@
     small[:, 8:16] = gsel[:, V + patches + 16:V + patches + 24]
     small[:, 16:24] = exact(gsel[:, V + patches:V + patches + slots], table, 1, 0)
     small[:, 24:24 + patches] = gsel[:, V:V + patches]
-    rows = 32 + patches
     small[:, 24 + patches:256] = jnp.zeros((W, 256 - 24 - patches), F32)
-    wide = jnp.broadcast_to(sum_b1, (FF, 128))
     for who, s in enumerate((sec, 1 - sec)):
         pack = pack_refs[who]
-        for b in range(3):
-            r = blocks["qkv"] + b * (W // 2)
-            pack[r:r + W // 2, :] = dot(dqkv_s[pl.ds(pl.multiple_of(s * (3 * W // 2) + b * (W // 2), 16), W // 2), :], a1_s[...], 1, 1).astype(BF)
-        r = blocks["small"]
-        pack[r:r + rows, :W // 2] = small[pl.ds(pl.multiple_of(s * (W // 2), 8), W // 2), :256].T[:rows].astype(BF)
-        pack[r:r + rows, W // 2:] = jnp.zeros((rows, W - W // 2), BF)
+        put(pack, blocks["qkv"], dot(dqkv_s[pl.ds(pl.multiple_of(s * (3 * W // 2), 16), 3 * W // 2), :], a1_s[...], 1, 1))
+        half = small[pl.ds(pl.multiple_of(s * (W // 2), 8), W // 2), :256].T[:32 + patches]
+        put(pack, blocks["small"], jnp.concatenate([half, jnp.zeros((32 + patches, 256 - W // 2), F32)], axis=1))
         b1_ref[...] = sum_b1
-        bias = jnp.broadcast_to(b1_ref[pl.ds(pl.multiple_of(s * (FF // 2), 8), FF // 2), :], (FF // 2, 128)).T[:16]
-        r = blocks["bias"]
-        for b in range(FF // 2 // W):
-            pack[r + 16 * b:r + 16 * b + 16, :] = bias[:, b * W:b * W + W].astype(BF)
+        put(pack, blocks["bias"], jnp.broadcast_to(b1_ref[pl.ds(pl.multiple_of(s * (FF // 2), 8), FF // 2), :], (FF // 2, 128)).T[:16])
+        pack[blocks["end"]:, :] = jnp.zeros((pack.shape[0] - blocks["end"], 128), BF)
+
+
+def put(pack, at, value):
+    n = value.shape[0]
+    for b in range(value.shape[1] // 128):
+        pack[at + b * n:at + b * n + n, :] = value[:, b * 128:b * 128 + 128].astype(BF)
 
 
 def dec_blocks(W, FF):
     at, rows = 0, {}
-    for name, count in (("qkv", 3 * W // 2), ("out", W // 2), ("up", FF // 2), ("down", FF // 2), ("small", 176), ("bias", 16 * (FF // 2 // W))):
+    for name, count in (("qkv", 3 * (3 * W // 2)), ("out", 3 * (W // 2)), ("up", 3 * (FF // 2)), ("down", 3 * (FF // 2)), ("small", 2 * 176), ("bias", 16 * (FF // 2 // 128))):
         rows[name] = at
         at += count
     rows["end"] = at
+    unit = 3 * 8 * 16
+    rows["all"] = -(-at // unit) * unit
     return rows
 
 
-def finish_kernel(pack_ref, qkv_ref, out_ref, up_ref, down_ref, vec_ref, bias_ref, time_ref, space_ref, sq_ref, *, W, FF, slots, patches):
+def finish(read, qkv_ref, out_ref, up_ref, down_ref, vec_ref, bias_ref, time_ref, space_ref, *, W, FF, slots, patches):
     blocks = dec_blocks(W, FF)
     total = jnp.zeros((8, 128), F32)
-    fold = lambda v: jnp.sum(jnp.sum((v * v).reshape(-1, 8, W), axis=0).reshape(8, W // 128, 128), axis=1)
-    read = lambda name, at, n: pack_ref[blocks[name] + at:blocks[name] + at + n, :].astype(F32)
-    g = read("qkv", 0, 3 * W // 2)
-    qkv_ref[...] = g
-    total += fold(g)
-    g = read("out", 0, W // 2)
-    out_ref[...] = g
-    total += fold(g)
-    for b in range(FF // 2 // W):
-        g = read("up", b * W, W)
-        up_ref[:, b * W:b * W + W] = g
-        total += fold(g)
-    for b in range(FF // W):
-        g = read("down", b * (W // 2), W // 2)
-        down_ref[:, b * W:b * W + W] = g
-        total += fold(g)
-    small = read("small", 0, 176)
-    total += fold(small)
-    vec_ref[...] = small[:9, :W // 2]
-    time_ref[...] = small[16:16 + slots, :W // 2]
-    space_ref[...] = small[16 + slots:16 + slots + patches, :W // 2]
-    for b in range(FF // 2 // W):
-        g = read("bias", 16 * b, 16)[:8]
-        bias_ref[:, b * W:b * W + W] = g
-        total += 0.125 * fold(g)
-    sq_ref[...] = total
-
-
-def finish_call(pack, W, FF, slots, patches):
-    vm = pl.BlockSpec(memory_space=pltpu.VMEM)
-    S = lambda *shape: jax.ShapeDtypeStruct(shape, F32)
-    half = W // 2
-    return pl.pallas_call(
-        functools.partial(finish_kernel, W=W, FF=FF, slots=slots, patches=patches),
-        in_specs=[vm],
-        out_specs=[vm] * 9,
-        out_shape=[S(3 * half, W), S(half, W), S(W, FF // 2), S(half, FF), S(9, half), S(8, FF // 2), S(slots, half), S(patches, half), S(8, 128)],
-        compiler_params=pltpu.CompilerParams(vmem_limit_bytes=63 * 1024 * 1024),
-        cost_estimate=pl.CostEstimate(flops=2_000_000, bytes_accessed=6_000_000, transcendentals=0),
-        name="decoder_gradients",
-    )(pack)
+    fold = lambda v: jnp.sum((v * v).reshape(-1, 8, 128), axis=0)
+    for name, ref, n, parts in (("qkv", qkv_ref, 3 * W // 2, 1), ("out", out_ref, W // 2, 1), ("up", up_ref, W, FF // 2 // W), ("down", down_ref, W // 2, FF // W)):
+        for b in range(3 * parts):
+            g = read(blocks[name] + b * n, n).astype(F32)
+            ref[:, b * 128:b * 128 + 128] = g
+            total += fold(g)
+    low = read(blocks["small"], 176).astype(F32)
+    high = read(blocks["small"] + 176, 176).astype(F32)
+    total += fold(low) + fold(high)
+    for ref, at, n in ((vec_ref, 0, 9), (time_ref, 16, slots), (space_ref, 16 + slots, patches)):
+        ref[:, :128] = low[at:at + n]
+        ref[:, 128:] = high[at:at + n, :W // 2 - 128]
+    for b in range(FF // 2 // 128):
+        g = read(blocks["bias"] + 16 * b, 16).astype(F32)
+        bias_ref[:, b * 128:b * 128 + 128] = g[:8]
+        total += 0.0625 * fold(g)
+    return total
 
 
 def dec_block_call(sec, frames, visible, proj, time_pos, space, vecs, wqkv, wo, w1, bias, w2, dy, TQ, TA):
@@ -330,7 +304,7 @@
         functools.partial(dec_kernel, W=W, L=L, H=H, FF=FF, V=V, slots=slots, patches=patches, TQ=TQ, TA=TA),
         in_specs=[sm, sm, sm] + [vm] * 9 + [pl.BlockSpec(memory_space=pl.ANY)],
         out_specs=[[vm] * 2, vm, [vm] * 2],
-        out_shape=[[S((W // 2, L), BF)] * 2, S((V, W), BF), [S((dec_blocks(W, FF)["end"], W), BF)] * 2],
+        out_shape=[[S((W // 2, L), BF)] * 2, S((V, W), BF), [S((dec_blocks(W, FF)["all"], 128), BF)] * 2],
         scratch_shapes=[
             pltpu.VMEM((W, L), F32),
             pltpu.VMEM((W, L), BF),
@@ -590,8 +564,16 @@
     return -(-rows // unit) * unit
 
 
-def weight_grad_kernel(idx_ref, acts_ref, came_ref, mine_ref, dcame_ref, give, keep, flat, acts, dy, dzt, small, sem, *, part, W, FF, WD):
+def part_rows(part, W, FF, WD, WF):
+    return flat_rows(part, W, FF, WD) + dec_blocks(WD, WF)["all"] // 3
+
+
+def weight_grad_kernel(idx_ref, acts_ref, came_ref, mine_ref, dcame_ref, pack_any, pack_came_any, give, keep, flat, acts, dy, dzt, small, pack, pack_came, sem, pack_sem, *, part, W, FF, WD):
     n = acts_ref.shape[0]
+    third = pack.shape[0]
+    packs = [pltpu.make_async_copy(a.at[pl.ds(part * third, third), :], b, pack_sem.at[i]) for i, (a, b) in enumerate(((pack_any, pack), (pack_came_any, pack_came)))]
+    for c in packs:
+        c.start()
     half = W // 2
     lhs = {"qkv": (0, W), "out": (W, W), "up": (2 * W, W), "down": (3 * W, FF), "proj": (3 * W + FF, W)}
     cols = {"down": (0, half), "up": (half, FF // 2), "out": (0, half), "qkv": (half, 3 * half)}
@@ -624,10 +606,13 @@
         for b in range(half // 128):
             flat[at:at + 8, :] = small[0:8, b * 128:b * 128 + 128].astype(BF)
             at += 8
-        tail = flat.shape[0] - at
+        tail = flat.shape[0] - third - at
         bias = [small[8 + t:9 + t, b * 128:b * 128 + 128] for t in range(FF // 2 // W) for b in range(W // 128)]
         bias = jnp.concatenate(bias + [jnp.zeros((tail - len(bias), 128), F32)], axis=0)
-        flat[at:, :] = bias.astype(BF)
+        flat[at:at + tail, :] = bias.astype(BF)
+    for c in packs:
+        c.wait()
+    flat[flat.shape[0] - third:, :] = (pack[...].astype(F32) + pack_came[...].astype(F32)).astype(BF)
     size = flat.shape[0] // PIECES
     me = idx_ref[1 + part]
 
@@ -642,28 +627,31 @@
     pltpu.make_async_copy(flat, flat, sem).wait()
 
 
-def weight_grad_call(part, idx, acts, came, mine, dcame, W, FF, WD):
+def weight_grad_call(part, idx, acts, came, mine, dcame, pack, pack_came, W, FF, WD, WF):
     n = acts.shape[0]
-    rows = flat_rows(part, W, FF, WD)
+    rows = part_rows(part, W, FF, WD, WF)
+    third = pack.shape[0] // 3
     vm, hbm = pl.BlockSpec(memory_space=pltpu.VMEM), pl.BlockSpec(memory_space=pl.ANY)
     S = jax.ShapeDtypeStruct
     return pl.pallas_call(
         functools.partial(weight_grad_kernel, part=part, W=W, FF=FF, WD=WD),
-        in_specs=[pl.BlockSpec(memory_space=pltpu.SMEM)] + [vm] * 4,
+        in_specs=[pl.BlockSpec(memory_space=pltpu.SMEM)] + [vm] * 4 + [hbm] * 2,
         out_specs=[hbm] * 2,
         out_shape=[S((rows // 2, 128), BF)] * 2,
         scratch_shapes=[pltpu.VMEM((rows, 128), BF), pltpu.VMEM((2 * n, FF if part == 0 else W), BF), pltpu.VMEM((2 * n, mine.shape[1]), BF),
-                        pltpu.VMEM((WD, 2 * n), BF), pltpu.VMEM((16, W), F32), pltpu.SemaphoreType.DMA],
+                        pltpu.VMEM((WD, 2 * n), BF), pltpu.VMEM((16, W), F32), pltpu.VMEM((third, 128), BF), pltpu.VMEM((third, 128), BF),
+                        pltpu.SemaphoreType.DMA, pltpu.SemaphoreType.DMA((2,))],
         compiler_params=pltpu.CompilerParams(vmem_limit_bytes=VMEM),
         cost_estimate=pl.CostEstimate(flops=600_000_000, bytes_accessed=8_000_000, transcendentals=0),
         name=("gradient_down", "gradient_up", "gradient_qkv_out_proj")[part],
-    )(idx, acts, came, mine, dcame)
-
-
-def unpack_kernel(idx_ref, own0, own1, own2, came0, came1, came2, dec_mine, dec_came, tok_mine, tok_came, vec_ref, qkv_ref, out_ref, up_ref, bias_ref, down_ref, proj_ref, sq_ref, dec_ref, tok_ref,
-                  flat0, flat1, flat2, sem, *, W, FF, WD):
-    sec = idx_ref[0]
-    flats = (flat0, flat1, flat2)
+    )(idx, acts, came, mine, dcame, pack, pack_came)
+
+
+def unpack_kernel(idx_ref, own0, own1, own2, came0, came1, came2, *refs, W, FF, WD, WF, slots, patches):
+    down, up, qkv, out, proj, vec_ref, bias_ref, sq_ref = refs[:8]
+    dec_refs, refs = refs[8:16], refs[16:]
+    flats, stages, pack, fetch_sem, store_sem = refs[:3], refs[3:8], refs[8], refs[9], refs[10]
+    third = pack.shape[0] // 3
     for i, (own, came) in enumerate(((own0, came0), (own1, came1), (own2, came2))):
         me = idx_ref[1 + i]
         size = flats[i].shape[0] // PIECES
@@ -671,58 +659,89 @@
         def fetch(p, k, own=own, came=came, me=me, flat=flats[i], size=size, i=i):
             to = lambda q: flat.at[pl.ds(pl.multiple_of((q ^ me) * size, 16), size), :]
             src = pl.ds(pl.multiple_of(p * size, 16), size)
-            pltpu.make_async_copy(own.at[src, :], to(p), sem.at[i]).start()
-            pltpu.make_async_copy(came.at[src, :], to(p + PIECES // 2), sem.at[i]).start()
+            pltpu.make_async_copy(own.at[src, :], to(p), fetch_sem.at[i]).start()
+            pltpu.make_async_copy(came.at[src, :], to(p + PIECES // 2), fetch_sem.at[i]).start()
             return k
 
         lax.fori_loop(0, PIECES // 2, fetch, 0)
+    named = dict(zip(("down", "up", "qkv", "out", "proj"), zip((down, up, qkv, out, proj), stages)))
+    enc = jnp.zeros((8, 128), F32)
+    dec = jnp.zeros((8, 128), F32)
+    fold = lambda v: jnp.sum((v * v).reshape(-1, 8, 128), axis=0)
+    stores = []
+    for part, flat in enumerate(flats):
+        pltpu.make_async_copy(flat, flat, fetch_sem.at[part]).wait()
+        pack[part * third:part * third + third, :] = flat[flat.shape[0] - third:, :]
+        at = 0
+        for name, rows, blocks in flat_blocks(W, FF, WD)[part]:
+            ref, stage = named[name]
+            for b in range(blocks):
+                g = flat[at:at + rows, :].astype(F32)
+                c = slice(b * 128, b * 128 + 128)
+                stage[:, c] = g
+                if name == "proj":
+                    dec += fold(g)
+                else:
+                    enc += fold(g)
+                at += rows
+                if b % 3 == 2:
+                    cols = pl.ds(b * 128 - 256, 384)
+                    stores.append(pltpu.make_async_copy(stage.at[:, cols], ref.at[:, cols], store_sem.at[len(stores)]))
+                    stores[-1].start()
+    for b in range(W // 2 // 128):
+        g = flat[at:at + 8, :].astype(F32)
+        enc += g * g
+        vec_ref[:, b * 128:b * 128 + 128] = g
+        at += 8
+    g = flat[at:at + 16, :].astype(F32)[:FF // 2 // 128]
+    bias_ref[...] = g
+    enc += jnp.concatenate([jnp.sum(g * g, axis=0, keepdims=True), jnp.zeros((7, 128), F32)], axis=0)
+    dec += finish(lambda at, n: pack[at:at + n, :], *dec_refs, W=WD, FF=WF, slots=slots, patches=patches)
+    sq_ref[:8, :] = enc
+    sq_ref[8:, :] = dec
+    for s in stores:
+        s.wait()
+
+
+def unpack_call(idx, own, came, slots, patches, W, FF, WD, WF):
+    vm, hbm = pl.BlockSpec(memory_space=pltpu.VMEM), pl.BlockSpec(memory_space=pl.ANY)
+    S = lambda *shape: jax.ShapeDtypeStruct(shape, F32)
+    half = W // 2
+    wh = WD // 2
+    dec = [S(3 * wh, WD), S(wh, WD), S(WD, WF // 2), S(wh, WF), S(9, wh), S(8, WF // 2), S(slots, wh), S(patches, wh)]
+    big = [S(FF, half), S(W, FF // 2), S(W, 3 * half), S(W, half), S(WD // 2, W)]
+    return pl.pallas_call(
+        functools.partial(unpack_kernel, W=W, FF=FF, WD=WD, WF=WF, slots=slots, patches=patches),
+        in_specs=[pl.BlockSpec(memory_space=pltpu.SMEM)] + [hbm] * 6,
+        out_specs=[hbm] * 5 + [vm] * 11,
+        out_shape=big + [S(8, half), S(FF // 2 // 128, 128), S(16, 128)] + dec,
+        scratch_shapes=[pltpu.VMEM((part_rows(i, W, FF, WD, WF), 128), BF) for i in range(3)] + [pltpu.VMEM(s.shape, F32) for s in big]
+        + [pltpu.VMEM((dec_blocks(WD, WF)["all"], 128), BF)]
+        + [pltpu.SemaphoreType.DMA((3,)), pltpu.SemaphoreType.DMA((sum(s.shape[1] // 384 for s in big),))],
+        compiler_params=pltpu.CompilerParams(vmem_limit_bytes=VMEM),
+        cost_estimate=pl.CostEstimate(flops=10_000_000, bytes_accessed=23_000_000, transcendentals=0),
+        name="unpack",
+    )(idx, *own, *came)
+
+
+def pair_kernel(sec_ref, dec_mine, dec_came, tok_mine, tok_came, dec_ref, tok_ref):
+    sec = sec_ref[0]
     for ref, mine, came in ((dec_ref, dec_mine, dec_came), (tok_ref, tok_mine, tok_came)):
         ref[sec] = mine[...]
         ref[1 - sec] = came[...]
-    refs = {"qkv": qkv_ref, "out": out_ref, "up": up_ref, "down": down_ref}
-    enc = jnp.zeros((8, 128), F32)
-    dec = jnp.zeros((8, 128), F32)
-    fold = lambda v: jnp.sum((v * v).reshape(-1, 8, 128), axis=0)
-    for part, flat in enumerate(flats):
-        pltpu.make_async_copy(flat, flat, sem.at[part]).wait()
-        at = 0
-        for name, rows, blocks in flat_blocks(W, FF, WD)[part]:
-            for b in range(blocks):
-                g = flat[at:at + rows, :].astype(F32)
-                if name == "proj":
-                    dec += fold(g)
-                    proj_ref[:, b * 128:b * 128 + 128] = g
-                else:
-                    enc += fold(g)
-                    refs[name][:, b * 128:b * 128 + 128] = g
-                at += rows
-    for b in range(W // 2 // 128):
-        g = flat2[at:at + 8, :].astype(F32)
-        enc += g * g
-        vec_ref[:, b * 128:b * 128 + 128] = g
-        at += 8
-    g = flat2[at:at + 16, :].astype(F32)[:FF // 2 // 128]
-    bias_ref[...] = g
-    enc += jnp.concatenate([jnp.sum(g * g, axis=0, keepdims=True), jnp.zeros((7, 128), F32)], axis=0)
-    sq_ref[:8, :] = enc
-    sq_ref[8:, :] = dec
-
-
-def unpack_call(idx, own, came, dec_mine, dec_came, tok_mine, tok_came, W, FF, WD):
-    vm, hbm = pl.BlockSpec(memory_space=pltpu.VMEM), pl.BlockSpec(memory_space=pl.ANY)
-    S = jax.ShapeDtypeStruct
-    half = W // 2
+
+
+def pair_call(sec, *arrays):
+    vm = pl.BlockSpec(memory_space=pltpu.VMEM)
     return pl.pallas_call(
-        functools.partial(unpack_kernel, W=W, FF=FF, WD=WD),
-        in_specs=[pl.BlockSpec(memory_space=pltpu.SMEM)] + [hbm] * 6 + [vm] * 4,
-        out_specs=[vm] * 10,
-        out_shape=[S((8, half), F32), S((W, 3 * half), F32), S((W, half), F32), S((W, FF // 2), F32), S((FF // 2 // 128, 128), F32),
-                   S((FF, half), F32), S((WD // 2, W), F32), S((16, 128), F32), S((2, *dec_mine.shape), BF), S((2, *tok_mine.shape), BF)],
-        scratch_shapes=[pltpu.VMEM((flat_rows(i, W, FF, WD), 128), BF) for i in range(3)] + [pltpu.SemaphoreType.DMA((3,))],
+        pair_kernel,
+        in_specs=[pl.BlockSpec(memory_space=pltpu.SMEM)] + [vm] * 4,
+        out_specs=[vm] * 2,
+        out_shape=[jax.ShapeDtypeStruct((2, *arrays[i].shape), BF) for i in (0, 2)],
         compiler_params=pltpu.CompilerParams(vmem_limit_bytes=VMEM),
-        cost_estimate=pl.CostEstimate(flops=10_000_000, bytes_accessed=23_000_000, transcendentals=0),
-        name="unpack",
-    )(idx, *own, *came, dec_mine, dec_came, tok_mine, tok_came)
+        cost_estimate=pl.CostEstimate(flops=0, bytes_accessed=3_000_000, transcendentals=0),
+        name="both_clips",
+    )(sec, *arrays)
 
 
 SIDE = 4
@@ -754,29 +773,31 @@
     return (left.astype(jnp.float32) + right.astype(jnp.float32)).astype(jnp.bfloat16)
 
 
-def piece_numbers():
-    place = coordinates(lax.axis_index("dp"))
-    near = [((p == 1) | (p == 2)).astype(jnp.int32) for p in place]
-    far = [(p >= 2).astype(jnp.int32) for p in place]
-    core = lax.axis_index("section")
-    bits = [jnp.where(core == 0, a, b) for a, b in zip(near, far)]
-    return [bits[i] * 4 + bits[(i + 1) % 3] * 2 + bits[(i + 2) % 3] for i in range(3)]
-
-
-def reduce_part(i, give, keep):
-    v = add(keep, swap(give, (i,), 0))
-    for step in (1, 2):
-        half = v.shape[0] // 2
-        v = add(v[:half], swap(v[half:], ((i + step) % 3,), 0))
-    for step in range(3):
-        v = add(v, swap(v, ((i + step) % 3,), 1))
-    return v
-
-
-def gather_part(i, v):
-    for step in (2, 1):
-        v = jnp.concatenate([v, swap(v, ((i + step) % 3,), 0)])
-    return (v, swap(v, (i,), 0))
+def piece_numbers(place, core):
+    near = [1 * ((p == 1) | (p == 2)) for p in place]
+    far = [1 * (p >= 2) for p in place]
+    first = [(1 - core) * a + core * b for a, b in zip(near, far)]
+    return [first[i] * 4 + first[(i + 1) % 3] * 2 + first[(i + 2) % 3] for i in range(3)]
+
+
+def halve(v, axis, far):
+    half = v.shape[0] // 2
+    return add(v[:half], swap(v[half:], (axis,), far))
+
+
+def sum_over_chips(pairs):
+    own, came = [], []
+    for i, (give, keep) in enumerate(pairs):
+        v = add(keep, swap(give, (i,), 0))
+        for step in (1, 2):
+            v = halve(v, (i + step) % 3, 0)
+        for step in range(3):
+            v = add(v, swap(v, ((i + step) % 3,), 1))
+        for step in (2, 1):
+            v = jnp.concatenate([v, swap(v, ((i + step) % 3,), 0)])
+        own.append(v)
+        came.append(swap(v, (i,), 0))
+    return (own, came)
 
 
 def from_partner(value):
@@ -811,7 +832,7 @@
     seen_count = visible.shape[1]
     section = lax.axis_index("section").astype(jnp.int32)
     core = section.reshape(1)
-    sizes = (enc_width, enc_hidden, dec_width)
+    sizes = (enc_width, enc_hidden, dec_width, dec_hidden)
     acts, qkv, mid, slopes, projected = enc_fwd_call(
         core, frames, seen_count, tokens, enc_vectors, enc_up_bias, enc_qkv, enc_out, enc_up, enc_down, proj_weight
     )
@@ -836,28 +857,29 @@
     dec_came = from_partner(dec_other)
     hidden_mine, hidden_other, hidden, small_sums = enc_bwd_hidden_call(core, grad_projected, slopes, proj_weight, enc_down)
     hidden_came = from_partner(hidden_other)
-    dec_local = add(dec_mine, dec_came)
-    dec_sum = lax.psum(dec_local, "dp")
-    decoded_came = from_partner(decoded_other)
-    places = jnp.stack([section, *piece_numbers()]).astype(jnp.int32)
-    places, dec_local = lax.optimization_barrier((places, dec_local))
-    parts = [weight_grad_call(i, places, acts, acts_came, hidden_mine, hidden_came, *sizes) for i in range(2)]
+    places = jnp.stack([section, *piece_numbers(coordinates(lax.axis_index("dp")), section)]).astype(jnp.int32)
     dy_mine, dy_other, token_mine, token_other = enc_bwd_call(
         core, frames, seen_count, grad_projected, tokens, enc_vectors, qkv, mid, hidden, small_sums, enc_up, enc_out, enc_qkv
     )
     dy_came = from_partner(dy_other)
+    order, dy_mine = lax.optimization_barrier((places, dy_mine))
+    first = weight_grad_call(0, order, acts, acts_came, hidden_mine, hidden_came, dec_mine, dec_came, *sizes)
+    order, first = lax.optimization_barrier((places, first))
+    last = weight_grad_call(2, order, acts, acts_came, dy_mine, dy_came, dec_mine, dec_came, *sizes)
+    order, last = lax.optimization_barrier((places, last))
+    middle = weight_grad_call(1, order, acts, acts_came, hidden_mine, hidden_came, dec_mine, dec_came, *sizes)
+    own, came = sum_over_chips((first, middle, last))
+    decoded_came = from_partner(decoded_other)
     token_came = from_partner(token_other)
-    parts.append(weight_grad_call(2, places, acts, acts_came, dy_mine, dy_came, *sizes))
-    parts = [reduce_part(i, give, keep) for i, (give, keep) in enumerate(parts)]
-    own, came = zip(*(gather_part(i, v) for i, v in enumerate(parts)))
-    g_vectors, g_enc_qkv, g_enc_out, g_enc_up, g_enc_bias, g_enc_down, g_proj, squares, decoded, token_grad = unpack_call(
-        places, own, came, decoded_mine, decoded_came, token_mine, token_came, *sizes
-    )
-    g_dec_qkv, g_dec_out, g_dec_up, g_dec_down, g_dec_vectors, g_dec_bias, g_time, g_space, dec_squares = finish_call(
-        dec_sum, dec_width, dec_hidden, slot_count, patch_count
-    )
-    norms = jnp.stack([jnp.sum(squares[:8]), jnp.sum(squares[8:]) + jnp.sum(dec_squares)])
-    norms = norms + from_partner(norms)
+    decoded, token_grad = pair_call(core, decoded_mine, decoded_came, token_mine, token_came)
+    (
+        g_enc_down, g_enc_up, g_enc_qkv, g_enc_out, g_proj, g_vectors, g_enc_bias, squares,
+        g_dec_qkv, g_dec_out, g_dec_up, g_dec_down, g_dec_vectors, g_dec_bias, g_time, g_space,
+    ) = unpack_call(places, own, came, slot_count, patch_count, *sizes)
+    enc_squares, dec_squares = squares[:8], squares[8:]
+    give = jnp.where(section == 0, dec_squares, enc_squares)
+    keep = jnp.where(section == 0, enc_squares, dec_squares)
+    norms = jnp.sum(keep + from_partner(give)).reshape(1)
     return (
         decoded.transpose(0, 2, 1),
         token_grad,
@@ -876,7 +898,7 @@
         g_dec_down.T,
         g_time,
         g_space,
-        lax.dynamic_slice_in_dim(norms, section, 1, 0),
+        norms,
     )
 
 

time: 285 us -> 257 us (0.902)
  between operations: 16.1 us -> 1.47 us
  other arithmetic: 17.5 us -> 11.4 us
  waiting for transfers between devices: 78.4 us -> 73.5 us
    psum x1 -> x0, waiting for transfers between devices: 15 us -> none  [shards(): dec_sum = lax.psum(dec_local, 'dp')]
    ppermute x27, waiting for transfers between devices: 60.5 us -> 70.1 us  [swap(): return lax.ppermute(value, ('section', 'dp'), pairs)]
    convert_element_type x19 -> x18, other arithmetic: 9.31 us -> 4.92 us  [add(): (left.astype(jnp.float32) + right.astype(jnp.float32)).astype(jnp.bfloat16)]
  transfers between devices with their start and end apart: 35 -> 34, of which waited for: 14 -> 21; matrix products, arithmetic and copies ran while one was open for 6% -> 4% of each run, Pallas kernels for 11% -> 12%
where the time goes in v4:
time: 257 us; the launch traced here: 252 us
  Pallas kernels  120 us (47%)
  waiting for transfers between devices  73.5 us (29%)
  starting transfers between devices  41.9 us (16%)
  other arithmetic  11.4 us (4%)
  local copies, waits for them, and re-layouts  3.89 us (2%)
    ppermute x27, waiting for transfers between devices, swap(): return lax.ppermute(value, ('section', 'dp'), pairs)  70.1 us
    pallas_call x1, Pallas kernels, dec_block_call(): pl.pallas_call(functools.partial(dec_kernel, W=W, L=L, H=H, FF=FF, V=V, s...  63.3 us
    ppermute x27, starting transfers between devices, swap(): return lax.ppermute(value, ('section', 'dp'), pairs)  31.8 us
    pallas_call x3, Pallas kernels, weight_grad_call(): pl.pallas_call(functools.partial(weight_grad_kernel, part=part, W=W, FF=F...  15.4 us
    pallas_call x1, Pallas kernels, enc_bwd_call(): pl.pallas_call(functools.partial(enc_bwd_kernel, W=W, FF=FF, seen=seen),...  12.4 us
    pallas_call x1, Pallas kernels, enc_fwd_call(): pl.pallas_call(functools.partial(enc_fwd_kernel, W=W, FF=FF, seen=seen),...  10.2 us
    pallas_call x1, Pallas kernels, unpack_call(): pl.pallas_call(functools.partial(unpack_kernel, W=W, FF=FF, WD=WD, WF=WF,...  10.1 us
    ppermute x7, starting transfers between devices, from_partner(): return lax.ppermute(value, 'section', [(0, 1), (1, 0)])  10 us
  transfers between devices with their start and end apart: 34, of which 21 were waited for; matrix products, arithmetic and copies ran while one was open for 4% of the time, Pallas kernels for 12%

profile of v4, /device:TPU:1, one launch (start us, length us, event | category | flops | bytes accessed | tf_op | source)
XLA Modules:
  0.0 252.4 jit_solution(17960032080052022105)
XLA Ops:
  0.7 10.2 %encoder_forward.1 = (bf16[112,6144]{1,0:T(8,128)(2,1)}, bf16[112,2304]{1,0:T(8,128)(2,1)}, f32[112,768]{1,0:T(8,128)}, bf16[112,3072]{1,0:T(8,128)(2,1)}, f32[112,384]{1,0:T(8,128)}) custom-call(s32[1]{0:T(128)} %bitcast.sec_ref, s32[2]{0:T(128)} %frames_ref.5, bf16[2,112,768]{2,1,0:T(8,128)(2,1)} %tok_ref.3, bf16[8,768]{1,0:T(8,128)(2,1)} %vec_ref.3, ...), custom_call_target="tpu_custom_call" | custom-call | flops 1700000000 | bytes 18000000 | tf_op jit(solution)/shard_map/encoder_forward/pallas_call | solution.py:416
  10.9 63.3 %decoder.1 = (bf16[192,1152]{1,0:T(8,128)(2,1)}, bf16[192,1152]{1,0:T(8,128)(2,1)}, bf16[112,384]{1,0:T(8,128)(2,1)}, bf16[7680,128]{1,0:T(8,128)(2,1)}, bf16[7680,128]{1,0:T(8,128)(2,1)}) custom-call(s32[1]{0:T(128)} %bitcast.sec_ref, s32[2]{0:T(128)} %frames_ref.5, s32[2,14]{1,0:T(2,128)} %vis_ref.1, f32[112,384]{1,0:T(8,128)} %get-tuple-element.68.proj_ref, ...), custom_call_target="tpu_custom_call" | custom-call | flops 28000000000 | bytes 12000000 | tf_op jit(solution)/shard_map/decoder/pallas_call | solution.py:303
  75.8 6.6 %encoder_backward_hidden.1 = (bf16[112,1920]{1,0:T(8,128)(2,1)}, bf16[112,1920]{1,0:T(8,128)(2,1)}, bf16[112,3840]{1,0:T(8,128)(2,1)}, f32[16,768]{1,0:T(8,128)}) custom-call(s32[1]{0:T(128)} %bitcast.sec_ref, bf16[112,384]{1,0:T(8,128)(2,1)} %get-tuple-element.71.dz_ref, bf16[112,3072]{1,0:T(8,128)(2,1)} %get-tuple-element.74.gp_ref, ...), custom_call_target="tpu_custom_call" | custom-call | flops 600000000 | bytes 8000000 | tf_op jit(solution)/shard_map/encoder_backward_hidden/pallas_call | solution.py:457
  83.7 12.4 %encoder_backward.1 = (bf16[128,1920]{1,0:T(8,128)(2,1)}, bf16[128,1920]{1,0:T(8,128)(2,1)}, bf16[112,384]{1,0:T(8,128)(2,1)}, bf16[112,384]{1,0:T(8,128)(2,1)}) custom-call(s32[1]{0:T(128)} %bitcast.sec_ref, s32[2]{0:T(128)} %frames_ref.5, bf16[112,384]{1,0:T(8,128)(2,1)} %get-tuple-element.71.dz_ref, bf16[2,112,768]{2,1,0:T(8,128)(2,1)} %tok_ref.3, ...), custom_call_target="tpu_custom_call" | custom-call | flops 1600000000 | bytes 12000000 | tf_op jit(solution)/shard_map/encoder_backward/pallas_call | solution.py:538
  96.9 5.2 %gradient_down.1 = (bf16[5888,128]{1,0:T(8,128)(2,1)}, bf16[5888,128]{1,0:T(8,128)(2,1)}) custom-call(s32[4]{0:T(128)} %pad_add_fusion.idx_ref, bf16[112,6144]{1,0:T(8,128)(2,1)} %get-tuple-element.83.acts_ref, bf16[112,6144]{1,0:T(8,128)(2,1)} %collective-permute-done.2.came_ref, bf16[112,1920]{1,0:T(8,128)(2,1)} %get-tuple-element.84.mine_ref, ...), custom_call_target="tpu_custom_call" | custom-call | flops 600000000 | bytes 8000000 | tf_op jit(solution)/shard_map/gradient_down/pallas_call | solution.py:636
  102.0 2.9 %collective-permute-start.5 = (bf16[5888,128]{1,0:T(8,128)(2,1)}, bf16[5888,128]{1,0:T(8,128)(2,1)}, u32[]{:S(2)}, u32[]{:S(2)}) collective-permute-start(bf16[5888,128]{1,0:T(8,128)(2,1)} %get-tuple-element.91), channel_id=1, source_target_pairs={{0,16},{1,17},{2,18},{3,19},{4,20},{5,21},{6,22},{7,23},{8,24},{9,... | collective-permute-start | bytes 4521992 | tf_op jit(solution)/shard_map/ppermute | solution.py:769
  107.6 5.2 %gradient_qkv_out_proj.1 = (bf16[6528,128]{1,0:T(8,128)(2,1)}, bf16[6528,128]{1,0:T(8,128)(2,1)}) custom-call(s32[4]{0:T(128)} %pad_add_fusion.idx_ref, bf16[112,6144]{1,0:T(8,128)(2,1)} %get-tuple-element.83.acts_ref, bf16[112,6144]{1,0:T(8,128)(2,1)} %collective-permute-done.2.came_ref, bf16[128,1920]{1,0:T(8,128)(2,1)} %get-tuple-element.93.mine_ref, ...), custom_call_target="tpu_custom_call" | custom-call | flops 600000000 | bytes 8000000 | tf_op jit(solution)/shard_map/gradient_qkv_out_proj/pallas_call | solution.py:636
  112.8 5.1 %gradient_up.1 = (bf16[5888,128]{1,0:T(8,128)(2,1)}, bf16[5888,128]{1,0:T(8,128)(2,1)}) custom-call(s32[4]{0:T(128)} %pad_add_fusion.idx_ref, bf16[112,6144]{1,0:T(8,128)(2,1)} %get-tuple-element.83.acts_ref, bf16[112,6144]{1,0:T(8,128)(2,1)} %collective-permute-done.2.came_ref, bf16[112,1920]{1,0:T(8,128)(2,1)} %get-tuple-element.84.mine_ref, ...), custom_call_target="tpu_custom_call" | custom-call | flops 600000000 | bytes 8000000 | tf_op jit(solution)/shard_map/gradient_up/pallas_call | solution.py:636
  117.9 3.8 %collective-permute-start.14 = (bf16[5888,128]{1,0:T(8,128)(2,1)}, bf16[5888,128]{1,0:T(8,128)(2,1)S(1)}, u32[]{:S(2)}, u32[]{:S(2)}) collective-permute-start(bf16[5888,128]{1,0:T(8,128)(2,1)} %get-tuple-element.99), channel_id=1, source_target_pairs={{0,4},{1,5},{2,6},{3,7},{4,0},{5,1},{6,2},{7,3},{8,12},{9,13},{10,... | collective-permute-start | bytes 4521992 | tf_op jit(solution)/shard_map/ppermute | solution.py:769
  128.5 10.5 %collective-permute-done.14 = bf16[5888,128]{1,0:T(8,128)(2,1)S(1)} collective-permute-done((bf16[5888,128]{1,0:T(8,128)(2,1)}, bf16[5888,128]{1,0:T(8,128)(2,1)S(1)}, u32[]{:S(2)}, u32[]{:S(2)}) %collective-permute-start.14) | collective-permute-done | bytes 1507360 | tf_op jit(solution)/shard_map/ppermute | solution.py:769
  147.4 2.8 %collective-permute-start.7 = (bf16[1472,128]{1,0:T(8,128)(2,1)S(1)}, bf16[1472,128]{1,0:T(8,128)(2,1)S(1)}, u32[]{:S(2)}, u32[]{:S(2)}) collective-permute-start(bf16[1472,128]{1,0:T(8,128)(2,1)S(1)} %slice.63), channel_id=1, source_target_pairs={{0,1},{1,0},{2,3},{3,2},{4,5},{5,4},{6,7},{7,6},{8,9},{9,8},{10,11... | collective-permute-start | bytes 1130504 | tf_op jit(solution)/shard_map/ppermute | solution.py:769
  152.3 4.3 %collective-permute-done.23 = bf16[3264,128]{1,0:T(8,128)(2,1)S(1)} collective-permute-done((bf16[3264,128]{1,0:T(8,128)(2,1)S(1)}, bf16[3264,128]{1,0:T(8,128)(2,1)S(1)}, u32[]{:S(2)}, u32[]{:S(2)}) %collective-permute-start.23) | collective-permute-done | bytes 835616 | tf_op jit(solution)/shard_map/ppermute | solution.py:769
  158.4 3.4 %collective-permute-done.16 = bf16[1472,128]{1,0:T(8,128)(2,1)S(1)} collective-permute-done((bf16[1472,128]{1,0:T(8,128)(2,1)S(1)}, bf16[1472,128]{1,0:T(8,128)(2,1)S(1)}, u32[]{:S(2)}, u32[]{:S(2)}) %collective-permute-start.16) | collective-permute-done | bytes 376864 | tf_op jit(solution)/shard_map/ppermute | solution.py:769
  162.1 5.1 %collective-permute-done.24 = bf16[1632,128]{1,0:T(8,128)(2,1)S(1)} collective-permute-done((bf16[1632,128]{1,0:T(8,128)(2,1)S(1)}, bf16[1632,128]{1,0:T(8,128)(2,1)S(1)}, u32[]{:S(2)}, u32[]{:S(2)}) %collective-permute-start.24) | collective-permute-done | bytes 417824 | tf_op jit(solution)/shard_map/ppermute | solution.py:769
  169.2 5.3 %collective-permute-done.25 = bf16[1632,128]{1,0:T(8,128)(2,1)S(1)} collective-permute-done((bf16[1632,128]{1,0:T(8,128)(2,1)S(1)}, bf16[1632,128]{1,0:T(8,128)(2,1)S(1)}, u32[]{:S(2)}, u32[]{:S(2)}) %collective-permute-start.25) | collective-permute-done | bytes 417824 | tf_op jit(solution)/shard_map/ppermute | solution.py:769
  178.8 3.1 %collective-permute-done.26 = bf16[1632,128]{1,0:T(8,128)(2,1)S(1)} collective-permute-done((bf16[1632,128]{1,0:T(8,128)(2,1)S(1)}, bf16[1632,128]{1,0:T(8,128)(2,1)S(1)}, u32[]{:S(2)}, u32[]{:S(2)}) %collective-permute-start.26) | collective-permute-done | bytes 417824 | tf_op jit(solution)/shard_map/ppermute | solution.py:769
  185.3 4.0 %collective-permute-done.27 = bf16[1632,128]{1,0:T(8,128)(2,1)S(1)} collective-permute-done((bf16[1632,128]{1,0:T(8,128)(2,1)S(1)}, bf16[1632,128]{1,0:T(8,128)(2,1)S(1)}, u32[]{:S(2)}, u32[]{:S(2)}) %collective-permute-start.27) | collective-permute-done | bytes 417824 | tf_op jit(solution)/shard_map/ppermute | solution.py:769
  192.8 4.9 %collective-permute-done.28 = bf16[1632,128]{1,0:T(8,128)(2,1)S(1)} collective-permute-done((bf16[1632,128]{1,0:T(8,128)(2,1)S(1)}, bf16[1632,128]{1,0:T(8,128)(2,1)S(1)}, u32[]{:S(2)}, u32[]{:S(2)}) %collective-permute-start.28) | collective-permute-done | bytes 417824 | tf_op jit(solution)/shard_map/ppermute | solution.py:769
  200.4 5.3 %collective-permute-done.12 = bf16[2944,128]{1,0:T(8,128)(2,1)S(1)} collective-permute-done((bf16[2944,128]{1,0:T(8,128)(2,1)S(1)}, bf16[2944,128]{1,0:T(8,128)(2,1)S(1)}, u32[]{:S(2)}, u32[]{:S(2)}) %collective-permute-start.12) | collective-permute-done | bytes 753696 | tf_op jit(solution)/shard_map/ppermute | solution.py:769
  207.2 3.2 %collective-permute-done.29 = bf16[3264,128]{1,0:T(8,128)(2,1)S(1)} collective-permute-done((bf16[3264,128]{1,0:T(8,128)(2,1)S(1)}, bf16[3264,128]{1,0:T(8,128)(2,1)S(1)}, u32[]{:S(2)}, u32[]{:S(2)}) %collective-permute-start.29) | collective-permute-done | bytes 835616 | tf_op jit(solution)/shard_map/ppermute | solution.py:769
  215.9 4.6 %collective-permute-start = (bf16[192,1152]{1,0:T(8,128)(2,1)S(1)}, bf16[192,1152]{1,0:T(8,128)(2,1)S(1)}, u32[]{:S(2)}, u32[]{:S(2)}) collective-permute-start(bf16[192,1152]{1,0:T(8,128)(2,1)S(1)} %copy-done.7), channel_id=1, source_target_pairs={{0,64},{64,0},{1,65},{65,1},{2,66},{66,2},{3,67},{67,3},{4,68},{68... | collective-permute-start | bytes 1327112 | tf_op jit(solution)/shard_map/ppermute | solution.py:804
  227.0 8.4 %collective-permute-done.31.came1 = bf16[5888,128]{1,0:T(8,128)(2,1)} collective-permute-done((bf16[5888,128]{1,0:T(8,128)(2,1)}, bf16[5888,128]{1,0:T(8,128)(2,1)}, u32[]{:S(2)}, u32[]{:S(2)}) %collective-permute-start.31) | collective-permute-done | bytes 1507360 | tf_op jit(solution)/shard_map/ppermute | solution.py:769
  235.5 10.1 %unpack.1 = (f32[3072,384]{1,0:T(8,128)}, f32[768,1536]{1,0:T(8,128)}, f32[768,1152]{1,0:T(8,128)}, f32[768,384]{1,0:T(8,128)}, f32[192,768]{1,0:T(8,128)}, /*in...) custom-call(s32[4]{0:T(128)} %pad_add_fusion.idx_ref, ...), custom_call_target="tpu_custom_call" | custom-call | flops 10000000 | bytes 23000000 | tf_op jit(solution)/shard_map/unpack/pallas_call | solution.py:713
  246.3 3.1 %collective-permute-start.33 = (f32[8,128]{1,0:T(8,128)S(1)}, f32[8,128]{1,0:T(8,128)S(1)}, u32[]{:S(2)}, u32[]{:S(2)}) collective-permute-start(f32[8,128]{1,0:T(8,128)S(1)} %slice_select_fusion), channel_id=1, source_target_pairs={{0,64},{64,0},{1,65},{65,1},{2,66},{66,2},{3,67},{67,3},{4,68},{68... | collective-permute-start | bytes 12296 | tf_op jit(solution)/shard_map/ppermute | solution.py:804
  (105 shorter events, 58.0 us)
Async XLA Ops:
  74.2 21.9 %collective-permute-start.4 = (bf16[7680,128]{1,0:T(8,128)(2,1)}, bf16[7680,128]{1,0:T(8,128)(2,1)}, u32[]{:S(2)}, u32[]{:S(2)}) collective-permute-start(bf16[7680,128]{1,0:T(8,128)(2,1)} %get-tuple-element.87), channel_id=1, source_target_pairs={{0,64},{64,0},{1,65},{65,1},{2,66},{66,2},{3,67},{67,3},{4,68},{68... | collective-permute-start | bytes 5898248 | tf_op jit(solution)/shard_map/ppermute | solution.py:804
  75.7 20.4 %collective-permute-start.2 = (bf16[112,6144]{1,0:T(8,128)(2,1)}, bf16[112,6144]{1,0:T(8,128)(2,1)}, u32[]{:S(2)}, u32[]{:S(2)}) collective-permute-start(bf16[112,6144]{1,0:T(8,128)(2,1)} %get-tuple-element.83.acts_ref), channel_id=1, source_target_pairs={{0,64},{64,0},{1,65},{65,1},{2,66},{66,2},{3,67},{67,3},{4,68},{68... | collective-permute-start | bytes 4128776 | tf_op jit(solution)/shard_map/ppermute | solution.py:804
  82.4 13.7 %collective-permute-start.3 = (bf16[112,1920]{1,0:T(8,128)(2,1)}, bf16[112,1920]{1,0:T(8,128)(2,1)S(1)}, u32[]{:S(2)}, u32[]{:S(2)}) collective-permute-start(bf16[112,1920]{1,0:T(8,128)(2,1)} %get-tuple-element.85), channel_id=1, source_target_pairs={{0,64},{64,0},{1,65},{65,1},{2,66},{66,2},{3,67},{67,3},{4,68},{68... | collective-permute-start | bytes 1290248 | tf_op jit(solution)/shard_map/ppermute | solution.py:804
  102.0 22.2 %collective-permute-start.5 = (bf16[5888,128]{1,0:T(8,128)(2,1)}, bf16[5888,128]{1,0:T(8,128)(2,1)}, u32[]{:S(2)}, u32[]{:S(2)}) collective-permute-start(bf16[5888,128]{1,0:T(8,128)(2,1)} %get-tuple-element.91), channel_id=1, source_target_pairs={{0,16},{1,17},{2,18},{3,19},{4,20},{5,21},{6,22},{7,23},{8,24},{9,... | collective-permute-start | bytes 4521992 | tf_op jit(solution)/shard_map/ppermute | solution.py:769
  117.9 21.1 %collective-permute-start.14 = (bf16[5888,128]{1,0:T(8,128)(2,1)}, bf16[5888,128]{1,0:T(8,128)(2,1)S(1)}, u32[]{:S(2)}, u32[]{:S(2)}) collective-permute-start(bf16[5888,128]{1,0:T(8,128)(2,1)} %get-tuple-element.99), channel_id=1, source_target_pairs={{0,4},{1,5},{2,6},{3,7},{4,0},{5,1},{6,2},{7,3},{8,12},{9,13},{10,... | collective-permute-start | bytes 4521992 | tf_op jit(solution)/shard_map/ppermute | solution.py:769
  121.7 21.7 %collective-permute-start.22 = (bf16[6528,128]{1,0:T(8,128)(2,1)}, bf16[6528,128]{1,0:T(8,128)(2,1)S(1)}, u32[]{:S(2)}, u32[]{:S(2)}) collective-permute-start(bf16[6528,128]{1,0:T(8,128)(2,1)} %get-tuple-element.101), channel_id=1, source_target_pairs={{0,1},{1,0},{2,3},{3,2},{4,5},{5,4},{6,7},{7,6},{8,9},{9,8},{10,11... | collective-permute-start | bytes 5013512 | tf_op jit(solution)/shard_map/ppermute | solution.py:769
  126.5 20.6 %collective-permute-start.6 = (bf16[2944,128]{1,0:T(8,128)(2,1)S(1)}, bf16[2944,128]{1,0:T(8,128)(2,1)S(1)}, u32[]{:S(2)}, u32[]{:S(2)}) collective-permute-start(bf16[2944,128]{1,0:T(8,128)(2,1)S(1)} %slice.61), channel_id=1, source_target_pairs={{0,4},{1,5},{2,6},{3,7},{4,0},{5,1},{6,2},{7,3},{8,12},{9,13},{10,... | collective-permute-start | bytes 2261000 | tf_op jit(solution)/shard_map/ppermute | solution.py:769
  139.5 12.0 %collective-permute-start.15 = (bf16[2944,128]{1,0:T(8,128)(2,1)S(1)}, bf16[2944,128]{1,0:T(8,128)(2,1)S(1)}, u32[]{:S(2)}, u32[]{:S(2)}) collective-permute-start(bf16[2944,128]{1,0:T(8,128)(2,1)S(1)} %slice.65), channel_id=1, source_target_pairs={{0,1},{1,0},{2,3},{3,2},{4,5},{5,4},{6,7},{7,6},{8,9},{9,8},{10,11... | collective-permute-start | bytes 2261000 | tf_op jit(solution)/shard_map/ppermute | solution.py:769
  144.0 12.7 %collective-permute-start.23 = (bf16[3264,128]{1,0:T(8,128)(2,1)S(1)}, bf16[3264,128]{1,0:T(8,128)(2,1)S(1)}, u32[]{:S(2)}, u32[]{:S(2)}) collective-permute-start(bf16[3264,128]{1,0:T(8,128)(2,1)S(1)} %slice.69), channel_id=1, source_target_pairs={{0,16},{1,17},{2,18},{3,19},{4,20},{5,21},{6,22},{7,23},{8,24},{9,... | collective-permute-start | bytes 2506760 | tf_op jit(solution)/shard_map/ppermute | solution.py:769
  147.4 10.9 %collective-permute-start.7 = (bf16[1472,128]{1,0:T(8,128)(2,1)S(1)}, bf16[1472,128]{1,0:T(8,128)(2,1)S(1)}, u32[]{:S(2)}, u32[]{:S(2)}) collective-permute-start(bf16[1472,128]{1,0:T(8,128)(2,1)S(1)} %slice.63), channel_id=1, source_target_pairs={{0,1},{1,0},{2,3},{3,2},{4,5},{5,4},{6,7},{7,6},{8,9},{9,8},{10,11... | collective-permute-start | bytes 1130504 | tf_op jit(solution)/shard_map/ppermute | solution.py:769
  151.8 10.1 %collective-permute-start.16 = (bf16[1472,128]{1,0:T(8,128)(2,1)S(1)}, bf16[1472,128]{1,0:T(8,128)(2,1)S(1)}, u32[]{:S(2)}, u32[]{:S(2)}) collective-permute-start(bf16[1472,128]{1,0:T(8,128)(2,1)S(1)} %slice.67), channel_id=1, source_target_pairs={{0,16},{1,17},{2,18},{3,19},{4,20},{5,21},{6,22},{7,23},{8,24},{9,... | collective-permute-start | bytes 1130504 | tf_op jit(solution)/shard_map/ppermute | solution.py:769
  156.9 10.3 %collective-permute-start.24 = (bf16[1632,128]{1,0:T(8,128)(2,1)S(1)}, bf16[1632,128]{1,0:T(8,128)(2,1)S(1)}, u32[]{:S(2)}, u32[]{:S(2)}) collective-permute-start(bf16[1632,128]{1,0:T(8,128)(2,1)S(1)} %slice.71), channel_id=1, source_target_pairs={{0,4},{1,5},{2,6},{3,7},{4,0},{5,1},{6,2},{7,3},{8,12},{9,13},{10,... | collective-permute-start | bytes 1253384 | tf_op jit(solution)/shard_map/ppermute | solution.py:769
  158.4 9.0 %collective-permute-start.8 = (bf16[1472,128]{1,0:T(8,128)(2,1)S(1)}, bf16[1472,128]{1,0:T(8,128)(2,1)S(1)}, u32[]{:S(2)}, u32[]{:S(2)}) collective-permute-start(bf16[1472,128]{1,0:T(8,128)(2,1)S(1)} %add_convert_fusion.17), channel_id=1, source_target_pairs={{0,48},{1,49},{2,50},{3,51},{4,52},{5,53},{6,54},{7,55},{8,56},{9,... | collective-permute-start | bytes 1130504 | tf_op jit(solution)/shard_map/ppermute | solution.py:769
  168.9 9.7 %collective-permute-start.18 = (bf16[1472,128]{1,0:T(8,128)(2,1)S(1)}, bf16[1472,128]{1,0:T(8,128)(2,1)S(1)}, u32[]{:S(2)}, u32[]{:S(2)}) collective-permute-start(bf16[1472,128]{1,0:T(8,128)(2,1)S(1)} %add_convert_fusion.12), channel_id=1, source_target_pairs={{0,3},{1,2},{2,1},{3,0},{4,7},{5,6},{6,5},{7,4},{8,11},{9,10},{10,... | collective-permute-start | bytes 1130504 | tf_op jit(solution)/shard_map/ppermute | solution.py:769
  178.7 10.8 %collective-permute-start.19 = (bf16[1472,128]{1,0:T(8,128)(2,1)S(1)}, bf16[1472,128]{1,0:T(8,128)(2,1)S(1)}, u32[]{:S(2)}, u32[]{:S(2)}) collective-permute-start(bf16[1472,128]{1,0:T(8,128)(2,1)S(1)} %add_convert_fusion.11), channel_id=1, source_target_pairs={{0,48},{1,49},{2,50},{3,51},{4,52},{5,53},{6,54},{7,55},{8,56},{9,... | collective-permute-start | bytes 1130504 | tf_op jit(solution)/shard_map/ppermute | solution.py:769
  182.7 8.0 %collective-permute-start.11 = (bf16[1472,128]{1,0:T(8,128)(2,1)S(1)}, bf16[1472,128]{1,0:T(8,128)(2,1)S(1)}, u32[]{:S(2)}, u32[]{:S(2)}) collective-permute-start(bf16[1472,128]{1,0:T(8,128)(2,1)S(1)} %add_convert_fusion.14), channel_id=1, source_target_pairs={{0,1},{1,0},{2,3},{3,2},{4,5},{5,4},{6,7},{7,6},{8,9},{9,8},{10,11... | collective-permute-start | bytes 1130504 | tf_op jit(solution)/shard_map/ppermute | solution.py:769
  189.4 8.2 %collective-permute-start.28 = (bf16[1632,128]{1,0:T(8,128)(2,1)S(1)}, bf16[1632,128]{1,0:T(8,128)(2,1)S(1)}, u32[]{:S(2)}, u32[]{:S(2)}) collective-permute-start(bf16[1632,128]{1,0:T(8,128)(2,1)S(1)} %add_convert_fusion.6), channel_id=1, source_target_pairs={{0,4},{1,5},{2,6},{3,7},{4,0},{5,1},{6,2},{7,3},{8,12},{9,13},{10,... | collective-permute-start | bytes 1253384 | tf_op jit(solution)/shard_map/ppermute | solution.py:769
  189.6 8.3 %collective-permute-start.20 = (bf16[1472,128]{1,0:T(8,128)(2,1)S(1)}, bf16[1472,128]{1,0:T(8,128)(2,1)S(1)}, u32[]{:S(2)}, u32[]{:S(2)}) collective-permute-start(bf16[1472,128]{1,0:T(8,128)(2,1)S(1)} %add_convert_fusion.10), channel_id=1, source_target_pairs={{0,16},{1,17},{2,18},{3,19},{4,20},{5,21},{6,22},{7,23},{8,24},{9,... | collective-permute-start | bytes 1130504 | tf_op jit(solution)/shard_map/ppermute | solution.py:769
  190.8 14.9 %collective-permute-start.12 = (bf16[2944,128]{1,0:T(8,128)(2,1)S(1)}, bf16[2944,128]{1,0:T(8,128)(2,1)S(1)}, u32[]{:S(2)}, u32[]{:S(2)}) collective-permute-start(bf16[2944,128]{1,0:T(8,128)(2,1)S(1)} %pad_maximum_fusion.4), channel_id=1, source_target_pairs={{0,4},{1,5},{2,6},{3,7},{4,0},{5,1},{6,2},{7,3},{8,12},{9,13},{10,... | collective-permute-start | bytes 2261000 | tf_op jit(solution)/shard_map/ppermute | solution.py:769
  197.7 12.7 %collective-permute-start.29 = (bf16[3264,128]{1,0:T(8,128)(2,1)S(1)}, bf16[3264,128]{1,0:T(8,128)(2,1)S(1)}, u32[]{:S(2)}, u32[]{:S(2)}) collective-permute-start(bf16[3264,128]{1,0:T(8,128)(2,1)S(1)} %pad_maximum_fusion.3), channel_id=1, source_target_pairs={{0,16},{1,17},{2,18},{3,19},{4,20},{5,21},{6,22},{7,23},{8,24},{9,... | collective-permute-start | bytes 2506760 | tf_op jit(solution)/shard_map/ppermute | solution.py:769
  198.0 16.1 %collective-permute-start.21 = (bf16[2944,128]{1,0:T(8,128)(2,1)S(1)}, bf16[2944,128]{1,0:T(8,128)(2,1)S(1)}, u32[]{:S(2)}, u32[]{:S(2)}) collective-permute-start(bf16[2944,128]{1,0:T(8,128)(2,1)S(1)} %pad_maximum_fusion.5), channel_id=1, source_target_pairs={{0,1},{1,0},{2,3},{3,2},{4,5},{5,4},{6,7},{7,6},{8,9},{9,8},{10,11... | collective-permute-start | bytes 2261000 | tf_op jit(solution)/shard_map/ppermute | solution.py:769
  206.9 20.1 %collective-permute-start.30 = (bf16[5888,128]{1,0:T(8,128)(2,1)}, bf16[5888,128]{1,0:T(8,128)(2,1)}, u32[]{:S(2)}, u32[]{:S(2)}) collective-permute-start(bf16[5888,128]{1,0:T(8,128)(2,1)} %pad_maximum_fusion.1.own0), channel_id=1, source_target_pairs={{0,16},{1,17},{2,18},{3,19},{4,20},{5,21},{6,22},{7,23},{8,24},{9,... | collective-permute-start | bytes 4521992 | tf_op jit(solution)/shard_map/ppermute | solution.py:769
  211.6 23.8 %collective-permute-start.32 = (bf16[6528,128]{1,0:T(8,128)(2,1)}, bf16[6528,128]{1,0:T(8,128)(2,1)}, u32[]{:S(2)}, u32[]{:S(2)}) collective-permute-start(bf16[6528,128]{1,0:T(8,128)(2,1)} %pad_maximum_fusion.own2), channel_id=1, source_target_pairs={{0,1},{1,0},{2,3},{3,2},{4,5},{5,4},{6,7},{7,6},{8,9},{9,8},{10,11... | collective-permute-start | bytes 5013512 | tf_op jit(solution)/shard_map/ppermute | solution.py:769
  215.4 20.1 %collective-permute-start.31 = (bf16[5888,128]{1,0:T(8,128)(2,1)}, bf16[5888,128]{1,0:T(8,128)(2,1)}, u32[]{:S(2)}, u32[]{:S(2)}) collective-permute-start(bf16[5888,128]{1,0:T(8,128)(2,1)} %pad_maximum_fusion.2.own1), channel_id=1, source_target_pairs={{0,4},{1,5},{2,6},{3,7},{4,0},{5,1},{6,2},{7,3},{8,12},{9,13},{10,... | collective-permute-start | bytes 4521992 | tf_op jit(solution)/shard_map/ppermute | solution.py:769
  (19 other events, 98.8 us)

commit v5 on v4

--- a/solution.py
+++ b/solution.py
@@ -367,8 +367,14 @@
                    wqkv_ref, wo_ref, w1_ref, w2_ref, wp_ref, sem, *, W, FF, seen):
     pairs = ((wqkv_any, wqkv_ref), (wo_any, wo_ref), (w1_any, w1_ref), (w2_any, w2_ref), (wp_any, wp_ref))
     copies = [pltpu.make_async_copy(a, b, sem.at[i]) for i, (a, b) in enumerate(pairs)]
-    for c in copies:
+    for c in copies[:2]:
         c.start()
+
+    def arrived(i):
+        copies[i].wait()
+        if i + 2 < len(copies):
+            copies[i + 2].start()
+
     sec = sec_ref[0]
     valid = frames_ref[sec] // 2 * seen
     vec = vec_ref[...].astype(F32)
@@ -378,7 +384,7 @@
     xh, _ = norm_r(x)
     a1 = (xh * row(0) + row(1)).astype(BF)
     acts_ref[:, :W] = a1
-    copies[0].wait()
+    arrived(0)
     j = dot(a1, wqkv_ref[...])
     qkv_ref[:, :W] = (j[:, :W] + row(2)).astype(BF)
     qkv_ref[:, W:2 * W] = j[:, W:2 * W].astype(BF)
@@ -389,22 +395,22 @@
         p = enc_probs(two_heads(q), qkv_ref[:, W + h * 128:W + h * 128 + 128], valid).astype(BF)
         v = two_heads(qkv_ref[:, 2 * W + h * 128:2 * W + h * 128 + 128])
         acts_ref[:, W + h * 128:W + h * 128 + 128] = (dot(p[:n], v[:n]) + dot(p[n:], v[n:])).astype(BF)
-    copies[1].wait()
+    arrived(1)
     mid = x + (dot(acts_ref[:, W:2 * W], wo_ref[...]) + row(4))
     mid_ref[...] = mid
     xh, _ = norm_r(mid)
     a2 = (xh * row(5) + row(6)).astype(BF)
     acts_ref[:, 2 * W:3 * W] = a2
-    copies[2].wait()
+    arrived(2)
     for f in range(0, FF, W):
         g, gp = gelu_pair(dot(a2, w1_ref[:, f:f + W]) + b1_ref[f:f + W].astype(F32).reshape(1, W))
         acts_ref[:, 3 * W + f:3 * W + f + W] = g.astype(BF)
         gp_ref[:, f:f + W] = gp.astype(BF)
-    copies[3].wait()
+    arrived(3)
     y = mid + (dot(acts_ref[:, 3 * W:3 * W + FF], w2_ref[...]) + row(7))
     enc = y.astype(BF)
     acts_ref[:, 3 * W + FF:] = enc
-    copies[4].wait()
+    arrived(4)
     proj_ref[...] = dot(enc, wp_ref[...])
 
 
@@ -429,46 +435,11 @@
     return ref[:, pl.ds(pl.multiple_of(start + s * (size // 2), 128), size // 2)]
 
 
-def enc_bwd_hidden_kernel(sec_ref, dz_ref, gp_ref, wp_any, w2_any, mine_ref, other_ref, full_ref, small_ref, wp_ref, w2_ref, sem, *, W, FF):
-    copies = [pltpu.make_async_copy(a, b, sem.at[i]) for i, (a, b) in enumerate(((wp_any, wp_ref), (w2_any, w2_ref)))]
-    for c in copies:
-        c.start()
-    sec = sec_ref[0]
-    small_ref[...] = jnp.zeros_like(small_ref)
-    copies[0].wait()
-    de = dot(dz_ref[...], wp_ref[...], 1, 1).astype(BF)
-    full_ref[:, :W] = de
-    small_ref[7:8, :] = jnp.sum(de.astype(F32), axis=0, keepdims=True)
-    copies[1].wait()
-    for f in range(0, FF, W):
-        duf = gp_ref[:, f:f + W].astype(F32) * dot(de, w2_ref[f:f + W, :], 1, 1)
-        full_ref[:, W + f:2 * W + f] = duf.astype(BF)
-        small_ref[8 + f // W:9 + f // W, :] = jnp.sum(duf, axis=0, keepdims=True)
-    for ref, s in ((mine_ref, sec), (other_ref, 1 - sec)):
-        ref[:, :W // 2] = half_of(full_ref, 0, W, s)
-        ref[:, W // 2:] = half_of(full_ref, W, FF, s)
-
-
-def enc_bwd_hidden_call(idx, dz, gp, wp, w2):
-    n, FF = gp.shape
-    W = w2.shape[1]
-    vm, hbm = pl.BlockSpec(memory_space=pltpu.VMEM), pl.BlockSpec(memory_space=pl.ANY)
-    S = jax.ShapeDtypeStruct
-    return pl.pallas_call(
-        functools.partial(enc_bwd_hidden_kernel, W=W, FF=FF),
-        in_specs=[pl.BlockSpec(memory_space=pltpu.SMEM), vm, vm, hbm, hbm],
-        out_specs=[vm] * 4,
-        out_shape=[S((n, (W + FF) // 2), BF), S((n, (W + FF) // 2), BF), S((n, W + FF), BF), S((16, W), F32)],
-        scratch_shapes=[pltpu.VMEM(w.shape, BF) for w in (wp, w2)] + [pltpu.SemaphoreType.DMA((2,))],
-        compiler_params=pltpu.CompilerParams(vmem_limit_bytes=VMEM),
-        cost_estimate=pl.CostEstimate(flops=600_000_000, bytes_accessed=8_000_000, transcendentals=0),
-        name="encoder_backward_hidden",
-    )(idx, dz, gp, wp, w2)
-
-
-def enc_bwd_kernel(sec_ref, frames_ref, dz_ref, tok_ref, vec_ref, qkv_ref, mid_ref, du_ref, small_ref, w1_any, wo_any, wqkv_any,
-                   mine_ref, other_ref, tok_mine_ref, tok_other_ref, w1_ref, wo_ref, wqkv_ref, full, tokg, small, sem, *, W, FF, seen):
-    copies = [pltpu.make_async_copy(a, b, sem.at[i]) for i, (a, b) in enumerate(((w1_any, w1_ref), (wo_any, wo_ref), (wqkv_any, wqkv_ref)))]
+def enc_bwd_kernel(sec_ref, frames_ref, dz_ref, tok_ref, vec_ref, qkv_ref, mid_ref, gp_ref, wp_any, w2_any, w1_any, wo_any, wqkv_any,
+                   mine_ref, other_ref, tok_mine_ref, tok_other_ref,
+                   wp_ref, w2_ref, w1_ref, wo_ref, wqkv_ref, full, tokg, small, sem, *, W, FF, seen):
+    pairs = ((wp_any, wp_ref), (w2_any, w2_ref), (w1_any, w1_ref), (wo_any, wo_ref), (wqkv_any, wqkv_ref))
+    copies = [pltpu.make_async_copy(a, b, sem.at[i]) for i, (a, b) in enumerate(pairs)]
     for c in copies:
         c.start()
     sec = sec_ref[0]
@@ -477,21 +448,30 @@
     row = lambda i: vec[i:i + 1, :]
     rsum = lambda v: jnp.sum(v, axis=0, keepdims=True)
     n = dz_ref.shape[0]
-    small[...] = small_ref[...]
-    def_ = du_ref[:, :W].astype(F32)
+    small[...] = jnp.zeros_like(small)
+    U, B, Q = W, W + FF, 2 * W + FF
     copies[0].wait()
-    da2 = dot(du_ref[:, W:], w1_ref[...], 1, 1)
+    de = dot(dz_ref[...], wp_ref[...], 1, 1).astype(BF)
+    full[:, :W] = de
+    def_ = de.astype(F32)
+    small[7:8, :W] = rsum(def_)
+    copies[1].wait()
+    for f in range(0, FF, W):
+        duf = gp_ref[:, f:f + W].astype(F32) * dot(de, w2_ref[f:f + W, :], 1, 1)
+        full[:, U + f:U + f + W] = duf.astype(BF)
+        small[8 + f // W:9 + f // W, :W] = rsum(duf)
+    copies[2].wait()
+    da2 = dot(full[:, U:U + FF], w1_ref[...], 1, 1)
     xh, r = norm_r(mid_ref[...])
-    small[5:6, :] = rsum(da2 * xh)
-    small[6:7, :] = rsum(da2)
+    small[5:6, :W] = rsum(da2 * xh)
+    small[6:7, :W] = rsum(da2)
     dg = da2 * row(5)
     dm = def_ + r * (dg - jnp.mean(dg, axis=1, keepdims=True) - xh * jnp.mean(dg * xh, axis=1, keepdims=True))
-    small[4:5, :] = rsum(dm)
+    small[4:5, :W] = rsum(dm)
     db = dm.astype(BF)
-    full[:, :W] = db
-    copies[1].wait()
+    full[:, B:B + W] = db
+    copies[3].wait()
     do = dot(db, wo_ref[...], 1, 1).astype(BF)
-    Q = W
     for h in range(W // 128):
         c = h * 128
         q = two_heads((qkv_ref[:, c:c + 128].astype(F32) * (0.125 * LOG2E)).astype(BF))
@@ -506,46 +486,48 @@
         full[:, Q + c:Q + c + 128] = ((dot(ds[:n], k2[:n]) + dot(ds[n:], k2[n:])) * 0.125).astype(BF)
         full[:, Q + W + c:Q + W + c + 128] = (dot(ds, q, 0, 0) * LN2).astype(BF)
         full[:, Q + 2 * W + c:Q + 2 * W + c + 128] = dot(p16, do2, 0, 0).astype(BF)
-    small[2:3, :] = rsum(full[:, Q:Q + W].astype(F32))
-    small[3:4, :] = rsum(full[:, Q + 2 * W:Q + 3 * W].astype(F32))
-    copies[2].wait()
+    small[2:3, :W] = rsum(full[:, Q:Q + W].astype(F32))
+    small[3:4, :W] = rsum(full[:, Q + 2 * W:Q + 3 * W].astype(F32))
+    copies[4].wait()
     da = dot(full[:, Q:Q + 3 * W], wqkv_ref[...], 1, 1)
     xh, r = norm_r(tok_ref[sec].astype(F32))
-    small[0:1, :] = rsum(da * xh)
-    small[1:2, :] = rsum(da)
+    small[0:1, :W] = rsum(da * xh)
+    small[1:2, :W] = rsum(da)
     dg = da * row(0)
     dx = dm + r * (dg - jnp.mean(dg, axis=1, keepdims=True) - xh * jnp.mean(dg * xh, axis=1, keepdims=True))
     tokg[...] = dx.astype(BF)
     half = W // 2
     for ref, tref, s in ((mine_ref, tok_mine_ref, sec), (other_ref, tok_other_ref, 1 - sec)):
-        tref[...] = half_of(tokg, 0, W, s)
-        ref[:n, :half] = half_of(full, 0, W, s)
-        ref[:n, half:4 * half] = half_of(full, Q, 3 * W, s)
-        ref[:n, 4 * half:] = dz_ref[...]
-        ref[n:, :half] = half_of(small, 0, W, s).astype(BF)
+        tref[...] = tokg[:, aligned(s * half, half)]
+        at = 0
+        for start, size in ((0, half), (U, FF // 2), (B, half), (Q, 3 * half)):
+            ref[:n, at:at + size] = full[:, pl.ds(pl.multiple_of(start + s * size, 128), size)]
+            at += size
+        ref[:n, at:] = dz_ref[...]
+        ref[n:, :half] = small[:, aligned(s * half, half)].astype(BF)
         ref[n:, half:] = jnp.zeros((16, ref.shape[1] - half), BF)
         for t in range(FF // 2 // W):
             b = jnp.where(s == 0, small[8 + t:9 + t, :], small[8 + FF // 2 // W + t:9 + FF // 2 // W + t, :])
             ref[n + 8 + t:n + 9 + t, :W] = b.astype(BF)
 
 
-def enc_bwd_call(sec, frames, seen, dz, tokens, vec, qkv, mid, du, small, w1, wo, wqkv):
+def enc_bwd_call(sec, frames, seen, dz, tokens, vec, qkv, mid, gp, wp, w2, w1, wo, wqkv):
     n, W = tokens.shape[1], tokens.shape[2]
     FF = w1.shape[1]
     vm, hbm = pl.BlockSpec(memory_space=pltpu.VMEM), pl.BlockSpec(memory_space=pl.ANY)
     S = jax.ShapeDtypeStruct
-    width = 2 * W + dz.shape[1]
+    width = (5 * W + FF) // 2 + wp.shape[1]
     return pl.pallas_call(
         functools.partial(enc_bwd_kernel, W=W, FF=FF, seen=seen),
-        in_specs=[pl.BlockSpec(memory_space=pltpu.SMEM)] * 2 + [vm] * 7 + [hbm] * 3,
+        in_specs=[pl.BlockSpec(memory_space=pltpu.SMEM)] * 2 + [vm] * 6 + [hbm] * 5,
         out_specs=[vm] * 4,
         out_shape=[S((n + 16, width), BF), S((n + 16, width), BF), S((n, W // 2), BF), S((n, W // 2), BF)],
-        scratch_shapes=[pltpu.VMEM(w.shape, BF) for w in (w1, wo, wqkv)]
-        + [pltpu.VMEM((n, 4 * W), BF), pltpu.VMEM((n, W), BF), pltpu.VMEM((16, W), F32), pltpu.SemaphoreType.DMA((3,))],
+        scratch_shapes=[pltpu.VMEM(w.shape, BF) for w in (wp, w2, w1, wo, wqkv)]
+        + [pltpu.VMEM((n, 5 * W + FF), BF), pltpu.VMEM((n, W), BF), pltpu.VMEM((16, W), F32), pltpu.SemaphoreType.DMA((5,))],
         compiler_params=pltpu.CompilerParams(vmem_limit_bytes=VMEM),
-        cost_estimate=pl.CostEstimate(flops=1_600_000_000, bytes_accessed=12_000_000, transcendentals=1_000_000),
+        cost_estimate=pl.CostEstimate(flops=2_000_000_000, bytes_accessed=18_000_000, transcendentals=1_000_000),
         name="encoder_backward",
-    )(sec, frames, dz, tokens, vec, qkv, mid, du, small, w1, wo, wqkv)
+    )(sec, frames, dz, tokens, vec, qkv, mid, gp, wp, w2, w1, wo, wqkv)
 
 
 PIECES = 8
@@ -564,86 +546,111 @@
     return -(-rows // unit) * unit
 
 
+def dec_share(part, W, FF, WD, WF):
+    total = dec_blocks(WD, WF)["all"]
+    flats = [flat_rows(i, W, FF, WD) for i in range(3)]
+    counts = [((sum(flats) + total) // 3 - f) // (PIECES * 16) * (PIECES * 16) for f in flats[:2]]
+    counts.append(total - sum(counts))
+    return (sum(counts[:part]), counts[part])
+
+
 def part_rows(part, W, FF, WD, WF):
-    return flat_rows(part, W, FF, WD) + dec_blocks(WD, WF)["all"] // 3
-
-
-def weight_grad_kernel(idx_ref, acts_ref, came_ref, mine_ref, dcame_ref, pack_any, pack_came_any, give, keep, flat, acts, dy, dzt, small, pack, pack_came, sem, pack_sem, *, part, W, FF, WD):
-    n = acts_ref.shape[0]
-    third = pack.shape[0]
-    packs = [pltpu.make_async_copy(a.at[pl.ds(part * third, third), :], b, pack_sem.at[i]) for i, (a, b) in enumerate(((pack_any, pack), (pack_came_any, pack_came)))]
-    for c in packs:
-        c.start()
+    return flat_rows(part, W, FF, WD) + dec_share(part, W, FF, WD, WF)[1]
+
+
+def weight_grad_kernel(idx_ref, acts_any, came_any, mine_any, dcame_any, pack_any, pack_came_any, give0, give1, give2, keep0, keep1, keep2,
+                       flat0, flat1, flat2, acts, dy, dzt, small, pack, pack_came, out_sem, in_sem, *, W, FF, WD, WF):
+    n = acts_any.shape[0]
     half = W // 2
     lhs = {"qkv": (0, W), "out": (W, W), "up": (2 * W, W), "down": (3 * W, FF), "proj": (3 * W + FF, W)}
-    cols = {"down": (0, half), "up": (half, FF // 2), "out": (0, half), "qkv": (half, 3 * half)}
-    dy[:n, :] = mine_ref[:n, :]
-    dy[n:, :] = dcame_ref[:n, :]
-    at = 0
+    cols = {"down": (0, half), "up": (half, FF // 2), "out": (half + FF // 2, half), "qkv": (2 * half + FF // 2, 3 * half)}
+    zc = 5 * half + FF // 2
+    copies = []
+
+    def fetch(src, dst):
+        copies.append(pltpu.make_async_copy(src, dst, in_sem.at[len(copies)]))
+        copies[-1].start()
+
+    both = lambda rows, c, dst: [fetch(src.at[pl.ds(rows.start, rows.stop - rows.start), pl.ds(*c)], dst.at[pl.ds(k * (rows.stop - rows.start), rows.stop - rows.start), pl.ds(*c)])
+                                 for k, src in enumerate((mine_any, dcame_any))]
+    own = lambda c: [fetch(src.at[:, pl.ds(*c)], acts.at[pl.ds(k * n, n), pl.ds(*c)]) for k, src in enumerate((acts_any, came_any))]
+    ready = {}
+    for name, d in (("down", (0, half)), ("up", (half, FF // 2)), ("qkv", (half + FF // 2, mine_any.shape[1] - half - FF // 2))):
+        both(slice(0, n), d, dy)
+        own(lhs[name])
+        ready[name] = len(copies)
+    for name in ("out", "proj"):
+        own(lhs[name])
+        ready[name] = len(copies)
+    both(slice(n, n + 16), (0, W), small)
+    fetch(pack_any, pack)
+    fetch(pack_came_any, pack_came)
+    waited = 0
     step = 384
-    for name, rows, blocks in flat_blocks(W, FF, WD)[part]:
-        a0, an = lhs[name]
-        acts[:n, :an] = acts_ref[:, a0:a0 + an]
-        acts[n:, :an] = came_ref[:, a0:a0 + an]
-        if name == "proj":
-            dzt[...] = dy[:, 4 * half:4 * half + WD].T
-            g = dot(dzt[pl.ds(pl.multiple_of(idx_ref[0] * (WD // 2), 16), WD // 2), :], acts[:, :an]).astype(BF)
-            for b in range(blocks):
-                flat[at:at + rows, :] = g[:, b * 128:b * 128 + 128]
-                at += rows
-            continue
-        c0, cn = cols[name]
-        for r in range(0, rows, W):
-            lt = acts[:, r:r + W].T
-            for c in range(0, cn, step):
-                g = dot(lt, dy[:, c0 + c:c0 + c + step]).astype(BF)
-                for b in range(step // 128):
-                    o = at + (c // 128 + b) * rows + r
-                    flat[o:o + W, :] = g[:, b * 128:b * 128 + 128]
-        at += rows * blocks
-    if part == 2:
-        small[...] = mine_ref[n:, :W].astype(F32) + dcame_ref[n:, :W].astype(F32)
-        for b in range(half // 128):
-            flat[at:at + 8, :] = small[0:8, b * 128:b * 128 + 128].astype(BF)
-            at += 8
-        tail = flat.shape[0] - third - at
-        bias = [small[8 + t:9 + t, b * 128:b * 128 + 128] for t in range(FF // 2 // W) for b in range(W // 128)]
-        bias = jnp.concatenate(bias + [jnp.zeros((tail - len(bias), 128), F32)], axis=0)
-        flat[at:at + tail, :] = bias.astype(BF)
-    for c in packs:
-        c.wait()
-    flat[flat.shape[0] - third:, :] = (pack[...].astype(F32) + pack_came[...].astype(F32)).astype(BF)
-    size = flat.shape[0] // PIECES
-    me = idx_ref[1 + part]
-
-    def send(p, k):
-        src = lambda q: flat.at[pl.ds(pl.multiple_of((q ^ me) * size, 16), size), :]
-        to = pl.ds(pl.multiple_of(p * size, 16), size)
-        pltpu.make_async_copy(src(p), keep.at[to, :], sem).start()
-        pltpu.make_async_copy(src(p + PIECES // 2), give.at[to, :], sem).start()
-        return k
-
-    lax.fori_loop(0, PIECES // 2, send, 0)
-    pltpu.make_async_copy(flat, flat, sem).wait()
-
-
-def weight_grad_call(part, idx, acts, came, mine, dcame, pack, pack_came, W, FF, WD, WF):
+    for part, (flat, give, keep) in enumerate(((flat0, give0, keep0), (flat1, give1, keep1), (flat2, give2, keep2))):
+        at = 0
+        for name, rows, blocks in flat_blocks(W, FF, WD)[part]:
+            while waited < ready[name]:
+                copies[waited].wait()
+                waited += 1
+            a0, an = lhs[name]
+            if name == "proj":
+                dzt[...] = dy[:, zc:zc + WD].T
+                g = dot(dzt[pl.ds(pl.multiple_of(idx_ref[0] * (WD // 2), 16), WD // 2), :], acts[:, a0:a0 + an]).astype(BF)
+                for b in range(blocks):
+                    flat[at:at + rows, :] = g[:, b * 128:b * 128 + 128]
+                    at += rows
+                continue
+            d0, dn = cols[name]
+            for r in range(0, rows, W):
+                lt = acts[:, a0 + r:a0 + r + W].T
+                for c in range(0, dn, step):
+                    g = dot(lt, dy[:, d0 + c:d0 + c + step]).astype(BF)
+                    for b in range(step // 128):
+                        o = at + (c // 128 + b) * rows + r
+                        flat[o:o + W, :] = g[:, b * 128:b * 128 + 128]
+            at += rows * blocks
+        if part == 0:
+            for c in copies[waited:]:
+                c.wait()
+            waited = len(copies)
+        first, count = dec_share(part, W, FF, WD, WF)
+        if part == 2:
+            total = small[:16, :].astype(F32) + small[16:, :].astype(F32)
+            for b in range(half // 128):
+                flat[at:at + 8, :] = total[0:8, b * 128:b * 128 + 128].astype(BF)
+                at += 8
+            tail = flat.shape[0] - count - at
+            bias = [total[8 + t:9 + t, b * 128:b * 128 + 128] for t in range(FF // 2 // W) for b in range(W // 128)]
+            bias = jnp.concatenate(bias + [jnp.zeros((tail - len(bias), 128), F32)], axis=0)
+            flat[at:at + tail, :] = bias.astype(BF)
+        flat[flat.shape[0] - count:, :] = (pack[first:first + count, :].astype(F32) + pack_came[first:first + count, :].astype(F32)).astype(BF)
+        size = flat.shape[0] // PIECES
+        me = idx_ref[1 + part]
+        for p in range(PIECES // 2):
+            src = lambda q: flat.at[pl.ds(pl.multiple_of((q ^ me) * size, 16), size), :]
+            to = pl.ds(p * size, size)
+            pltpu.make_async_copy(src(p), keep.at[to, :], out_sem.at[part]).start()
+            pltpu.make_async_copy(src(p + PIECES // 2), give.at[to, :], out_sem.at[part]).start()
+    for part, flat in enumerate((flat0, flat1, flat2)):
+        pltpu.make_async_copy(flat, flat, out_sem.at[part]).wait()
+
+
+def weight_grad_call(idx, acts, came, mine, dcame, pack, pack_came, W, FF, WD, WF):
     n = acts.shape[0]
-    rows = part_rows(part, W, FF, WD, WF)
-    third = pack.shape[0] // 3
-    vm, hbm = pl.BlockSpec(memory_space=pltpu.VMEM), pl.BlockSpec(memory_space=pl.ANY)
-    S = jax.ShapeDtypeStruct
+    rows = [part_rows(i, W, FF, WD, WF) for i in range(3)]
+    hbm = pl.BlockSpec(memory_space=pl.ANY)
     return pl.pallas_call(
-        functools.partial(weight_grad_kernel, part=part, W=W, FF=FF, WD=WD),
-        in_specs=[pl.BlockSpec(memory_space=pltpu.SMEM)] + [vm] * 4 + [hbm] * 2,
-        out_specs=[hbm] * 2,
-        out_shape=[S((rows // 2, 128), BF)] * 2,
-        scratch_shapes=[pltpu.VMEM((rows, 128), BF), pltpu.VMEM((2 * n, FF if part == 0 else W), BF), pltpu.VMEM((2 * n, mine.shape[1]), BF),
-                        pltpu.VMEM((WD, 2 * n), BF), pltpu.VMEM((16, W), F32), pltpu.VMEM((third, 128), BF), pltpu.VMEM((third, 128), BF),
-                        pltpu.SemaphoreType.DMA, pltpu.SemaphoreType.DMA((2,))],
+        functools.partial(weight_grad_kernel, W=W, FF=FF, WD=WD, WF=WF),
+        in_specs=[pl.BlockSpec(memory_space=pltpu.SMEM)] + [hbm] * 6,
+        out_specs=[hbm] * 6,
+        out_shape=[jax.ShapeDtypeStruct((r // 2, 128), BF) for r in rows] * 2,
+        scratch_shapes=[pltpu.VMEM((r, 128), BF) for r in rows] + [pltpu.VMEM((2 * n, acts.shape[1]), BF), pltpu.VMEM((2 * n, mine.shape[1]), BF),
+                        pltpu.VMEM((WD, 2 * n), BF), pltpu.VMEM((32, W), BF), pltpu.VMEM(pack.shape, BF), pltpu.VMEM(pack.shape, BF),
+                        pltpu.SemaphoreType.DMA((3,)), pltpu.SemaphoreType.DMA((24,))],
         compiler_params=pltpu.CompilerParams(vmem_limit_bytes=VMEM),
-        cost_estimate=pl.CostEstimate(flops=600_000_000, bytes_accessed=8_000_000, transcendentals=0),
-        name=("gradient_down", "gradient_up", "gradient_qkv_out_proj")[part],
+        cost_estimate=pl.CostEstimate(flops=1_700_000_000, bytes_accessed=20_000_000, transcendentals=0),
+        name="encoder_weight_gradients",
     )(idx, acts, came, mine, dcame, pack, pack_came)
 
 
@@ -651,7 +658,6 @@
     down, up, qkv, out, proj, vec_ref, bias_ref, sq_ref = refs[:8]
     dec_refs, refs = refs[8:16], refs[16:]
     flats, stages, pack, fetch_sem, store_sem = refs[:3], refs[3:8], refs[8], refs[9], refs[10]
-    third = pack.shape[0] // 3
     for i, (own, came) in enumerate(((own0, came0), (own1, came1), (own2, came2))):
         me = idx_ref[1 + i]
         size = flats[i].shape[0] // PIECES
@@ -671,7 +677,8 @@
     stores = []
     for part, flat in enumerate(flats):
         pltpu.make_async_copy(flat, flat, fetch_sem.at[part]).wait()
-        pack[part * third:part * third + third, :] = flat[flat.shape[0] - third:, :]
+        first, count = dec_share(part, W, FF, WD, WF)
+        pack[first:first + count, :] = flat[flat.shape[0] - count:, :]
         at = 0
         for name, rows, blocks in flat_blocks(W, FF, WD)[part]:
             ref, stage = named[name]
@@ -739,7 +746,7 @@
         out_specs=[vm] * 2,
         out_shape=[jax.ShapeDtypeStruct((2, *arrays[i].shape), BF) for i in (0, 2)],
         compiler_params=pltpu.CompilerParams(vmem_limit_bytes=VMEM),
-        cost_estimate=pl.CostEstimate(flops=0, bytes_accessed=3_000_000, transcendentals=0),
+        cost_estimate=pl.CostEstimate(flops=1000, bytes_accessed=1000, transcendentals=0),
         name="both_clips",
     )(sec, *arrays)
 
@@ -855,20 +862,13 @@
         TA=640,
     )
     dec_came = from_partner(dec_other)
-    hidden_mine, hidden_other, hidden, small_sums = enc_bwd_hidden_call(core, grad_projected, slopes, proj_weight, enc_down)
-    hidden_came = from_partner(hidden_other)
-    places = jnp.stack([section, *piece_numbers(coordinates(lax.axis_index("dp")), section)]).astype(jnp.int32)
     dy_mine, dy_other, token_mine, token_other = enc_bwd_call(
-        core, frames, seen_count, grad_projected, tokens, enc_vectors, qkv, mid, hidden, small_sums, enc_up, enc_out, enc_qkv
+        core, frames, seen_count, grad_projected, tokens, enc_vectors, qkv, mid, slopes, proj_weight, enc_down, enc_up, enc_out, enc_qkv
     )
     dy_came = from_partner(dy_other)
-    order, dy_mine = lax.optimization_barrier((places, dy_mine))
-    first = weight_grad_call(0, order, acts, acts_came, hidden_mine, hidden_came, dec_mine, dec_came, *sizes)
-    order, first = lax.optimization_barrier((places, first))
-    last = weight_grad_call(2, order, acts, acts_came, dy_mine, dy_came, dec_mine, dec_came, *sizes)
-    order, last = lax.optimization_barrier((places, last))
-    middle = weight_grad_call(1, order, acts, acts_came, hidden_mine, hidden_came, dec_mine, dec_came, *sizes)
-    own, came = sum_over_chips((first, middle, last))
+    places = jnp.stack([section, *piece_numbers(coordinates(lax.axis_index("dp")), section)]).astype(jnp.int32)
+    pieces = weight_grad_call(places, acts, acts_came, dy_mine, dy_came, dec_mine, dec_came, *sizes)
+    own, came = sum_over_chips(list(zip(pieces[:3], pieces[3:])))
     decoded_came = from_partner(decoded_other)
     token_came = from_partner(token_other)
     decoded, token_grad = pair_call(core, decoded_mine, decoded_came, token_mine, token_came)

time: 257 us -> 246 us (0.957)
  waiting for transfers between devices: 73.5 us -> 58.7 us
  starting transfers between devices: 41.9 us -> 56.6 us
  Pallas kernels: 120 us -> 111 us
    ppermute x27, starting transfers between devices: 31.8 us -> 47.4 us  [swap(): return lax.ppermute(value, ('section', 'dp'), pairs)]
    ppermute x27, waiting for transfers between devices: 70.1 us -> 55.7 us  [swap(): return lax.ppermute(value, ('section', 'dp'), pairs)]
    pallas_call x4 -> x1, Pallas kernels: 22 us -> 10.3 us  [weight_grad_call(): pl.pallas_call(functools.partial(weight_grad_kernel, W=W, FF=FF, WD=WD, W...]
    ppermute x7 -> x6, starting transfers between devices: 10 us -> 9.2 us  [from_partner(): return lax.ppermute(value, 'section', [(0, 1), (1, 0)])]
  transfers between devices with their start and end apart: 34 -> 33, of which waited for: 21 -> 23; matrix products, arithmetic and copies ran while one was open for 4% -> 4% of each run, Pallas kernels for 12% -> 7%
where the time goes in v5:
time: 246 us; the launch traced here: 242 us
  Pallas kernels  111 us (45%)
  waiting for transfers between devices  58.7 us (24%)
  starting transfers between devices  56.6 us (23%)
  other arithmetic  11 us (4%)
  local copies, waits for them, and re-layouts  3.32 us (1%)
    pallas_call x1, Pallas kernels, dec_block_call(): pl.pallas_call(functools.partial(dec_kernel, W=W, L=L, H=H, FF=FF, V=V, s...  63.4 us
    ppermute x27, waiting for transfers between devices, swap(): return lax.ppermute(value, ('section', 'dp'), pairs)  55.7 us
    ppermute x27, starting transfers between devices, swap(): return lax.ppermute(value, ('section', 'dp'), pairs)  47.4 us
    pallas_call x1, Pallas kernels, enc_bwd_call(): pl.pallas_call(functools.partial(enc_bwd_kernel, W=W, FF=FF, seen=seen),...  14.5 us
    pallas_call x1, Pallas kernels, enc_fwd_call(): pl.pallas_call(functools.partial(enc_fwd_kernel, W=W, FF=FF, seen=seen),...  10.3 us
    pallas_call x1, Pallas kernels, weight_grad_call(): pl.pallas_call(functools.partial(weight_grad_kernel, W=W, FF=FF, WD=WD, W...  10.3 us
    pallas_call x1, Pallas kernels, unpack_call(): pl.pallas_call(functools.partial(unpack_kernel, W=W, FF=FF, WD=WD, WF=WF,...  10.2 us
    ppermute x6, starting transfers between devices, from_partner(): return lax.ppermute(value, 'section', [(0, 1), (1, 0)])  9.2 us
  transfers between devices with their start and end apart: 33, of which 23 were waited for; matrix products, arithmetic and copies ran while one was open for 4% of the time, Pallas kernels for 7%

profile of v5, /device:TPU:1, one launch (start us, length us, event | category | flops | bytes accessed | tf_op | source)
XLA Modules:
  0.0 241.9 jit_solution(14379752934358441897)
XLA Ops:
  0.7 10.3 %encoder_forward.1 = (bf16[112,6144]{1,0:T(8,128)(2,1)}, bf16[112,2304]{1,0:T(8,128)(2,1)}, f32[112,768]{1,0:T(8,128)}, bf16[112,3072]{1,0:T(8,128)(2,1)}, f32[112,384]{1,0:T(8,128)}) custom-call(s32[1]{0:T(128)} %bitcast.sec_ref, s32[2]{0:T(128)} %frames_ref.5, bf16[2,112,768]{2,1,0:T(8,128)(2,1)} %tok_ref.3, bf16[8,768]{1,0:T(8,128)(2,1)} %vec_ref.3, ...), custom_call_target="tpu_custom_call" | custom-call | flops 1700000000 | bytes 18000000 | tf_op jit(solution)/shard_map/encoder_forward/pallas_call | solution.py:422
  11.0 63.4 %decoder.1 = (bf16[192,1152]{1,0:T(8,128)(2,1)}, bf16[192,1152]{1,0:T(8,128)(2,1)}, bf16[112,384]{1,0:T(8,128)(2,1)}, bf16[7680,128]{1,0:T(8,128)(2,1)}, bf16[7680,128]{1,0:T(8,128)(2,1)}) custom-call(s32[1]{0:T(128)} %bitcast.sec_ref, s32[2]{0:T(128)} %frames_ref.5, s32[2,14]{1,0:T(2,128)} %vis_ref.1, f32[112,384]{1,0:T(8,128)} %get-tuple-element.56.proj_ref, ...), custom_call_target="tpu_custom_call" | custom-call | flops 28000000000 | bytes 12000000 | tf_op jit(solution)/shard_map/decoder/pallas_call | solution.py:303
  76.2 14.5 %encoder_backward.1 = (bf16[128,3840]{1,0:T(8,128)(2,1)}, bf16[128,3840]{1,0:T(8,128)(2,1)}, bf16[112,384]{1,0:T(8,128)(2,1)}, bf16[112,384]{1,0:T(8,128)(2,1)}) custom-call(s32[1]{0:T(128)} %bitcast.sec_ref, s32[2]{0:T(128)} %frames_ref.5, bf16[112,384]{1,0:T(8,128)(2,1)} %get-tuple-element.59.dz_ref, bf16[2,112,768]{2,1,0:T(8,128)(2,1)} %tok_ref.3, ...), custom_call_target="tpu_custom_call" | custom-call | flops 2000000000 | bytes 18000000 | tf_op jit(solution)/shard_map/encoder_backward/pallas_call | solution.py:520
  94.5 10.3 %encoder_weight_gradients.1 = (bf16[6080,128]{1,0:T(8,128)(2,1)}, bf16[6080,128]{1,0:T(8,128)(2,1)}, bf16[6144,128]{1,0:T(8,128)(2,1)}, bf16[6080,128]{1,0:T(8,1...) custom-call(s32[4]{0:T(128)} %pad_add_fusion.idx_ref, bf16[112,6144]{1,0:T(8,128)(2,1)} %get-tuple-element.67.acts_any, ...), custom_call_target="tpu_custom_call" | custom-call | flops 1700000000 | bytes 20000000 | tf_op jit(solution)/shard_map/encoder_weight_gradients/pallas_call | solution.py:643
  104.7 2.9 %collective-permute-start.5 = (bf16[6080,128]{1,0:T(8,128)(2,1)}, bf16[6080,128]{1,0:T(8,128)(2,1)S(1)}, u32[]{:S(2)}, u32[]{:S(2)}) collective-permute-start(bf16[6080,128]{1,0:T(8,128)(2,1)} %get-tuple-element.73), channel_id=1, source_target_pairs={{0,16},{1,17},{2,18},{3,19},{4,20},{5,21},{6,22},{7,23},{8,24},{9,... | collective-permute-start | bytes 4669448 | tf_op jit(solution)/shard_map/ppermute | solution.py:776
  107.6 3.8 %collective-permute-start.13 = (bf16[6080,128]{1,0:T(8,128)(2,1)}, bf16[6080,128]{1,0:T(8,128)(2,1)S(1)}, u32[]{:S(2)}, u32[]{:S(2)}) collective-permute-start(bf16[6080,128]{1,0:T(8,128)(2,1)} %get-tuple-element.75), channel_id=1, source_target_pairs={{0,4},{1,5},{2,6},{3,7},{4,0},{5,1},{6,2},{7,3},{8,12},{9,13},{10,... | collective-permute-start | bytes 4669448 | tf_op jit(solution)/shard_map/ppermute | solution.py:776
  113.9 11.6 %collective-permute-done.5 = bf16[6080,128]{1,0:T(8,128)(2,1)S(1)} collective-permute-done((bf16[6080,128]{1,0:T(8,128)(2,1)}, bf16[6080,128]{1,0:T(8,128)(2,1)S(1)}, u32[]{:S(2)}, u32[]{:S(2)}) %collective-permute-start.5) | collective-permute-done | bytes 1556512 | tf_op jit(solution)/shard_map/ppermute | solution.py:776
  127.3 3.8 %collective-permute-start.6 = (bf16[3040,128]{1,0:T(8,128)(2,1)S(1)}, bf16[3040,128]{1,0:T(8,128)(2,1)S(1)}, u32[]{:S(2)}, u32[]{:S(2)}) collective-permute-start(bf16[3040,128]{1,0:T(8,128)(2,1)S(1)} %slice.61), channel_id=1, source_target_pairs={{0,4},{1,5},{2,6},{3,7},{4,0},{5,1},{6,2},{7,3},{8,12},{9,13},{10,... | collective-permute-start | bytes 2334728 | tf_op jit(solution)/shard_map/ppermute | solution.py:776
  131.7 2.8 %collective-permute-start.14 = (bf16[3040,128]{1,0:T(8,128)(2,1)S(1)}, bf16[3040,128]{1,0:T(8,128)(2,1)S(1)}, u32[]{:S(2)}, u32[]{:S(2)}) collective-permute-start(bf16[3040,128]{1,0:T(8,128)(2,1)S(1)} %slice.65), channel_id=1, source_target_pairs={{0,1},{1,0},{2,3},{3,2},{4,5},{5,4},{6,7},{7,6},{8,9},{9,8},{10,11... | collective-permute-start | bytes 2334728 | tf_op jit(solution)/shard_map/ppermute | solution.py:776
  134.9 2.8 %collective-permute-start.22 = (bf16[3072,128]{1,0:T(8,128)(2,1)S(1)}, bf16[3072,128]{1,0:T(8,128)(2,1)S(1)}, u32[]{:S(2)}, u32[]{:S(2)}) collective-permute-start(bf16[3072,128]{1,0:T(8,128)(2,1)S(1)} %slice.69), channel_id=1, source_target_pairs={{0,16},{1,17},{2,18},{3,19},{4,20},{5,21},{6,22},{7,23},{8,24},{9,... | collective-permute-start | bytes 2359304 | tf_op jit(solution)/shard_map/ppermute | solution.py:776
  137.7 2.8 %collective-permute-done.6 = bf16[3040,128]{1,0:T(8,128)(2,1)S(1)} collective-permute-done((bf16[3040,128]{1,0:T(8,128)(2,1)S(1)}, bf16[3040,128]{1,0:T(8,128)(2,1)S(1)}, u32[]{:S(2)}, u32[]{:S(2)}) %collective-permute-start.6) | collective-permute-done | bytes 778272 | tf_op jit(solution)/shard_map/ppermute | solution.py:776
  144.2 2.8 %collective-permute-start.15 = (bf16[1520,128]{1,0:T(8,128)(2,1)S(1)}, bf16[1520,128]{1,0:T(8,128)(2,1)S(1)}, u32[]{:S(2)}, u32[]{:S(2)}) collective-permute-start(bf16[1520,128]{1,0:T(8,128)(2,1)S(1)} %slice.67), channel_id=1, source_target_pairs={{0,16},{1,17},{2,18},{3,19},{4,20},{5,21},{6,22},{7,23},{8,24},{9,... | collective-permute-start | bytes 1167368 | tf_op jit(solution)/shard_map/ppermute | solution.py:776
  149.5 3.1 %collective-permute-done.15 = bf16[1520,128]{1,0:T(8,128)(2,1)S(1)} collective-permute-done((bf16[1520,128]{1,0:T(8,128)(2,1)S(1)}, bf16[1520,128]{1,0:T(8,128)(2,1)S(1)}, u32[]{:S(2)}, u32[]{:S(2)}) %collective-permute-start.15) | collective-permute-done | bytes 389152 | tf_op jit(solution)/shard_map/ppermute | solution.py:776
  152.8 2.8 %collective-permute-done.23 = bf16[1536,128]{1,0:T(8,128)(2,1)S(1)} collective-permute-done((bf16[1536,128]{1,0:T(8,128)(2,1)S(1)}, bf16[1536,128]{1,0:T(8,128)(2,1)S(1)}, u32[]{:S(2)}, u32[]{:S(2)}) %collective-permute-start.23) | collective-permute-done | bytes 393248 | tf_op jit(solution)/shard_map/ppermute | solution.py:776
  156.5 3.1 %collective-permute-done.16 = bf16[1520,128]{1,0:T(8,128)(2,1)S(1)} collective-permute-done((bf16[1520,128]{1,0:T(8,128)(2,1)S(1)}, bf16[1520,128]{1,0:T(8,128)(2,1)S(1)}, u32[]{:S(2)}, u32[]{:S(2)}) %collective-permute-start.16) | collective-permute-done | bytes 389152 | tf_op jit(solution)/shard_map/ppermute | solution.py:776
  159.8 2.8 %collective-permute-done.24 = bf16[1536,128]{1,0:T(8,128)(2,1)S(1)} collective-permute-done((bf16[1536,128]{1,0:T(8,128)(2,1)S(1)}, bf16[1536,128]{1,0:T(8,128)(2,1)S(1)}, u32[]{:S(2)}, u32[]{:S(2)}) %collective-permute-start.24) | collective-permute-done | bytes 393248 | tf_op jit(solution)/shard_map/ppermute | solution.py:776
  167.0 2.7 %collective-permute-done.25 = bf16[1536,128]{1,0:T(8,128)(2,1)S(1)} collective-permute-done((bf16[1536,128]{1,0:T(8,128)(2,1)S(1)}, bf16[1536,128]{1,0:T(8,128)(2,1)S(1)}, u32[]{:S(2)}, u32[]{:S(2)}) %collective-permute-start.25) | collective-permute-done | bytes 393248 | tf_op jit(solution)/shard_map/ppermute | solution.py:776
  173.5 3.3 %collective-permute-done.26 = bf16[1536,128]{1,0:T(8,128)(2,1)S(1)} collective-permute-done((bf16[1536,128]{1,0:T(8,128)(2,1)S(1)}, bf16[1536,128]{1,0:T(8,128)(2,1)S(1)}, u32[]{:S(2)}, u32[]{:S(2)}) %collective-permute-start.26) | collective-permute-done | bytes 393248 | tf_op jit(solution)/shard_map/ppermute | solution.py:776
  182.8 2.8 %collective-permute-start.19 = (bf16[1520,128]{1,0:T(8,128)(2,1)S(1)}, bf16[1520,128]{1,0:T(8,128)(2,1)S(1)}, u32[]{:S(2)}, u32[]{:S(2)}) collective-permute-start(bf16[1520,128]{1,0:T(8,128)(2,1)S(1)} %add_convert_fusion.10), channel_id=1, source_target_pairs={{0,16},{1,17},{2,18},{3,19},{4,20},{5,21},{6,22},{7,23},{8,24},{9,... | collective-permute-start | bytes 1167368 | tf_op jit(solution)/shard_map/ppermute | solution.py:776
  204.9 3.5 %collective-permute-start = (bf16[192,1152]{1,0:T(8,128)(2,1)S(1)}, bf16[192,1152]{1,0:T(8,128)(2,1)S(1)}, u32[]{:S(2)}, u32[]{:S(2)}) collective-permute-start(bf16[192,1152]{1,0:T(8,128)(2,1)S(1)} %copy-done.5), channel_id=1, source_target_pairs={{0,64},{64,0},{1,65},{65,1},{2,66},{66,2},{3,67},{67,3},{4,68},{68... | collective-permute-start | bytes 1327112 | tf_op jit(solution)/shard_map/ppermute | solution.py:811
  212.9 3.4 %collective-permute-done.29.came0 = bf16[6080,128]{1,0:T(8,128)(2,1)} collective-permute-done((bf16[6080,128]{1,0:T(8,128)(2,1)}, bf16[6080,128]{1,0:T(8,128)(2,1)}, u32[]{:S(2)}, u32[]{:S(2)}) %collective-permute-start.29) | collective-permute-done | bytes 1556512 | tf_op jit(solution)/shard_map/ppermute | solution.py:776
  216.3 8.5 %collective-permute-done.30.came1 = bf16[6080,128]{1,0:T(8,128)(2,1)} collective-permute-done((bf16[6080,128]{1,0:T(8,128)(2,1)}, bf16[6080,128]{1,0:T(8,128)(2,1)}, u32[]{:S(2)}, u32[]{:S(2)}) %collective-permute-start.30) | collective-permute-done | bytes 1556512 | tf_op jit(solution)/shard_map/ppermute | solution.py:776
  224.9 10.2 %unpack.1 = (f32[3072,384]{1,0:T(8,128)}, f32[768,1536]{1,0:T(8,128)}, f32[768,1152]{1,0:T(8,128)}, f32[768,384]{1,0:T(8,128)}, f32[192,768]{1,0:T(8,128)}, /*in...) custom-call(s32[4]{0:T(128)} %pad_add_fusion.idx_ref, ...), custom_call_target="tpu_custom_call" | custom-call | flops 10000000 | bytes 23000000 | tf_op jit(solution)/shard_map/unpack/pallas_call | solution.py:720
  235.7 3.1 %collective-permute-start.32 = (f32[8,128]{1,0:T(8,128)S(1)}, f32[8,128]{1,0:T(8,128)S(1)}, u32[]{:S(2)}, u32[]{:S(2)}) collective-permute-start(f32[8,128]{1,0:T(8,128)S(1)} %slice_select_fusion), channel_id=1, source_target_pairs={{0,64},{64,0},{1,65},{65,1},{2,66},{66,2},{3,67},{67,3},{4,68},{68... | collective-permute-start | bytes 12296 | tf_op jit(solution)/shard_map/ppermute | solution.py:811
  (96 shorter events, 59.6 us)
Async XLA Ops:
  74.4 19.2 %collective-permute-start.4 = (bf16[7680,128]{1,0:T(8,128)(2,1)}, bf16[7680,128]{1,0:T(8,128)(2,1)}, u32[]{:S(2)}, u32[]{:S(2)}) collective-permute-start(bf16[7680,128]{1,0:T(8,128)(2,1)} %get-tuple-element.71), channel_id=1, source_target_pairs={{0,64},{64,0},{1,65},{65,1},{2,66},{66,2},{3,67},{67,3},{4,68},{68... | collective-permute-start | bytes 5898248 | tf_op jit(solution)/shard_map/ppermute | solution.py:811
  75.9 17.7 %collective-permute-start.2 = (bf16[112,6144]{1,0:T(8,128)(2,1)}, bf16[112,6144]{1,0:T(8,128)(2,1)}, u32[]{:S(2)}, u32[]{:S(2)}) collective-permute-start(bf16[112,6144]{1,0:T(8,128)(2,1)} %get-tuple-element.67.acts_any), channel_id=1, source_target_pairs={{0,64},{64,0},{1,65},{65,1},{2,66},{66,2},{3,67},{67,3},{4,68},{68... | collective-permute-start | bytes 4128776 | tf_op jit(solution)/shard_map/ppermute | solution.py:811
  104.7 20.7 %collective-permute-start.5 = (bf16[6080,128]{1,0:T(8,128)(2,1)}, bf16[6080,128]{1,0:T(8,128)(2,1)S(1)}, u32[]{:S(2)}, u32[]{:S(2)}) collective-permute-start(bf16[6080,128]{1,0:T(8,128)(2,1)} %get-tuple-element.73), channel_id=1, source_target_pairs={{0,16},{1,17},{2,18},{3,19},{4,20},{5,21},{6,22},{7,23},{8,24},{9,... | collective-permute-start | bytes 4669448 | tf_op jit(solution)/shard_map/ppermute | solution.py:776
  107.6 23.6 %collective-permute-start.13 = (bf16[6080,128]{1,0:T(8,128)(2,1)}, bf16[6080,128]{1,0:T(8,128)(2,1)S(1)}, u32[]{:S(2)}, u32[]{:S(2)}) collective-permute-start(bf16[6080,128]{1,0:T(8,128)(2,1)} %get-tuple-element.75), channel_id=1, source_target_pairs={{0,4},{1,5},{2,6},{3,7},{4,0},{5,1},{6,2},{7,3},{8,12},{9,13},{10,... | collective-permute-start | bytes 4669448 | tf_op jit(solution)/shard_map/ppermute | solution.py:776
  111.4 23.1 %collective-permute-start.21 = (bf16[6144,128]{1,0:T(8,128)(2,1)}, bf16[6144,128]{1,0:T(8,128)(2,1)S(1)}, u32[]{:S(2)}, u32[]{:S(2)}) collective-permute-start(bf16[6144,128]{1,0:T(8,128)(2,1)} %get-tuple-element.77), channel_id=1, source_target_pairs={{0,1},{1,0},{2,3},{3,2},{4,5},{5,4},{6,7},{7,6},{8,9},{9,8},{10,11... | collective-permute-start | bytes 4718600 | tf_op jit(solution)/shard_map/ppermute | solution.py:776
  127.3 13.1 %collective-permute-start.6 = (bf16[3040,128]{1,0:T(8,128)(2,1)S(1)}, bf16[3040,128]{1,0:T(8,128)(2,1)S(1)}, u32[]{:S(2)}, u32[]{:S(2)}) collective-permute-start(bf16[3040,128]{1,0:T(8,128)(2,1)S(1)} %slice.61), channel_id=1, source_target_pairs={{0,4},{1,5},{2,6},{3,7},{4,0},{5,1},{6,2},{7,3},{8,12},{9,13},{10,... | collective-permute-start | bytes 2334728 | tf_op jit(solution)/shard_map/ppermute | solution.py:776
  131.7 12.3 %collective-permute-start.14 = (bf16[3040,128]{1,0:T(8,128)(2,1)S(1)}, bf16[3040,128]{1,0:T(8,128)(2,1)S(1)}, u32[]{:S(2)}, u32[]{:S(2)}) collective-permute-start(bf16[3040,128]{1,0:T(8,128)(2,1)S(1)} %slice.65), channel_id=1, source_target_pairs={{0,1},{1,0},{2,3},{3,2},{4,5},{5,4},{6,7},{7,6},{8,9},{9,8},{10,11... | collective-permute-start | bytes 2334728 | tf_op jit(solution)/shard_map/ppermute | solution.py:776
  134.9 12.1 %collective-permute-start.22 = (bf16[3072,128]{1,0:T(8,128)(2,1)S(1)}, bf16[3072,128]{1,0:T(8,128)(2,1)S(1)}, u32[]{:S(2)}, u32[]{:S(2)}) collective-permute-start(bf16[3072,128]{1,0:T(8,128)(2,1)S(1)} %slice.69), channel_id=1, source_target_pairs={{0,16},{1,17},{2,18},{3,19},{4,20},{5,21},{6,22},{7,23},{8,24},{9,... | collective-permute-start | bytes 2359304 | tf_op jit(solution)/shard_map/ppermute | solution.py:776
  140.7 8.6 %collective-permute-start.7 = (bf16[1520,128]{1,0:T(8,128)(2,1)S(1)}, bf16[1520,128]{1,0:T(8,128)(2,1)S(1)}, u32[]{:S(2)}, u32[]{:S(2)}) collective-permute-start(bf16[1520,128]{1,0:T(8,128)(2,1)S(1)} %slice.63), channel_id=1, source_target_pairs={{0,1},{1,0},{2,3},{3,2},{4,5},{5,4},{6,7},{7,6},{8,9},{9,8},{10,11... | collective-permute-start | bytes 1167368 | tf_op jit(solution)/shard_map/ppermute | solution.py:776
  144.2 8.3 %collective-permute-start.15 = (bf16[1520,128]{1,0:T(8,128)(2,1)S(1)}, bf16[1520,128]{1,0:T(8,128)(2,1)S(1)}, u32[]{:S(2)}, u32[]{:S(2)}) collective-permute-start(bf16[1520,128]{1,0:T(8,128)(2,1)S(1)} %slice.67), channel_id=1, source_target_pairs={{0,16},{1,17},{2,18},{3,19},{4,20},{5,21},{6,22},{7,23},{8,24},{9,... | collective-permute-start | bytes 1167368 | tf_op jit(solution)/shard_map/ppermute | solution.py:776
  147.3 8.2 %collective-permute-start.23 = (bf16[1536,128]{1,0:T(8,128)(2,1)S(1)}, bf16[1536,128]{1,0:T(8,128)(2,1)S(1)}, u32[]{:S(2)}, u32[]{:S(2)}) collective-permute-start(bf16[1536,128]{1,0:T(8,128)(2,1)S(1)} %slice.71), channel_id=1, source_target_pairs={{0,4},{1,5},{2,6},{3,7},{4,0},{5,1},{6,2},{7,3},{8,12},{9,13},{10,... | collective-permute-start | bytes 1179656 | tf_op jit(solution)/shard_map/ppermute | solution.py:776
  156.5 7.3 %collective-permute-start.9 = (bf16[1520,128]{1,0:T(8,128)(2,1)S(1)}, bf16[1520,128]{1,0:T(8,128)(2,1)S(1)}, u32[]{:S(2)}, u32[]{:S(2)}) collective-permute-start(bf16[1520,128]{1,0:T(8,128)(2,1)S(1)} %add_convert_fusion.16), channel_id=1, source_target_pairs={{0,12},{1,13},{2,14},{3,15},{4,8},{5,9},{6,10},{7,11},{8,4},{9,5},... | collective-permute-start | bytes 1167368 | tf_op jit(solution)/shard_map/ppermute | solution.py:776
  159.7 7.1 %collective-permute-start.17 = (bf16[1520,128]{1,0:T(8,128)(2,1)S(1)}, bf16[1520,128]{1,0:T(8,128)(2,1)S(1)}, u32[]{:S(2)}, u32[]{:S(2)}) collective-permute-start(bf16[1520,128]{1,0:T(8,128)(2,1)S(1)} %add_convert_fusion.12), channel_id=1, source_target_pairs={{0,3},{1,2},{2,1},{3,0},{4,7},{5,6},{6,5},{7,4},{8,11},{9,10},{10,... | collective-permute-start | bytes 1167368 | tf_op jit(solution)/shard_map/ppermute | solution.py:776
  163.9 7.1 %collective-permute-start.10 = (bf16[1520,128]{1,0:T(8,128)(2,1)S(1)}, bf16[1520,128]{1,0:T(8,128)(2,1)S(1)}, u32[]{:S(2)}, u32[]{:S(2)}) collective-permute-start(bf16[1520,128]{1,0:T(8,128)(2,1)S(1)} %add_convert_fusion.15), channel_id=1, source_target_pairs={{0,3},{1,2},{2,1},{3,0},{4,7},{5,6},{6,5},{7,4},{8,11},{9,10},{10,... | collective-permute-start | bytes 1167368 | tf_op jit(solution)/shard_map/ppermute | solution.py:776
  166.9 15.8 %collective-permute-start.18 = (bf16[1520,128]{1,0:T(8,128)(2,1)S(1)}, bf16[1520,128]{1,0:T(8,128)(2,1)S(1)}, u32[]{:S(2)}, u32[]{:S(2)}) collective-permute-start(bf16[1520,128]{1,0:T(8,128)(2,1)S(1)} %add_convert_fusion.11), channel_id=1, source_target_pairs={{0,48},{1,49},{2,50},{3,51},{4,52},{5,53},{6,54},{7,55},{8,56},{9,... | collective-permute-start | bytes 1167368 | tf_op jit(solution)/shard_map/ppermute | solution.py:776
  171.1 9.0 %collective-permute-start.11 = (bf16[1520,128]{1,0:T(8,128)(2,1)S(1)}, bf16[1520,128]{1,0:T(8,128)(2,1)S(1)}, u32[]{:S(2)}, u32[]{:S(2)}) collective-permute-start(bf16[1520,128]{1,0:T(8,128)(2,1)S(1)} %add_convert_fusion.14), channel_id=1, source_target_pairs={{0,1},{1,0},{2,3},{3,2},{4,5},{5,4},{6,7},{7,6},{8,9},{9,8},{10,11... | collective-permute-start | bytes 1167368 | tf_op jit(solution)/shard_map/ppermute | solution.py:776
  177.0 9.1 %collective-permute-start.27 = (bf16[1536,128]{1,0:T(8,128)(2,1)S(1)}, bf16[1536,128]{1,0:T(8,128)(2,1)S(1)}, u32[]{:S(2)}, u32[]{:S(2)}) collective-permute-start(bf16[1536,128]{1,0:T(8,128)(2,1)S(1)} %add_convert_fusion.6), channel_id=1, source_target_pairs={{0,4},{1,5},{2,6},{3,7},{4,0},{5,1},{6,2},{7,3},{8,12},{9,13},{10,... | collective-permute-start | bytes 1179656 | tf_op jit(solution)/shard_map/ppermute | solution.py:776
  180.1 14.4 %collective-permute-start.12 = (bf16[3040,128]{1,0:T(8,128)(2,1)S(1)}, bf16[3040,128]{1,0:T(8,128)(2,1)S(1)}, u32[]{:S(2)}, u32[]{:S(2)}) collective-permute-start(bf16[3040,128]{1,0:T(8,128)(2,1)S(1)} %pad_maximum_fusion.4), channel_id=1, source_target_pairs={{0,4},{1,5},{2,6},{3,7},{4,0},{5,1},{6,2},{7,3},{8,12},{9,13},{10,... | collective-permute-start | bytes 2334728 | tf_op jit(solution)/shard_map/ppermute | solution.py:776
  182.8 7.9 %collective-permute-start.19 = (bf16[1520,128]{1,0:T(8,128)(2,1)S(1)}, bf16[1520,128]{1,0:T(8,128)(2,1)S(1)}, u32[]{:S(2)}, u32[]{:S(2)}) collective-permute-start(bf16[1520,128]{1,0:T(8,128)(2,1)S(1)} %add_convert_fusion.10), channel_id=1, source_target_pairs={{0,16},{1,17},{2,18},{3,19},{4,20},{5,21},{6,22},{7,23},{8,24},{9,... | collective-permute-start | bytes 1167368 | tf_op jit(solution)/shard_map/ppermute | solution.py:776
  186.2 13.0 %collective-permute-start.28 = (bf16[3072,128]{1,0:T(8,128)(2,1)S(1)}, bf16[3072,128]{1,0:T(8,128)(2,1)S(1)}, u32[]{:S(2)}, u32[]{:S(2)}) collective-permute-start(bf16[3072,128]{1,0:T(8,128)(2,1)S(1)} %pad_maximum_fusion.3), channel_id=1, source_target_pairs={{0,16},{1,17},{2,18},{3,19},{4,20},{5,21},{6,22},{7,23},{8,24},{9,... | collective-permute-start | bytes 2359304 | tf_op jit(solution)/shard_map/ppermute | solution.py:776
  190.8 12.1 %collective-permute-start.20 = (bf16[3040,128]{1,0:T(8,128)(2,1)S(1)}, bf16[3040,128]{1,0:T(8,128)(2,1)S(1)}, u32[]{:S(2)}, u32[]{:S(2)}) collective-permute-start(bf16[3040,128]{1,0:T(8,128)(2,1)S(1)} %pad_maximum_fusion.5), channel_id=1, source_target_pairs={{0,1},{1,0},{2,3},{3,2},{4,5},{5,4},{6,7},{7,6},{8,9},{9,8},{10,11... | collective-permute-start | bytes 2334728 | tf_op jit(solution)/shard_map/ppermute | solution.py:776
  195.7 20.6 %collective-permute-start.29 = (bf16[6080,128]{1,0:T(8,128)(2,1)}, bf16[6080,128]{1,0:T(8,128)(2,1)}, u32[]{:S(2)}, u32[]{:S(2)}) collective-permute-start(bf16[6080,128]{1,0:T(8,128)(2,1)} %pad_maximum_fusion.1.own0), channel_id=1, source_target_pairs={{0,16},{1,17},{2,18},{3,19},{4,20},{5,21},{6,22},{7,23},{8,24},{9,... | collective-permute-start | bytes 4669448 | tf_op jit(solution)/shard_map/ppermute | solution.py:776
  200.5 24.4 %collective-permute-start.31 = (bf16[6144,128]{1,0:T(8,128)(2,1)}, bf16[6144,128]{1,0:T(8,128)(2,1)}, u32[]{:S(2)}, u32[]{:S(2)}) collective-permute-start(bf16[6144,128]{1,0:T(8,128)(2,1)} %pad_maximum_fusion.own2), channel_id=1, source_target_pairs={{0,1},{1,0},{2,3},{3,2},{4,5},{5,4},{6,7},{7,6},{8,9},{9,8},{10,11... | collective-permute-start | bytes 4718600 | tf_op jit(solution)/shard_map/ppermute | solution.py:776
  204.2 20.6 %collective-permute-start.30 = (bf16[6080,128]{1,0:T(8,128)(2,1)}, bf16[6080,128]{1,0:T(8,128)(2,1)}, u32[]{:S(2)}, u32[]{:S(2)}) collective-permute-start(bf16[6080,128]{1,0:T(8,128)(2,1)} %pad_maximum_fusion.2.own1), channel_id=1, source_target_pairs={{0,4},{1,5},{2,6},{3,7},{4,0},{5,1},{6,2},{7,3},{8,12},{9,13},{10,... | collective-permute-start | bytes 4669448 | tf_op jit(solution)/shard_map/ppermute | solution.py:776
  (16 other events, 70.7 us)

commit v6 on v5

--- a/solution.py
+++ b/solution.py
@@ -533,29 +533,49 @@
 PIECES = 8
 
 
-def flat_blocks(W, FF, WD):
+def part_layout(part, W, FF, WD):
     half = W // 2
-    return ((("down", FF, half // 128),), (("up", W, FF // 2 // 128),), (("qkv", W, 3 * half // 128), ("out", W, half // 128), ("proj", WD // 2, W // 128)))
-
-
-def flat_rows(part, W, FF, WD):
-    rows = sum(r * b for _, r, b in flat_blocks(W, FF, WD)[part])
+    if part == 0:
+        blocks = [("down", r, c, W) for r in range(0, FF, W) for c in range(0, half, 128)]
+    elif part == 1:
+        blocks = [("up", 0, c, W) for c in range(0, FF // 2, 128)]
+    else:
+        blocks = [("qkv", 0, c, W) for c in range(0, 3 * half, 128)] + [("out", 0, c, W) for c in range(0, half, 128)]
+    halves = [blocks[:len(blocks) // 2], blocks[len(blocks) // 2:]]
     if part == 2:
-        rows += 8 * (W // 2 // 128) + FF // 2 // 128
-    unit = PIECES * 16
-    return -(-rows // unit) * unit
+        halves[0] = halves[0] + [("proj", 0, c, WD // 2) for c in range(0, W, 128)]
+    return halves
+
+
+def half_rows(part, W, FF, WD):
+    rows = [sum(n for _, _, _, n in h) for h in part_layout(part, W, FF, WD)]
+    if part == 2:
+        rows[1] += 128
+    return rows
 
 
 def dec_share(part, W, FF, WD, WF):
     total = dec_blocks(WD, WF)["all"]
-    flats = [flat_rows(i, W, FF, WD) for i in range(3)]
+    flats = [sum(half_rows(i, W, FF, WD)) for i in range(3)]
     counts = [((sum(flats) + total) // 3 - f) // (PIECES * 16) * (PIECES * 16) for f in flats[:2]]
     counts.append(total - sum(counts))
-    return (sum(counts[:part]), counts[part])
+    size = (flats[part] + counts[part]) // 2
+    rows = half_rows(part, W, FF, WD)
+    return (sum(counts[:part]), size - rows[0], size - rows[1])
 
 
 def part_rows(part, W, FF, WD, WF):
-    return flat_rows(part, W, FF, WD) + dec_share(part, W, FF, WD, WF)[1]
+    return sum(half_rows(part, W, FF, WD)) + sum(dec_share(part, W, FF, WD, WF)[1:])
+
+
+def placed(part, W, FF, WD, WF):
+    at = {}
+    for h, blocks in enumerate(part_layout(part, W, FF, WD)):
+        row = h * part_rows(part, W, FF, WD, WF) // 2
+        for name, r, c, n in blocks:
+            at[name, r, c] = row
+            row += n
+    return at
 
 
 def weight_grad_kernel(idx_ref, acts_any, came_any, mine_any, dcame_any, pack_any, pack_came_any, give0, give1, give2, keep0, keep1, keep2,
@@ -588,8 +608,8 @@
     waited = 0
     step = 384
     for part, (flat, give, keep) in enumerate(((flat0, give0, keep0), (flat1, give1, keep1), (flat2, give2, keep2))):
-        at = 0
-        for name, rows, blocks in flat_blocks(W, FF, WD)[part]:
+        at = placed(part, W, FF, WD, WF)
+        for name in (("down",), ("up",), ("qkv", "out", "proj"))[part]:
             while waited < ready[name]:
                 copies[waited].wait()
                 waited += 1
@@ -597,34 +617,31 @@
             if name == "proj":
                 dzt[...] = dy[:, zc:zc + WD].T
                 g = dot(dzt[pl.ds(pl.multiple_of(idx_ref[0] * (WD // 2), 16), WD // 2), :], acts[:, a0:a0 + an]).astype(BF)
-                for b in range(blocks):
-                    flat[at:at + rows, :] = g[:, b * 128:b * 128 + 128]
-                    at += rows
+                for c in range(0, W, 128):
+                    flat[at[name, 0, c]:at[name, 0, c] + WD // 2, :] = g[:, c:c + 128]
                 continue
             d0, dn = cols[name]
-            for r in range(0, rows, W):
+            for r in range(0, an, W):
                 lt = acts[:, a0 + r:a0 + r + W].T
                 for c in range(0, dn, step):
                     g = dot(lt, dy[:, d0 + c:d0 + c + step]).astype(BF)
-                    for b in range(step // 128):
-                        o = at + (c // 128 + b) * rows + r
-                        flat[o:o + W, :] = g[:, b * 128:b * 128 + 128]
-            at += rows * blocks
+                    for b in range(0, step, 128):
+                        o = at[name, r, c + b]
+                        flat[o:o + W, :] = g[:, b:b + 128]
         if part == 0:
             for c in copies[waited:]:
                 c.wait()
             waited = len(copies)
-        first, count = dec_share(part, W, FF, WD, WF)
+        first, low, high = dec_share(part, W, FF, WD, WF)
+        middle = flat.shape[0] // 2
         if part == 2:
             total = small[:16, :].astype(F32) + small[16:, :].astype(F32)
-            for b in range(half // 128):
-                flat[at:at + 8, :] = total[0:8, b * 128:b * 128 + 128].astype(BF)
-                at += 8
-            tail = flat.shape[0] - count - at
-            bias = [total[8 + t:9 + t, b * 128:b * 128 + 128] for t in range(FF // 2 // W) for b in range(W // 128)]
-            bias = jnp.concatenate(bias + [jnp.zeros((tail - len(bias), 128), F32)], axis=0)
-            flat[at:at + tail, :] = bias.astype(BF)
-        flat[flat.shape[0] - count:, :] = (pack[first:first + count, :].astype(F32) + pack_came[first:first + count, :].astype(F32)).astype(BF)
+            rows = [total[0:8, c:c + 128] for c in range(0, half, 128)]
+            rows += [total[8 + t:9 + t, c:c + 128] for t in range(FF // 2 // W) for c in range(0, W, 128)]
+            used = 8 * (half // 128) + FF // 2 // 128
+            flat[flat.shape[0] - high - 128:flat.shape[0] - high, :] = jnp.concatenate(rows + [jnp.zeros((128 - used, 128), F32)], axis=0).astype(BF)
+        for row, p0, n in ((middle - low, first, low), (flat.shape[0] - high, first + low, high)):
+            flat[row:row + n, :] = (pack[p0:p0 + n, :].astype(F32) + pack_came[p0:p0 + n, :].astype(F32)).astype(BF)
         size = flat.shape[0] // PIECES
         me = idx_ref[1 + part]
         for p in range(PIECES // 2):
@@ -654,81 +671,157 @@
     )(idx, acts, came, mine, dcame, pack, pack_came)
 
 
-def unpack_kernel(idx_ref, own0, own1, own2, came0, came1, came2, *refs, W, FF, WD, WF, slots, patches):
-    down, up, qkv, out, proj, vec_ref, bias_ref, sq_ref = refs[:8]
-    dec_refs, refs = refs[8:16], refs[16:]
-    flats, stages, pack, fetch_sem, store_sem = refs[:3], refs[3:8], refs[8], refs[9], refs[10]
-    for i, (own, came) in enumerate(((own0, came0), (own1, came1), (own2, came2))):
-        me = idx_ref[1 + i]
-        size = flats[i].shape[0] // PIECES
-
-        def fetch(p, k, own=own, came=came, me=me, flat=flats[i], size=size, i=i):
-            to = lambda q: flat.at[pl.ds(pl.multiple_of((q ^ me) * size, 16), size), :]
-            src = pl.ds(pl.multiple_of(p * size, 16), size)
-            pltpu.make_async_copy(own.at[src, :], to(p), fetch_sem.at[i]).start()
-            pltpu.make_async_copy(came.at[src, :], to(p + PIECES // 2), fetch_sem.at[i]).start()
-            return k
-
-        lax.fori_loop(0, PIECES // 2, fetch, 0)
-    named = dict(zip(("down", "up", "qkv", "out", "proj"), zip((down, up, qkv, out, proj), stages)))
+def unpack_half(part, h, flat, named, stage, sem, started, sizes):
+    W, FF, WD, WF = sizes
     enc = jnp.zeros((8, 128), F32)
-    dec = jnp.zeros((8, 128), F32)
-    fold = lambda v: jnp.sum((v * v).reshape(-1, 8, 128), axis=0)
-    stores = []
-    for part, flat in enumerate(flats):
+    proj = jnp.zeros((8, 128), F32)
+    row = 0
+    for i, (name, r, c, n) in enumerate(part_layout(part, W, FF, WD)[h]):
+        g = flat[row:row + n, :].astype(F32)
+        stage[row:row + n, :] = g
+        squares = jnp.sum((g * g).reshape(-1, 8, 128), axis=0)
+        if name == "proj":
+            proj += squares
+        else:
+            enc += squares
+        copy = pltpu.make_async_copy(stage.at[pl.ds(row, n), :], named[name].at[pl.ds(r, n), pl.ds(c, 128)], sem.at[i])
+        copy.start()
+        started.append(copy)
+        row += n
+    return enc, proj
+
+
+def unpack_own_kernel(idx_ref, own0, own1, own2, down, up, qkv, out, proj, sq_ref, flat0, flat1, flat2, stage0, stage1, stage2, fetch_sem, sem, *, sizes):
+    unpack_halves(idx_ref, (own0, own1, own2), (down, up, qkv, out, proj), sq_ref, (flat0, flat1, flat2), (stage0, stage1, stage2), fetch_sem, sem, False, sizes)
+
+
+def unpack_halves(idx_ref, arrays, outs, sq_ref, flats, stages, fetch_sem, sem, other, sizes, between=None):
+    named = dict(zip(("down", "up", "qkv", "out", "proj"), outs))
+    quarter = PIECES // 2
+    for i, (array, flat) in enumerate(zip(arrays, flats)):
+        size = flat.shape[0] // quarter
+        low = idx_ref[1 + i] & (quarter - 1)
+        for p in range(quarter):
+            to = flat.at[pl.ds(pl.multiple_of((p ^ low) * size, 16), size), :]
+            pltpu.make_async_copy(array.at[pl.ds(p * size, size), :], to, fetch_sem.at[i]).start()
+    sq_ref[...] = jnp.zeros_like(sq_ref)
+    for part, (flat, stage) in enumerate(zip(flats, stages)):
         pltpu.make_async_copy(flat, flat, fetch_sem.at[part]).wait()
-        first, count = dec_share(part, W, FF, WD, WF)
-        pack[first:first + count, :] = flat[flat.shape[0] - count:, :]
-        at = 0
-        for name, rows, blocks in flat_blocks(W, FF, WD)[part]:
-            ref, stage = named[name]
-            for b in range(blocks):
-                g = flat[at:at + rows, :].astype(F32)
-                c = slice(b * 128, b * 128 + 128)
-                stage[:, c] = g
-                if name == "proj":
-                    dec += fold(g)
-                else:
-                    enc += fold(g)
-                at += rows
-                if b % 3 == 2:
-                    cols = pl.ds(b * 128 - 256, 384)
-                    stores.append(pltpu.make_async_copy(stage.at[:, cols], ref.at[:, cols], store_sem.at[len(stores)]))
-                    stores[-1].start()
-    for b in range(W // 2 // 128):
-        g = flat[at:at + 8, :].astype(F32)
-        enc += g * g
-        vec_ref[:, b * 128:b * 128 + 128] = g
-        at += 8
-    g = flat[at:at + 16, :].astype(F32)[:FF // 2 // 128]
-    bias_ref[...] = g
-    enc += jnp.concatenate([jnp.sum(g * g, axis=0, keepdims=True), jnp.zeros((7, 128), F32)], axis=0)
-    dec += finish(lambda at, n: pack[at:at + n, :], *dec_refs, W=WD, FF=WF, slots=slots, patches=patches)
-    sq_ref[:8, :] = enc
-    sq_ref[8:, :] = dec
-    for s in stores:
-        s.wait()
-
-
-def unpack_call(idx, own, came, slots, patches, W, FF, WD, WF):
+        top = idx_ref[1 + part] // quarter
+        if other:
+            top = 1 - top
+        for h in range(2):
+            @pl.when(top == h)
+            def _(part=part, h=h, flat=flat, stage=stage):
+                started = []
+                enc, proj = unpack_half(part, h, flat, named, stage, sem.at[part], started, sizes)
+                sq_ref[:8, :] = sq_ref[:8, :] + enc
+                sq_ref[8:, :] = sq_ref[8:, :] + proj
+    if between is not None:
+        between()
+    for part, stage in enumerate(stages):
+        top = idx_ref[1 + part] // quarter
+        if other:
+            top = 1 - top
+        W, FF, WD, WF = sizes
+        for h in range(2):
+            @pl.when(top == h)
+            def _(part=part, h=h, stage=stage):
+                row = 0
+                for i, (name, r, c, n) in enumerate(part_layout(part, W, FF, WD)[h]):
+                    pltpu.make_async_copy(stage.at[pl.ds(row, n), :], named[name].at[pl.ds(r, n), pl.ds(c, 128)], sem.at[part, i]).wait()
+                    row += n
+
+
+def unpack_scratch(sizes):
+    W, FF, WD, WF = sizes
+    rows = [part_rows(i, *sizes) // 2 for i in range(3)]
+    return ([pltpu.VMEM((r, 128), BF) for r in rows] + [pltpu.VMEM((max(sum(b[3] for b in h) for h in part_layout(i, W, FF, WD)), 128), F32) for i in range(3)]
+            + [pltpu.SemaphoreType.DMA((3,)), pltpu.SemaphoreType.DMA((3, 16))])
+
+
+def big_shapes(sizes):
+    W, FF, WD, WF = sizes
+    S = lambda *shape: jax.ShapeDtypeStruct(shape, F32)
+    half = W // 2
+    return [S(FF, half), S(W, FF // 2), S(W, 3 * half), S(W, half), S(WD // 2, W)]
+
+
+def unpack_own_call(idx, own, *sizes):
+    vm, hbm = pl.BlockSpec(memory_space=pltpu.VMEM), pl.BlockSpec(memory_space=pl.ANY)
+    return pl.pallas_call(
+        functools.partial(unpack_own_kernel, sizes=sizes),
+        in_specs=[pl.BlockSpec(memory_space=pltpu.SMEM)] + [hbm] * 3,
+        out_specs=[hbm] * 5 + [vm],
+        out_shape=big_shapes(sizes) + [jax.ShapeDtypeStruct((16, 128), F32)],
+        scratch_shapes=unpack_scratch(sizes),
+        compiler_params=pltpu.CompilerParams(vmem_limit_bytes=VMEM),
+        cost_estimate=pl.CostEstimate(flops=10_000_000, bytes_accessed=12_000_000, transcendentals=0),
+        name="unpack_own_half",
+    )(idx, *own)
+
+
+def unpack_kernel(idx_ref, came0, came1, came2, own0, own1, own2, sq_in, b0, b1, b2, b3, b4, down, up, qkv, out, proj, vec_ref, bias_ref, sq_ref,
+                  d0, d1, d2, d3, d4, d5, d6, d7, flat0, flat1, flat2, stage0, stage1, stage2, fetch_sem, sem, rest0, rest1, rest2, pack, rest_sem, *, sizes, slots, patches):
+    W, FF, WD, WF = sizes
+    quarter = PIECES // 2
+    rests, flats = (rest0, rest1, rest2), (flat0, flat1, flat2)
+    copies = []
+    for i, (own, rest) in enumerate(zip((own0, own1, own2), rests)):
+        size = rest.shape[0]
+        p = (quarter - 1) ^ (idx_ref[1 + i] & (quarter - 1))
+        copies.append(pltpu.make_async_copy(own.at[pl.ds(pl.multiple_of(p * size, 16), size), :], rest, rest_sem.at[i]))
+        copies[-1].start()
+
+    def between():
+        for c in copies:
+            c.wait()
+        for part, (rest, flat) in enumerate(zip(rests, flats)):
+            first, low, high = dec_share(part, *sizes)
+            top = idx_ref[1 + part] // quarter
+            for h in range(2):
+                @pl.when(top == h)
+                def _(part=part, h=h, rest=rest, flat=flat, first=first, low=low, high=high):
+                    zero, one = (rest, flat) if h == 0 else (flat, rest)
+                    pack[first:first + low, :] = zero[zero.shape[0] - low:, :]
+                    pack[first + low:first + low + high, :] = one[one.shape[0] - high:, :]
+                    if part == 2:
+                        at = one.shape[0] - high - 128
+                        enc = jnp.zeros((8, 128), F32)
+                        for b in range(W // 2 // 128):
+                            g = one[at + 8 * b:at + 8 * b + 8, :].astype(F32)
+                            enc += g * g
+                            vec_ref[:, b * 128:b * 128 + 128] = g
+                        at += 8 * (W // 2 // 128)
+                        g = one[at:at + 16, :].astype(F32)[:FF // 2 // 128]
+                        bias_ref[...] = g
+                        enc += jnp.concatenate([jnp.sum(g * g, axis=0, keepdims=True), jnp.zeros((7, 128), F32)], axis=0)
+                        sq_ref[:8, :] = sq_ref[:8, :] + enc
+        dec = finish(lambda at, n: pack[at:at + n, :], d0, d1, d2, d3, d4, d5, d6, d7, W=WD, FF=WF, slots=slots, patches=patches)
+        sq_ref[8:, :] = sq_ref[8:, :] + dec
+        sq_ref[...] = sq_ref[...] + sq_in[...]
+
+    unpack_halves(idx_ref, (came0, came1, came2), (down, up, qkv, out, proj), sq_ref, flats, (stage0, stage1, stage2), fetch_sem, sem, True, sizes, between)
+
+
+def unpack_call(idx, own, came, big, squares, slots, patches, *sizes):
+    W, FF, WD, WF = sizes
     vm, hbm = pl.BlockSpec(memory_space=pltpu.VMEM), pl.BlockSpec(memory_space=pl.ANY)
     S = lambda *shape: jax.ShapeDtypeStruct(shape, F32)
-    half = W // 2
     wh = WD // 2
     dec = [S(3 * wh, WD), S(wh, WD), S(WD, WF // 2), S(wh, WF), S(9, wh), S(8, WF // 2), S(slots, wh), S(patches, wh)]
-    big = [S(FF, half), S(W, FF // 2), S(W, 3 * half), S(W, half), S(WD // 2, W)]
     return pl.pallas_call(
-        functools.partial(unpack_kernel, W=W, FF=FF, WD=WD, WF=WF, slots=slots, patches=patches),
-        in_specs=[pl.BlockSpec(memory_space=pltpu.SMEM)] + [hbm] * 6,
+        functools.partial(unpack_kernel, sizes=sizes, slots=slots, patches=patches),
+        in_specs=[pl.BlockSpec(memory_space=pltpu.SMEM)] + [hbm] * 6 + [vm] + [hbm] * 5,
         out_specs=[hbm] * 5 + [vm] * 11,
-        out_shape=big + [S(8, half), S(FF // 2 // 128, 128), S(16, 128)] + dec,
-        scratch_shapes=[pltpu.VMEM((part_rows(i, W, FF, WD, WF), 128), BF) for i in range(3)] + [pltpu.VMEM(s.shape, F32) for s in big]
-        + [pltpu.VMEM((dec_blocks(WD, WF)["all"], 128), BF)]
-        + [pltpu.SemaphoreType.DMA((3,)), pltpu.SemaphoreType.DMA((sum(s.shape[1] // 384 for s in big),))],
+        out_shape=big_shapes(sizes) + [S(8, W // 2), S(FF // 2 // 128, 128), S(16, 128)] + dec,
+        input_output_aliases={8 + i: i for i in range(5)},
+        scratch_shapes=unpack_scratch(sizes) + [pltpu.VMEM((part_rows(i, *sizes) // PIECES, 128), BF) for i in range(3)]
+        + [pltpu.VMEM((dec_blocks(WD, WF)["all"], 128), BF), pltpu.SemaphoreType.DMA((3,))],
         compiler_params=pltpu.CompilerParams(vmem_limit_bytes=VMEM),
-        cost_estimate=pl.CostEstimate(flops=10_000_000, bytes_accessed=23_000_000, transcendentals=0),
-        name="unpack",
-    )(idx, *own, *came)
+        cost_estimate=pl.CostEstimate(flops=10_000_000, bytes_accessed=15_000_000, transcendentals=0),
+        name="unpack_other_half",
+    )(idx, *came, *own, squares, *big)
 
 
 def pair_kernel(sec_ref, dec_mine, dec_came, tok_mine, tok_came, dec_ref, tok_ref):
@@ -872,10 +965,11 @@
     decoded_came = from_partner(decoded_other)
     token_came = from_partner(token_other)
     decoded, token_grad = pair_call(core, decoded_mine, decoded_came, token_mine, token_came)
+    *big, squares = unpack_own_call(places, own, *sizes)
     (
         g_enc_down, g_enc_up, g_enc_qkv, g_enc_out, g_proj, g_vectors, g_enc_bias, squares,
         g_dec_qkv, g_dec_out, g_dec_up, g_dec_down, g_dec_vectors, g_dec_bias, g_time, g_space,
-    ) = unpack_call(places, own, came, slot_count, patch_count, *sizes)
+    ) = unpack_call(places, own, came, big, squares, slot_count, patch_count, *sizes)
     enc_squares, dec_squares = squares[:8], squares[8:]
     give = jnp.where(section == 0, dec_squares, enc_squares)
     keep = jnp.where(section == 0, enc_squares, dec_squares)

time: 246 us -> 243 us (0.988)
  waiting for transfers between devices: 58.7 us -> 53.2 us
  Pallas kernels: 111 us -> 114 us
    ppermute x27, waiting for transfers between devices: 55.7 us -> 49.9 us  [swap(): return lax.ppermute(value, ('section', 'dp'), pairs)]
    pallas_call x1 -> x2, Pallas kernels: 10.2 us -> 13.7 us  [the longest x1 7.54 us: unpack_call(): pl.pallas_call(functools.partial(unpack_kernel, sizes=sizes, slots=slots,...]
  transfers between devices with their start and end apart: 33 -> 33, of which waited for: 23 -> 22; matrix products, arithmetic and copies ran while one was open for 4% -> 4% of each run, Pallas kernels for 7% -> 10%
where the time goes in v6:
time: 243 us; the launch traced here: 239 us
  Pallas kernels  114 us (47%)
  starting transfers between devices  55.9 us (23%)
  waiting for transfers between devices  53.2 us (22%)
  other arithmetic  11 us (5%)
  local copies, waits for them, and re-layouts  3.32 us (1%)
    pallas_call x1, Pallas kernels, dec_block_call(): pl.pallas_call(functools.partial(dec_kernel, W=W, L=L, H=H, FF=FF, V=V, s...  63.4 us
    ppermute x27, waiting for transfers between devices, swap(): return lax.ppermute(value, ('section', 'dp'), pairs)  49.9 us
    ppermute x27, starting transfers between devices, swap(): return lax.ppermute(value, ('section', 'dp'), pairs)  47.4 us
    pallas_call x1, Pallas kernels, enc_bwd_call(): pl.pallas_call(functools.partial(enc_bwd_kernel, W=W, FF=FF, seen=seen),...  14.5 us
    pallas_call x1, Pallas kernels, enc_fwd_call(): pl.pallas_call(functools.partial(enc_fwd_kernel, W=W, FF=FF, seen=seen),...  10.3 us
    pallas_call x1, Pallas kernels, weight_grad_call(): pl.pallas_call(functools.partial(weight_grad_kernel, W=W, FF=FF, WD=WD, W...  10.2 us
    ppermute x6, starting transfers between devices, from_partner(): return lax.ppermute(value, 'section', [(0, 1), (1, 0)])  8.44 us
    pallas_call x1, Pallas kernels, unpack_call(): pl.pallas_call(functools.partial(unpack_kernel, sizes=sizes, slots=slots,...  7.54 us
  transfers between devices with their start and end apart: 33, of which 22 were waited for; matrix products, arithmetic and copies ran while one was open for 4% of the time, Pallas kernels for 10%

profile of v6, /device:TPU:1, one launch (start us, length us, event | category | flops | bytes accessed | tf_op | source)
XLA Modules:
  0.0 238.8 jit_solution(8565582033560495702)
XLA Ops:
  0.7 10.3 %encoder_forward.1 = (bf16[112,6144]{1,0:T(8,128)(2,1)}, bf16[112,2304]{1,0:T(8,128)(2,1)}, f32[112,768]{1,0:T(8,128)}, bf16[112,3072]{1,0:T(8,128)(2,1)}, f32[112,384]{1,0:T(8,128)}) custom-call(s32[1]{0:T(128)} %bitcast.sec_ref, s32[2]{0:T(128)} %frames_ref.5, bf16[2,112,768]{2,1,0:T(8,128)(2,1)} %tok_ref.3, bf16[8,768]{1,0:T(8,128)(2,1)} %vec_ref.3, ...), custom_call_target="tpu_custom_call" | custom-call | flops 1700000000 | bytes 18000000 | tf_op jit(solution)/shard_map/encoder_forward/pallas_call | solution.py:422
  11.0 63.4 %decoder.1 = (bf16[192,1152]{1,0:T(8,128)(2,1)}, bf16[192,1152]{1,0:T(8,128)(2,1)}, bf16[112,384]{1,0:T(8,128)(2,1)}, bf16[7680,128]{1,0:T(8,128)(2,1)}, bf16[7680,128]{1,0:T(8,128)(2,1)}) custom-call(s32[1]{0:T(128)} %bitcast.sec_ref, s32[2]{0:T(128)} %frames_ref.5, s32[2,14]{1,0:T(2,128)} %vis_ref.1, f32[112,384]{1,0:T(8,128)} %get-tuple-element.62.proj_ref, ...), custom_call_target="tpu_custom_call" | custom-call | flops 28000000000 | bytes 12000000 | tf_op jit(solution)/shard_map/decoder/pallas_call | solution.py:303
  76.2 14.5 %encoder_backward.1 = (bf16[128,3840]{1,0:T(8,128)(2,1)}, bf16[128,3840]{1,0:T(8,128)(2,1)}, bf16[112,384]{1,0:T(8,128)(2,1)}, bf16[112,384]{1,0:T(8,128)(2,1)}) custom-call(s32[1]{0:T(128)} %bitcast.sec_ref, s32[2]{0:T(128)} %frames_ref.5, bf16[112,384]{1,0:T(8,128)(2,1)} %get-tuple-element.65.dz_ref, bf16[2,112,768]{2,1,0:T(8,128)(2,1)} %tok_ref.3, ...), custom_call_target="tpu_custom_call" | custom-call | flops 2000000000 | bytes 18000000 | tf_op jit(solution)/shard_map/encoder_backward/pallas_call | solution.py:520
  94.5 10.2 %encoder_weight_gradients.1 = (bf16[6080,128]{1,0:T(8,128)(2,1)}, bf16[6080,128]{1,0:T(8,128)(2,1)}, bf16[6144,128]{1,0:T(8,128)(2,1)}, bf16[6080,128]{1,0:T(8,1...) custom-call(s32[4]{0:T(128)} %pad_add_fusion.idx_ref, bf16[112,6144]{1,0:T(8,128)(2,1)} %get-tuple-element.73.acts_any, ...), custom_call_target="tpu_custom_call" | custom-call | flops 1700000000 | bytes 20000000 | tf_op jit(solution)/shard_map/encoder_weight_gradients/pallas_call | solution.py:660
  104.7 2.9 %collective-permute-start.5 = (bf16[6080,128]{1,0:T(8,128)(2,1)}, bf16[6080,128]{1,0:T(8,128)(2,1)S(1)}, u32[]{:S(2)}, u32[]{:S(2)}) collective-permute-start(bf16[6080,128]{1,0:T(8,128)(2,1)} %get-tuple-element.79), channel_id=1, source_target_pairs={{0,16},{1,17},{2,18},{3,19},{4,20},{5,21},{6,22},{7,23},{8,24},{9,... | collective-permute-start | bytes 4669448 | tf_op jit(solution)/shard_map/ppermute | solution.py:869
  107.6 3.8 %collective-permute-start.14 = (bf16[6080,128]{1,0:T(8,128)(2,1)}, bf16[6080,128]{1,0:T(8,128)(2,1)S(1)}, u32[]{:S(2)}, u32[]{:S(2)}) collective-permute-start(bf16[6080,128]{1,0:T(8,128)(2,1)} %get-tuple-element.81), channel_id=1, source_target_pairs={{0,4},{1,5},{2,6},{3,7},{4,0},{5,1},{6,2},{7,3},{8,12},{9,13},{10,... | collective-permute-start | bytes 4669448 | tf_op jit(solution)/shard_map/ppermute | solution.py:869
  113.8 11.6 %collective-permute-done.5 = bf16[6080,128]{1,0:T(8,128)(2,1)S(1)} collective-permute-done((bf16[6080,128]{1,0:T(8,128)(2,1)}, bf16[6080,128]{1,0:T(8,128)(2,1)S(1)}, u32[]{:S(2)}, u32[]{:S(2)}) %collective-permute-start.5) | collective-permute-done | bytes 1556512 | tf_op jit(solution)/shard_map/ppermute | solution.py:869
  127.3 3.8 %collective-permute-start.6 = (bf16[3040,128]{1,0:T(8,128)(2,1)S(1)}, bf16[3040,128]{1,0:T(8,128)(2,1)S(1)}, u32[]{:S(2)}, u32[]{:S(2)}) collective-permute-start(bf16[3040,128]{1,0:T(8,128)(2,1)S(1)} %slice.61), channel_id=1, source_target_pairs={{0,4},{1,5},{2,6},{3,7},{4,0},{5,1},{6,2},{7,3},{8,12},{9,13},{10,... | collective-permute-start | bytes 2334728 | tf_op jit(solution)/shard_map/ppermute | solution.py:869
  131.6 3.0 %collective-permute-start.15 = (bf16[3040,128]{1,0:T(8,128)(2,1)S(1)}, bf16[3040,128]{1,0:T(8,128)(2,1)S(1)}, u32[]{:S(2)}, u32[]{:S(2)}) collective-permute-start(bf16[3040,128]{1,0:T(8,128)(2,1)S(1)} %slice.65), channel_id=1, source_target_pairs={{0,1},{1,0},{2,3},{3,2},{4,5},{5,4},{6,7},{7,6},{8,9},{9,8},{10,11... | collective-permute-start | bytes 2334728 | tf_op jit(solution)/shard_map/ppermute | solution.py:869
  135.1 2.8 %collective-permute-start.24 = (bf16[3072,128]{1,0:T(8,128)(2,1)S(1)}, bf16[3072,128]{1,0:T(8,128)(2,1)S(1)}, u32[]{:S(2)}, u32[]{:S(2)}) collective-permute-start(bf16[3072,128]{1,0:T(8,128)(2,1)S(1)} %slice.69), channel_id=1, source_target_pairs={{0,16},{1,17},{2,18},{3,19},{4,20},{5,21},{6,22},{7,23},{8,24},{9,... | collective-permute-start | bytes 2359304 | tf_op jit(solution)/shard_map/ppermute | solution.py:869
  137.8 2.6 %collective-permute-done.6 = bf16[3040,128]{1,0:T(8,128)(2,1)S(1)} collective-permute-done((bf16[3040,128]{1,0:T(8,128)(2,1)S(1)}, bf16[3040,128]{1,0:T(8,128)(2,1)S(1)}, u32[]{:S(2)}, u32[]{:S(2)}) %collective-permute-start.6) | collective-permute-done | bytes 778272 | tf_op jit(solution)/shard_map/ppermute | solution.py:869
  144.3 2.8 %collective-permute-start.16 = (bf16[1520,128]{1,0:T(8,128)(2,1)S(1)}, bf16[1520,128]{1,0:T(8,128)(2,1)S(1)}, u32[]{:S(2)}, u32[]{:S(2)}) collective-permute-start(bf16[1520,128]{1,0:T(8,128)(2,1)S(1)} %slice.67), channel_id=1, source_target_pairs={{0,16},{1,17},{2,18},{3,19},{4,20},{5,21},{6,22},{7,23},{8,24},{9,... | collective-permute-start | bytes 1167368 | tf_op jit(solution)/shard_map/ppermute | solution.py:869
  149.4 3.4 %collective-permute-done.16 = bf16[1520,128]{1,0:T(8,128)(2,1)S(1)} collective-permute-done((bf16[1520,128]{1,0:T(8,128)(2,1)S(1)}, bf16[1520,128]{1,0:T(8,128)(2,1)S(1)}, u32[]{:S(2)}, u32[]{:S(2)}) %collective-permute-start.16) | collective-permute-done | bytes 389152 | tf_op jit(solution)/shard_map/ppermute | solution.py:869
  153.0 2.6 %collective-permute-done.25 = bf16[1536,128]{1,0:T(8,128)(2,1)S(1)} collective-permute-done((bf16[1536,128]{1,0:T(8,128)(2,1)S(1)}, bf16[1536,128]{1,0:T(8,128)(2,1)S(1)}, u32[]{:S(2)}, u32[]{:S(2)}) %collective-permute-start.25) | collective-permute-done | bytes 393248 | tf_op jit(solution)/shard_map/ppermute | solution.py:869
  156.5 3.4 %collective-permute-done.17 = bf16[1520,128]{1,0:T(8,128)(2,1)S(1)} collective-permute-done((bf16[1520,128]{1,0:T(8,128)(2,1)S(1)}, bf16[1520,128]{1,0:T(8,128)(2,1)S(1)}, u32[]{:S(2)}, u32[]{:S(2)}) %collective-permute-start.17) | collective-permute-done | bytes 389152 | tf_op jit(solution)/shard_map/ppermute | solution.py:869
  160.1 2.7 %collective-permute-done.26 = bf16[1536,128]{1,0:T(8,128)(2,1)S(1)} collective-permute-done((bf16[1536,128]{1,0:T(8,128)(2,1)S(1)}, bf16[1536,128]{1,0:T(8,128)(2,1)S(1)}, u32[]{:S(2)}, u32[]{:S(2)}) %collective-permute-start.26) | collective-permute-done | bytes 393248 | tf_op jit(solution)/shard_map/ppermute | solution.py:869
  167.2 2.7 %collective-permute-done.27 = bf16[1536,128]{1,0:T(8,128)(2,1)S(1)} collective-permute-done((bf16[1536,128]{1,0:T(8,128)(2,1)S(1)}, bf16[1536,128]{1,0:T(8,128)(2,1)S(1)}, u32[]{:S(2)}, u32[]{:S(2)}) %collective-permute-start.27) | collective-permute-done | bytes 393248 | tf_op jit(solution)/shard_map/ppermute | solution.py:869
  173.7 3.3 %collective-permute-done.28 = bf16[1536,128]{1,0:T(8,128)(2,1)S(1)} collective-permute-done((bf16[1536,128]{1,0:T(8,128)(2,1)S(1)}, bf16[1536,128]{1,0:T(8,128)(2,1)S(1)}, u32[]{:S(2)}, u32[]{:S(2)}) %collective-permute-start.28) | collective-permute-done | bytes 393248 | tf_op jit(solution)/shard_map/ppermute | solution.py:869
  182.8 2.8 %collective-permute-start.20 = (bf16[1520,128]{1,0:T(8,128)(2,1)S(1)}, bf16[1520,128]{1,0:T(8,128)(2,1)S(1)}, u32[]{:S(2)}, u32[]{:S(2)}) collective-permute-start(bf16[1520,128]{1,0:T(8,128)(2,1)S(1)} %add_convert_fusion.10), channel_id=1, source_target_pairs={{0,16},{1,17},{2,18},{3,19},{4,20},{5,21},{6,22},{7,23},{8,24},{9,... | collective-permute-start | bytes 1167368 | tf_op jit(solution)/shard_map/ppermute | solution.py:869
  205.0 3.1 %collective-permute-start = (bf16[192,1152]{1,0:T(8,128)(2,1)S(1)}, bf16[192,1152]{1,0:T(8,128)(2,1)S(1)}, u32[]{:S(2)}, u32[]{:S(2)}) collective-permute-start(bf16[192,1152]{1,0:T(8,128)(2,1)S(1)} %copy-done.5), channel_id=1, source_target_pairs={{0,64},{64,0},{1,65},{65,1},{2,66},{66,2},{3,67},{67,3},{4,68},{68... | collective-permute-start | bytes 1327112 | tf_op jit(solution)/shard_map/ppermute | solution.py:904
  212.7 6.1 %unpack_own_half.1 = (f32[3072,384]{1,0:T(8,128)}, f32[768,1536]{1,0:T(8,128)}, f32[768,1152]{1,0:T(8,128)}, f32[768,384]{1,0:T(8,128)}, f32[192,768]{1,0:T(8,128)}, /*index=5*/f32[16,128]{1,0:T(8,128)}) custom-call(s32[4]{0:T(128)} %pad_add_fusion.idx_ref, bf16[6080,128]{1,0:T(8,128)(2,1)} %pad_maximum_fusion.1.own0, ...), custom_call_target="tpu_custom_call" | custom-call | flops 10000000 | bytes 12000000 | tf_op jit(solution)/shard_map/unpack_own_half/pallas_call | solution.py:752
  218.8 6.0 %collective-permute-done.22.came1 = bf16[6080,128]{1,0:T(8,128)(2,1)} collective-permute-done((bf16[6080,128]{1,0:T(8,128)(2,1)}, bf16[6080,128]{1,0:T(8,128)(2,1)}, u32[]{:S(2)}, u32[]{:S(2)}) %collective-permute-start.22) | collective-permute-done | bytes 1556512 | tf_op jit(solution)/shard_map/ppermute | solution.py:869
  224.8 7.5 %unpack_other_half.1 = (f32[3072,384]{1,0:T(8,128)}, f32[768,1536]{1,0:T(8,128)}, f32[768,1152]{1,0:T(8,128)}, f32[768,384]{1,0:T(8,128)}, f32[192,768]{1,0:T(8,...) custom-call(s32[4]{0:T(128)} %pad_add_fusion.idx_ref, ...), custom_call_target="tpu_custom_call", output_to_operand_aliasing={{0}: (8, {}), {1}: (9, {}), {2}: (10, {}), {3}: (11, {}), {... | custom-call | flops 10000000 | bytes 15000000 | tf_op jit(solution)/shard_map/unpack_other_half/pallas_call | solution.py:813
  233.0 2.9 %collective-permute-start.32 = (f32[8,128]{1,0:T(8,128)S(1)}, f32[8,128]{1,0:T(8,128)S(1)}, u32[]{:S(2)}, u32[]{:S(2)}) collective-permute-start(f32[8,128]{1,0:T(8,128)S(1)} %slice_select_fusion), channel_id=1, source_target_pairs={{0,64},{64,0},{1,65},{65,1},{2,66},{66,2},{3,67},{67,3},{4,68},{68... | collective-permute-start | bytes 12296 | tf_op jit(solution)/shard_map/ppermute | solution.py:904
  (97 shorter events, 59.5 us)
Async XLA Ops:
  74.4 19.2 %collective-permute-start.4 = (bf16[7680,128]{1,0:T(8,128)(2,1)}, bf16[7680,128]{1,0:T(8,128)(2,1)}, u32[]{:S(2)}, u32[]{:S(2)}) collective-permute-start(bf16[7680,128]{1,0:T(8,128)(2,1)} %get-tuple-element.77), channel_id=1, source_target_pairs={{0,64},{64,0},{1,65},{65,1},{2,66},{66,2},{3,67},{67,3},{4,68},{68... | collective-permute-start | bytes 5898248 | tf_op jit(solution)/shard_map/ppermute | solution.py:904
  75.9 17.7 %collective-permute-start.2 = (bf16[112,6144]{1,0:T(8,128)(2,1)}, bf16[112,6144]{1,0:T(8,128)(2,1)}, u32[]{:S(2)}, u32[]{:S(2)}) collective-permute-start(bf16[112,6144]{1,0:T(8,128)(2,1)} %get-tuple-element.73.acts_any), channel_id=1, source_target_pairs={{0,64},{64,0},{1,65},{65,1},{2,66},{66,2},{3,67},{67,3},{4,68},{68... | collective-permute-start | bytes 4128776 | tf_op jit(solution)/shard_map/ppermute | solution.py:904
  104.7 20.7 %collective-permute-start.5 = (bf16[6080,128]{1,0:T(8,128)(2,1)}, bf16[6080,128]{1,0:T(8,128)(2,1)S(1)}, u32[]{:S(2)}, u32[]{:S(2)}) collective-permute-start(bf16[6080,128]{1,0:T(8,128)(2,1)} %get-tuple-element.79), channel_id=1, source_target_pairs={{0,16},{1,17},{2,18},{3,19},{4,20},{5,21},{6,22},{7,23},{8,24},{9,... | collective-permute-start | bytes 4669448 | tf_op jit(solution)/shard_map/ppermute | solution.py:869
  107.6 23.6 %collective-permute-start.14 = (bf16[6080,128]{1,0:T(8,128)(2,1)}, bf16[6080,128]{1,0:T(8,128)(2,1)S(1)}, u32[]{:S(2)}, u32[]{:S(2)}) collective-permute-start(bf16[6080,128]{1,0:T(8,128)(2,1)} %get-tuple-element.81), channel_id=1, source_target_pairs={{0,4},{1,5},{2,6},{3,7},{4,0},{5,1},{6,2},{7,3},{8,12},{9,13},{10,... | collective-permute-start | bytes 4669448 | tf_op jit(solution)/shard_map/ppermute | solution.py:869
  111.4 23.2 %collective-permute-start.23 = (bf16[6144,128]{1,0:T(8,128)(2,1)}, bf16[6144,128]{1,0:T(8,128)(2,1)S(1)}, u32[]{:S(2)}, u32[]{:S(2)}) collective-permute-start(bf16[6144,128]{1,0:T(8,128)(2,1)} %get-tuple-element.83), channel_id=1, source_target_pairs={{0,1},{1,0},{2,3},{3,2},{4,5},{5,4},{6,7},{7,6},{8,9},{9,8},{10,11... | collective-permute-start | bytes 4718600 | tf_op jit(solution)/shard_map/ppermute | solution.py:869
  127.3 13.1 %collective-permute-start.6 = (bf16[3040,128]{1,0:T(8,128)(2,1)S(1)}, bf16[3040,128]{1,0:T(8,128)(2,1)S(1)}, u32[]{:S(2)}, u32[]{:S(2)}) collective-permute-start(bf16[3040,128]{1,0:T(8,128)(2,1)S(1)} %slice.61), channel_id=1, source_target_pairs={{0,4},{1,5},{2,6},{3,7},{4,0},{5,1},{6,2},{7,3},{8,12},{9,13},{10,... | collective-permute-start | bytes 2334728 | tf_op jit(solution)/shard_map/ppermute | solution.py:869
  131.6 12.4 %collective-permute-start.15 = (bf16[3040,128]{1,0:T(8,128)(2,1)S(1)}, bf16[3040,128]{1,0:T(8,128)(2,1)S(1)}, u32[]{:S(2)}, u32[]{:S(2)}) collective-permute-start(bf16[3040,128]{1,0:T(8,128)(2,1)S(1)} %slice.65), channel_id=1, source_target_pairs={{0,1},{1,0},{2,3},{3,2},{4,5},{5,4},{6,7},{7,6},{8,9},{9,8},{10,11... | collective-permute-start | bytes 2334728 | tf_op jit(solution)/shard_map/ppermute | solution.py:869
  135.1 12.1 %collective-permute-start.24 = (bf16[3072,128]{1,0:T(8,128)(2,1)S(1)}, bf16[3072,128]{1,0:T(8,128)(2,1)S(1)}, u32[]{:S(2)}, u32[]{:S(2)}) collective-permute-start(bf16[3072,128]{1,0:T(8,128)(2,1)S(1)} %slice.69), channel_id=1, source_target_pairs={{0,16},{1,17},{2,18},{3,19},{4,20},{5,21},{6,22},{7,23},{8,24},{9,... | collective-permute-start | bytes 2359304 | tf_op jit(solution)/shard_map/ppermute | solution.py:869
  140.7 8.6 %collective-permute-start.7 = (bf16[1520,128]{1,0:T(8,128)(2,1)S(1)}, bf16[1520,128]{1,0:T(8,128)(2,1)S(1)}, u32[]{:S(2)}, u32[]{:S(2)}) collective-permute-start(bf16[1520,128]{1,0:T(8,128)(2,1)S(1)} %slice.63), channel_id=1, source_target_pairs={{0,1},{1,0},{2,3},{3,2},{4,5},{5,4},{6,7},{7,6},{8,9},{9,8},{10,11... | collective-permute-start | bytes 1167368 | tf_op jit(solution)/shard_map/ppermute | solution.py:869
  144.3 8.5 %collective-permute-start.16 = (bf16[1520,128]{1,0:T(8,128)(2,1)S(1)}, bf16[1520,128]{1,0:T(8,128)(2,1)S(1)}, u32[]{:S(2)}, u32[]{:S(2)}) collective-permute-start(bf16[1520,128]{1,0:T(8,128)(2,1)S(1)} %slice.67), channel_id=1, source_target_pairs={{0,16},{1,17},{2,18},{3,19},{4,20},{5,21},{6,22},{7,23},{8,24},{9,... | collective-permute-start | bytes 1167368 | tf_op jit(solution)/shard_map/ppermute | solution.py:869
  147.4 8.2 %collective-permute-start.25 = (bf16[1536,128]{1,0:T(8,128)(2,1)S(1)}, bf16[1536,128]{1,0:T(8,128)(2,1)S(1)}, u32[]{:S(2)}, u32[]{:S(2)}) collective-permute-start(bf16[1536,128]{1,0:T(8,128)(2,1)S(1)} %slice.71), channel_id=1, source_target_pairs={{0,4},{1,5},{2,6},{3,7},{4,0},{5,1},{6,2},{7,3},{8,12},{9,13},{10,... | collective-permute-start | bytes 1179656 | tf_op jit(solution)/shard_map/ppermute | solution.py:869
  156.4 7.6 %collective-permute-start.9 = (bf16[1520,128]{1,0:T(8,128)(2,1)S(1)}, bf16[1520,128]{1,0:T(8,128)(2,1)S(1)}, u32[]{:S(2)}, u32[]{:S(2)}) collective-permute-start(bf16[1520,128]{1,0:T(8,128)(2,1)S(1)} %add_convert_fusion.16), channel_id=1, source_target_pairs={{0,12},{1,13},{2,14},{3,15},{4,8},{5,9},{6,10},{7,11},{8,4},{9,5},... | collective-permute-start | bytes 1167368 | tf_op jit(solution)/shard_map/ppermute | solution.py:869
  162.9 7.0 %collective-permute-start.27 = (bf16[1536,128]{1,0:T(8,128)(2,1)S(1)}, bf16[1536,128]{1,0:T(8,128)(2,1)S(1)}, u32[]{:S(2)}, u32[]{:S(2)}) collective-permute-start(bf16[1536,128]{1,0:T(8,128)(2,1)S(1)} %add_convert_fusion.8), channel_id=1, source_target_pairs={{0,48},{1,49},{2,50},{3,51},{4,52},{5,53},{6,54},{7,55},{8,56},{9,... | collective-permute-start | bytes 1179656 | tf_op jit(solution)/shard_map/ppermute | solution.py:869
  167.1 15.6 %collective-permute-start.19 = (bf16[1520,128]{1,0:T(8,128)(2,1)S(1)}, bf16[1520,128]{1,0:T(8,128)(2,1)S(1)}, u32[]{:S(2)}, u32[]{:S(2)}) collective-permute-start(bf16[1520,128]{1,0:T(8,128)(2,1)S(1)} %add_convert_fusion.11), channel_id=1, source_target_pairs={{0,48},{1,49},{2,50},{3,51},{4,52},{5,53},{6,54},{7,55},{8,56},{9,... | collective-permute-start | bytes 1167368 | tf_op jit(solution)/shard_map/ppermute | solution.py:869
  170.0 7.0 %collective-permute-start.28 = (bf16[1536,128]{1,0:T(8,128)(2,1)S(1)}, bf16[1536,128]{1,0:T(8,128)(2,1)S(1)}, u32[]{:S(2)}, u32[]{:S(2)}) collective-permute-start(bf16[1536,128]{1,0:T(8,128)(2,1)S(1)} %add_convert_fusion.7), channel_id=1, source_target_pairs={{0,12},{1,13},{2,14},{3,15},{4,8},{5,9},{6,10},{7,11},{8,4},{9,5},... | collective-permute-start | bytes 1179656 | tf_op jit(solution)/shard_map/ppermute | solution.py:869
  171.2 8.8 %collective-permute-start.11 = (bf16[1520,128]{1,0:T(8,128)(2,1)S(1)}, bf16[1520,128]{1,0:T(8,128)(2,1)S(1)}, u32[]{:S(2)}, u32[]{:S(2)}) collective-permute-start(bf16[1520,128]{1,0:T(8,128)(2,1)S(1)} %add_convert_fusion.14), channel_id=1, source_target_pairs={{0,1},{1,0},{2,3},{3,2},{4,5},{5,4},{6,7},{7,6},{8,9},{9,8},{10,11... | collective-permute-start | bytes 1167368 | tf_op jit(solution)/shard_map/ppermute | solution.py:869
  177.1 9.0 %collective-permute-start.29 = (bf16[1536,128]{1,0:T(8,128)(2,1)S(1)}, bf16[1536,128]{1,0:T(8,128)(2,1)S(1)}, u32[]{:S(2)}, u32[]{:S(2)}) collective-permute-start(bf16[1536,128]{1,0:T(8,128)(2,1)S(1)} %add_convert_fusion.6), channel_id=1, source_target_pairs={{0,4},{1,5},{2,6},{3,7},{4,0},{5,1},{6,2},{7,3},{8,12},{9,13},{10,... | collective-permute-start | bytes 1179656 | tf_op jit(solution)/shard_map/ppermute | solution.py:869
  180.1 14.4 %collective-permute-start.12 = (bf16[3040,128]{1,0:T(8,128)(2,1)S(1)}, bf16[3040,128]{1,0:T(8,128)(2,1)S(1)}, u32[]{:S(2)}, u32[]{:S(2)}) collective-permute-start(bf16[3040,128]{1,0:T(8,128)(2,1)S(1)} %pad_maximum_fusion.4), channel_id=1, source_target_pairs={{0,4},{1,5},{2,6},{3,7},{4,0},{5,1},{6,2},{7,3},{8,12},{9,13},{10,... | collective-permute-start | bytes 2334728 | tf_op jit(solution)/shard_map/ppermute | solution.py:869
  182.8 7.9 %collective-permute-start.20 = (bf16[1520,128]{1,0:T(8,128)(2,1)S(1)}, bf16[1520,128]{1,0:T(8,128)(2,1)S(1)}, u32[]{:S(2)}, u32[]{:S(2)}) collective-permute-start(bf16[1520,128]{1,0:T(8,128)(2,1)S(1)} %add_convert_fusion.10), channel_id=1, source_target_pairs={{0,16},{1,17},{2,18},{3,19},{4,20},{5,21},{6,22},{7,23},{8,24},{9,... | collective-permute-start | bytes 1167368 | tf_op jit(solution)/shard_map/ppermute | solution.py:869
  186.1 13.0 %collective-permute-start.30 = (bf16[3072,128]{1,0:T(8,128)(2,1)S(1)}, bf16[3072,128]{1,0:T(8,128)(2,1)S(1)}, u32[]{:S(2)}, u32[]{:S(2)}) collective-permute-start(bf16[3072,128]{1,0:T(8,128)(2,1)S(1)} %pad_maximum_fusion.3), channel_id=1, source_target_pairs={{0,16},{1,17},{2,18},{3,19},{4,20},{5,21},{6,22},{7,23},{8,24},{9,... | collective-permute-start | bytes 2359304 | tf_op jit(solution)/shard_map/ppermute | solution.py:869
  190.8 12.1 %collective-permute-start.21 = (bf16[3040,128]{1,0:T(8,128)(2,1)S(1)}, bf16[3040,128]{1,0:T(8,128)(2,1)S(1)}, u32[]{:S(2)}, u32[]{:S(2)}) collective-permute-start(bf16[3040,128]{1,0:T(8,128)(2,1)S(1)} %pad_maximum_fusion.5), channel_id=1, source_target_pairs={{0,1},{1,0},{2,3},{3,2},{4,5},{5,4},{6,7},{7,6},{8,9},{9,8},{10,11... | collective-permute-start | bytes 2334728 | tf_op jit(solution)/shard_map/ppermute | solution.py:869
  195.7 23.1 %collective-permute-start.13 = (bf16[6080,128]{1,0:T(8,128)(2,1)}, bf16[6080,128]{1,0:T(8,128)(2,1)}, u32[]{:S(2)}, u32[]{:S(2)}) collective-permute-start(bf16[6080,128]{1,0:T(8,128)(2,1)} %pad_maximum_fusion.1.own0), channel_id=1, source_target_pairs={{0,16},{1,17},{2,18},{3,19},{4,20},{5,21},{6,22},{7,23},{8,24},{9,... | collective-permute-start | bytes 4669448 | tf_op jit(solution)/shard_map/ppermute | solution.py:869
  200.4 24.4 %collective-permute-start.31 = (bf16[6144,128]{1,0:T(8,128)(2,1)}, bf16[6144,128]{1,0:T(8,128)(2,1)}, u32[]{:S(2)}, u32[]{:S(2)}) collective-permute-start(bf16[6144,128]{1,0:T(8,128)(2,1)} %pad_maximum_fusion.own2), channel_id=1, source_target_pairs={{0,1},{1,0},{2,3},{3,2},{4,5},{5,4},{6,7},{7,6},{8,9},{9,8},{10,11... | collective-permute-start | bytes 4718600 | tf_op jit(solution)/shard_map/ppermute | solution.py:869
  204.2 20.6 %collective-permute-start.22 = (bf16[6080,128]{1,0:T(8,128)(2,1)}, bf16[6080,128]{1,0:T(8,128)(2,1)}, u32[]{:S(2)}, u32[]{:S(2)}) collective-permute-start(bf16[6080,128]{1,0:T(8,128)(2,1)} %pad_maximum_fusion.2.own1), channel_id=1, source_target_pairs={{0,4},{1,5},{2,6},{3,7},{4,0},{5,1},{6,2},{7,3},{8,12},{9,13},{10,... | collective-permute-start | bytes 4669448 | tf_op jit(solution)/shard_map/ppermute | solution.py:869
  (16 other events, 70.1 us)

commit v7 on v6

--- a/solution.py
+++ b/solution.py
@@ -755,7 +755,7 @@
         out_specs=[hbm] * 5 + [vm],
         out_shape=big_shapes(sizes) + [jax.ShapeDtypeStruct((16, 128), F32)],
         scratch_shapes=unpack_scratch(sizes),
-        compiler_params=pltpu.CompilerParams(vmem_limit_bytes=VMEM),
+        compiler_params=pltpu.CompilerParams(vmem_limit_bytes=18 * 1024 * 1024),
         cost_estimate=pl.CostEstimate(flops=10_000_000, bytes_accessed=12_000_000, transcendentals=0),
         name="unpack_own_half",
     )(idx, *own)
@@ -818,7 +818,7 @@
         input_output_aliases={8 + i: i for i in range(5)},
         scratch_shapes=unpack_scratch(sizes) + [pltpu.VMEM((part_rows(i, *sizes) // PIECES, 128), BF) for i in range(3)]
         + [pltpu.VMEM((dec_blocks(WD, WF)["all"], 128), BF), pltpu.SemaphoreType.DMA((3,))],
-        compiler_params=pltpu.CompilerParams(vmem_limit_bytes=VMEM),
+        compiler_params=pltpu.CompilerParams(vmem_limit_bytes=28 * 1024 * 1024),
         cost_estimate=pl.CostEstimate(flops=10_000_000, bytes_accessed=15_000_000, transcendentals=0),
         name="unpack_other_half",
     )(idx, *came, *own, squares, *big)
@@ -838,7 +838,7 @@
         in_specs=[pl.BlockSpec(memory_space=pltpu.SMEM)] + [vm] * 4,
         out_specs=[vm] * 2,
         out_shape=[jax.ShapeDtypeStruct((2, *arrays[i].shape), BF) for i in (0, 2)],
-        compiler_params=pltpu.CompilerParams(vmem_limit_bytes=VMEM),
+        compiler_params=pltpu.CompilerParams(vmem_limit_bytes=8 * 1024 * 1024),
         cost_estimate=pl.CostEstimate(flops=1000, bytes_accessed=1000, transcendentals=0),
         name="both_clips",
     )(sec, *arrays)

time: 243 us -> 241 us (level)
  other arithmetic: 11 us -> 7.28 us
  waiting for transfers between devices: 53.2 us -> 55.9 us
  transfers between devices with their start and end apart: 33 -> 33, of which waited for: 22 -> 25; matrix products, arithmetic and copies ran while one was open for 4% -> 3% of each run, Pallas kernels for 10% -> 9%
where the time goes in v7:
time: 241 us; the launch traced here: 237 us
  Pallas kernels  114 us (47%)
  starting transfers between devices  56.2 us (23%)
  waiting for transfers between devices  55.9 us (23%)
  other arithmetic  7.28 us (3%)
  local copies, waits for them, and re-layouts  2.82 us (1%)
    pallas_call x1, Pallas kernels, dec_block_call(): pl.pallas_call(functools.partial(dec_kernel, W=W, L=L, H=H, FF=FF, V=V, s...  63.4 us
    ppermute x27, waiting for transfers between devices, swap(): return lax.ppermute(value, ('section', 'dp'), pairs)  52 us
    ppermute x27, starting transfers between devices, swap(): return lax.ppermute(value, ('section', 'dp'), pairs)  46.9 us
    pallas_call x1, Pallas kernels, enc_bwd_call(): pl.pallas_call(functools.partial(enc_bwd_kernel, W=W, FF=FF, seen=seen),...  14.5 us
    pallas_call x1, Pallas kernels, enc_fwd_call(): pl.pallas_call(functools.partial(enc_fwd_kernel, W=W, FF=FF, seen=seen),...  10.3 us
    pallas_call x1, Pallas kernels, weight_grad_call(): pl.pallas_call(functools.partial(weight_grad_kernel, W=W, FF=FF, WD=WD, W...  10.2 us
    ppermute x6, starting transfers between devices, from_partner(): return lax.ppermute(value, 'section', [(0, 1), (1, 0)])  9.31 us
    pallas_call x1, Pallas kernels, unpack_call(): pl.pallas_call(functools.partial(unpack_kernel, sizes=sizes, slots=slots,...  7.53 us
  transfers between devices with their start and end apart: 33, of which 25 were waited for; matrix products, arithmetic and copies ran while one was open for 3% of the time, Pallas kernels for 9%

profile of v7, /device:TPU:1, one launch (start us, length us, event | category | flops | bytes accessed | tf_op | source)
XLA Modules:
  0.0 236.9 jit_solution(6211450356990404230)
XLA Ops:
  0.7 10.3 %encoder_forward.1 = (bf16[112,6144]{1,0:T(8,128)(2,1)}, bf16[112,2304]{1,0:T(8,128)(2,1)}, f32[112,768]{1,0:T(8,128)}, bf16[112,3072]{1,0:T(8,128)(2,1)}, f32[112,384]{1,0:T(8,128)}) custom-call(s32[1]{0:T(128)} %bitcast.sec_ref, s32[2]{0:T(128)} %frames_ref.5, bf16[2,112,768]{2,1,0:T(8,128)(2,1)} %tok_ref.3, bf16[8,768]{1,0:T(8,128)(2,1)} %vec_ref.3, ...), custom_call_target="tpu_custom_call" | custom-call | flops 1700000000 | bytes 18000000 | tf_op jit(solution)/shard_map/encoder_forward/pallas_call | solution.py:422
  11.0 63.4 %decoder.1 = (bf16[192,1152]{1,0:T(8,128)(2,1)}, bf16[192,1152]{1,0:T(8,128)(2,1)}, bf16[112,384]{1,0:T(8,128)(2,1)}, bf16[7680,128]{1,0:T(8,128)(2,1)}, bf16[7680,128]{1,0:T(8,128)(2,1)}) custom-call(s32[1]{0:T(128)} %bitcast.sec_ref, s32[2]{0:T(128)} %frames_ref.5, s32[2,14]{1,0:T(2,128)} %vis_ref.1, f32[112,384]{1,0:T(8,128)} %get-tuple-element.62.proj_ref, ...), custom_call_target="tpu_custom_call" | custom-call | flops 28000000000 | bytes 12000000 | tf_op jit(solution)/shard_map/decoder/pallas_call | solution.py:303
  76.2 14.5 %encoder_backward.1 = (bf16[128,3840]{1,0:T(8,128)(2,1)}, bf16[128,3840]{1,0:T(8,128)(2,1)}, bf16[112,384]{1,0:T(8,128)(2,1)}, bf16[112,384]{1,0:T(8,128)(2,1)}) custom-call(s32[1]{0:T(128)} %bitcast.sec_ref, s32[2]{0:T(128)} %frames_ref.5, bf16[112,384]{1,0:T(8,128)(2,1)} %get-tuple-element.65.dz_ref, bf16[2,112,768]{2,1,0:T(8,128)(2,1)} %tok_ref.3, ...), custom_call_target="tpu_custom_call" | custom-call | flops 2000000000 | bytes 18000000 | tf_op jit(solution)/shard_map/encoder_backward/pallas_call | solution.py:520
  94.5 10.2 %encoder_weight_gradients.1 = (bf16[6080,128]{1,0:T(8,128)(2,1)}, bf16[6080,128]{1,0:T(8,128)(2,1)}, bf16[6144,128]{1,0:T(8,128)(2,1)}, bf16[6080,128]{1,0:T(8,1...) custom-call(s32[4]{0:T(128)} %pad_add_fusion.idx_ref, bf16[112,6144]{1,0:T(8,128)(2,1)} %get-tuple-element.73.acts_any, ...), custom_call_target="tpu_custom_call" | custom-call | flops 1700000000 | bytes 20000000 | tf_op jit(solution)/shard_map/encoder_weight_gradients/pallas_call | solution.py:660
  104.7 2.9 %collective-permute-start.5 = (bf16[6080,128]{1,0:T(8,128)(2,1)}, bf16[6080,128]{1,0:T(8,128)(2,1)S(1)}, u32[]{:S(2)}, u32[]{:S(2)}) collective-permute-start(bf16[6080,128]{1,0:T(8,128)(2,1)} %get-tuple-element.79), channel_id=1, source_target_pairs={{0,16},{1,17},{2,18},{3,19},{4,20},{5,21},{6,22},{7,23},{8,24},{9,... | collective-permute-start | bytes 4669448 | tf_op jit(solution)/shard_map/ppermute | solution.py:869
  107.6 3.8 %collective-permute-start.14 = (bf16[6080,128]{1,0:T(8,128)(2,1)}, bf16[6080,128]{1,0:T(8,128)(2,1)S(1)}, u32[]{:S(2)}, u32[]{:S(2)}) collective-permute-start(bf16[6080,128]{1,0:T(8,128)(2,1)} %get-tuple-element.81), channel_id=1, source_target_pairs={{0,4},{1,5},{2,6},{3,7},{4,0},{5,1},{6,2},{7,3},{8,12},{9,13},{10,... | collective-permute-start | bytes 4669448 | tf_op jit(solution)/shard_map/ppermute | solution.py:869
  113.8 11.6 %collective-permute-done.5 = bf16[6080,128]{1,0:T(8,128)(2,1)S(1)} collective-permute-done((bf16[6080,128]{1,0:T(8,128)(2,1)}, bf16[6080,128]{1,0:T(8,128)(2,1)S(1)}, u32[]{:S(2)}, u32[]{:S(2)}) %collective-permute-start.5) | collective-permute-done | bytes 1556512 | tf_op jit(solution)/shard_map/ppermute | solution.py:869
  127.3 3.8 %collective-permute-start.6 = (bf16[3040,128]{1,0:T(8,128)(2,1)S(1)}, bf16[3040,128]{1,0:T(8,128)(2,1)S(1)}, u32[]{:S(2)}, u32[]{:S(2)}) collective-permute-start(bf16[3040,128]{1,0:T(8,128)(2,1)S(1)} %slice.61), channel_id=1, source_target_pairs={{0,4},{1,5},{2,6},{3,7},{4,0},{5,1},{6,2},{7,3},{8,12},{9,13},{10,... | collective-permute-start | bytes 2334728 | tf_op jit(solution)/shard_map/ppermute | solution.py:869
  131.6 3.0 %collective-permute-start.15 = (bf16[3040,128]{1,0:T(8,128)(2,1)S(1)}, bf16[3040,128]{1,0:T(8,128)(2,1)S(1)}, u32[]{:S(2)}, u32[]{:S(2)}) collective-permute-start(bf16[3040,128]{1,0:T(8,128)(2,1)S(1)} %slice.65), channel_id=1, source_target_pairs={{0,1},{1,0},{2,3},{3,2},{4,5},{5,4},{6,7},{7,6},{8,9},{9,8},{10,11... | collective-permute-start | bytes 2334728 | tf_op jit(solution)/shard_map/ppermute | solution.py:869
  135.1 2.8 %collective-permute-start.24 = (bf16[3072,128]{1,0:T(8,128)(2,1)S(1)}, bf16[3072,128]{1,0:T(8,128)(2,1)S(1)}, u32[]{:S(2)}, u32[]{:S(2)}) collective-permute-start(bf16[3072,128]{1,0:T(8,128)(2,1)S(1)} %slice.69), channel_id=1, source_target_pairs={{0,16},{1,17},{2,18},{3,19},{4,20},{5,21},{6,22},{7,23},{8,24},{9,... | collective-permute-start | bytes 2359304 | tf_op jit(solution)/shard_map/ppermute | solution.py:869
  137.8 2.6 %collective-permute-done.6 = bf16[3040,128]{1,0:T(8,128)(2,1)S(1)} collective-permute-done((bf16[3040,128]{1,0:T(8,128)(2,1)S(1)}, bf16[3040,128]{1,0:T(8,128)(2,1)S(1)}, u32[]{:S(2)}, u32[]{:S(2)}) %collective-permute-start.6) | collective-permute-done | bytes 778272 | tf_op jit(solution)/shard_map/ppermute | solution.py:869
  144.3 2.8 %collective-permute-start.16 = (bf16[1520,128]{1,0:T(8,128)(2,1)S(1)}, bf16[1520,128]{1,0:T(8,128)(2,1)S(1)}, u32[]{:S(2)}, u32[]{:S(2)}) collective-permute-start(bf16[1520,128]{1,0:T(8,128)(2,1)S(1)} %slice.67), channel_id=1, source_target_pairs={{0,16},{1,17},{2,18},{3,19},{4,20},{5,21},{6,22},{7,23},{8,24},{9,... | collective-permute-start | bytes 1167368 | tf_op jit(solution)/shard_map/ppermute | solution.py:869
  149.4 3.4 %collective-permute-done.16 = bf16[1520,128]{1,0:T(8,128)(2,1)S(1)} collective-permute-done((bf16[1520,128]{1,0:T(8,128)(2,1)S(1)}, bf16[1520,128]{1,0:T(8,128)(2,1)S(1)}, u32[]{:S(2)}, u32[]{:S(2)}) %collective-permute-start.16) | collective-permute-done | bytes 389152 | tf_op jit(solution)/shard_map/ppermute | solution.py:869
  153.0 2.6 %collective-permute-done.25 = bf16[1536,128]{1,0:T(8,128)(2,1)S(1)} collective-permute-done((bf16[1536,128]{1,0:T(8,128)(2,1)S(1)}, bf16[1536,128]{1,0:T(8,128)(2,1)S(1)}, u32[]{:S(2)}, u32[]{:S(2)}) %collective-permute-start.25) | collective-permute-done | bytes 393248 | tf_op jit(solution)/shard_map/ppermute | solution.py:869
  156.5 3.4 %collective-permute-done.17 = bf16[1520,128]{1,0:T(8,128)(2,1)S(1)} collective-permute-done((bf16[1520,128]{1,0:T(8,128)(2,1)S(1)}, bf16[1520,128]{1,0:T(8,128)(2,1)S(1)}, u32[]{:S(2)}, u32[]{:S(2)}) %collective-permute-start.17) | collective-permute-done | bytes 389152 | tf_op jit(solution)/shard_map/ppermute | solution.py:869
  160.1 2.7 %collective-permute-done.26 = bf16[1536,128]{1,0:T(8,128)(2,1)S(1)} collective-permute-done((bf16[1536,128]{1,0:T(8,128)(2,1)S(1)}, bf16[1536,128]{1,0:T(8,128)(2,1)S(1)}, u32[]{:S(2)}, u32[]{:S(2)}) %collective-permute-start.26) | collective-permute-done | bytes 393248 | tf_op jit(solution)/shard_map/ppermute | solution.py:869
  167.2 2.7 %collective-permute-done.27 = bf16[1536,128]{1,0:T(8,128)(2,1)S(1)} collective-permute-done((bf16[1536,128]{1,0:T(8,128)(2,1)S(1)}, bf16[1536,128]{1,0:T(8,128)(2,1)S(1)}, u32[]{:S(2)}, u32[]{:S(2)}) %collective-permute-start.27) | collective-permute-done | bytes 393248 | tf_op jit(solution)/shard_map/ppermute | solution.py:869
  173.7 3.3 %collective-permute-done.28 = bf16[1536,128]{1,0:T(8,128)(2,1)S(1)} collective-permute-done((bf16[1536,128]{1,0:T(8,128)(2,1)S(1)}, bf16[1536,128]{1,0:T(8,128)(2,1)S(1)}, u32[]{:S(2)}, u32[]{:S(2)}) %collective-permute-start.28) | collective-permute-done | bytes 393248 | tf_op jit(solution)/shard_map/ppermute | solution.py:869
  182.8 2.8 %collective-permute-start.20 = (bf16[1520,128]{1,0:T(8,128)(2,1)S(1)}, bf16[1520,128]{1,0:T(8,128)(2,1)S(1)}, u32[]{:S(2)}, u32[]{:S(2)}) collective-permute-start(bf16[1520,128]{1,0:T(8,128)(2,1)S(1)} %add_convert_fusion.10), channel_id=1, source_target_pairs={{0,16},{1,17},{2,18},{3,19},{4,20},{5,21},{6,22},{7,23},{8,24},{9,... | collective-permute-start | bytes 1167368 | tf_op jit(solution)/shard_map/ppermute | solution.py:869
  204.2 3.9 %collective-permute-start = (bf16[192,1152]{1,0:T(8,128)(2,1)}, bf16[192,1152]{1,0:T(8,128)(2,1)}, u32[]{:S(2)}, u32[]{:S(2)}) collective-permute-start(bf16[192,1152]{1,0:T(8,128)(2,1)} %get-tuple-element.64), channel_id=1, source_target_pairs={{0,64},{64,0},{1,65},{65,1},{2,66},{66,2},{3,67},{67,3},{4,68},{68... | collective-permute-start | bytes 1327112 | tf_op jit(solution)/shard_map/ppermute | solution.py:904
  213.0 5.6 %unpack_own_half.1 = (f32[3072,384]{1,0:T(8,128)}, f32[768,1536]{1,0:T(8,128)}, f32[768,1152]{1,0:T(8,128)}, f32[768,384]{1,0:T(8,128)}, f32[192,768]{1,0:T(8,128)}, /*index=5*/f32[16,128]{1,0:T(8,128)S(1)}) custom-call(s32[4]{0:T(128)S(1)} %copy-done.2, bf16[6080,128]{1,0:T(8,128)(2,1)S(1)} %pad_maximum_fusion.1.own0, ...), custom_call_target="tpu_custom_call" | custom-call | flops 10000000 | bytes 12000000 | tf_op jit(solution)/shard_map/unpack_own_half/pallas_call | solution.py:752
  218.6 6.0 %collective-permute-done.22.came1 = bf16[6080,128]{1,0:T(8,128)(2,1)} collective-permute-done((bf16[6080,128]{1,0:T(8,128)(2,1)}, bf16[6080,128]{1,0:T(8,128)(2,1)}, u32[]{:S(2)}, u32[]{:S(2)}) %collective-permute-start.22) | collective-permute-done | bytes 1556512 | tf_op jit(solution)/shard_map/ppermute | solution.py:869
  224.7 7.5 %unpack_other_half.1 = (f32[3072,384]{1,0:T(8,128)}, f32[768,1536]{1,0:T(8,128)}, f32[768,1152]{1,0:T(8,128)}, f32[768,384]{1,0:T(8,128)}, f32[192,768]{1,0:T(8,...) custom-call(s32[4]{0:T(128)S(1)} %copy-done.2, ...), custom_call_target="tpu_custom_call", output_to_operand_aliasing={{0}: (8, {}), {1}: (9, {}), {2}: (10, {}), {3}: (11, {}), {... | custom-call | flops 10000000 | bytes 15000000 | tf_op jit(solution)/shard_map/unpack_other_half/pallas_call | solution.py:813
  232.2 3.1 %collective-permute-start.32 = (f32[8,128]{1,0:T(8,128)S(1)}, f32[8,128]{1,0:T(8,128)S(1)}, u32[]{:S(2)}, u32[]{:S(2)}) collective-permute-start(f32[8,128]{1,0:T(8,128)S(1)} %slice_select_fusion), channel_id=1, source_target_pairs={{0,64},{64,0},{1,65},{65,1},{2,66},{66,2},{3,67},{67,3},{4,68},{68... | collective-permute-start | bytes 12296 | tf_op jit(solution)/shard_map/ppermute | solution.py:904
  (97 shorter events, 57.2 us)
Async XLA Ops:
  74.4 19.2 %collective-permute-start.4 = (bf16[7680,128]{1,0:T(8,128)(2,1)}, bf16[7680,128]{1,0:T(8,128)(2,1)}, u32[]{:S(2)}, u32[]{:S(2)}) collective-permute-start(bf16[7680,128]{1,0:T(8,128)(2,1)} %get-tuple-element.77), channel_id=1, source_target_pairs={{0,64},{64,0},{1,65},{65,1},{2,66},{66,2},{3,67},{67,3},{4,68},{68... | collective-permute-start | bytes 5898248 | tf_op jit(solution)/shard_map/ppermute | solution.py:904
  75.9 17.7 %collective-permute-start.2 = (bf16[112,6144]{1,0:T(8,128)(2,1)}, bf16[112,6144]{1,0:T(8,128)(2,1)}, u32[]{:S(2)}, u32[]{:S(2)}) collective-permute-start(bf16[112,6144]{1,0:T(8,128)(2,1)} %get-tuple-element.73.acts_any), channel_id=1, source_target_pairs={{0,64},{64,0},{1,65},{65,1},{2,66},{66,2},{3,67},{67,3},{4,68},{68... | collective-permute-start | bytes 4128776 | tf_op jit(solution)/shard_map/ppermute | solution.py:904
  104.7 20.7 %collective-permute-start.5 = (bf16[6080,128]{1,0:T(8,128)(2,1)}, bf16[6080,128]{1,0:T(8,128)(2,1)S(1)}, u32[]{:S(2)}, u32[]{:S(2)}) collective-permute-start(bf16[6080,128]{1,0:T(8,128)(2,1)} %get-tuple-element.79), channel_id=1, source_target_pairs={{0,16},{1,17},{2,18},{3,19},{4,20},{5,21},{6,22},{7,23},{8,24},{9,... | collective-permute-start | bytes 4669448 | tf_op jit(solution)/shard_map/ppermute | solution.py:869
  107.6 23.6 %collective-permute-start.14 = (bf16[6080,128]{1,0:T(8,128)(2,1)}, bf16[6080,128]{1,0:T(8,128)(2,1)S(1)}, u32[]{:S(2)}, u32[]{:S(2)}) collective-permute-start(bf16[6080,128]{1,0:T(8,128)(2,1)} %get-tuple-element.81), channel_id=1, source_target_pairs={{0,4},{1,5},{2,6},{3,7},{4,0},{5,1},{6,2},{7,3},{8,12},{9,13},{10,... | collective-permute-start | bytes 4669448 | tf_op jit(solution)/shard_map/ppermute | solution.py:869
  111.4 23.2 %collective-permute-start.23 = (bf16[6144,128]{1,0:T(8,128)(2,1)}, bf16[6144,128]{1,0:T(8,128)(2,1)S(1)}, u32[]{:S(2)}, u32[]{:S(2)}) collective-permute-start(bf16[6144,128]{1,0:T(8,128)(2,1)} %get-tuple-element.83), channel_id=1, source_target_pairs={{0,1},{1,0},{2,3},{3,2},{4,5},{5,4},{6,7},{7,6},{8,9},{9,8},{10,11... | collective-permute-start | bytes 4718600 | tf_op jit(solution)/shard_map/ppermute | solution.py:869
  127.3 13.1 %collective-permute-start.6 = (bf16[3040,128]{1,0:T(8,128)(2,1)S(1)}, bf16[3040,128]{1,0:T(8,128)(2,1)S(1)}, u32[]{:S(2)}, u32[]{:S(2)}) collective-permute-start(bf16[3040,128]{1,0:T(8,128)(2,1)S(1)} %slice.61), channel_id=1, source_target_pairs={{0,4},{1,5},{2,6},{3,7},{4,0},{5,1},{6,2},{7,3},{8,12},{9,13},{10,... | collective-permute-start | bytes 2334728 | tf_op jit(solution)/shard_map/ppermute | solution.py:869
  131.6 12.4 %collective-permute-start.15 = (bf16[3040,128]{1,0:T(8,128)(2,1)S(1)}, bf16[3040,128]{1,0:T(8,128)(2,1)S(1)}, u32[]{:S(2)}, u32[]{:S(2)}) collective-permute-start(bf16[3040,128]{1,0:T(8,128)(2,1)S(1)} %slice.65), channel_id=1, source_target_pairs={{0,1},{1,0},{2,3},{3,2},{4,5},{5,4},{6,7},{7,6},{8,9},{9,8},{10,11... | collective-permute-start | bytes 2334728 | tf_op jit(solution)/shard_map/ppermute | solution.py:869
  135.1 12.1 %collective-permute-start.24 = (bf16[3072,128]{1,0:T(8,128)(2,1)S(1)}, bf16[3072,128]{1,0:T(8,128)(2,1)S(1)}, u32[]{:S(2)}, u32[]{:S(2)}) collective-permute-start(bf16[3072,128]{1,0:T(8,128)(2,1)S(1)} %slice.69), channel_id=1, source_target_pairs={{0,16},{1,17},{2,18},{3,19},{4,20},{5,21},{6,22},{7,23},{8,24},{9,... | collective-permute-start | bytes 2359304 | tf_op jit(solution)/shard_map/ppermute | solution.py:869
  140.7 8.6 %collective-permute-start.7 = (bf16[1520,128]{1,0:T(8,128)(2,1)S(1)}, bf16[1520,128]{1,0:T(8,128)(2,1)S(1)}, u32[]{:S(2)}, u32[]{:S(2)}) collective-permute-start(bf16[1520,128]{1,0:T(8,128)(2,1)S(1)} %slice.63), channel_id=1, source_target_pairs={{0,1},{1,0},{2,3},{3,2},{4,5},{5,4},{6,7},{7,6},{8,9},{9,8},{10,11... | collective-permute-start | bytes 1167368 | tf_op jit(solution)/shard_map/ppermute | solution.py:869
  144.3 8.5 %collective-permute-start.16 = (bf16[1520,128]{1,0:T(8,128)(2,1)S(1)}, bf16[1520,128]{1,0:T(8,128)(2,1)S(1)}, u32[]{:S(2)}, u32[]{:S(2)}) collective-permute-start(bf16[1520,128]{1,0:T(8,128)(2,1)S(1)} %slice.67), channel_id=1, source_target_pairs={{0,16},{1,17},{2,18},{3,19},{4,20},{5,21},{6,22},{7,23},{8,24},{9,... | collective-permute-start | bytes 1167368 | tf_op jit(solution)/shard_map/ppermute | solution.py:869
  147.4 8.2 %collective-permute-start.25 = (bf16[1536,128]{1,0:T(8,128)(2,1)S(1)}, bf16[1536,128]{1,0:T(8,128)(2,1)S(1)}, u32[]{:S(2)}, u32[]{:S(2)}) collective-permute-start(bf16[1536,128]{1,0:T(8,128)(2,1)S(1)} %slice.71), channel_id=1, source_target_pairs={{0,4},{1,5},{2,6},{3,7},{4,0},{5,1},{6,2},{7,3},{8,12},{9,13},{10,... | collective-permute-start | bytes 1179656 | tf_op jit(solution)/shard_map/ppermute | solution.py:869
  155.8 7.0 %collective-permute-start.26 = (bf16[1536,128]{1,0:T(8,128)(2,1)S(1)}, bf16[1536,128]{1,0:T(8,128)(2,1)S(1)}, u32[]{:S(2)}, u32[]{:S(2)}) collective-permute-start(bf16[1536,128]{1,0:T(8,128)(2,1)S(1)} %add_convert_fusion.9), channel_id=1, source_target_pairs={{0,3},{1,2},{2,1},{3,0},{4,7},{5,6},{6,5},{7,4},{8,11},{9,10},{10,... | collective-permute-start | bytes 1179656 | tf_op jit(solution)/shard_map/ppermute | solution.py:869
  156.4 7.6 %collective-permute-start.9 = (bf16[1520,128]{1,0:T(8,128)(2,1)S(1)}, bf16[1520,128]{1,0:T(8,128)(2,1)S(1)}, u32[]{:S(2)}, u32[]{:S(2)}) collective-permute-start(bf16[1520,128]{1,0:T(8,128)(2,1)S(1)} %add_convert_fusion.16), channel_id=1, source_target_pairs={{0,12},{1,13},{2,14},{3,15},{4,8},{5,9},{6,10},{7,11},{8,4},{9,5},... | collective-permute-start | bytes 1167368 | tf_op jit(solution)/shard_map/ppermute | solution.py:869
  167.1 15.6 %collective-permute-start.19 = (bf16[1520,128]{1,0:T(8,128)(2,1)S(1)}, bf16[1520,128]{1,0:T(8,128)(2,1)S(1)}, u32[]{:S(2)}, u32[]{:S(2)}) collective-permute-start(bf16[1520,128]{1,0:T(8,128)(2,1)S(1)} %add_convert_fusion.11), channel_id=1, source_target_pairs={{0,48},{1,49},{2,50},{3,51},{4,52},{5,53},{6,54},{7,55},{8,56},{9,... | collective-permute-start | bytes 1167368 | tf_op jit(solution)/shard_map/ppermute | solution.py:869
  170.0 7.0 %collective-permute-start.28 = (bf16[1536,128]{1,0:T(8,128)(2,1)S(1)}, bf16[1536,128]{1,0:T(8,128)(2,1)S(1)}, u32[]{:S(2)}, u32[]{:S(2)}) collective-permute-start(bf16[1536,128]{1,0:T(8,128)(2,1)S(1)} %add_convert_fusion.7), channel_id=1, source_target_pairs={{0,12},{1,13},{2,14},{3,15},{4,8},{5,9},{6,10},{7,11},{8,4},{9,5},... | collective-permute-start | bytes 1179656 | tf_op jit(solution)/shard_map/ppermute | solution.py:869
  171.2 8.8 %collective-permute-start.11 = (bf16[1520,128]{1,0:T(8,128)(2,1)S(1)}, bf16[1520,128]{1,0:T(8,128)(2,1)S(1)}, u32[]{:S(2)}, u32[]{:S(2)}) collective-permute-start(bf16[1520,128]{1,0:T(8,128)(2,1)S(1)} %add_convert_fusion.14), channel_id=1, source_target_pairs={{0,1},{1,0},{2,3},{3,2},{4,5},{5,4},{6,7},{7,6},{8,9},{9,8},{10,11... | collective-permute-start | bytes 1167368 | tf_op jit(solution)/shard_map/ppermute | solution.py:869
  177.1 9.0 %collective-permute-start.29 = (bf16[1536,128]{1,0:T(8,128)(2,1)S(1)}, bf16[1536,128]{1,0:T(8,128)(2,1)S(1)}, u32[]{:S(2)}, u32[]{:S(2)}) collective-permute-start(bf16[1536,128]{1,0:T(8,128)(2,1)S(1)} %add_convert_fusion.6), channel_id=1, source_target_pairs={{0,4},{1,5},{2,6},{3,7},{4,0},{5,1},{6,2},{7,3},{8,12},{9,13},{10,... | collective-permute-start | bytes 1179656 | tf_op jit(solution)/shard_map/ppermute | solution.py:869
  180.1 14.4 %collective-permute-start.12 = (bf16[3040,128]{1,0:T(8,128)(2,1)S(1)}, bf16[3040,128]{1,0:T(8,128)(2,1)S(1)}, u32[]{:S(2)}, u32[]{:S(2)}) collective-permute-start(bf16[3040,128]{1,0:T(8,128)(2,1)S(1)} %pad_maximum_fusion.4), channel_id=1, source_target_pairs={{0,4},{1,5},{2,6},{3,7},{4,0},{5,1},{6,2},{7,3},{8,12},{9,13},{10,... | collective-permute-start | bytes 2334728 | tf_op jit(solution)/shard_map/ppermute | solution.py:869
  182.8 7.9 %collective-permute-start.20 = (bf16[1520,128]{1,0:T(8,128)(2,1)S(1)}, bf16[1520,128]{1,0:T(8,128)(2,1)S(1)}, u32[]{:S(2)}, u32[]{:S(2)}) collective-permute-start(bf16[1520,128]{1,0:T(8,128)(2,1)S(1)} %add_convert_fusion.10), channel_id=1, source_target_pairs={{0,16},{1,17},{2,18},{3,19},{4,20},{5,21},{6,22},{7,23},{8,24},{9,... | collective-permute-start | bytes 1167368 | tf_op jit(solution)/shard_map/ppermute | solution.py:869
  186.1 13.0 %collective-permute-start.30 = (bf16[3072,128]{1,0:T(8,128)(2,1)S(1)}, bf16[3072,128]{1,0:T(8,128)(2,1)S(1)}, u32[]{:S(2)}, u32[]{:S(2)}) collective-permute-start(bf16[3072,128]{1,0:T(8,128)(2,1)S(1)} %pad_maximum_fusion.3), channel_id=1, source_target_pairs={{0,16},{1,17},{2,18},{3,19},{4,20},{5,21},{6,22},{7,23},{8,24},{9,... | collective-permute-start | bytes 2359304 | tf_op jit(solution)/shard_map/ppermute | solution.py:869
  190.8 12.0 %collective-permute-start.21 = (bf16[3040,128]{1,0:T(8,128)(2,1)S(1)}, bf16[3040,128]{1,0:T(8,128)(2,1)S(1)}, u32[]{:S(2)}, u32[]{:S(2)}) collective-permute-start(bf16[3040,128]{1,0:T(8,128)(2,1)S(1)} %pad_maximum_fusion.5), channel_id=1, source_target_pairs={{0,1},{1,0},{2,3},{3,2},{4,5},{5,4},{6,7},{7,6},{8,9},{9,8},{10,11... | collective-permute-start | bytes 2334728 | tf_op jit(solution)/shard_map/ppermute | solution.py:869
  194.5 24.1 %collective-permute-start.13 = (bf16[6080,128]{1,0:T(8,128)(2,1)S(1)}, bf16[6080,128]{1,0:T(8,128)(2,1)}, u32[]{:S(2)}, u32[]{:S(2)}) collective-permute-start(bf16[6080,128]{1,0:T(8,128)(2,1)S(1)} %pad_maximum_fusion.1.own0), channel_id=1, source_target_pairs={{0,16},{1,17},{2,18},{3,19},{4,20},{5,21},{6,22},{7,23},{8,24},{9,... | collective-permute-start | bytes 4669448 | tf_op jit(solution)/shard_map/ppermute | solution.py:869
  199.3 25.4 %collective-permute-start.31 = (bf16[6144,128]{1,0:T(8,128)(2,1)S(1)}, bf16[6144,128]{1,0:T(8,128)(2,1)}, u32[]{:S(2)}, u32[]{:S(2)}) collective-permute-start(bf16[6144,128]{1,0:T(8,128)(2,1)S(1)} %pad_maximum_fusion.own2), channel_id=1, source_target_pairs={{0,1},{1,0},{2,3},{3,2},{4,5},{5,4},{6,7},{7,6},{8,9},{9,8},{10,11... | collective-permute-start | bytes 4718600 | tf_op jit(solution)/shard_map/ppermute | solution.py:869
  204.1 20.6 %collective-permute-start.22 = (bf16[6080,128]{1,0:T(8,128)(2,1)}, bf16[6080,128]{1,0:T(8,128)(2,1)}, u32[]{:S(2)}, u32[]{:S(2)}) collective-permute-start(bf16[6080,128]{1,0:T(8,128)(2,1)} %pad_maximum_fusion.2.own1), channel_id=1, source_target_pairs={{0,4},{1,5},{2,6},{3,7},{4,0},{5,1},{6,2},{7,3},{8,12},{9,13},{10,... | collective-permute-start | bytes 4669448 | tf_op jit(solution)/shard_map/ppermute | solution.py:869
  (16 other events, 91.5 us)
